TPU v7x, 32 devices: a whole 2x2x4 slice. The times are simulated.
32 devices in a mesh: tm: 8 (over y, x, core), dp: 4 (over z).
Axes of the slice: x: 2, y: 2, z: 4, core: 2. Of those that a mesh axis runs over, the one named last changes fastest.
Arguments:
- frames_in: bfloat16 [4, 1024, 1024], P('dp', 'tm'), may hold values from -6 to 6
- valid_frames: int32 [4], P('dp'), may hold values from 512 to 1024, as said below
- kernel: float32 [9, 1024], replicated, may hold values from -2 to 2
- w_qkv: bfloat16 [1024, 3072], replicated, may hold values from -0.1875 to 0.1875
- cotangent: bfloat16 [4, 1024, 1024], P('dp', 'tm'), may hold values from -6 to 6
Outputs:
- attended: bfloat16 [4, 1024, 1024], P('dp', 'tm')
- grad_in: bfloat16 [4, 1024, 1024], P('dp', 'tm')
- qkv_grad: float32 [24, 128, 1024], P('dp', None, 'tm')
Inputs may be any that keep to these rules, and one draw needn't show every extreme that they name: `valid_frames`: valid frames of each recording, counted from its start; some recording has all 1024 and some exactly 512.
All inputs are finite; a program needn't handle non-finite values.
Results may differ from a plain program's by a relative error of at most 0.025.
Values may be sent and summed in bfloat16 or wider, within the bound.
No kernel may reach another device: no remote copies, remote signals or barrier semaphores. Data moves between devices by JAX's collectives and lax.ppermute only.
A program may use at most 64 MiB of HBM per device.

v0:
```python
import jax
import jax.numpy as jnp
from jax import lax
from jax.sharding import PartitionSpec as P

HEADS = 8
HEAD = 128
KERNEL = 9
LEFT = 70


def from_behind(value, axis, steps):
    count = lax.axis_size(axis)
    leading, last = (max(0, -steps), min(count, count - steps))
    return lax.ppermute(value, axis, [(source, source + steps) for source in range(leading, last)])


def conv_rows(extended, taps, count):
    total = jnp.zeros((count, extended.shape[1]), jnp.float32)
    for offset in range(KERNEL):
        total = total + taps[offset] * extended[offset : offset + count]
    return total


def band_pass(queries, keys_ext, vals_ext, grad_out, query_pos, key_pos, count):
    factor = HEAD ** (-0.5)
    offset = query_pos[:, None] - key_pos[None, :]
    allowed = (
        (offset >= 0)
        & (offset <= LEFT)
        & (key_pos[None, :] >= 0)
        & (key_pos[None, :] < count)
        & (query_pos[:, None] < count)
    )
    q_heads = queries.reshape(-1, HEADS, HEAD)
    k_heads = keys_ext.reshape(-1, HEADS, HEAD)
    v_heads = vals_ext.reshape(-1, HEADS, HEAD)
    g_heads = grad_out.reshape(-1, HEADS, HEAD)
    scores = (
        jnp.einsum("fhe,ghe->hfg", q_heads, k_heads, preferred_element_type=jnp.float32) * factor
    )
    raised = jnp.where(allowed[None], jnp.exp(scores), 0.0)
    missing = 1.0 - (query_pos < count).astype(jnp.float32)
    prob = raised / (jnp.sum(raised, axis=-1, keepdims=True) + missing[None, :, None])
    prob_low = prob.astype(jnp.bfloat16)
    attended = jnp.einsum("hfg,ghe->fhe", prob_low, v_heads, preferred_element_type=jnp.float32)
    attended = attended.reshape(queries.shape).astype(jnp.bfloat16)
    grad_prob = jnp.einsum("fhe,ghe->hfg", g_heads, v_heads, preferred_element_type=jnp.float32)
    grad_score = (
        prob * (grad_prob - jnp.sum(prob * grad_prob, axis=-1, keepdims=True)) * factor
    ).astype(jnp.bfloat16)
    grad_query = jnp.einsum(
        "hfg,ghe->fhe", grad_score, k_heads, preferred_element_type=jnp.float32
    ).reshape(queries.shape)
    grad_key = jnp.einsum(
        "hfg,fhe->ghe", grad_score, q_heads, preferred_element_type=jnp.float32
    ).reshape(keys_ext.shape)
    grad_value = jnp.einsum(
        "hfg,fhe->ghe", prob_low, g_heads, preferred_element_type=jnp.float32
    ).reshape(vals_ext.shape)
    return (attended, grad_query, grad_key, grad_value)


def on_device(frames_in, valid_frames, kernel, w_qkv, cotangent):
    record = frames_in[0]
    count = valid_frames[0]
    cot_rec = cotangent[0]
    frames = record.shape[0]
    width = record.shape[1]
    begin = lax.axis_index("tm") * frames
    positions = begin + jnp.arange(frames, dtype=jnp.int32)
    live = (positions < count)[:, None]
    masked = jnp.where(live, record, jnp.zeros_like(record))
    rim = from_behind(masked[frames - (KERNEL - 1) :], "tm", 1)
    extended = jnp.concatenate([rim, masked], axis=0).astype(jnp.float32)
    conv = conv_rows(extended, kernel, frames)
    hidden = (masked.astype(jnp.float32) + jax.nn.silu(conv)).astype(jnp.bfloat16)
    qkv = jnp.dot(hidden, w_qkv, preferred_element_type=jnp.float32).astype(jnp.bfloat16)
    pairs_halo = from_behind(qkv[frames - LEFT :, width:], "tm", 1)
    pairs = jnp.concatenate([pairs_halo, qkv[:, width:]], axis=0)
    grad_out = jnp.where(live, cot_rec, jnp.zeros_like(cot_rec))
    key_pos = begin - LEFT + jnp.arange(frames + LEFT, dtype=jnp.int32)
    attended, grad_query, grad_key, grad_value = band_pass(
        qkv[:, :width], pairs[:, :width], pairs[:, width:], grad_out, positions, key_pos, count
    )
    split = frames - LEFT
    own_key = grad_key[LEFT:]
    own_value = grad_value[LEFT:]
    logistic = jax.nn.sigmoid(conv)
    slope = logistic * (1.0 + conv * (1.0 - logistic))
    first_rows = jnp.concatenate(
        [grad_query[: KERNEL - 1], own_key[: KERNEL - 1], own_value[: KERNEL - 1]], axis=1
    )
    first_rows = lax.optimization_barrier(first_rows.astype(jnp.bfloat16)).astype(jnp.float32)
    outgoing = jnp.concatenate(
        [
            grad_key[:LEFT],
            grad_value[:LEFT],
            first_rows.reshape(3 * (KERNEL - 1), width),
            slope[: KERNEL - 1],
        ],
        axis=0,
    )
    incoming = from_behind(outgoing.astype(jnp.bfloat16), "tm", -1).astype(outgoing.dtype)
    late = jnp.concatenate(
        [
            grad_query[split:],
            own_key[split:] + incoming[:LEFT],
            own_value[split:] + incoming[LEFT : 2 * LEFT],
        ],
        axis=1,
    )
    early = jnp.concatenate([grad_query[:split], own_key[:split], own_value[:split]], axis=1)
    grad_qkv = jnp.concatenate([early, late], axis=0).astype(jnp.bfloat16)
    next_rows = (
        incoming[2 * LEFT : 2 * LEFT + 3 * (KERNEL - 1)]
        .reshape(KERNEL - 1, 3 * width)
        .astype(jnp.bfloat16)
    )
    next_slope = incoming[2 * LEFT + 3 * (KERNEL - 1) :]
    stacked = jnp.concatenate([grad_qkv, next_rows], axis=0)
    all_hidden = lax.dot_general(
        stacked, w_qkv, (((1,), (1,)), ((), ())), preferred_element_type=jnp.float32
    )
    grad_hidden = all_hidden[:frames]
    tail = jnp.concatenate([grad_hidden * slope, all_hidden[frames:] * next_slope], axis=0)
    spread = conv_rows(tail, kernel[::-1], frames)
    grad_in = jnp.where(live, grad_hidden + spread, 0.0).astype(jnp.bfloat16)
    factor = float(lax.axis_size("dp") * lax.axis_size("tm") * frames) ** (-0.5)
    by_time = lax.psum_scatter(
        lax.dot_general(
            hidden, grad_qkv, (((0,), (0,)), ((), ())), preferred_element_type=jnp.float32
        ).astype(jnp.bfloat16),
        "tm",
        scatter_dimension=0,
        tiled=True,
    )
    summed = lax.psum_scatter(by_time, "dp", scatter_dimension=1, tiled=True).astype(jnp.float32)
    qkv_grad = summed.reshape(summed.shape[0], -1, HEAD).transpose(1, 2, 0)
    return (attended[None], grad_in[None], qkv_grad * factor)


def solution(mesh):
    return jax.shard_map(
        on_device,
        mesh=mesh,
        in_specs=(P("dp", "tm", None), P("dp"), P(), P(), P("dp", "tm", None)),
        out_specs=(P("dp", "tm", None), P("dp", "tm", None), P("dp", None, "tm")),
        check_vma=False,
    )
```

profile of v0, /device:TPU:0, one launch (start us, length us, event | category | flops | bytes accessed | tf_op | source)
XLA Modules:
  0.0 151.2 jit_solution(3050105912850048382)
XLA Ops:
  7.9 1.0 bitcast_select_fusion
  8.9 2.4 %collective-permute-start = (bf16[8,1024]{1,0:T(8,128)(2,1)S(1)}, bf16[8,1024]{1,0:T(8,128)(2,1)S(1)}, u32[]{:S(2)}, u32[]{:S(2)}) collective-permute-start(bf16[8,1024]{1,0:T(8,128)(2,1)S(1)} %slice.283), channel_id=1, source_target_pairs={{0,4},{4,8},{8,12},{12,16},{16,20},{20,24},{24,28},{1,5},{5,9},{9,... | collective-permute-start | bytes 49160 | tf_op jit(solution)/shard_map/ppermute | solution.py:15
  11.3 1.1 fusion.95
  12.5 1.0 copy.37
  13.5 0.7 add_multiply_fusion
  14.3 2.0 %copy-done.16 = bf16[1024,3072]{1,0:T(8,128)(2,1)S(1)} copy-done((bf16[1024,3072]{1,0:T(8,128)(2,1)S(1)}, bf16[1024,3072]{1,0:T(8,128)(2,1)}, u32[]{:S(2)}) %copy-start.16) | copy-done | bytes 6291480
  16.3 1.1 convolution_convert_fusion.1
  17.4 4.6 %collective-permute-start.1 = (bf16[70,2048]{1,0:T(8,128)(2,1)S(1)}, bf16[70,2048]{1,0:T(8,128)(2,1)S(1)}, u32[]{:S(2)}, u32[]{:S(2)}) collective-permute-start(bf16[70,2048]{1,0:T(8,128)(2,1)S(1)} %slice.293), channel_id=1, source_target_pairs={{0,4},{4,8},{8,12},{12,16},{16,20},{20,24},{24,28},{1,5},{5,9},{9,... | collective-permute-start | bytes 860168 | tf_op jit(solution)/shard_map/ppermute | solution.py:15
  22.2 0.9 collective-permute-done.1
  23.5 1.3 fusion.96
  24.9 0.4 fusion.66
  25.3 2.8 %fusion.7 = bf16[128,8,128]{2,0,1:T(8,128)(2,1)} fusion(f32[8,128,198]{1,2,0:T(8,128)S(1)} %fusion.66, bf16[198,8,128]{2,1,0:T(8,128)(2,1)} %copy-done.1, f32[8,128,198]{1,2,0:T(8,128)} %get-tuple-element.27, f32[8,128]{1,0:T(8,128)S(1)} %broadcast_add_fusion), kind=kOutput, calls=%fused_computation.21 | convolution fusion | flops 53456068 | bytes 2293760 | tf_op jit(solution)/shard_map/hfg,ghe->fhe/dot_general | solution.py:52
  28.1 2.8 %fusion.98 = (bf16[198,8,128]{2,0,1:T(8,128)(2,1)S(1)}, f32[198,8,128]{2,0,1:T(8,128)}) fusion(f32[8,128,198]{1,2,0:T(8,128)S(1)} %fusion.66, f32[8,128,198]{1,2,0:T(8,128)} %get-tuple-element.27, f32[8,128]{1,0:T(8,128)S(1)} %broadcast_add_fusion, bf16[128,3072]{1,0:T(8,128)(2,1)S(1)} %convolution_convert_fusion.1), kind=kOutput, calls=%fused_computation.157 | convolution fusion | flops 53527748 | bytes 4763648 | tf_op jit(solution)/shard_map/hfg,fhe->ghe/dot_general | solution.py:55
  30.9 0.8 copy-done.2
  31.7 0.9 slice.303
  32.7 2.6 %fusion.97 = (bf16[198,8,128]{2,0,1:T(8,128)(2,1)S(1)}, f32[198,8,128]{2,0,1:T(8,128)}) fusion(f32[8,128,198]{1,2,0:T(8,128)} %get-tuple-element.27, f32[8,128]{1,0:T(8,128)S(1)} %broadcast_add_fusion, bf16[128,8,128]{2,1,0:T(8,128)(2,1)S(1)} %bitcast.93, pred[128]{0:T(512)(128)(4,1)S(1)} %copy-done.12), kind=kOutput, calls=%fused_computation.156 | convolution fusion | flops 52643840 | bytes 2293888 | tf_op jit(solution)/shard_map/hfg,fhe->ghe/dot_general | solution.py:58
  35.6 1.3 collective-permute-start.2
  36.9 1.0 slice.299
  38.0 1.0 slice.302
  39.5 1.0 slice.310
  40.8 1.2 collective-permute-done.2
  42.2 4.5 %convolution_convert_fusion = bf16[1024,3072]{1,0:T(8,128)(2,1)} fusion(bf16[70,1024]{1,0:T(8,128)(2,1)S(1)} %get-tuple-element.16, bf16[70,1024]{1,0:T(8,128)(2,1)S(1)} %get-tuple-element.15, bf16[70,1024]{1,0:T(8,128)(2,1)S(1)} %bitcast.99, bf16[58,3072]{1,0:T(8,128)(2,1)S(1)} %constant_dynamic-update-slice_fusion, f32[128,1024]{1,0:T(8,128)S(1)} %get-tuple-element.10, ...), kind=kOutput, calls=%fused_computation.1 | convolution fusion | flops 812515328 | bytes 7864320 | tf_op jit(solution)/shard_map/dot_general | solution.py:131
  46.8 70.0 %reduce-scatter.3.cloned.1.call-done = bf16[128,3072]{1,0:T(8,128)(2,1)} async-done(((bf16[1024,3072]{1,0:T(8,128)(2,1)}), bf16[128,3072]{1,0:T(8,128)(2,1)}) %reduce-scatter.3.cloned.1.call-update) | async-done | bytes 786448 | tf_op jit(solution)/shard_map/reduce_scatter | solution.py:130
  116.9 1.5 convolution_convert_fusion.3
  118.4 0.9 copy.33
  119.3 5.0 %fusion.12 = f32[136,1024]{1,0:T(8,128)S(1)} fusion(bf16[1024,3072]{1,0:T(8,128)(2,1)} %param.8, bf16[8,3072]{1,0:T(8,128)(2,1)S(1)} %convert_element_type.72, bf16[70,1024]{1,0:T(8,128)(2,1)S(1)} %get-tuple-element.16, bf16[70,1024]{1,0:T(8,128)(2,1)S(1)} %get-tuple-element.15, bf16[70,1024]{1,0:T(8,128)(2,1)S(1)} %bitcast.100, ...), kind=kOutput, calls=%fused_computation.25 | convolution fusion | flops 859815936 | bytes 7684096 | tf_op jit(solution)/shard_map/dot_general | solution.py:122
  124.4 0.2 slice_multiply_fusion.9
  124.6 0.4 copy-done.4
  125.0 1.3 fusion.75
  126.3 16.2 %reduce-scatter.5.cloned.1.call-done = bf16[128,768]{1,0:T(8,128)(2,1)} async-done(((bf16[128,3072]{1,0:T(8,128)(2,1)}), bf16[128,768]{1,0:T(8,128)(2,1)}) %reduce-scatter.5.cloned.1.call-update) | async-done | bytes 196624 | tf_op jit(solution)/shard_map/reduce_scatter | solution.py:138
  142.5 1.0 convert_multiply_fusion
  143.5 0.9 copy.32
  (95 shorter events, 2.1 us)
Async XLA Ops:
  7.2 109.7 %reduce-scatter.3.cloned.1.call-start = ((), (), s32[]{:S(2)}) async-start(), calls=%async_computation.2 | async-start | bytes 7077888 | tf_op jit(solution)/shard_map/reduce_scatter | solution.py:130
  7.9 14.1 %copy-start.11 = (pred[128]{0:T(512)(128)(4,1)}, pred[128]{0:T(512)(128)(4,1)S(1)}, u32[]{:S(2)}) copy-start(pred[128]{0:T(512)(128)(4,1)S(1)} %get-tuple-element.12) | copy-start | bytes 388
  8.9 4.5 %collective-permute-start = (bf16[8,1024]{1,0:T(8,128)(2,1)S(1)}, bf16[8,1024]{1,0:T(8,128)(2,1)S(1)}, u32[]{:S(2)}, u32[]{:S(2)}) collective-permute-start(bf16[8,1024]{1,0:T(8,128)(2,1)S(1)} %slice.283), channel_id=1, source_target_pairs={{0,4},{4,8},{8,12},{12,16},{16,20},{20,24},{24,28},{1,5},{5,9},{9,... | collective-permute-start | bytes 49160 | tf_op jit(solution)/shard_map/ppermute | solution.py:15
  12.4 1.8 %copy-start.3 = (f32[1,1024]{1,0:T(1,128)}, f32[1,1024]{1,0:T(1,128)S(1)}, u32[]{:S(2)}) copy-start(f32[1,1024]{1,0:T(1,128)S(1)} %get-tuple-element.22) | copy-start | bytes 12292
  12.4 1.8 %copy-start.5 = (f32[1,1024]{1,0:T(1,128)}, f32[1,1024]{1,0:T(1,128)S(1)}, u32[]{:S(2)}) copy-start(f32[1,1024]{1,0:T(1,128)S(1)} %get-tuple-element.23) | copy-start | bytes 12292
  12.4 1.8 %copy-start.7 = (f32[1,1024]{1,0:T(1,128)}, f32[1,1024]{1,0:T(1,128)S(1)}, u32[]{:S(2)}) copy-start(f32[1,1024]{1,0:T(1,128)S(1)} %get-tuple-element.24) | copy-start | bytes 12292
  12.4 1.8 %copy-start.9 = (f32[1,1024]{1,0:T(1,128)}, f32[1,1024]{1,0:T(1,128)S(1)}, u32[]{:S(2)}) copy-start(f32[1,1024]{1,0:T(1,128)S(1)} %get-tuple-element.25) | copy-start | bytes 12292
  13.5 2.8 %copy-start.16 = (bf16[1024,3072]{1,0:T(8,128)(2,1)S(1)}, bf16[1024,3072]{1,0:T(8,128)(2,1)}, u32[]{:S(2)}) copy-start(bf16[1024,3072]{1,0:T(8,128)(2,1)} %param.8) | copy-start | bytes 18874372
  17.4 5.7 %collective-permute-start.1 = (bf16[70,2048]{1,0:T(8,128)(2,1)S(1)}, bf16[70,2048]{1,0:T(8,128)(2,1)S(1)}, u32[]{:S(2)}, u32[]{:S(2)}) collective-permute-start(bf16[70,2048]{1,0:T(8,128)(2,1)S(1)} %slice.293), channel_id=1, source_target_pairs={{0,4},{4,8},{8,12},{12,16},{16,20},{20,24},{24,28},{1,5},{5,9},{9,... | collective-permute-start | bytes 860168 | tf_op jit(solution)/shard_map/ppermute | solution.py:15
  23.4 1.4 copy-start.1
  23.4 1.4 copy-start.12
  24.8 7.8 %copy-start.14 = (f32[8,128]{1,0:T(8,128)}, f32[8,128]{1,0:T(8,128)S(1)}, u32[]{:S(2)}) copy-start(f32[8,128]{1,0:T(8,128)S(1)} %broadcast_add_fusion) | copy-start | bytes 12292
  30.9 0.8 copy-start.2
  32.7 2.6 %copy-start = (bf16[128,8,128]{2,0,1:T(8,128)(2,1)S(1)}, bf16[128,8,128]{2,0,1:T(8,128)(2,1)}, u32[]{:S(2)}) copy-start(bf16[128,8,128]{2,0,1:T(8,128)(2,1)} %fusion.7) | copy-start | bytes 786436
  35.6 6.5 %collective-permute-start.2 = (bf16[172,1024]{1,0:T(8,128)(2,1)S(1)}, bf16[172,1024]{1,0:T(8,128)(2,1)S(1)}, u32[]{:S(2)}, u32[]{:S(2)}) collective-permute-start(bf16[172,1024]{1,0:T(8,128)(2,1)S(1)} %pad_maximum_fusion.2), channel_id=1, source_target_pairs={{4,0},{8,4},{12,8},{16,12},{20,16},{24,20},{28,24},{5,1},{9,5},{13... | collective-permute-start | bytes 1056776 | tf_op jit(solution)/shard_map/ppermute | solution.py:15
  37.9 1.4 slice-start
  46.8 70.1 %copy-start.15 = (f32[8,128]{1,0:T(8,128)S(1)}, f32[8,128]{1,0:T(8,128)}, u32[]{:S(2)}) copy-start(f32[8,128]{1,0:T(8,128)} %copy-done.14) | copy-start | bytes 12292
  46.8 95.8 %reduce-scatter.5.cloned.1.call-start = ((), (), s32[]{:S(2)}) async-start(), calls=%async_computation.3 | async-start | bytes 983040 | tf_op jit(solution)/shard_map/reduce_scatter | solution.py:138
  124.3 0.7 copy-start.4
  124.3 0.7 copy-start.6
  124.3 0.7 copy-start.8
  124.3 0.7 copy-start.10
  124.3 0.7 copy-start.13
Sparse Core Ops, SparseCore 0:
  46.9 69.8 reduce-scatter.2
  119.2 23.2 reduce-scatter.4
where the time goes:
time: 152 us; the launch traced here: 151 us
  waiting for transfers between devices  88.4 us (58%)
  matrix products  22 us (14%)
  between operations  15.4 us (10%)
  local copies, waits for them, and re-layouts  12.3 us (8%)
  starting transfers between devices  8.28 us (5%)
  other arithmetic  4.78 us (3%)
    reduce_scatter x1, waiting for transfers between devices, on_device(): lax.psum_scatter(lax.dot_general(hidden, grad_qkv, (((0,), (0,)), ((), ()...  70 us
    reduce_scatter x1, waiting for transfers between devices, on_device(): lax.psum_scatter(by_time, 'dp', scatter_dimension=1, tiled=True)  16.2 us
    ppermute x3, starting transfers between devices, from_behind(): lax.ppermute(value, axis, [(source, source + steps) for source in range(l...  8.2 us
    unnamed x56, local copies, waits for them, and re-layouts  5.65 us
    dot_general x1, matrix products, on_device(): lax.dot_general(stacked, w_qkv, (((1,), (1,)), ((), ())), preferred_eleme...  5.01 us
    dot_general x1, matrix products, on_device(): lax.dot_general(hidden, grad_qkv, (((0,), (0,)), ((), ())), preferred_ele...  4.53 us
  transfers between devices with their start and end apart: 5, of which 4 were waited for; matrix products, arithmetic and copies ran while one was open for 10% of the time, Pallas kernels for 0%

commit v1 on v0

v1 whole, which is shorter than its diff:
```python
import functools

import jax
import jax.numpy as jnp
from jax import lax
from jax.experimental import pallas as pl
from jax.experimental.pallas import tpu as pltpu
from jax.sharding import PartitionSpec as P

HEADS = 8
HEAD = 128
KERNEL = 9
LEFT = 70
HALO = 80
EDGE = 16
MIB = 1024 * 1024
F32 = jnp.float32
BF16 = jnp.bfloat16


def params(mib):
    return pltpu.CompilerParams(vmem_limit_bytes=mib * MIB)


def vmem(count):
    return [pl.BlockSpec(memory_space=pltpu.VMEM)] * count


def cost(flops, moved):
    return pl.CostEstimate(flops=flops, bytes_accessed=moved, transcendentals=0)


def dot(a, b, left, right):
    return lax.dot_general(a, b, (((left,), (right,)), ((), ())), preferred_element_type=F32)


def project_kernel(place, prev, own, after, taps, w, hidden_out, conv_out, qkv, ext, hidden):
    frames, width = own.shape
    rows = frames + 2 * HALO
    begin, count = place[0], place[1]
    position = begin - HALO + lax.broadcasted_iota(jnp.int32, (rows, 128), 0)
    live = position < count
    for col in range(0, width, 128):
        cols = pl.ds(col, 128)
        raw = jnp.concatenate([prev[:, cols], own[:, cols], after[:HALO, cols]], axis=0)
        masked = jnp.where(live, raw.astype(F32), 0.0)
        ext[: KERNEL - 1, cols] = jnp.zeros((KERNEL - 1, 128), F32)
        ext[KERNEL - 1 :, cols] = masked
        conv = taps[0:1, cols] * ext[0:rows, cols]
        for tap in range(1, KERNEL):
            conv = conv + taps[tap : tap + 1, cols] * ext[tap : tap + rows, cols]
        conv_out[:, cols] = conv[HALO : HALO + frames + EDGE]
        hidden[:, cols] = (masked + conv / (1.0 + jnp.exp(-conv))).astype(BF16)
    hidden_out[...] = hidden[HALO : HALO + frames]
    for col in range(0, 3 * width, 512):
        cols = pl.ds(col, 512)
        low = HALO if col < width else 0
        qkv[low:rows, cols] = dot(hidden[low:], w[:, cols], 1, 0).astype(BF16)
    qkv[rows:, :] = jnp.zeros((qkv.shape[0] - rows, 3 * width), BF16)


def attend_kernel(place, qkv, cot, after, attended, grads, sends, later):
    frames, width = cot.shape
    span = frames + HALO
    begin, count, chip = place[0], place[1], place[2]

    def mask(shift, wanted):
        key = lax.broadcasted_iota(jnp.int32, (span, frames), 0)
        query = lax.broadcasted_iota(jnp.int32, (span, frames), 1)
        first = begin if shift else begin + frames
        gap = query + (HALO if shift else frames) - key
        seen = first + query - gap
        alive = (first + query < count) & (query < wanted)
        allowed = (gap >= 0) & (gap <= LEFT) & (seen >= 0) & alive
        return allowed, jnp.where(alive[:1], 0.0, 1.0)

    masks = [mask(True, frames), mask(False, HALO)]
    row = lax.broadcasted_iota(jnp.int32, (frames, width), 0)
    later[:HALO] = jnp.where(
        begin + frames + row[:HALO] < count, after[HALO:], jnp.zeros((HALO, width), BF16)
    )
    later[HALO:] = jnp.zeros((frames - HALO, width), BF16)
    factor = HEAD**-0.5

    def band(query, key, value, grad, allowed, missing):
        raised = jnp.where(allowed, jnp.exp(dot(key, query, 1, 1) * factor), 0.0)
        prob = raised * (1.0 / (jnp.sum(raised, axis=0, keepdims=True) + missing))
        grad_prob = dot(value, grad, 1, 1)
        mean = jnp.sum(prob * grad_prob, axis=0, keepdims=True)
        return prob.astype(BF16), (prob * (grad_prob - mean) * factor).astype(BF16)

    own_live = begin + lax.broadcasted_iota(jnp.int32, (frames, HEAD), 0) < count
    for head in range(HEADS):
        q_cols = pl.ds(head * HEAD, HEAD)
        k_cols = pl.ds(width + head * HEAD, HEAD)
        v_cols = pl.ds(2 * width + head * HEAD, HEAD)
        query = qkv[HALO : HALO + frames, q_cols]
        query_b = qkv[HALO + frames : HALO + 2 * frames, q_cols]
        key = qkv[: HALO + span, k_cols]
        value = qkv[: HALO + span, v_cols]
        grad = jnp.where(own_live, cot[:, q_cols], jnp.zeros((frames, HEAD), BF16))
        grad_b = later[:, q_cols]
        prob, score = band(query, key[:span], value[:span], grad, *masks[0])
        prob_b, score_b = band(query_b, key[HALO:], value[HALO:], grad_b, *masks[1])
        attended[:, q_cols] = dot(prob, value[:span], 0, 0).astype(BF16)
        grads[:frames, q_cols] = dot(score, key[:span], 0, 0).astype(BF16)
        grads[frames:, q_cols] = dot(score_b, key[HALO:], 0, 0)[:EDGE].astype(BF16)
        for cols, mine, here, theirs, there in (
            (k_cols, score, query, score_b, query_b),
            (v_cols, prob, grad, prob_b, grad_b),
        ):
            total = dot(theirs[: frames + EDGE], there, 1, 0)
            grads[:frames, cols] = (total[:frames] + dot(mine[HALO:], here, 1, 0)).astype(BF16)
            grads[frames:, cols] = total[frames:].astype(BF16)
    if sends is None:
        return
    for k in range(4):
        slot = chip ^ k
        for i in range(4):
            block = 6 * i + k + (k + 1) // 2
            sends[slot, :, i * HEAD : (i + 1) * HEAD] = grads[:frames, pl.ds(block * HEAD, HEAD)]
        side = (k % 2) * (HEAD // 2)
        for pair in range(2):
            halves = []
            for i in (2 * pair, 2 * pair + 1):
                start = (6 * i + 1 + 3 * (k // 2)) * HEAD + side
                halves.append(grads[:frames, start : start + HEAD // 2])
            at = (4 + pair) * HEAD
            sends[slot, :, at : at + HEAD] = jnp.concatenate(halves, axis=1)


def attend_alone(place, qkv, cot, after, attended, grads, later):
    attend_kernel(place, qkv, cot, after, attended, grads, None, later)


def input_grad_kernel(place, grads, w, conv, taps, grad_in, slopes):
    frames, width = grad_in.shape
    begin, count = place[0], place[1]
    live = begin + lax.broadcasted_iota(jnp.int32, (frames, 256), 0) < count
    for col in range(0, width, 256):
        cols = pl.ds(col, 256)
        grad_hidden = dot(grads[...], w[cols, :], 1, 1)
        value = conv[:, cols]
        logistic = 1.0 / (1.0 + jnp.exp(-value))
        slopes[:, cols] = grad_hidden * (logistic * (1.0 + value * (1.0 - logistic)))
        total = grad_hidden[:frames]
        for tap in range(KERNEL):
            low = KERNEL - 1 - tap
            total = total + taps[tap : tap + 1, cols] * slopes[low : low + frames, cols]
        grad_in[:, cols] = jnp.where(live, total, 0.0).astype(BF16)


def weight_kernel(place, a0, a1, a2, a3, b, b1, b2, b3, send, keep):
    core = place[3]
    left = jnp.concatenate([b[0], b1[...], b2[...], b3[...]], axis=0)
    for k in range(4):
        for out, parity in ((send, 1 - core), (keep, core)):
            cols = pl.ds(pl.multiple_of((2 * k + parity) * HEAD, HEAD), HEAD)
            right = jnp.concatenate([a[:, cols] for a in (a0, a1, a2, a3)], axis=0)
            out[:, k * HEAD : (k + 1) * HEAD] = dot(left, right, 0, 0).astype(out.dtype)


def core_sum_kernel(place, keep, got, own, sends):
    me = place[4]
    whole, half = HEAD, HEAD // 2
    for i in range(4):
        one = keep[i * whole : (i + 1) * whole] + got[i * whole : (i + 1) * whole].astype(F32)
        rows = pl.ds(4 * whole + i * half, half)
        two = keep[rows] + got[rows].astype(F32)
        sends[i ^ me, :whole] = one.astype(BF16)
        sends[i ^ me, whole:] = two.astype(BF16)

        @pl.when(i == me)
        def _():
            own[:whole] = one
            own[whole:] = two


def part_sum_kernel(place, own, g1, g2, g3, sends):
    chip = place[2]
    for k in range(4):
        cols = pl.ds(k * HEAD, HEAD)
        total = own[:, cols] + g1[:, cols].astype(F32)
        total = total + (g2[:, cols].astype(F32) + g3[:, cols].astype(F32))
        sends[k ^ chip] = total.astype(BF16)


def place_kernel(scale, place, own, g1, g2, g3, out):
    chip = place[2]
    for slot, ref in enumerate((own.at[0], g1, g2, g3)):
        k = chip ^ slot
        value = ref[...].astype(F32) * scale
        out[k + (k + 1) // 2] = value[:HEAD]
        start = pl.multiple_of((k % 2) * (HEAD // 2), HEAD // 2)
        out[1 + 3 * (k // 2), pl.ds(start, HEAD // 2)] = value[HEAD:]


def call(kernel, name, outs, place, operands, scratch=(), mib=16, flops=1000000, moved=1000000):
    return pl.pallas_call(
        kernel,
        name=name,
        out_shape=[jax.ShapeDtypeStruct(shape, dtype) for shape, dtype in outs],
        in_specs=[pl.BlockSpec(memory_space=pltpu.SMEM)] + vmem(len(operands)),
        out_specs=vmem(len(outs)),
        scratch_shapes=[pltpu.VMEM(shape, dtype) for shape, dtype in scratch],
        compiler_params=params(mib),
        cost_estimate=cost(flops, moved),
    )(place, *operands)


def shift(value, axis, steps):
    count = lax.axis_size(axis)
    pairs = [(i, i + steps) for i in range(count) if 0 <= i + steps < count]
    return lax.ppermute(value, axis, pairs)


def swap(value, axis, mask):
    return lax.ppermute(value, axis, [(i, i ^ mask) for i in range(lax.axis_size(axis))])


def on_device(frames_in, valid_frames, kernel, w_qkv, cotangent):
    record, cot = frames_in[0], cotangent[0]
    frames, width = record.shape
    span = frames + HALO
    parts, recs = lax.axis_size("tm"), lax.axis_size("dp")
    me = lax.axis_index("tm")
    place = jnp.stack(
        [me * frames, valid_frames[0], me // 2, me % 2, lax.axis_index("dp")]
    ).astype(jnp.int32)
    before = shift(record[frames - HALO :], "tm", 1)
    after = shift(jnp.concatenate([record[:HALO], cot[:HALO]], axis=0), "tm", -1)
    rows = span + HALO
    hidden, conv, qkv = call(
        project_kernel,
        "project",
        [
            ((frames, width), BF16),
            ((frames + EDGE, width), F32),
            ((HALO + 2 * frames, 3 * width), BF16),
        ],
        place,
        [before, record, after, kernel, w_qkv],
        [((rows + KERNEL - 1, width), F32), ((rows, width), BF16)],
        mib=24,
        flops=rows * width * 3 * width * 2,
        moved=9000000,
    )
    split = parts == 8 and recs == 4
    if split:
        peers = [swap(hidden, "tm", mask) for mask in (2, 4, 6)]
    outs = [((frames, width), BF16), ((frames + EDGE, 3 * width), BF16)]
    attended, grads, *sends = call(
        attend_kernel if split else attend_alone,
        "attend",
        outs + [((4, frames, 3 * width // 4), BF16)] * split,
        place,
        [qkv, cot, after],
        [((frames, width), BF16)],
        mib=16,
        flops=8 * 12 * span * 128 * 128 * 2 * 8,
        moved=5000000,
    )
    if split:
        sends = sends[0]
        got = [swap(sends[slot], "tm", 2 * slot) for slot in (1, 2, 3)]
    (grad_in,) = call(
        input_grad_kernel,
        "input_grad",
        [((frames, width), BF16)],
        place,
        [grads, w_qkv, conv, kernel],
        [((frames + EDGE, width), F32)],
        mib=20,
        flops=(frames + EDGE) * width * 3 * width * 2,
        moved=9000000,
    )
    scale = float(recs * parts * frames) ** (-0.5)
    if split:
        cols = 3 * width // 4
        shard = cols // 4
        send, keep = call(
            weight_kernel,
            "weight_grad",
            [((cols, width // 2), BF16), ((cols, width // 2), F32)],
            place,
            [hidden, *peers, sends, *got],
            mib=20,
            flops=cols * width * frames * 8,
            moved=6000000,
        )
        sibling = swap(send, "tm", 1)
        own, shards = call(
            core_sum_kernel,
            "core_sum",
            [((shard, width // 2), F32), ((4, shard, width // 2), BF16)],
            place,
            [keep, sibling],
        )
        others = [swap(shards[mask], "dp", mask) for mask in (1, 2, 3)]
        (blocks,) = call(
            part_sum_kernel,
            "part_sum",
            [((4, shard, HEAD), BF16)],
            place,
            [own, *others],
        )
        last = [swap(blocks[slot], "tm", 2 * slot) for slot in (1, 2, 3)]
        (qkv_grad,) = call(
            functools.partial(place_kernel, scale),
            "place",
            [((3 * HEADS // 4, HEAD, HEAD), F32)],
            place,
            [blocks, *last],
        )
    else:
        partial = dot(hidden, grads[:frames], 0, 0).astype(BF16)
        by_time = lax.psum_scatter(partial, "tm", scatter_dimension=0, tiled=True)
        summed = lax.psum_scatter(by_time, "dp", scatter_dimension=1, tiled=True).astype(F32)
        qkv_grad = summed.reshape(summed.shape[0], -1, HEAD).transpose(1, 2, 0) * scale
    return (attended[None], grad_in[None], qkv_grad)


def solution(mesh):
    return jax.shard_map(
        on_device,
        mesh=mesh,
        in_specs=(P("dp", "tm", None), P("dp"), P(), P(), P("dp", "tm", None)),
        out_specs=(P("dp", "tm", None), P("dp", "tm", None), P("dp", None, "tm")),
        check_vma=False,
    )
```

time: 152 us -> 85.8 us (0.56)
  waiting for transfers between devices: 88.4 us -> 35.2 us
  matrix products: 22 us -> 0 us
  Pallas kernels: 0 us -> 18.2 us
  starting transfers between devices: 8.28 us -> 24.7 us
  between operations: 15.4 us -> 1.42 us
  local copies, waits for them, and re-layouts: 12.3 us -> 5.88 us
  other arithmetic: 4.78 us -> 0.02 us
    reduce_scatter x2 -> x0, waiting for transfers between devices: 86.2 us -> none  [the longest x1 70 us: on_device(): lax.psum_scatter(lax.dot_general(hidden, grad_qkv, (((0,), (0,)), ((), ()...]
    ppermute x3 -> x15, waiting for transfers between devices: 2.18 us -> 35.2 us  [the longest x13 35 us: swap(): lax.ppermute(value, axis, [(i, i ^ mask) for i in range(lax.axis_size(axi...]
    dot_general x9 -> x0, matrix products: 22 us -> none  [the longest x1 5.01 us: on_device(): lax.dot_general(stacked, w_qkv, (((1,), (1,)), ((), ())), preferred_eleme...]
    pallas_call x0 -> x7, Pallas kernels: none -> 18.2 us  [call(): pl.pallas_call(kernel, name=name, out_shape=[jax.ShapeDtypeStruct(shape,...]
    ppermute x3 -> x15, starting transfers between devices: 8.2 us -> 24.7 us  [the longest x13 20.4 us: swap(): lax.ppermute(value, axis, [(i, i ^ mask) for i in range(lax.axis_size(axi...]
    slice x26 -> x1, local copies, waits for them, and re-layouts: 5.65 us -> 1.11 us  [on_device(): record[:HALO]]
    mul x4 -> x0, other arithmetic: 1.85 us -> none  [the longest x1 0.95 us: on_device(): return (attended[None], grad_in[None], qkv_grad * factor)]
    unnamed x56 -> x14, local copies, waits for them, and re-layouts: 5.65 us -> 4.59 us
  transfers between devices with their start and end apart: 5 -> 15, of which waited for: 4 -> 7; matrix products, arithmetic and copies ran while one was open for 10% -> 0% of each run, Pallas kernels for 0% -> 5%
where the time goes in v1:
time: 85.8 us; the launch traced here: 85.5 us
  waiting for transfers between devices  35.2 us (41%)
  starting transfers between devices  24.7 us (29%)
  Pallas kernels  18.2 us (21%)
  local copies, waits for them, and re-layouts  5.88 us (7%)
  between operations  1.42 us (2%)
    ppermute x13, waiting for transfers between devices, swap(): lax.ppermute(value, axis, [(i, i ^ mask) for i in range(lax.axis_size(axi...  35 us
    ppermute x13, starting transfers between devices, swap(): lax.ppermute(value, axis, [(i, i ^ mask) for i in range(lax.axis_size(axi...  20.4 us
    pallas_call x7, Pallas kernels, call(): pl.pallas_call(kernel, name=name, out_shape=[jax.ShapeDtypeStruct(shape,...  18.2 us
    unnamed x14, local copies, waits for them, and re-layouts  4.59 us
    ppermute x2, starting transfers between devices, shift(): return lax.ppermute(value, axis, pairs)  4.33 us
  transfers between devices with their start and end apart: 15, of which 7 were waited for; matrix products, arithmetic and copies ran while one was open for 0% of the time, Pallas kernels for 5%

profile of v1, /device:TPU:0, one launch (start us, length us, event | category | flops | bytes accessed | tf_op | source)
XLA Modules:
  0.0 85.5 jit_solution(415679496768732761)
XLA Ops:
  0.6 1.1 %slice_bitcast_fusion.7 = (bf16[80,1024]{1,0:T(8,128)(2,1)S(1)}, bf16[80,1024]{1,0:T(8,128)(2,1)S(1)}, bf16[80,1024]{1,0:T(8,128)(2,1)S(1)}) fusion(bf16[1,128,1024]{2,1,0:T(8,128)(2,1)} %param.5, bf16[1,128,1024]{2,1,0:T(8,128)(2,1)} %param.9), kind=kLoop, calls=%fused_computation.8 | loop fusion | bytes 983040 | tf_op jit(solution)/shard_map/slice | solution.py:231
  1.8 1.3 %collective-permute-start.1 = (bf16[160,1024]{1,0:T(8,128)(2,1)S(1)}, bf16[160,1024]{1,0:T(8,128)(2,1)S(1)}, u32[]{:S(2)}, u32[]{:S(2)}) collective-permute-start(bf16[160,1024]{1,0:T(8,128)(2,1)S(1)} %pad_maximum_fusion), channel_id=1, source_target_pairs={{4,0},{8,4},{12,8},{16,12},{20,16},{24,20},{28,24},{5,1},{9,5},{13... | collective-permute-start | bytes 983048 | tf_op jit(solution)/shard_map/ppermute | solution.py:214
  3.1 3.0 %collective-permute-start = (bf16[80,1024]{1,0:T(8,128)(2,1)S(1)}, bf16[80,1024]{1,0:T(8,128)(2,1)S(1)}, u32[]{:S(2)}, u32[]{:S(2)}) collective-permute-start(bf16[80,1024]{1,0:T(8,128)(2,1)S(1)} %get-tuple-element.30), channel_id=1, source_target_pairs={{0,4},{4,8},{8,12},{12,16},{16,20},{20,24},{24,28},{1,5},{5,9},{9,... | collective-permute-start | bytes 491528 | tf_op jit(solution)/shard_map/ppermute | solution.py:214
  6.8 0.1 stack.19.place
  6.9 0.2 collective-permute-done.prev
  7.1 2.8 %copy-done = bf16[1024,3072]{1,0:T(8,128)(2,1)S(1)} copy-done((bf16[1024,3072]{1,0:T(8,128)(2,1)S(1)}, bf16[1024,3072]{1,0:T(8,128)(2,1)}, u32[]{:S(2)}) %copy-start) | copy-done | bytes 6291480
  9.9 0.9 %copy-done.1 = bf16[1,128,1024]{2,1,0:T(8,128)(2,1)S(1)} copy-done((bf16[1,128,1024]{2,1,0:T(8,128)(2,1)S(1)}, bf16[1,128,1024]{2,1,0:T(8,128)(2,1)}, u32[]{:S(2)}) %copy-start.1) | copy-done | bytes 262168
  10.9 0.8 copy-done.2
  11.7 4.1 %project.1 = (bf16[128,1024]{1,0:T(8,128)(2,1)S(1)}, f32[144,1024]{1,0:T(8,128)S(1)}, bf16[336,3072]{1,0:T(8,128)(2,1)S(1)}) custom-call(s32[5]{0:T(128)S(1)} %stack.19.place, bf16[80,1024]{1,0:T(8,128)(2,1)S(1)} %collective-permute-done.prev, bf16[128,1024]{1,0:T(8,128)(2,1)S(1)} %bitcast.34, bf16[160,1024]{1,0:T(8,128)(2,1)S(1)} %collective-permute-done.1.after, ...), custom_call_target="tpu_custom_call" | custom-call | flops 1811939328 | bytes 9000000 | tf_op jit(solution)/shard_map/project/pallas_call | solution.py:199
  15.9 4.7 %attend.1 = (bf16[128,1024]{1,0:T(8,128)(2,1)}, bf16[144,3072]{1,0:T(8,128)(2,1)S(1)}, bf16[4,128,768]{2,1,0:T(8,128)(2,1)S(1)}) custom-call(s32[5]{0:T(128)S(1)} %stack.19.place, bf16[336,3072]{1,0:T(8,128)(2,1)S(1)} %get-tuple-element.13.qkv, bf16[128,1024]{1,0:T(8,128)(2,1)S(1)} %bitcast.35, bf16[160,1024]{1,0:T(8,128)(2,1)S(1)} %collective-permute-done.1.after), custom_call_target="tpu_custom_call" | custom-call | flops 5234491392 | bytes 5000000 | tf_op jit(solution)/shard_map/attend/pallas_call | solution.py:199
  20.6 8.7 %collective-permute-start.7 = (bf16[128,768]{1,0:T(8,128)(2,1)S(1)}, bf16[128,768]{1,0:T(8,128)(2,1)S(1)}, u32[]{:S(2)}, u32[]{:S(2)}) collective-permute-start(bf16[128,768]{1,0:T(8,128)(2,1)S(1)} %get-tuple-element.26), channel_id=1, source_target_pairs={{0,24},{4,28},{8,16},{12,20},{16,8},{20,12},{24,0},{28,4},{1,25},{... | collective-permute-start | bytes 589832 | tf_op jit(solution)/shard_map/ppermute | solution.py:218
  29.3 0.1 collective-permute-start.4
  29.4 2.1 %collective-permute-start.3 = (bf16[128,1024]{1,0:T(8,128)(2,1)S(1)}, bf16[128,1024]{1,0:T(8,128)(2,1)S(1)}, u32[]{:S(2)}, u32[]{:S(2)}) collective-permute-start(bf16[128,1024]{1,0:T(8,128)(2,1)S(1)} %get-tuple-element.17.a0), channel_id=1, source_target_pairs={{0,16},{4,20},{8,24},{12,28},{16,0},{20,4},{24,8},{28,12},{1,17},{... | collective-permute-start | bytes 786440 | tf_op jit(solution)/shard_map/ppermute | solution.py:218
  31.5 1.3 %collective-permute-start.2 = (bf16[128,1024]{1,0:T(8,128)(2,1)S(1)}, bf16[128,1024]{1,0:T(8,128)(2,1)S(1)}, u32[]{:S(2)}, u32[]{:S(2)}) collective-permute-start(bf16[128,1024]{1,0:T(8,128)(2,1)S(1)} %get-tuple-element.17.a0), channel_id=1, source_target_pairs={{0,8},{4,12},{8,0},{12,4},{16,24},{20,28},{24,16},{28,20},{1,9},{5... | collective-permute-start | bytes 786440 | tf_op jit(solution)/shard_map/ppermute | solution.py:218
  32.8 2.4 %collective-permute-done.7.b3 = bf16[128,768]{1,0:T(8,128)(2,1)S(1)} collective-permute-done((bf16[128,768]{1,0:T(8,128)(2,1)S(1)}, bf16[128,768]{1,0:T(8,128)(2,1)S(1)}, u32[]{:S(2)}, u32[]{:S(2)}) %collective-permute-start.7) | collective-permute-done | bytes 196640 | tf_op jit(solution)/shard_map/ppermute | solution.py:218
  35.2 0.1 collective-permute-start.5
  35.4 13.0 %collective-permute-done.6.b2 = bf16[128,768]{1,0:T(8,128)(2,1)S(1)} collective-permute-done((bf16[128,768]{1,0:T(8,128)(2,1)S(1)}, bf16[128,768]{1,0:T(8,128)(2,1)S(1)}, u32[]{:S(2)}, u32[]{:S(2)}) %collective-permute-start.6) | collective-permute-done | bytes 196640 | tf_op jit(solution)/shard_map/ppermute | solution.py:218
  48.4 1.1 %collective-permute-done.5.b1 = bf16[128,768]{1,0:T(8,128)(2,1)S(1)} collective-permute-done((bf16[128,768]{1,0:T(8,128)(2,1)S(1)}, bf16[128,768]{1,0:T(8,128)(2,1)S(1)}, u32[]{:S(2)}, u32[]{:S(2)}) %collective-permute-start.5) | collective-permute-done | bytes 196640 | tf_op jit(solution)/shard_map/ppermute | solution.py:218
  49.4 2.4 %weight_grad.1 = (bf16[768,512]{1,0:T(8,128)(2,1)S(1)}, f32[768,512]{1,0:T(8,128)S(1)}) custom-call(s32[5]{0:T(128)S(1)} %stack.19.place, bf16[128,1024]{1,0:T(8,128)(2,1)S(1)} %get-tuple-element.17.a0, bf16[128,1024]{1,0:T(8,128)(2,1)S(1)} %collective-permute-done.2.a1, bf16[128,1024]{1,0:T(8,128)(2,1)S(1)} %collective-permute-done.3.a2, ...), custom_call_target="tpu_custom_call" | custom-call | flops 805306368 | bytes 6000000 | tf_op jit(solution)/shard_map/weight_grad/pallas_call | solution.py:199
  51.8 0.1 collective-permute-start.8
  51.9 2.3 %collective-permute-done.8.got = bf16[768,512]{1,0:T(8,128)(2,1)S(1)} collective-permute-done((bf16[768,512]{1,0:T(8,128)(2,1)S(1)}, bf16[768,512]{1,0:T(8,128)(2,1)S(1)}, u32[]{:S(2)}, u32[]{:S(2)}) %collective-permute-start.8) | collective-permute-done | bytes 786464 | tf_op jit(solution)/shard_map/ppermute | solution.py:218
  54.1 0.7 core_sum.1
  54.9 3.7 %collective-permute-start.11 = (bf16[192,512]{1,0:T(8,128)(2,1)S(1)}, bf16[192,512]{1,0:T(8,128)(2,1)S(1)}, u32[]{:S(2)}, u32[]{:S(2)}) collective-permute-start(bf16[192,512]{1,0:T(8,128)(2,1)S(1)} %get-tuple-element.23), channel_id=1, source_target_pairs={{0,3},{1,2},{2,1},{3,0},{4,7},{5,6},{6,5},{7,4},{8,11},{9,10},{10,... | collective-permute-start | bytes 589832 | tf_op jit(solution)/shard_map/ppermute | solution.py:218
  58.6 0.8 collective-permute-start.9
  59.4 5.3 %collective-permute-done.11.g3 = bf16[192,512]{1,0:T(8,128)(2,1)S(1)} collective-permute-done((bf16[192,512]{1,0:T(8,128)(2,1)S(1)}, bf16[192,512]{1,0:T(8,128)(2,1)S(1)}, u32[]{:S(2)}, u32[]{:S(2)}) %collective-permute-start.11) | collective-permute-done | bytes 196640 | tf_op jit(solution)/shard_map/ppermute | solution.py:218
  64.7 10.9 %collective-permute-done.10.g2 = bf16[192,512]{1,0:T(8,128)(2,1)S(1)} collective-permute-done((bf16[192,512]{1,0:T(8,128)(2,1)S(1)}, bf16[192,512]{1,0:T(8,128)(2,1)S(1)}, u32[]{:S(2)}, u32[]{:S(2)}) %collective-permute-start.10) | collective-permute-done | bytes 196640 | tf_op jit(solution)/shard_map/ppermute | solution.py:218
  75.6 0.6 part_sum.1.own
  76.2 1.7 %collective-permute-start.14 = (bf16[192,128]{1,0:T(8,128)(2,1)S(1)}, bf16[192,128]{1,0:T(8,128)(2,1)S(1)}, u32[]{:S(2)}, u32[]{:S(2)}) collective-permute-start(bf16[192,128]{1,0:T(8,128)(2,1)S(1)} %get-tuple-element.31), channel_id=1, source_target_pairs={{0,24},{4,28},{8,16},{12,20},{16,8},{20,12},{24,0},{28,4},{1,25},{... | collective-permute-start | bytes 147464 | tf_op jit(solution)/shard_map/ppermute | solution.py:218
  77.9 1.7 %collective-permute-start.13 = (bf16[192,128]{1,0:T(8,128)(2,1)S(1)}, bf16[192,128]{1,0:T(8,128)(2,1)S(1)}, u32[]{:S(2)}, u32[]{:S(2)}) collective-permute-start(bf16[192,128]{1,0:T(8,128)(2,1)S(1)} %get-tuple-element.32), channel_id=1, source_target_pairs={{0,16},{4,20},{8,24},{12,28},{16,0},{20,4},{24,8},{28,12},{1,17},{... | collective-permute-start | bytes 147464 | tf_op jit(solution)/shard_map/ppermute | solution.py:218
  79.7 0.1 collective-permute-start.12
  79.8 4.3 %input_grad.1 = bf16[128,1024]{1,0:T(8,128)(2,1)} custom-call(s32[5]{0:T(128)S(1)} %stack.19.place, bf16[144,3072]{1,0:T(8,128)(2,1)S(1)} %get-tuple-element.15.grads, bf16[1024,3072]{1,0:T(8,128)(2,1)S(1)} %bitcast.33, f32[144,1024]{1,0:T(8,128)S(1)} %get-tuple-element.16.conv, f32[9,1024]{1,0:T(8,128)S(1)} %copy-done.3), custom_call_target="tpu_custom_call" | custom-call | flops 905969664 | bytes 9000000 | tf_op jit(solution)/shard_map/input_grad/pallas_call | solution.py:199
  84.1 1.4 %place.1 = f32[6,128,128]{2,1,0:T(8,128)} custom-call(s32[5]{0:T(128)S(1)} %stack.19.place, bf16[4,192,128]{2,1,0:T(8,128)(2,1)S(1)} %part_sum.1.own, bf16[192,128]{1,0:T(8,128)(2,1)S(1)} %collective-permute-done.12.g1, bf16[192,128]{1,0:T(8,128)(2,1)S(1)} %collective-permute-done.13.g2, bf16[192,128]{1,0:T(8,128)(2,1)S(1)} %collective-permute-done.14.g3), custom_call_target="tpu_custom_call" | custom-call | flops 1000000 | bytes 1000000 | tf_op jit(solution)/shard_map/place/pallas_call | solution.py:199
  (26 shorter events, 0.2 us)
Async XLA Ops:
  1.8 5.4 %collective-permute-start.1 = (bf16[160,1024]{1,0:T(8,128)(2,1)S(1)}, bf16[160,1024]{1,0:T(8,128)(2,1)S(1)}, u32[]{:S(2)}, u32[]{:S(2)}) collective-permute-start(bf16[160,1024]{1,0:T(8,128)(2,1)S(1)} %pad_maximum_fusion), channel_id=1, source_target_pairs={{4,0},{8,4},{12,8},{16,12},{20,16},{24,20},{28,24},{5,1},{9,5},{13... | collective-permute-start | bytes 983048 | tf_op jit(solution)/shard_map/ppermute | solution.py:214
  3.1 4.0 %collective-permute-start = (bf16[80,1024]{1,0:T(8,128)(2,1)S(1)}, bf16[80,1024]{1,0:T(8,128)(2,1)S(1)}, u32[]{:S(2)}, u32[]{:S(2)}) collective-permute-start(bf16[80,1024]{1,0:T(8,128)(2,1)S(1)} %get-tuple-element.30), channel_id=1, source_target_pairs={{0,4},{4,8},{8,12},{12,16},{16,20},{20,24},{24,28},{1,5},{5,9},{9,... | collective-permute-start | bytes 491528 | tf_op jit(solution)/shard_map/ppermute | solution.py:214
  7.1 2.8 %copy-start = (bf16[1024,3072]{1,0:T(8,128)(2,1)S(1)}, bf16[1024,3072]{1,0:T(8,128)(2,1)}, u32[]{:S(2)}) copy-start(bf16[1024,3072]{1,0:T(8,128)(2,1)} %w.3) | copy-start | bytes 18874372
  9.9 0.9 %copy-start.1 = (bf16[1,128,1024]{2,1,0:T(8,128)(2,1)S(1)}, bf16[1,128,1024]{2,1,0:T(8,128)(2,1)}, u32[]{:S(2)}) copy-start(bf16[1,128,1024]{2,1,0:T(8,128)(2,1)} %param.5) | copy-start | bytes 786436
  10.9 0.8 copy-start.2
  11.7 4.1 %copy-start.4 = (bf16[1,128,1024]{2,1,0:T(8,128)(2,1)S(1)}, bf16[1,128,1024]{2,1,0:T(8,128)(2,1)}, u32[]{:S(2)}) copy-start(bf16[1,128,1024]{2,1,0:T(8,128)(2,1)} %param.9) | copy-start | bytes 786436
  11.7 68.1 %slice-start = ((s8[6291456]{0:T(1024)(128)(4,1)}), s8[2097152]{0:T(1024)(128)(4,1)S(1)}, s32[]{:S(2)}) async-start(s8[6291456]{0:T(1024)(128)(4,1)} %bitcast.32), calls=%async_computation | async-start | bytes 4194304
  15.8 64.0 %slice-start.1 = ((s8[6291456]{0:T(1024)(128)(4,1)}), s8[4194304]{0:T(1024)(128)(4,1)S(1)}, s32[]{:S(2)}) async-start(s8[6291456]{0:T(1024)(128)(4,1)} %bitcast.32), calls=%async_computation.1 | async-start | bytes 8388608
  20.6 14.6 %collective-permute-start.7 = (bf16[128,768]{1,0:T(8,128)(2,1)S(1)}, bf16[128,768]{1,0:T(8,128)(2,1)S(1)}, u32[]{:S(2)}, u32[]{:S(2)}) collective-permute-start(bf16[128,768]{1,0:T(8,128)(2,1)S(1)} %get-tuple-element.26), channel_id=1, source_target_pairs={{0,24},{4,28},{8,16},{12,20},{16,8},{20,12},{24,0},{28,4},{1,25},{... | collective-permute-start | bytes 589832 | tf_op jit(solution)/shard_map/ppermute | solution.py:218
  29.3 20.1 %collective-permute-start.4 = (bf16[128,1024]{1,0:T(8,128)(2,1)S(1)}, bf16[128,1024]{1,0:T(8,128)(2,1)S(1)}, u32[]{:S(2)}, u32[]{:S(2)}) collective-permute-start(bf16[128,1024]{1,0:T(8,128)(2,1)S(1)} %get-tuple-element.17.a0), channel_id=1, source_target_pairs={{0,24},{4,28},{8,16},{12,20},{16,8},{20,12},{24,0},{28,4},{1,25},{... | collective-permute-start | bytes 786440 | tf_op jit(solution)/shard_map/ppermute | solution.py:218
  29.4 20.0 %collective-permute-start.3 = (bf16[128,1024]{1,0:T(8,128)(2,1)S(1)}, bf16[128,1024]{1,0:T(8,128)(2,1)S(1)}, u32[]{:S(2)}, u32[]{:S(2)}) collective-permute-start(bf16[128,1024]{1,0:T(8,128)(2,1)S(1)} %get-tuple-element.17.a0), channel_id=1, source_target_pairs={{0,16},{4,20},{8,24},{12,28},{16,0},{20,4},{24,8},{28,12},{1,17},{... | collective-permute-start | bytes 786440 | tf_op jit(solution)/shard_map/ppermute | solution.py:218
  31.5 17.9 %collective-permute-start.2 = (bf16[128,1024]{1,0:T(8,128)(2,1)S(1)}, bf16[128,1024]{1,0:T(8,128)(2,1)S(1)}, u32[]{:S(2)}, u32[]{:S(2)}) collective-permute-start(bf16[128,1024]{1,0:T(8,128)(2,1)S(1)} %get-tuple-element.17.a0), channel_id=1, source_target_pairs={{0,8},{4,12},{8,0},{12,4},{16,24},{20,28},{24,16},{28,20},{1,9},{5... | collective-permute-start | bytes 786440 | tf_op jit(solution)/shard_map/ppermute | solution.py:218
  32.8 15.5 %collective-permute-start.6 = (bf16[128,768]{1,0:T(8,128)(2,1)S(1)}, bf16[128,768]{1,0:T(8,128)(2,1)S(1)}, u32[]{:S(2)}, u32[]{:S(2)}) collective-permute-start(bf16[128,768]{1,0:T(8,128)(2,1)S(1)} %get-tuple-element.27), channel_id=1, source_target_pairs={{0,16},{4,20},{8,24},{12,28},{16,0},{20,4},{24,8},{28,12},{1,17},{... | collective-permute-start | bytes 589832 | tf_op jit(solution)/shard_map/ppermute | solution.py:218
  35.2 14.2 %collective-permute-start.5 = (bf16[128,768]{1,0:T(8,128)(2,1)S(1)}, bf16[128,768]{1,0:T(8,128)(2,1)S(1)}, u32[]{:S(2)}, u32[]{:S(2)}) collective-permute-start(bf16[128,768]{1,0:T(8,128)(2,1)S(1)} %get-tuple-element.28), channel_id=1, source_target_pairs={{0,8},{4,12},{8,0},{12,4},{16,24},{20,28},{24,16},{28,20},{1,9},{5... | collective-permute-start | bytes 589832 | tf_op jit(solution)/shard_map/ppermute | solution.py:218
  51.8 2.4 %collective-permute-start.8 = (bf16[768,512]{1,0:T(8,128)(2,1)S(1)}, bf16[768,512]{1,0:T(8,128)(2,1)S(1)}, u32[]{:S(2)}, u32[]{:S(2)}) collective-permute-start(bf16[768,512]{1,0:T(8,128)(2,1)S(1)} %get-tuple-element.20), channel_id=1, source_target_pairs={{0,4},{4,0},{8,12},{12,8},{16,20},{20,16},{24,28},{28,24},{1,5},{5... | collective-permute-start | bytes 2359304 | tf_op jit(solution)/shard_map/ppermute | solution.py:218
  54.1 25.7 %copy-start.3 = (f32[9,1024]{1,0:T(8,128)S(1)}, f32[9,1024]{1,0:T(8,128)}, u32[]{:S(2)}) copy-start(f32[9,1024]{1,0:T(8,128)} %taps.3) | copy-start | bytes 110596
  54.9 9.7 %collective-permute-start.11 = (bf16[192,512]{1,0:T(8,128)(2,1)S(1)}, bf16[192,512]{1,0:T(8,128)(2,1)S(1)}, u32[]{:S(2)}, u32[]{:S(2)}) collective-permute-start(bf16[192,512]{1,0:T(8,128)(2,1)S(1)} %get-tuple-element.23), channel_id=1, source_target_pairs={{0,3},{1,2},{2,1},{3,0},{4,7},{5,6},{6,5},{7,4},{8,11},{9,10},{10,... | collective-permute-start | bytes 589832 | tf_op jit(solution)/shard_map/ppermute | solution.py:218
  58.6 17.0 %collective-permute-start.10 = (bf16[192,512]{1,0:T(8,128)(2,1)S(1)}, bf16[192,512]{1,0:T(8,128)(2,1)S(1)}, u32[]{:S(2)}, u32[]{:S(2)}) collective-permute-start(bf16[192,512]{1,0:T(8,128)(2,1)S(1)} %get-tuple-element.24), channel_id=1, source_target_pairs={{0,2},{1,3},{2,0},{3,1},{4,6},{5,7},{6,4},{7,5},{8,10},{9,11},{10,... | collective-permute-start | bytes 589832 | tf_op jit(solution)/shard_map/ppermute | solution.py:218
  58.6 17.0 %collective-permute-start.9 = (bf16[192,512]{1,0:T(8,128)(2,1)S(1)}, bf16[192,512]{1,0:T(8,128)(2,1)S(1)}, u32[]{:S(2)}, u32[]{:S(2)}) collective-permute-start(bf16[192,512]{1,0:T(8,128)(2,1)S(1)} %get-tuple-element.25), channel_id=1, source_target_pairs={{0,1},{1,0},{2,3},{3,2},{4,5},{5,4},{6,7},{7,6},{8,9},{9,8},{10,11... | collective-permute-start | bytes 589832 | tf_op jit(solution)/shard_map/ppermute | solution.py:218
  76.2 7.9 %collective-permute-start.14 = (bf16[192,128]{1,0:T(8,128)(2,1)S(1)}, bf16[192,128]{1,0:T(8,128)(2,1)S(1)}, u32[]{:S(2)}, u32[]{:S(2)}) collective-permute-start(bf16[192,128]{1,0:T(8,128)(2,1)S(1)} %get-tuple-element.31), channel_id=1, source_target_pairs={{0,24},{4,28},{8,16},{12,20},{16,8},{20,12},{24,0},{28,4},{1,25},{... | collective-permute-start | bytes 147464 | tf_op jit(solution)/shard_map/ppermute | solution.py:218
  77.9 6.2 %collective-permute-start.13 = (bf16[192,128]{1,0:T(8,128)(2,1)S(1)}, bf16[192,128]{1,0:T(8,128)(2,1)S(1)}, u32[]{:S(2)}, u32[]{:S(2)}) collective-permute-start(bf16[192,128]{1,0:T(8,128)(2,1)S(1)} %get-tuple-element.32), channel_id=1, source_target_pairs={{0,16},{4,20},{8,24},{12,28},{16,0},{20,4},{24,8},{28,12},{1,17},{... | collective-permute-start | bytes 147464 | tf_op jit(solution)/shard_map/ppermute | solution.py:218
  79.7 4.5 %collective-permute-start.12 = (bf16[192,128]{1,0:T(8,128)(2,1)S(1)}, bf16[192,128]{1,0:T(8,128)(2,1)S(1)}, u32[]{:S(2)}, u32[]{:S(2)}) collective-permute-start(bf16[192,128]{1,0:T(8,128)(2,1)S(1)} %get-tuple-element.33), channel_id=1, source_target_pairs={{0,8},{4,12},{8,0},{12,4},{16,24},{20,28},{24,16},{28,20},{1,9},{5... | collective-permute-start | bytes 147464 | tf_op jit(solution)/shard_map/ppermute | solution.py:218

commit v2 on v1

--- a/solution.py
+++ b/solution.py
@@ -34,24 +34,74 @@
     return lax.dot_general(a, b, (((left,), (right,)), ((), ())), preferred_element_type=F32)
 
 
-def project_kernel(place, prev, own, after, taps, w, hidden_out, conv_out, qkv, ext, hidden):
+def conv_hidden(ext, taps, cols, low, rows, masked):
+    conv = taps[0:1, cols] * ext[low : low + rows, cols]
+    for tap in range(1, KERNEL):
+        conv = conv + taps[tap : tap + 1, cols] * ext[low + tap : low + tap + rows, cols]
+    return conv, (masked + conv / (1.0 + jnp.exp(-conv))).astype(BF16)
+
+
+def live_rows(first, rows, count):
+    return first + lax.broadcasted_iota(jnp.int32, (rows, 128), 0) < count
+
+
+def own_kernel(
+    place, far_own, far_taps, w, hidden, conv_out, qkv, own, taps, w_out, ext, sems, small
+):
     frames, width = own.shape
-    rows = frames + 2 * HALO
-    begin, count = place[0], place[1]
-    position = begin - HALO + lax.broadcasted_iota(jnp.int32, (rows, 128), 0)
-    live = position < count
+    rows = frames - EDGE
+    arrivals = [
+        pltpu.make_async_copy(source, target, small.at[i])
+        for i, (source, target) in enumerate(((far_own, own), (far_taps, taps)))
+    ]
+    for copy in arrivals:
+        copy.start()
+    copies = [
+        pltpu.make_async_copy(w.at[:, pl.ds(col, 512)], w_out.at[:, pl.ds(col, 512)], sems.at[i])
+        for i, col in enumerate(range(0, 3 * width, 512))
+    ]
+    for copy in copies:
+        copy.start()
+    for copy in arrivals:
+        copy.wait()
+    live = live_rows(place[0], frames, place[1])
     for col in range(0, width, 128):
         cols = pl.ds(col, 128)
-        raw = jnp.concatenate([prev[:, cols], own[:, cols], after[:HALO, cols]], axis=0)
-        masked = jnp.where(live, raw.astype(F32), 0.0)
-        ext[: KERNEL - 1, cols] = jnp.zeros((KERNEL - 1, 128), F32)
-        ext[KERNEL - 1 :, cols] = masked
-        conv = taps[0:1, cols] * ext[0:rows, cols]
-        for tap in range(1, KERNEL):
-            conv = conv + taps[tap : tap + 1, cols] * ext[tap : tap + rows, cols]
-        conv_out[:, cols] = conv[HALO : HALO + frames + EDGE]
-        hidden[:, cols] = (masked + conv / (1.0 + jnp.exp(-conv))).astype(BF16)
-    hidden_out[...] = hidden[HALO : HALO + frames]
+        masked = jnp.where(live, own[:, cols].astype(F32), 0.0)
+        ext[:, cols] = masked
+        conv, low = conv_hidden(ext, taps, cols, EDGE - KERNEL + 1, rows, masked[EDGE:])
+        conv_out[:, cols] = conv
+        hidden[:, cols] = low
+    for i, copy in enumerate(copies):
+        copy.wait()
+        cols = pl.ds(i * 512, 512)
+        qkv[:, cols] = dot(hidden[...], w_out[:, cols], 1, 0).astype(BF16)
+
+
+def rim_kernel(place, prev, own, after, taps, w, first, conv_out, qkv, ext, hidden):
+    frames, width = own.shape
+    begin, count = place[0], place[1]
+    head, back = HALO + EDGE, KERNEL - 1
+    live_a = live_rows(begin - HALO, head, count)
+    live_b = live_rows(begin + frames - back, HALO + back, count)
+    for col in range(0, width, 128):
+        cols = pl.ds(col, 128)
+        raw = jnp.concatenate([prev[:, cols], own[:EDGE, cols]], axis=0).astype(F32)
+        masked = jnp.where(live_a, raw, 0.0)
+        ext[:back, cols] = jnp.zeros((back, 128), F32)
+        ext[back : back + head, cols] = masked
+        conv, low = conv_hidden(ext, taps, cols, 0, head, masked)
+        conv_out[:EDGE, cols] = conv[HALO:]
+        hidden[:head, cols] = low
+        tail = own[frames - EDGE :, cols].astype(F32)[EDGE - back :]
+        raw = jnp.concatenate([tail, after[:HALO, cols].astype(F32)], axis=0)
+        masked = jnp.where(live_b, raw, 0.0)
+        ext[back + head :, cols] = masked
+        conv, low = conv_hidden(ext, taps, cols, back + head, HALO, masked[back:])
+        conv_out[EDGE:, cols] = conv[:EDGE]
+        hidden[head:, cols] = low
+    first[...] = hidden[HALO:head]
+    rows = head + HALO
     for col in range(0, 3 * width, 512):
         cols = pl.ds(col, 512)
         low = HALO if col < width else 0
@@ -59,9 +109,35 @@
     qkv[rows:, :] = jnp.zeros((qkv.shape[0] - rows, 3 * width), BF16)
 
 
-def attend_kernel(place, qkv, cot, after, attended, grads, sends, later):
+def ends_kernel(place, f0, f1, f2, f3, _, out):
+    for slot, ref in enumerate((f0, f1, f2, f3)):
+        out[slot * EDGE : (slot + 1) * EDGE] = ref[ref.shape[0] - EDGE :]
+
+
+def peers_kernel(place, f1, f2, f3, tails, taps, hidden, ext):
+    frames, width = f1.shape
+    count, chip, core = place[1], place[2], place[3]
+    for slot, ref in ((1, f1), (2, f2), (3, f3)):
+        peer = chip ^ slot
+        begin = (2 * peer + core) * frames
+        source = jnp.where(core == 1, slot, chip ^ jnp.maximum(peer - 1, 0))
+        start = pl.multiple_of(source * EDGE, EDGE)
+        live = live_rows(begin - EDGE, frames + EDGE, count)
+        real = begin - EDGE + lax.broadcasted_iota(jnp.int32, (frames + EDGE, 128), 0) >= 0
+        live = live & real
+        for col in range(0, width, 128):
+            cols = pl.ds(col, 128)
+            raw = jnp.concatenate([tails[pl.ds(start, EDGE), cols], ref[:, cols]], axis=0)
+            masked = jnp.where(live, raw.astype(F32), 0.0)
+            ext[:, cols] = masked
+            _, low = conv_hidden(ext, taps, cols, EDGE - KERNEL + 1, frames, masked[EDGE:])
+            hidden[(slot - 1) * frames : slot * frames, cols] = low
+
+
+def attend_kernel(place, rim, mid, cot, after, attended, grads, sends, later):
     frames, width = cot.shape
     span = frames + HALO
+    head_rows = HALO + EDGE
     begin, count, chip = place[0], place[1], place[2]
 
     def mask(shift, wanted):
@@ -94,10 +170,15 @@
         q_cols = pl.ds(head * HEAD, HEAD)
         k_cols = pl.ds(width + head * HEAD, HEAD)
         v_cols = pl.ds(2 * width + head * HEAD, HEAD)
-        query = qkv[HALO : HALO + frames, q_cols]
-        query_b = qkv[HALO + frames : HALO + 2 * frames, q_cols]
-        key = qkv[: HALO + span, k_cols]
-        value = qkv[: HALO + span, v_cols]
+        query = jnp.concatenate([rim[HALO:head_rows, q_cols], mid[:, q_cols]], axis=0)
+        query_b = rim[head_rows:, q_cols]
+        key, value = (
+            jnp.concatenate(
+                [rim[:head_rows, cols], mid[:, cols], rim[head_rows : head_rows + HALO, cols]],
+                axis=0,
+            )
+            for cols in (k_cols, v_cols)
+        )
         grad = jnp.where(own_live, cot[:, q_cols], jnp.zeros((frames, HEAD), BF16))
         grad_b = later[:, q_cols]
         prob, score = band(query, key[:span], value[:span], grad, *masks[0])
@@ -129,18 +210,20 @@
             sends[slot, :, at : at + HEAD] = jnp.concatenate(halves, axis=1)
 
 
-def attend_alone(place, qkv, cot, after, attended, grads, later):
-    attend_kernel(place, qkv, cot, after, attended, grads, None, later)
-
-
-def input_grad_kernel(place, grads, w, conv, taps, grad_in, slopes):
+def attend_alone(place, rim, mid, cot, after, attended, grads, later):
+    attend_kernel(place, rim, mid, cot, after, attended, grads, None, later)
+
+
+def input_grad_kernel(place, grads, w, conv_mid, conv_rim, taps, grad_in, done, slopes):
     frames, width = grad_in.shape
     begin, count = place[0], place[1]
+    done[...] = jnp.zeros(done.shape, F32)
     live = begin + lax.broadcasted_iota(jnp.int32, (frames, 256), 0) < count
     for col in range(0, width, 256):
         cols = pl.ds(col, 256)
         grad_hidden = dot(grads[...], w[cols, :], 1, 1)
-        value = conv[:, cols]
+        rim = conv_rim[:, cols]
+        value = jnp.concatenate([rim[:EDGE], conv_mid[:, cols], rim[EDGE:]], axis=0)
         logistic = 1.0 / (1.0 + jnp.exp(-value))
         slopes[:, cols] = grad_hidden * (logistic * (1.0 + value * (1.0 - logistic)))
         total = grad_hidden[:frames]
@@ -150,38 +233,39 @@
         grad_in[:, cols] = jnp.where(live, total, 0.0).astype(BF16)
 
 
-def weight_kernel(place, a0, a1, a2, a3, b, b1, b2, b3, send, keep):
-    core = place[3]
+def weight_kernel(keep, place, first, mid, peers, b, b1, b2, b3, _, out):
+    parity = place[3] if keep else 1 - place[3]
     left = jnp.concatenate([b[0], b1[...], b2[...], b3[...]], axis=0)
     for k in range(4):
-        for out, parity in ((send, 1 - core), (keep, core)):
-            cols = pl.ds(pl.multiple_of((2 * k + parity) * HEAD, HEAD), HEAD)
-            right = jnp.concatenate([a[:, cols] for a in (a0, a1, a2, a3)], axis=0)
-            out[:, k * HEAD : (k + 1) * HEAD] = dot(left, right, 0, 0).astype(out.dtype)
-
-
-def core_sum_kernel(place, keep, got, own, sends):
+        cols = pl.ds(pl.multiple_of((2 * k + parity) * HEAD, HEAD), HEAD)
+        right = jnp.concatenate([a[:, cols] for a in (first, mid, peers)], axis=0)
+        out[:, k * HEAD : (k + 1) * HEAD] = dot(left, right, 0, 0).astype(out.dtype)
+
+
+def core_sum_kernel(place, keep, got, own, near, cross, ahead):
     me = place[4]
-    whole, half = HEAD, HEAD // 2
-    for i in range(4):
-        one = keep[i * whole : (i + 1) * whole] + got[i * whole : (i + 1) * whole].astype(F32)
-        rows = pl.ds(4 * whole + i * half, half)
-        two = keep[rows] + got[rows].astype(F32)
-        sends[i ^ me, :whole] = one.astype(BF16)
-        sends[i ^ me, whole:] = two.astype(BF16)
-
-        @pl.when(i == me)
-        def _():
-            own[:whole] = one
-            own[whole:] = two
-
-
-def part_sum_kernel(place, own, g1, g2, g3, sends):
+    outer, inner = 3 * (1 - me % 2), 2 - me // 2
+    for out, i in ((near, outer), (cross, inner), (ahead, 6 - me - outer - inner), (own, me)):
+        at = 0
+        for size, base in ((HEAD, 0), (HEAD // 2, 4 * HEAD)):
+            rows = pl.ds(pl.multiple_of(base + i * size, size), size)
+            out[at : at + size] = (keep[rows] + got[rows].astype(F32)).astype(out.dtype)
+            at += size
+
+
+def forward_kernel(place, ahead, got, out):
+    inside = (place[4] == 1) | (place[4] == 2)
+    out[...] = (ahead[...] + jnp.where(inside, got[...].astype(F32), 0.0)).astype(BF16)
+
+
+def part_sum_kernel(place, own, g1, g2, g3, g4, sends):
     chip = place[2]
+    outside = (place[4] == 0) | (place[4] == 3)
     for k in range(4):
         cols = pl.ds(k * HEAD, HEAD)
-        total = own[:, cols] + g1[:, cols].astype(F32)
-        total = total + (g2[:, cols].astype(F32) + g3[:, cols].astype(F32))
+        total = own[:, cols] + jnp.where(outside, g1[:, cols].astype(F32), 0.0)
+        for got in (g2, g3, g4):
+            total = total + got[:, cols].astype(F32)
         sends[k ^ chip] = total.astype(BF16)
 
 
@@ -195,17 +279,23 @@
         out[1 + 3 * (k // 2), pl.ds(start, HEAD // 2)] = value[HEAD:]
 
 
-def call(kernel, name, outs, place, operands, scratch=(), mib=16, flops=1000000, moved=1000000):
+def call(
+    kernel, name, outs, place, operands, scratch=(), mib=16, flops=1000000, moved=1000000,
+    remote=(), after=()
+):
     return pl.pallas_call(
         kernel,
         name=name,
         out_shape=[jax.ShapeDtypeStruct(shape, dtype) for shape, dtype in outs],
-        in_specs=[pl.BlockSpec(memory_space=pltpu.SMEM)] + vmem(len(operands)),
+        in_specs=[pl.BlockSpec(memory_space=pltpu.SMEM)]
+        + vmem(len(operands))
+        + [pl.BlockSpec(memory_space=pltpu.HBM)] * len(remote)
+        + [pl.BlockSpec(memory_space=pl.ANY)] * len(after),
         out_specs=vmem(len(outs)),
-        scratch_shapes=[pltpu.VMEM(shape, dtype) for shape, dtype in scratch],
+        scratch_shapes=[pltpu.VMEM(*x) if isinstance(x, tuple) else x for x in scratch],
         compiler_params=params(mib),
         cost_estimate=cost(flops, moved),
-    )(place, *operands)
+    )(place, *operands, *remote, *after)
 
 
 def shift(value, axis, steps):
@@ -227,34 +317,57 @@
     place = jnp.stack(
         [me * frames, valid_frames[0], me // 2, me % 2, lax.axis_index("dp")]
     ).astype(jnp.int32)
+    split = parts == 8 and recs == 4
     before = shift(record[frames - HALO :], "tm", 1)
     after = shift(jnp.concatenate([record[:HALO], cot[:HALO]], axis=0), "tm", -1)
-    rows = span + HALO
-    hidden, conv, qkv = call(
-        project_kernel,
-        "project",
+    rows = frames - EDGE
+    mid, conv_mid, qkv_mid, near, taps, w_near = call(
+        own_kernel,
+        "own_rows",
         [
+            ((rows, width), BF16),
+            ((rows, width), F32),
+            ((rows, 3 * width), BF16),
             ((frames, width), BF16),
-            ((frames + EDGE, width), F32),
-            ((HALO + 2 * frames, 3 * width), BF16),
+            (kernel.shape, F32),
+            (w_qkv.shape, BF16),
         ],
         place,
-        [before, record, after, kernel, w_qkv],
-        [((rows + KERNEL - 1, width), F32), ((rows, width), BF16)],
-        mib=24,
+        [],
+        [
+            ((frames, width), F32),
+            pltpu.SemaphoreType.DMA((3 * width // 512,)),
+            pltpu.SemaphoreType.DMA((2,)),
+        ],
         flops=rows * width * 3 * width * 2,
         moved=9000000,
-    )
-    split = parts == 8 and recs == 4
+        remote=[record, kernel, w_qkv],
+        mib=42,
+    )
     if split:
-        peers = [swap(hidden, "tm", mask) for mask in (2, 4, 6)]
+        peers = [swap(near, "tm", mask) for mask in (2, 4, 6)]
+    rows = 2 * HALO + EDGE
+    first, conv_rim, qkv_rim = call(
+        rim_kernel,
+        "rim_rows",
+        [
+            ((EDGE, width), BF16),
+            ((2 * EDGE, width), F32),
+            ((HALO + EDGE + frames, 3 * width), BF16),
+        ],
+        place,
+        [before, near, after, taps, w_near],
+        [((rows + 2 * (KERNEL - 1), width), F32), ((rows, width), BF16)],
+        flops=rows * width * 3 * width * 2,
+        moved=9000000,
+    )
     outs = [((frames, width), BF16), ((frames + EDGE, 3 * width), BF16)]
     attended, grads, *sends = call(
         attend_kernel if split else attend_alone,
         "attend",
         outs + [((4, frames, 3 * width // 4), BF16)] * split,
         place,
-        [qkv, cot, after],
+        [qkv_rim, qkv_mid, cot, after],
         [((frames, width), BF16)],
         mib=16,
         flops=8 * 12 * span * 128 * 128 * 2 * 8,
@@ -263,12 +376,12 @@
     if split:
         sends = sends[0]
         got = [swap(sends[slot], "tm", 2 * slot) for slot in (1, 2, 3)]
-    (grad_in,) = call(
+    grad_in, done = call(
         input_grad_kernel,
         "input_grad",
-        [((frames, width), BF16)],
+        [((frames, width), BF16), ((8, 128), F32)],
         place,
-        [grads, w_qkv, conv, kernel],
+        [grads, w_near, conv_mid, conv_rim, taps],
         [((frames + EDGE, width), F32)],
         mib=20,
         flops=(frames + EDGE) * width * 3 * width * 2,
@@ -278,31 +391,54 @@
     if split:
         cols = 3 * width // 4
         shard = cols // 4
-        send, keep = call(
-            weight_kernel,
-            "weight_grad",
-            [((cols, width // 2), BF16), ((cols, width // 2), F32)],
+        (ends,) = call(
+            ends_kernel, "ends", [((4 * EDGE, width), BF16)], place, [near, *peers], after=[grads]
+        )
+        (hidden,) = call(
+            peers_kernel,
+            "peer_hidden",
+            [((3 * frames, width), BF16)],
             place,
-            [hidden, *peers, sends, *got],
-            mib=20,
-            flops=cols * width * frames * 8,
-            moved=6000000,
+            [*peers, swap(ends, "tm", 1), taps],
+            [((frames + EDGE, width), F32)],
+            flops=3 * frames * width * 40,
+            moved=2000000,
+        )
+        send, keep = (
+            call(
+                functools.partial(weight_kernel, mine),
+                "weight_" + ("keep" if mine else "send"),
+                [((cols, width // 2), F32 if mine else BF16)],
+                place,
+                [first, mid, hidden, sends, *got],
+                mib=20,
+                flops=cols * width * frames * 4,
+                moved=6000000,
+                after=[done],
+            )[0]
+            for mine in (False, True)
         )
         sibling = swap(send, "tm", 1)
-        own, shards = call(
+        own, near, cross, ahead = call(
             core_sum_kernel,
             "core_sum",
-            [((shard, width // 2), F32), ((4, shard, width // 2), BF16)],
+            [((shard, width // 2), dtype) for dtype in (F32, BF16, BF16, F32)],
             place,
             [keep, sibling],
         )
-        others = [swap(shards[mask], "dp", mask) for mask in (1, 2, 3)]
+        g1 = swap(near, "dp", 1)
+        g2 = lax.ppermute(cross, "dp", [(0, 2), (3, 1)])
+        g3 = lax.ppermute(cross, "dp", [(1, 2), (2, 1)])
+        (ahead,) = call(
+            forward_kernel, "forward", [((shard, width // 2), BF16)], place, [ahead, g1]
+        )
+        g4 = lax.ppermute(ahead, "dp", [(0, 1), (1, 3), (2, 0), (3, 2)])
         (blocks,) = call(
             part_sum_kernel,
             "part_sum",
             [((4, shard, HEAD), BF16)],
             place,
-            [own, *others],
+            [own, g1, g2, g3, g4],
         )
         last = [swap(blocks[slot], "tm", 2 * slot) for slot in (1, 2, 3)]
         (qkv_grad,) = call(
@@ -313,6 +449,7 @@
             [blocks, *last],
         )
     else:
+        hidden = jnp.concatenate([first, mid], axis=0)
         partial = dot(hidden, grads[:frames], 0, 0).astype(BF16)
         by_time = lax.psum_scatter(partial, "tm", scatter_dimension=0, tiled=True)
         summed = lax.psum_scatter(by_time, "dp", scatter_dimension=1, tiled=True).astype(F32)

time: 85.8 us -> 74.7 us (0.87)
  waiting for transfers between devices: 35.2 us -> 17.8 us
  Pallas kernels: 18.2 us -> 26 us
  local copies, waits for them, and re-layouts: 5.88 us -> 3.88 us
    ppermute x13 -> x12, waiting for transfers between devices: 35 us -> 6.28 us  [swap(): lax.ppermute(value, axis, [(i, i ^ mask) for i in range(lax.axis_size(axi...]
    ppermute x0 -> x3, waiting for transfers between devices: none -> 11.5 us  [the longest x1 9.3 us: on_device(): g4 = lax.ppermute(ahead, 'dp', [(0, 1), (1, 3), (2, 0), (3, 2)])]
    pallas_call x7 -> x12, Pallas kernels: 18.2 us -> 26 us  [call(): pl.pallas_call(kernel, name=name, out_shape=[jax.ShapeDtypeStruct(shape,...]
    ppermute x0 -> x3, starting transfers between devices: none -> 6.8 us  [the longest x1 4.5 us: on_device(): g2 = lax.ppermute(cross, 'dp', [(0, 2), (3, 1)])]
    ppermute x13 -> x12, starting transfers between devices: 20.4 us -> 14.1 us  [swap(): lax.ppermute(value, axis, [(i, i ^ mask) for i in range(lax.axis_size(axi...]
    unnamed x14 -> x6, local copies, waits for them, and re-layouts: 4.59 us -> 1.79 us
    slice x0 -> x1, local copies, waits for them, and re-layouts: none -> 0.93 us  [on_device(): cot[:HALO]]
  transfers between devices with their start and end apart: 15 -> 17, of which waited for: 7 -> 10; matrix products, arithmetic and copies ran while one was open for 0% -> 0% of each run, Pallas kernels for 5% -> 29%
where the time goes in v2:
time: 74.7 us; the launch traced here: 74.4 us
  Pallas kernels  26 us (35%)
  starting transfers between devices  25.3 us (34%)
  waiting for transfers between devices  17.8 us (24%)
  local copies, waits for them, and re-layouts  3.88 us (5%)
  between operations  1.45 us (2%)
    pallas_call x12, Pallas kernels, call(): pl.pallas_call(kernel, name=name, out_shape=[jax.ShapeDtypeStruct(shape,...  26 us
    ppermute x12, starting transfers between devices, swap(): lax.ppermute(value, axis, [(i, i ^ mask) for i in range(lax.axis_size(axi...  14.1 us
    ppermute x1, waiting for transfers between devices, on_device(): g4 = lax.ppermute(ahead, 'dp', [(0, 1), (1, 3), (2, 0), (3, 2)])  9.3 us
    ppermute x12, waiting for transfers between devices, swap(): lax.ppermute(value, axis, [(i, i ^ mask) for i in range(lax.axis_size(axi...  6.28 us
    ppermute x1, starting transfers between devices, on_device(): g2 = lax.ppermute(cross, 'dp', [(0, 2), (3, 1)])  4.5 us
    ppermute x2, starting transfers between devices, shift(): return lax.ppermute(value, axis, pairs)  4.33 us
    ppermute x1, waiting for transfers between devices, on_device(): g2 = lax.ppermute(cross, 'dp', [(0, 2), (3, 1)])  2.23 us
    unnamed x6, local copies, waits for them, and re-layouts  1.79 us
  transfers between devices with their start and end apart: 17, of which 10 were waited for; matrix products, arithmetic and copies ran while one was open for 0% of the time, Pallas kernels for 29%

profile of v2, /device:TPU:0, one launch (start us, length us, event | category | flops | bytes accessed | tf_op | source)
XLA Modules:
  0.0 74.4 jit_solution(1382411821744179909)
XLA Ops:
  0.6 1.0 %slice_bitcast_fusion.4 = (bf16[80,1024]{1,0:T(8,128)(2,1)S(1)}, bf16[80,1024]{1,0:T(8,128)(2,1)S(1)}) fusion(bf16[1,128,1024]{2,1,0:T(8,128)(2,1)} %param.5), kind=kLoop, calls=%fused_computation.5 | loop fusion | bytes 655360 | tf_op jit(solution)/shard_map/slice | solution.py:322
  1.7 0.9 %slice_bitcast_fusion.3 = bf16[80,1024]{1,0:T(8,128)(2,1)S(1)} fusion(bf16[1,128,1024]{2,1,0:T(8,128)(2,1)} %param.9), kind=kLoop, calls=%fused_computation.4 | loop fusion | bytes 327680 | tf_op jit(solution)/shard_map/slice | solution.py:322
  2.6 1.3 %collective-permute-start.1 = (bf16[160,1024]{1,0:T(8,128)(2,1)S(1)}, bf16[160,1024]{1,0:T(8,128)(2,1)S(1)}, u32[]{:S(2)}, u32[]{:S(2)}) collective-permute-start(bf16[160,1024]{1,0:T(8,128)(2,1)S(1)} %pad_maximum_fusion), channel_id=1, source_target_pairs={{4,0},{8,4},{12,8},{16,12},{20,16},{24,20},{28,24},{5,1},{9,5},{13... | collective-permute-start | bytes 983048 | tf_op jit(solution)/shard_map/ppermute | solution.py:304
  3.9 3.0 %collective-permute-start = (bf16[80,1024]{1,0:T(8,128)(2,1)S(1)}, bf16[80,1024]{1,0:T(8,128)(2,1)S(1)}, u32[]{:S(2)}, u32[]{:S(2)}) collective-permute-start(bf16[80,1024]{1,0:T(8,128)(2,1)S(1)} %get-tuple-element.43), channel_id=1, source_target_pairs={{0,4},{4,8},{8,12},{12,16},{16,20},{20,24},{24,28},{1,5},{5,9},{9,... | collective-permute-start | bytes 491528 | tf_op jit(solution)/shard_map/ppermute | solution.py:304
  7.7 0.9 %copy-done = bf16[1,128,1024]{2,1,0:T(8,128)(2,1)S(1)} copy-done((bf16[1,128,1024]{2,1,0:T(8,128)(2,1)S(1)}, bf16[1,128,1024]{2,1,0:T(8,128)(2,1)}, u32[]{:S(2)}) %copy-start) | copy-done | bytes 262168
  8.7 0.8 %copy-done.2 = f32[9,1024]{1,0:T(8,128)S(1)} copy-done((f32[9,1024]{1,0:T(8,128)S(1)}, f32[9,1024]{1,0:T(8,128)}, u32[]{:S(2)}) %copy-start.2) | copy-done | bytes 36888
  9.5 3.9 %own_rows.1 = (bf16[112,1024]{1,0:T(8,128)(2,1)S(1)}, f32[112,1024]{1,0:T(8,128)S(1)}, bf16[112,3072]{1,0:T(8,128)(2,1)S(1)}, bf16[128,1024]{1,0:T(8,128)(2,1)S(...) custom-call(s32[5]{0:T(128)S(1)} %stack.19.place, bf16[128,1024]{1,0:T(8,128)(2,1)S(1)} %bitcast.26, ...), custom_call_target="tpu_custom_call" | custom-call | flops 704643072 | bytes 9000000 | tf_op jit(solution)/shard_map/own_rows/pallas_call | solution.py:286
  13.4 3.0 %collective-permute-start.2 = (bf16[128,1024]{1,0:T(8,128)(2,1)S(1)}, bf16[128,1024]{1,0:T(8,128)(2,1)S(1)}, u32[]{:S(2)}, u32[]{:S(2)}) collective-permute-start(bf16[128,1024]{1,0:T(8,128)(2,1)S(1)} %get-tuple-element.21.own.f0), channel_id=1, source_target_pairs={{0,8},{4,12},{8,0},{12,4},{16,24},{20,28},{24,16},{28,20},{1,9},{5... | collective-permute-start | bytes 786440 | tf_op jit(solution)/shard_map/ppermute | solution.py:308
  16.4 1.5 %collective-permute-start.3 = (bf16[128,1024]{1,0:T(8,128)(2,1)S(1)}, bf16[128,1024]{1,0:T(8,128)(2,1)S(1)}, u32[]{:S(2)}, u32[]{:S(2)}) collective-permute-start(bf16[128,1024]{1,0:T(8,128)(2,1)S(1)} %get-tuple-element.21.own.f0), channel_id=1, source_target_pairs={{0,16},{4,20},{8,24},{12,28},{16,0},{20,4},{24,8},{28,12},{1,17},{... | collective-permute-start | bytes 786440 | tf_op jit(solution)/shard_map/ppermute | solution.py:308
  18.3 2.9 %rim_rows.1 = (bf16[16,1024]{1,0:T(8,128)(2,1)S(1)}, f32[32,1024]{1,0:T(8,128)S(1)}, bf16[224,3072]{1,0:T(8,128)(2,1)S(1)}) custom-call(s32[5]{0:T(128)S(1)} %stack.19.place, bf16[80,1024]{1,0:T(8,128)(2,1)S(1)} %collective-permute-done.prev, bf16[128,1024]{1,0:T(8,128)(2,1)S(1)} %get-tuple-element.21.own.f0, ...), custom_call_target="tpu_custom_call" | custom-call | flops 1107296256 | bytes 9000000 | tf_op jit(solution)/shard_map/rim_rows/pallas_call | solution.py:286
  21.2 4.7 %attend.1 = (bf16[128,1024]{1,0:T(8,128)(2,1)}, bf16[144,3072]{1,0:T(8,128)(2,1)S(1)}, bf16[4,128,768]{2,1,0:T(8,128)(2,1)S(1)}) custom-call(s32[5]{0:T(128)S(1)} %stack.19.place, bf16[224,3072]{1,0:T(8,128)(2,1)S(1)} %get-tuple-element.24.rim, bf16[112,3072]{1,0:T(8,128)(2,1)S(1)} %get-tuple-element.25.mid, bf16[128,1024]{1,0:T(8,128)(2,1)S(1)} %bitcast.27, ...), custom_call_target="tpu_custom_call" | custom-call | flops 5234491392 | bytes 5000000 | tf_op jit(solution)/shard_map/attend/pallas_call | solution.py:286
  26.0 1.7 %collective-permute-start.6 = (bf16[128,768]{1,0:T(8,128)(2,1)S(1)}, bf16[128,768]{1,0:T(8,128)(2,1)S(1)}, u32[]{:S(2)}, u32[]{:S(2)}) collective-permute-start(bf16[128,768]{1,0:T(8,128)(2,1)S(1)} %get-tuple-element.41), channel_id=1, source_target_pairs={{0,8},{4,12},{8,0},{12,4},{16,24},{20,28},{24,16},{28,20},{1,9},{5... | collective-permute-start | bytes 589832 | tf_op jit(solution)/shard_map/ppermute | solution.py:308
  27.6 1.5 %collective-permute-start.7 = (bf16[128,768]{1,0:T(8,128)(2,1)S(1)}, bf16[128,768]{1,0:T(8,128)(2,1)S(1)}, u32[]{:S(2)}, u32[]{:S(2)}) collective-permute-start(bf16[128,768]{1,0:T(8,128)(2,1)S(1)} %get-tuple-element.40), channel_id=1, source_target_pairs={{0,16},{4,20},{8,24},{12,28},{16,0},{20,4},{24,8},{28,12},{1,17},{... | collective-permute-start | bytes 589832 | tf_op jit(solution)/shard_map/ppermute | solution.py:308
  29.5 0.6 collective-permute-done.3.f2
  30.2 0.9 %collective-permute-done.4.f3 = bf16[128,1024]{1,0:T(8,128)(2,1)S(1)} collective-permute-done((bf16[128,1024]{1,0:T(8,128)(2,1)S(1)}, bf16[128,1024]{1,0:T(8,128)(2,1)S(1)}, u32[]{:S(2)}, u32[]{:S(2)}) %collective-permute-start.4) | collective-permute-done | bytes 262176 | tf_op jit(solution)/shard_map/ppermute | solution.py:308
  31.9 4.3 %input_grad.1 = (bf16[128,1024]{1,0:T(8,128)(2,1)}, f32[8,128]{1,0:T(8,128)S(1)}) custom-call(s32[5]{0:T(128)S(1)} %stack.19.place, bf16[144,3072]{1,0:T(8,128)(2,1)S(1)} %get-tuple-element.27.grads._, bf16[1024,3072]{1,0:T(8,128)(2,1)S(1)} %get-tuple-element.23.w, f32[112,1024]{1,0:T(8,128)S(1)} %get-tuple-element.28.conv_mid, ...), custom_call_target="tpu_custom_call" | custom-call | flops 905969664 | bytes 9000000 | tf_op jit(solution)/shard_map/input_grad/pallas_call | solution.py:286
  36.2 3.2 %peer_hidden.1.peers = bf16[384,1024]{1,0:T(8,128)(2,1)S(1)} custom-call(s32[5]{0:T(128)S(1)} %stack.19.place, bf16[128,1024]{1,0:T(8,128)(2,1)S(1)} %collective-permute-done.2.f1, bf16[128,1024]{1,0:T(8,128)(2,1)S(1)} %collective-permute-done.3.f2, bf16[128,1024]{1,0:T(8,128)(2,1)S(1)} %collective-permute-done.4.f3, ...), custom_call_target="tpu_custom_call" | custom-call | flops 15728640 | bytes 2000000 | tf_op jit(solution)/shard_map/peer_hidden/pallas_call | solution.py:286
  39.6 1.6 %weight_send.1 = bf16[768,512]{1,0:T(8,128)(2,1)S(1)} custom-call(s32[5]{0:T(128)S(1)} %stack.19.place, bf16[16,1024]{1,0:T(8,128)(2,1)S(1)} %get-tuple-element.31.first, bf16[112,1024]{1,0:T(8,128)(2,1)S(1)} %get-tuple-element.32.mid, bf16[384,1024]{1,0:T(8,128)(2,1)S(1)} %peer_hidden.1.peers, bf16[4,128,768]{2,1,0:T(8,128)(2,1)S(1)} %get-tuple-element.33.b, ...), custom_call_target="tpu_custom_call" | custom-call | flops 402653184 | bytes 6000000 | tf_op jit(solution)/shard_map/weight_send/pallas_call | solution.py:286
  41.4 1.5 %weight_keep.1.keep = f32[768,512]{1,0:T(8,128)S(1)} custom-call(s32[5]{0:T(128)S(1)} %stack.19.place, bf16[16,1024]{1,0:T(8,128)(2,1)S(1)} %get-tuple-element.31.first, bf16[112,1024]{1,0:T(8,128)(2,1)S(1)} %get-tuple-element.32.mid, bf16[384,1024]{1,0:T(8,128)(2,1)S(1)} %peer_hidden.1.peers, bf16[4,128,768]{2,1,0:T(8,128)(2,1)S(1)} %get-tuple-element.33.b, ...), custom_call_target="tpu_custom_call" | custom-call | flops 402653184 | bytes 6000000 | tf_op jit(solution)/shard_map/weight_keep/pallas_call | solution.py:286
  43.5 0.7 core_sum.1
  44.2 1.6 %collective-permute-start.10 = (bf16[192,512]{1,0:T(8,128)(2,1)S(1)}, bf16[192,512]{1,0:T(8,128)(2,1)S(1)}, u32[]{:S(2)}, u32[]{:S(2)}) collective-permute-start(bf16[192,512]{1,0:T(8,128)(2,1)S(1)} %get-tuple-element.36), channel_id=1, source_target_pairs={{0,1},{1,0},{2,3},{3,2},{4,5},{5,4},{6,7},{7,6},{8,9},{9,8},{10,11... | collective-permute-start | bytes 589832 | tf_op jit(solution)/shard_map/ppermute | solution.py:308
  45.9 4.5 %collective-permute-start.11 = (bf16[192,512]{1,0:T(8,128)(2,1)S(1)}, bf16[192,512]{1,0:T(8,128)(2,1)S(1)}, u32[]{:S(2)}, u32[]{:S(2)}) collective-permute-start(bf16[192,512]{1,0:T(8,128)(2,1)S(1)} %get-tuple-element.37), channel_id=1, source_target_pairs={{0,2},{3,1},{4,6},{7,5},{8,10},{11,9},{12,14},{15,13},{16,18},{19,... | collective-permute-start | bytes 589832 | tf_op jit(solution)/shard_map/ppermute | solution.py:430
  50.4 0.7 collective-permute-start.12
  51.8 1.6 %collective-permute-start.13 = (bf16[192,512]{1,0:T(8,128)(2,1)S(1)}, bf16[192,512]{1,0:T(8,128)(2,1)S(1)}, u32[]{:S(2)}, u32[]{:S(2)}) collective-permute-start(bf16[192,512]{1,0:T(8,128)(2,1)S(1)} %forward.1), channel_id=1, source_target_pairs={{0,1},{1,3},{2,0},{3,2},{4,5},{5,7},{6,4},{7,6},{8,9},{9,11},{10,8... | collective-permute-start | bytes 589832 | tf_op jit(solution)/shard_map/ppermute | solution.py:435
  53.5 2.2 %collective-permute-done.11.g2 = bf16[192,512]{1,0:T(8,128)(2,1)S(1)} collective-permute-done((bf16[192,512]{1,0:T(8,128)(2,1)S(1)}, bf16[192,512]{1,0:T(8,128)(2,1)S(1)}, u32[]{:S(2)}, u32[]{:S(2)}) %collective-permute-start.11) | collective-permute-done | bytes 196640 | tf_op jit(solution)/shard_map/ppermute | solution.py:430
  55.7 9.3 %collective-permute-done.13.g4 = bf16[192,512]{1,0:T(8,128)(2,1)S(1)} collective-permute-done((bf16[192,512]{1,0:T(8,128)(2,1)S(1)}, bf16[192,512]{1,0:T(8,128)(2,1)S(1)}, u32[]{:S(2)}, u32[]{:S(2)}) %collective-permute-start.13) | collective-permute-done | bytes 196640 | tf_op jit(solution)/shard_map/ppermute | solution.py:435
  65.0 0.7 part_sum.1.own
  66.3 1.8 %collective-permute-start.15 = (bf16[192,128]{1,0:T(8,128)(2,1)S(1)}, bf16[192,128]{1,0:T(8,128)(2,1)S(1)}, u32[]{:S(2)}, u32[]{:S(2)}) collective-permute-start(bf16[192,128]{1,0:T(8,128)(2,1)S(1)} %get-tuple-element.45), channel_id=1, source_target_pairs={{0,16},{4,20},{8,24},{12,28},{16,0},{20,4},{24,8},{28,12},{1,17},{... | collective-permute-start | bytes 147464 | tf_op jit(solution)/shard_map/ppermute | solution.py:308
  68.1 1.2 %collective-permute-start.16 = (bf16[192,128]{1,0:T(8,128)(2,1)S(1)}, bf16[192,128]{1,0:T(8,128)(2,1)S(1)}, u32[]{:S(2)}, u32[]{:S(2)}) collective-permute-start(bf16[192,128]{1,0:T(8,128)(2,1)S(1)} %get-tuple-element.44), channel_id=1, source_target_pairs={{0,24},{4,28},{8,16},{12,20},{16,8},{20,12},{24,0},{28,4},{1,25},{... | collective-permute-start | bytes 147464 | tf_op jit(solution)/shard_map/ppermute | solution.py:308
  69.3 0.9 %collective-permute-done.14.g1 = bf16[192,128]{1,0:T(8,128)(2,1)S(1)} collective-permute-done((bf16[192,128]{1,0:T(8,128)(2,1)S(1)}, bf16[192,128]{1,0:T(8,128)(2,1)S(1)}, u32[]{:S(2)}, u32[]{:S(2)}) %collective-permute-start.14) | collective-permute-done | bytes 49184 | tf_op jit(solution)/shard_map/ppermute | solution.py:308
  70.4 2.7 %collective-permute-done.16.g3 = bf16[192,128]{1,0:T(8,128)(2,1)S(1)} collective-permute-done((bf16[192,128]{1,0:T(8,128)(2,1)S(1)}, bf16[192,128]{1,0:T(8,128)(2,1)S(1)}, u32[]{:S(2)}, u32[]{:S(2)}) %collective-permute-start.16) | collective-permute-done | bytes 49184 | tf_op jit(solution)/shard_map/ppermute | solution.py:308
  73.1 1.4 %place.1 = f32[6,128,128]{2,1,0:T(8,128)} custom-call(s32[5]{0:T(128)S(1)} %stack.19.place, bf16[4,192,128]{2,1,0:T(8,128)(2,1)S(1)} %part_sum.1.own, bf16[192,128]{1,0:T(8,128)(2,1)S(1)} %collective-permute-done.14.g1, bf16[192,128]{1,0:T(8,128)(2,1)S(1)} %collective-permute-done.15.g2, bf16[192,128]{1,0:T(8,128)(2,1)S(1)} %collective-permute-done.16.g3), custom_call_target="tpu_custom_call" | custom-call | flops 1000000 | bytes 1000000 | tf_op jit(solution)/shard_map/place/pallas_call | solution.py:286
  (26 shorter events, 4.2 us)
Async XLA Ops:
  2.6 15.6 %collective-permute-start.1 = (bf16[160,1024]{1,0:T(8,128)(2,1)S(1)}, bf16[160,1024]{1,0:T(8,128)(2,1)S(1)}, u32[]{:S(2)}, u32[]{:S(2)}) collective-permute-start(bf16[160,1024]{1,0:T(8,128)(2,1)S(1)} %pad_maximum_fusion), channel_id=1, source_target_pairs={{4,0},{8,4},{12,8},{16,12},{20,16},{24,20},{28,24},{5,1},{9,5},{13... | collective-permute-start | bytes 983048 | tf_op jit(solution)/shard_map/ppermute | solution.py:304
  3.9 14.3 %collective-permute-start = (bf16[80,1024]{1,0:T(8,128)(2,1)S(1)}, bf16[80,1024]{1,0:T(8,128)(2,1)S(1)}, u32[]{:S(2)}, u32[]{:S(2)}) collective-permute-start(bf16[80,1024]{1,0:T(8,128)(2,1)S(1)} %get-tuple-element.43), channel_id=1, source_target_pairs={{0,4},{4,8},{8,12},{12,16},{16,20},{20,24},{24,28},{1,5},{5,9},{9,... | collective-permute-start | bytes 491528 | tf_op jit(solution)/shard_map/ppermute | solution.py:304
  7.7 1.0 %copy-start = (bf16[1,128,1024]{2,1,0:T(8,128)(2,1)S(1)}, bf16[1,128,1024]{2,1,0:T(8,128)(2,1)}, u32[]{:S(2)}) copy-start(bf16[1,128,1024]{2,1,0:T(8,128)(2,1)} %param.5) | copy-start | bytes 786436
  8.7 0.8 %copy-start.2 = (f32[9,1024]{1,0:T(8,128)S(1)}, f32[9,1024]{1,0:T(8,128)}, u32[]{:S(2)}) copy-start(f32[9,1024]{1,0:T(8,128)} %far_taps.1) | copy-start | bytes 110596
  9.5 11.7 %copy-start.1 = (bf16[1,128,1024]{2,1,0:T(8,128)(2,1)S(1)}, bf16[1,128,1024]{2,1,0:T(8,128)(2,1)}, u32[]{:S(2)}) copy-start(bf16[1,128,1024]{2,1,0:T(8,128)(2,1)} %param.9) | copy-start | bytes 786436
  13.4 15.8 %collective-permute-start.2 = (bf16[128,1024]{1,0:T(8,128)(2,1)S(1)}, bf16[128,1024]{1,0:T(8,128)(2,1)S(1)}, u32[]{:S(2)}, u32[]{:S(2)}) collective-permute-start(bf16[128,1024]{1,0:T(8,128)(2,1)S(1)} %get-tuple-element.21.own.f0), channel_id=1, source_target_pairs={{0,8},{4,12},{8,0},{12,4},{16,24},{20,28},{24,16},{28,20},{1,9},{5... | collective-permute-start | bytes 786440 | tf_op jit(solution)/shard_map/ppermute | solution.py:308
  16.4 13.8 %collective-permute-start.3 = (bf16[128,1024]{1,0:T(8,128)(2,1)S(1)}, bf16[128,1024]{1,0:T(8,128)(2,1)S(1)}, u32[]{:S(2)}, u32[]{:S(2)}) collective-permute-start(bf16[128,1024]{1,0:T(8,128)(2,1)S(1)} %get-tuple-element.21.own.f0), channel_id=1, source_target_pairs={{0,16},{4,20},{8,24},{12,28},{16,0},{20,4},{24,8},{28,12},{1,17},{... | collective-permute-start | bytes 786440 | tf_op jit(solution)/shard_map/ppermute | solution.py:308
  17.9 13.1 %collective-permute-start.4 = (bf16[128,1024]{1,0:T(8,128)(2,1)S(1)}, bf16[128,1024]{1,0:T(8,128)(2,1)S(1)}, u32[]{:S(2)}, u32[]{:S(2)}) collective-permute-start(bf16[128,1024]{1,0:T(8,128)(2,1)S(1)} %get-tuple-element.21.own.f0), channel_id=1, source_target_pairs={{0,24},{4,28},{8,16},{12,20},{16,8},{20,12},{24,0},{28,4},{1,25},{... | collective-permute-start | bytes 786440 | tf_op jit(solution)/shard_map/ppermute | solution.py:308
  26.0 13.5 %collective-permute-start.6 = (bf16[128,768]{1,0:T(8,128)(2,1)S(1)}, bf16[128,768]{1,0:T(8,128)(2,1)S(1)}, u32[]{:S(2)}, u32[]{:S(2)}) collective-permute-start(bf16[128,768]{1,0:T(8,128)(2,1)S(1)} %get-tuple-element.41), channel_id=1, source_target_pairs={{0,8},{4,12},{8,0},{12,4},{16,24},{20,28},{24,16},{28,20},{1,9},{5... | collective-permute-start | bytes 589832 | tf_op jit(solution)/shard_map/ppermute | solution.py:308
  27.6 12.0 %collective-permute-start.7 = (bf16[128,768]{1,0:T(8,128)(2,1)S(1)}, bf16[128,768]{1,0:T(8,128)(2,1)S(1)}, u32[]{:S(2)}, u32[]{:S(2)}) collective-permute-start(bf16[128,768]{1,0:T(8,128)(2,1)S(1)} %get-tuple-element.40), channel_id=1, source_target_pairs={{0,16},{4,20},{8,24},{12,28},{16,0},{20,4},{24,8},{28,12},{1,17},{... | collective-permute-start | bytes 589832 | tf_op jit(solution)/shard_map/ppermute | solution.py:308
  29.2 10.4 %collective-permute-start.8 = (bf16[128,768]{1,0:T(8,128)(2,1)S(1)}, bf16[128,768]{1,0:T(8,128)(2,1)S(1)}, u32[]{:S(2)}, u32[]{:S(2)}) collective-permute-start(bf16[128,768]{1,0:T(8,128)(2,1)S(1)} %get-tuple-element.39), channel_id=1, source_target_pairs={{0,24},{4,28},{8,16},{12,20},{16,8},{20,12},{24,0},{28,4},{1,25},{... | collective-permute-start | bytes 589832 | tf_op jit(solution)/shard_map/ppermute | solution.py:308
  31.6 4.6 %collective-permute-start.5 = (bf16[64,1024]{1,0:T(8,128)(2,1)S(1)}, bf16[64,1024]{1,0:T(8,128)(2,1)S(1)}, u32[]{:S(2)}, u32[]{:S(2)}) collective-permute-start(bf16[64,1024]{1,0:T(8,128)(2,1)S(1)} %ends.1), channel_id=1, source_target_pairs={{0,4},{4,0},{8,12},{12,8},{16,20},{20,16},{24,28},{28,24},{1,5},{5... | collective-permute-start | bytes 393224 | tf_op jit(solution)/shard_map/ppermute | solution.py:308
  41.2 2.4 %collective-permute-start.9 = (bf16[768,512]{1,0:T(8,128)(2,1)S(1)}, bf16[768,512]{1,0:T(8,128)(2,1)S(1)}, u32[]{:S(2)}, u32[]{:S(2)}) collective-permute-start(bf16[768,512]{1,0:T(8,128)(2,1)S(1)} %weight_send.1), channel_id=1, source_target_pairs={{0,4},{4,0},{8,12},{12,8},{16,20},{20,16},{24,28},{28,24},{1,5},{5... | collective-permute-start | bytes 2359304 | tf_op jit(solution)/shard_map/ppermute | solution.py:308
  44.2 7.0 %collective-permute-start.10 = (bf16[192,512]{1,0:T(8,128)(2,1)S(1)}, bf16[192,512]{1,0:T(8,128)(2,1)S(1)}, u32[]{:S(2)}, u32[]{:S(2)}) collective-permute-start(bf16[192,512]{1,0:T(8,128)(2,1)S(1)} %get-tuple-element.36), channel_id=1, source_target_pairs={{0,1},{1,0},{2,3},{3,2},{4,5},{5,4},{6,7},{7,6},{8,9},{9,8},{10,11... | collective-permute-start | bytes 589832 | tf_op jit(solution)/shard_map/ppermute | solution.py:308
  45.9 9.8 %collective-permute-start.11 = (bf16[192,512]{1,0:T(8,128)(2,1)S(1)}, bf16[192,512]{1,0:T(8,128)(2,1)S(1)}, u32[]{:S(2)}, u32[]{:S(2)}) collective-permute-start(bf16[192,512]{1,0:T(8,128)(2,1)S(1)} %get-tuple-element.37), channel_id=1, source_target_pairs={{0,2},{3,1},{4,6},{7,5},{8,10},{11,9},{12,14},{15,13},{16,18},{19,... | collective-permute-start | bytes 589832 | tf_op jit(solution)/shard_map/ppermute | solution.py:430
  50.4 5.3 %collective-permute-start.12 = (bf16[192,512]{1,0:T(8,128)(2,1)S(1)}, bf16[192,512]{1,0:T(8,128)(2,1)S(1)}, u32[]{:S(2)}, u32[]{:S(2)}) collective-permute-start(bf16[192,512]{1,0:T(8,128)(2,1)S(1)} %get-tuple-element.37), channel_id=1, source_target_pairs={{1,2},{2,1},{5,6},{6,5},{9,10},{10,9},{13,14},{14,13},{17,18},{18,... | collective-permute-start | bytes 589832 | tf_op jit(solution)/shard_map/ppermute | solution.py:431
  51.8 13.2 %collective-permute-start.13 = (bf16[192,512]{1,0:T(8,128)(2,1)S(1)}, bf16[192,512]{1,0:T(8,128)(2,1)S(1)}, u32[]{:S(2)}, u32[]{:S(2)}) collective-permute-start(bf16[192,512]{1,0:T(8,128)(2,1)S(1)} %forward.1), channel_id=1, source_target_pairs={{0,1},{1,3},{2,0},{3,2},{4,5},{5,7},{6,4},{7,6},{8,9},{9,11},{10,8... | collective-permute-start | bytes 589832 | tf_op jit(solution)/shard_map/ppermute | solution.py:435
  65.7 4.5 %collective-permute-start.14 = (bf16[192,128]{1,0:T(8,128)(2,1)S(1)}, bf16[192,128]{1,0:T(8,128)(2,1)S(1)}, u32[]{:S(2)}, u32[]{:S(2)}) collective-permute-start(bf16[192,128]{1,0:T(8,128)(2,1)S(1)} %get-tuple-element.46), channel_id=1, source_target_pairs={{0,8},{4,12},{8,0},{12,4},{16,24},{20,28},{24,16},{28,20},{1,9},{5... | collective-permute-start | bytes 147464 | tf_op jit(solution)/shard_map/ppermute | solution.py:308
  66.3 4.1 %collective-permute-start.15 = (bf16[192,128]{1,0:T(8,128)(2,1)S(1)}, bf16[192,128]{1,0:T(8,128)(2,1)S(1)}, u32[]{:S(2)}, u32[]{:S(2)}) collective-permute-start(bf16[192,128]{1,0:T(8,128)(2,1)S(1)} %get-tuple-element.45), channel_id=1, source_target_pairs={{0,16},{4,20},{8,24},{12,28},{16,0},{20,4},{24,8},{28,12},{1,17},{... | collective-permute-start | bytes 147464 | tf_op jit(solution)/shard_map/ppermute | solution.py:308
  68.1 5.0 %collective-permute-start.16 = (bf16[192,128]{1,0:T(8,128)(2,1)S(1)}, bf16[192,128]{1,0:T(8,128)(2,1)S(1)}, u32[]{:S(2)}, u32[]{:S(2)}) collective-permute-start(bf16[192,128]{1,0:T(8,128)(2,1)S(1)} %get-tuple-element.44), channel_id=1, source_target_pairs={{0,24},{4,28},{8,16},{12,20},{16,8},{20,12},{24,0},{28,4},{1,25},{... | collective-permute-start | bytes 147464 | tf_op jit(solution)/shard_map/ppermute | solution.py:308

commit v3 on v2

--- a/solution.py
+++ b/solution.py
@@ -14,6 +14,7 @@
 HALO = 80
 EDGE = 16
 MIB = 1024 * 1024
+OWN = 42
 F32 = jnp.float32
 BF16 = jnp.bfloat16
 
@@ -45,29 +46,24 @@
     return first + lax.broadcasted_iota(jnp.int32, (rows, 128), 0) < count
 
 
-def own_kernel(
-    place, far_own, far_taps, w, hidden, conv_out, qkv, own, taps, w_out, ext, sems, small
-):
-    frames, width = own.shape
+def parts_of(both, frames):
+    return both.at[:frames], both.at[frames : 2 * frames], both.at[2 * frames :]
+
+
+def own_kernel(place, both, w, hidden, conv_out, qkv, w_out, ext, sems):
+    frames, width = ext.shape
+    own, _, taps = parts_of(both, frames)
     rows = frames - EDGE
-    arrivals = [
-        pltpu.make_async_copy(source, target, small.at[i])
-        for i, (source, target) in enumerate(((far_own, own), (far_taps, taps)))
-    ]
-    for copy in arrivals:
-        copy.start()
     copies = [
         pltpu.make_async_copy(w.at[:, pl.ds(col, 512)], w_out.at[:, pl.ds(col, 512)], sems.at[i])
         for i, col in enumerate(range(0, 3 * width, 512))
     ]
     for copy in copies:
         copy.start()
-    for copy in arrivals:
-        copy.wait()
     live = live_rows(place[0], frames, place[1])
     for col in range(0, width, 128):
         cols = pl.ds(col, 128)
-        masked = jnp.where(live, own[:, cols].astype(F32), 0.0)
+        masked = jnp.where(live, own[:, cols], 0.0)
         ext[:, cols] = masked
         conv, low = conv_hidden(ext, taps, cols, EDGE - KERNEL + 1, rows, masked[EDGE:])
         conv_out[:, cols] = conv
@@ -78,23 +74,27 @@
         qkv[:, cols] = dot(hidden[...], w_out[:, cols], 1, 0).astype(BF16)
 
 
-def rim_kernel(place, prev, own, after, taps, w, first, conv_out, qkv, ext, hidden):
-    frames, width = own.shape
+def rim_kernel(place, near, far, both, w, first, conv_out, qkv, ext, hidden):
+    frames, width = qkv.shape[0] - HALO - EDGE, w.shape[0]
+    own, _, taps = parts_of(both, frames)
+    low_core = place[3] == 0
     begin, count = place[0], place[1]
     head, back = HALO + EDGE, KERNEL - 1
     live_a = live_rows(begin - HALO, head, count)
     live_b = live_rows(begin + frames - back, HALO + back, count)
     for col in range(0, width, 128):
         cols = pl.ds(col, 128)
-        raw = jnp.concatenate([prev[:, cols], own[:EDGE, cols]], axis=0).astype(F32)
+        mate, other = near[:HALO, cols].astype(F32), far[:HALO, cols].astype(F32)
+        prev = jnp.where(low_core, other, mate)
+        raw = jnp.concatenate([prev, own[:EDGE, cols]], axis=0)
         masked = jnp.where(live_a, raw, 0.0)
         ext[:back, cols] = jnp.zeros((back, 128), F32)
         ext[back : back + head, cols] = masked
         conv, low = conv_hidden(ext, taps, cols, 0, head, masked)
         conv_out[:EDGE, cols] = conv[HALO:]
         hidden[:head, cols] = low
-        tail = own[frames - EDGE :, cols].astype(F32)[EDGE - back :]
-        raw = jnp.concatenate([tail, after[:HALO, cols].astype(F32)], axis=0)
+        tail = own[frames - back :, cols]
+        raw = jnp.concatenate([tail, jnp.where(low_core, mate, other)], axis=0)
         masked = jnp.where(live_b, raw, 0.0)
         ext[back + head :, cols] = masked
         conv, low = conv_hidden(ext, taps, cols, back + head, HALO, masked[back:])
@@ -109,13 +109,16 @@
     qkv[rows:, :] = jnp.zeros((qkv.shape[0] - rows, 3 * width), BF16)
 
 
-def ends_kernel(place, f0, f1, f2, f3, _, out):
-    for slot, ref in enumerate((f0, f1, f2, f3)):
-        out[slot * EDGE : (slot + 1) * EDGE] = ref[ref.shape[0] - EDGE :]
-
-
-def peers_kernel(place, f1, f2, f3, tails, taps, hidden, ext):
+def ends_kernel(place, both, f1, f2, f3, _, out):
+    frames = f1.shape[0]
+    out[:EDGE] = both[frames - EDGE : frames].astype(BF16)
+    for slot, ref in ((1, f1), (2, f2), (3, f3)):
+        out[slot * EDGE : (slot + 1) * EDGE] = ref[frames - EDGE :]
+
+
+def peers_kernel(place, f1, f2, f3, tails, both, hidden, ext):
     frames, width = f1.shape
+    taps = parts_of(both, frames)[2]
     count, chip, core = place[1], place[2], place[3]
     for slot, ref in ((1, f1), (2, f2), (3, f3)):
         peer = chip ^ slot
@@ -134,27 +137,29 @@
             hidden[(slot - 1) * frames : slot * frames, cols] = low
 
 
-def attend_kernel(place, rim, mid, cot, after, attended, grads, sends, later):
-    frames, width = cot.shape
+def attend_kernel(place, rim, mid, both, near, far, attended, grads, sends, later):
+    frames, width = attended.shape
+    cot = parts_of(both, frames)[1]
     span = frames + HALO
     head_rows = HALO + EDGE
     begin, count, chip = place[0], place[1], place[2]
 
-    def mask(shift, wanted):
-        key = lax.broadcasted_iota(jnp.int32, (span, frames), 0)
-        query = lax.broadcasted_iota(jnp.int32, (span, frames), 1)
-        first = begin if shift else begin + frames
-        gap = query + (HALO if shift else frames) - key
+    skip = (frames - LEFT) // EDGE * EDGE
+
+    def mask(start, wanted):
+        key = lax.broadcasted_iota(jnp.int32, (start + wanted, frames), 0)
+        query = lax.broadcasted_iota(jnp.int32, (start + wanted, frames), 1)
+        first = begin if wanted == frames else begin + frames
+        gap = query + start - key
         seen = first + query - gap
         alive = (first + query < count) & (query < wanted)
         allowed = (gap >= 0) & (gap <= LEFT) & (seen >= 0) & alive
         return allowed, jnp.where(alive[:1], 0.0, 1.0)
 
-    masks = [mask(True, frames), mask(False, HALO)]
+    masks = [mask(HALO, frames), mask(frames - skip, HALO)]
     row = lax.broadcasted_iota(jnp.int32, (frames, width), 0)
-    later[:HALO] = jnp.where(
-        begin + frames + row[:HALO] < count, after[HALO:], jnp.zeros((HALO, width), BF16)
-    )
+    after = jnp.where(place[3] == 0, near[HALO:].astype(F32), far[HALO:].astype(F32))
+    later[:HALO] = jnp.where(begin + frames + row[:HALO] < count, after, 0.0).astype(BF16)
     later[HALO:] = jnp.zeros((frames - HALO, width), BF16)
     factor = HEAD**-0.5
 
@@ -179,20 +184,22 @@
             )
             for cols in (k_cols, v_cols)
         )
-        grad = jnp.where(own_live, cot[:, q_cols], jnp.zeros((frames, HEAD), BF16))
+        grad = jnp.where(own_live, cot[:, q_cols], 0.0).astype(BF16)
         grad_b = later[:, q_cols]
         prob, score = band(query, key[:span], value[:span], grad, *masks[0])
-        prob_b, score_b = band(query_b, key[HALO:], value[HALO:], grad_b, *masks[1])
+        prob_b, score_b = band(query_b, key[HALO + skip :], value[HALO + skip :], grad_b, *masks[1])
         attended[:, q_cols] = dot(prob, value[:span], 0, 0).astype(BF16)
         grads[:frames, q_cols] = dot(score, key[:span], 0, 0).astype(BF16)
-        grads[frames:, q_cols] = dot(score_b, key[HALO:], 0, 0)[:EDGE].astype(BF16)
+        grads[frames:, q_cols] = dot(score_b[:, :EDGE], key[HALO + skip :], 0, 0).astype(BF16)
         for cols, mine, here, theirs, there in (
             (k_cols, score, query, score_b, query_b),
             (v_cols, prob, grad, prob_b, grad_b),
         ):
-            total = dot(theirs[: frames + EDGE], there, 1, 0)
-            grads[:frames, cols] = (total[:frames] + dot(mine[HALO:], here, 1, 0)).astype(BF16)
-            grads[frames:, cols] = total[frames:].astype(BF16)
+            late = dot(theirs[: frames - skip + EDGE], there, 1, 0)
+            total = dot(mine[HALO:], here, 1, 0)
+            grads[:skip, cols] = total[:skip].astype(BF16)
+            grads[skip:frames, cols] = (total[skip:] + late[: frames - skip]).astype(BF16)
+            grads[frames:, cols] = late[frames - skip :].astype(BF16)
     if sends is None:
         return
     for k in range(4):
@@ -210,12 +217,14 @@
             sends[slot, :, at : at + HEAD] = jnp.concatenate(halves, axis=1)
 
 
-def attend_alone(place, rim, mid, cot, after, attended, grads, later):
-    attend_kernel(place, rim, mid, cot, after, attended, grads, None, later)
-
-
-def input_grad_kernel(place, grads, w, conv_mid, conv_rim, taps, grad_in, done, slopes):
+def attend_alone(place, rim, mid, both, near, far, attended, grads, later):
+    attend_kernel(place, rim, mid, both, near, far, attended, grads, None, later)
+
+
+def input_grad_kernel(place, grads, w, conv_mid, conv_rim, both, *refs):
+    grad_in, done, slopes = refs[-3:]
     frames, width = grad_in.shape
+    taps = parts_of(both, frames)[2]
     begin, count = place[0], place[1]
     done[...] = jnp.zeros(done.shape, F32)
     live = begin + lax.broadcasted_iota(jnp.int32, (frames, 256), 0) < count
@@ -233,7 +242,7 @@
         grad_in[:, cols] = jnp.where(live, total, 0.0).astype(BF16)
 
 
-def weight_kernel(keep, place, first, mid, peers, b, b1, b2, b3, _, out):
+def weight_kernel(keep, place, first, mid, peers, b, b1, b2, b3, out):
     parity = place[3] if keep else 1 - place[3]
     left = jnp.concatenate([b[0], b1[...], b2[...], b3[...]], axis=0)
     for k in range(4):
@@ -243,9 +252,8 @@
 
 
 def core_sum_kernel(place, keep, got, own, near, cross, ahead):
-    me = place[4]
-    outer, inner = 3 * (1 - me % 2), 2 - me // 2
-    for out, i in ((near, outer), (cross, inner), (ahead, 6 - me - outer - inner), (own, me)):
+    for mask, out in ((2, near), (3, ahead), (1, cross), (0, own)):
+        i = place[4] ^ mask
         at = 0
         for size, base in ((HEAD, 0), (HEAD // 2, 4 * HEAD)):
             rows = pl.ds(pl.multiple_of(base + i * size, size), size)
@@ -254,18 +262,14 @@
 
 
 def forward_kernel(place, ahead, got, out):
-    inside = (place[4] == 1) | (place[4] == 2)
-    out[...] = (ahead[...] + jnp.where(inside, got[...].astype(F32), 0.0)).astype(BF16)
-
-
-def part_sum_kernel(place, own, g1, g2, g3, g4, sends):
+    out[...] = (ahead[...] + got[...].astype(F32)).astype(BF16)
+
+
+def part_sum_kernel(place, own, g1, g2, _, sends):
     chip = place[2]
-    outside = (place[4] == 0) | (place[4] == 3)
     for k in range(4):
         cols = pl.ds(k * HEAD, HEAD)
-        total = own[:, cols] + jnp.where(outside, g1[:, cols].astype(F32), 0.0)
-        for got in (g2, g3, g4):
-            total = total + got[:, cols].astype(F32)
+        total = own[:, cols] + g1[:, cols].astype(F32) + g2[:, cols].astype(F32)
         sends[k ^ chip] = total.astype(BF16)
 
 
@@ -298,12 +302,6 @@
     )(place, *operands, *remote, *after)
 
 
-def shift(value, axis, steps):
-    count = lax.axis_size(axis)
-    pairs = [(i, i + steps) for i in range(count) if 0 <= i + steps < count]
-    return lax.ppermute(value, axis, pairs)
-
-
 def swap(value, axis, mask):
     return lax.ppermute(value, axis, [(i, i ^ mask) for i in range(lax.axis_size(axis))])
 
@@ -318,34 +316,38 @@
         [me * frames, valid_frames[0], me // 2, me % 2, lax.axis_index("dp")]
     ).astype(jnp.int32)
     split = parts == 8 and recs == 4
-    before = shift(record[frames - HALO :], "tm", 1)
-    after = shift(jnp.concatenate([record[:HALO], cot[:HALO]], axis=0), "tm", -1)
+    both = lax.optimization_barrier(
+        jnp.concatenate([record.astype(F32), cot.astype(F32), kernel], axis=0)
+    )
+    last = jnp.concatenate([both[frames - HALO : frames]] * 2, axis=0)
+    first = jnp.concatenate([both[:HALO], both[frames : frames + HALO]], axis=0)
+    low_core = me % 2 == 0
+    near = swap(jnp.where(low_core, last, first).astype(BF16), "tm", 1)
+    far = lax.ppermute(
+        jnp.where(low_core, first, last).astype(BF16),
+        "tm",
+        [(i, i + 1 if i % 2 else i - 1) for i in range(1, parts - 1)],
+    )
+    if split:
+        peers = [swap(record, "tm", mask) for mask in (2, 4, 6)]
     rows = frames - EDGE
-    mid, conv_mid, qkv_mid, near, taps, w_near = call(
+    mid, conv_mid, qkv_mid, w_near = call(
         own_kernel,
         "own_rows",
         [
             ((rows, width), BF16),
             ((rows, width), F32),
             ((rows, 3 * width), BF16),
-            ((frames, width), BF16),
-            (kernel.shape, F32),
             (w_qkv.shape, BF16),
         ],
         place,
-        [],
-        [
-            ((frames, width), F32),
-            pltpu.SemaphoreType.DMA((3 * width // 512,)),
-            pltpu.SemaphoreType.DMA((2,)),
-        ],
+        [both],
+        [((frames, width), F32), pltpu.SemaphoreType.DMA((3 * width // 512,))],
         flops=rows * width * 3 * width * 2,
         moved=9000000,
-        remote=[record, kernel, w_qkv],
-        mib=42,
-    )
-    if split:
-        peers = [swap(near, "tm", mask) for mask in (2, 4, 6)]
+        remote=[w_qkv],
+        mib=OWN,
+    )
     rows = 2 * HALO + EDGE
     first, conv_rim, qkv_rim = call(
         rim_kernel,
@@ -356,7 +358,7 @@
             ((HALO + EDGE + frames, 3 * width), BF16),
         ],
         place,
-        [before, near, after, taps, w_near],
+        [near, far, both, w_near],
         [((rows + 2 * (KERNEL - 1), width), F32), ((rows, width), BF16)],
         flops=rows * width * 3 * width * 2,
         moved=9000000,
@@ -367,7 +369,7 @@
         "attend",
         outs + [((4, frames, 3 * width // 4), BF16)] * split,
         place,
-        [qkv_rim, qkv_mid, cot, after],
+        [qkv_rim, qkv_mid, both, near, far],
         [((frames, width), BF16)],
         mib=16,
         flops=8 * 12 * span * 128 * 128 * 2 * 8,
@@ -376,30 +378,19 @@
     if split:
         sends = sends[0]
         got = [swap(sends[slot], "tm", 2 * slot) for slot in (1, 2, 3)]
-    grad_in, done = call(
-        input_grad_kernel,
-        "input_grad",
-        [((frames, width), BF16), ((8, 128), F32)],
-        place,
-        [grads, w_near, conv_mid, conv_rim, taps],
-        [((frames + EDGE, width), F32)],
-        mib=20,
-        flops=(frames + EDGE) * width * 3 * width * 2,
-        moved=9000000,
-    )
     scale = float(recs * parts * frames) ** (-0.5)
     if split:
         cols = 3 * width // 4
         shard = cols // 4
         (ends,) = call(
-            ends_kernel, "ends", [((4 * EDGE, width), BF16)], place, [near, *peers], after=[grads]
+            ends_kernel, "ends", [((4 * EDGE, width), BF16)], place, [both, *peers], after=[grads]
         )
         (hidden,) = call(
             peers_kernel,
             "peer_hidden",
             [((3 * frames, width), BF16)],
             place,
-            [*peers, swap(ends, "tm", 1), taps],
+            [*peers, swap(ends, "tm", 1), both],
             [((frames + EDGE, width), F32)],
             flops=3 * frames * width * 40,
             moved=2000000,
@@ -414,7 +405,6 @@
                 mib=20,
                 flops=cols * width * frames * 4,
                 moved=6000000,
-                after=[done],
             )[0]
             for mine in (False, True)
         )
@@ -426,19 +416,31 @@
             place,
             [keep, sibling],
         )
-        g1 = swap(near, "dp", 1)
-        g2 = lax.ppermute(cross, "dp", [(0, 2), (3, 1)])
-        g3 = lax.ppermute(cross, "dp", [(1, 2), (2, 1)])
+        late = [near]
+        grad_in, done = call(
+            input_grad_kernel,
+            "input_grad",
+            [((frames, width), BF16), ((8, 128), F32)],
+            place,
+            [grads, w_near, conv_mid, conv_rim, both],
+            [((frames + EDGE, width), F32)],
+            mib=20,
+            flops=(frames + EDGE) * width * 3 * width * 2,
+            moved=9000000,
+            after=late,
+        )
+        got_near, got_cross = swap(near, "dp", 1), swap(cross, "dp", 1)
         (ahead,) = call(
-            forward_kernel, "forward", [((shard, width // 2), BF16)], place, [ahead, g1]
-        )
-        g4 = lax.ppermute(ahead, "dp", [(0, 1), (1, 3), (2, 0), (3, 2)])
+            forward_kernel, "forward", [((shard, width // 2), BF16)], place, [ahead, got_near]
+        )
+        summed = [swap(ahead, "dp", 3), got_cross]
         (blocks,) = call(
             part_sum_kernel,
             "part_sum",
             [((4, shard, HEAD), BF16)],
             place,
-            [own, g1, g2, g3, g4],
+            [own, *summed],
+            after=[done],
         )
         last = [swap(blocks[slot], "tm", 2 * slot) for slot in (1, 2, 3)]
         (qkv_grad,) = call(
@@ -449,6 +451,19 @@
             [blocks, *last],
         )
     else:
+        late = []
+        grad_in, done = call(
+            input_grad_kernel,
+            "input_grad",
+            [((frames, width), BF16), ((8, 128), F32)],
+            place,
+            [grads, w_near, conv_mid, conv_rim, both],
+            [((frames + EDGE, width), F32)],
+            mib=20,
+            flops=(frames + EDGE) * width * 3 * width * 2,
+            moved=9000000,
+            after=late,
+        )
         hidden = jnp.concatenate([first, mid], axis=0)
         partial = dot(hidden, grads[:frames], 0, 0).astype(BF16)
         by_time = lax.psum_scatter(partial, "tm", scatter_dimension=0, tiled=True)

time: 74.7 us -> 68.4 us (0.916)
  local copies, waits for them, and re-layouts: 3.88 us -> 0.21 us
  starting transfers between devices: 25.3 us -> 22.5 us
  other arithmetic: 0.02 us -> 2.23 us
  waiting for transfers between devices: 17.8 us -> 16.1 us
    ppermute x5 -> x1, waiting for transfers between devices: 11.5 us -> 0.01 us  [on_device(): lax.ppermute(jnp.where(low_core, first, last).astype(BF16), 'tm', [(i, i...]
    ppermute x5 -> x1, starting transfers between devices: 11.1 us -> 0.68 us  [on_device(): lax.ppermute(jnp.where(low_core, first, last).astype(BF16), 'tm', [(i, i...]
    ppermute x12 -> x15, waiting for transfers between devices: 6.28 us -> 16.1 us  [swap(): lax.ppermute(value, axis, [(i, i ^ mask) for i in range(lax.axis_size(axi...]
    ppermute x12 -> x15, starting transfers between devices: 14.1 us -> 21.9 us  [swap(): lax.ppermute(value, axis, [(i, i ^ mask) for i in range(lax.axis_size(axi...]
    convert_element_type x0 -> x3, other arithmetic: none -> 2.15 us  [the longest x1 1.02 us: on_device(): cot.astype(F32)]
    slice x2 -> x1, local copies, waits for them, and re-layouts: 1.95 us -> 0.06 us  [on_device(): first = jnp.concatenate([both[:HALO], both[frames:frames + HALO]], axis=0)]
    unnamed x6 -> x4, local copies, waits for them, and re-layouts: 1.79 us -> 0.01 us
  transfers between devices with their start and end apart: 17 -> 16, of which waited for: 10 -> 9; matrix products, arithmetic and copies ran while one was open for 0% -> 0% of each run, Pallas kernels for 29% -> 31%
where the time goes in v3:
time: 68.4 us; the launch traced here: 68.2 us
  Pallas kernels  25.6 us (37%)
  starting transfers between devices  22.5 us (33%)
  waiting for transfers between devices  16.1 us (24%)
  other arithmetic  2.23 us (3%)
  between operations  1.5 us (2%)
    pallas_call x12, Pallas kernels, call(): pl.pallas_call(kernel, name=name, out_shape=[jax.ShapeDtypeStruct(shape,...  25.6 us
    ppermute x15, starting transfers between devices, swap(): lax.ppermute(value, axis, [(i, i ^ mask) for i in range(lax.axis_size(axi...  21.9 us
    ppermute x15, waiting for transfers between devices, swap(): lax.ppermute(value, axis, [(i, i ^ mask) for i in range(lax.axis_size(axi...  16.1 us
  transfers between devices with their start and end apart: 16, of which 9 were waited for; matrix products, arithmetic and copies ran while one was open for 0% of the time, Pallas kernels for 31%

profile of v3, /device:TPU:0, one launch (start us, length us, event | category | flops | bytes accessed | tf_op | source)
XLA Modules:
  0.0 68.2 jit_solution(18365693953513508858)
XLA Ops:
  0.7 1.0 %bitcast_convert_fusion = f32[128,1024]{1,0:T(8,128)S(1)} fusion(bf16[1,128,1024]{2,1,0:T(8,128)(2,1)} %param.9), kind=kLoop, calls=%fused_computation.7 | loop fusion | flops 131072 | bytes 786432 | tf_op jit(solution)/shard_map/convert_element_type | solution.py:320
  1.7 1.0 %bitcast_convert_fusion.1 = f32[128,1024]{1,0:T(8,128)S(1)} fusion(bf16[1,128,1024]{2,1,0:T(8,128)(2,1)} %param.5), kind=kLoop, calls=%fused_computation.14 | loop fusion | flops 131072 | bytes 786432 | tf_op jit(solution)/shard_map/convert_element_type | solution.py:320
  3.0 0.7 collective-permute-start.1
  3.7 4.3 %collective-permute-start = (bf16[160,1024]{1,0:T(8,128)(2,1)S(1)}, bf16[160,1024]{1,0:T(8,128)(2,1)S(1)}, u32[]{:S(2)}, u32[]{:S(2)}) collective-permute-start(bf16[160,1024]{1,0:T(8,128)(2,1)S(1)} %get-tuple-element.42), channel_id=1, source_target_pairs={{0,4},{4,0},{8,12},{12,8},{16,20},{20,16},{24,28},{28,24},{1,5},{5... | collective-permute-start | bytes 983048 | tf_op jit(solution)/shard_map/ppermute | solution.py:306
  8.0 1.5 %collective-permute-start.3 = (bf16[128,1024]{1,0:T(8,128)(2,1)S(1)}, bf16[128,1024]{1,0:T(8,128)(2,1)S(1)}, u32[]{:S(2)}, u32[]{:S(2)}) collective-permute-start(bf16[128,1024]{1,0:T(8,128)(2,1)S(1)} %bitcast.23), channel_id=1, source_target_pairs={{0,16},{4,20},{8,24},{12,28},{16,0},{20,4},{24,8},{28,12},{1,17},{... | collective-permute-start | bytes 786440 | tf_op jit(solution)/shard_map/ppermute | solution.py:306
  9.6 2.0 %collective-permute-start.4 = (bf16[128,1024]{1,0:T(8,128)(2,1)S(1)}, bf16[128,1024]{1,0:T(8,128)(2,1)S(1)}, u32[]{:S(2)}, u32[]{:S(2)}) collective-permute-start(bf16[128,1024]{1,0:T(8,128)(2,1)S(1)} %bitcast.25), channel_id=1, source_target_pairs={{0,24},{4,28},{8,16},{12,20},{16,8},{20,12},{24,0},{28,4},{1,25},{... | collective-permute-start | bytes 786440 | tf_op jit(solution)/shard_map/ppermute | solution.py:306
  12.3 3.7 %own_rows.1 = (bf16[112,1024]{1,0:T(8,128)(2,1)S(1)}, f32[112,1024]{1,0:T(8,128)S(1)}, bf16[112,3072]{1,0:T(8,128)(2,1)S(1)}, bf16[1024,3072]{1,0:T(8,128)(2,1)S(1)}) custom-call(s32[5]{0:T(128)S(1)} %stack.19.place, f32[265,1024]{1,0:T(8,128)S(1)} %pad_maximum_fusion.both, bf16[1024,3072]{1,0:T(8,128)(2,1)} %w.1), custom_call_target="tpu_custom_call" | custom-call | flops 704643072 | bytes 9000000 | tf_op jit(solution)/shard_map/own_rows/pallas_call | solution.py:290
  16.0 3.0 %rim_rows.1 = (bf16[16,1024]{1,0:T(8,128)(2,1)S(1)}, f32[32,1024]{1,0:T(8,128)S(1)}, bf16[224,3072]{1,0:T(8,128)(2,1)S(1)}) custom-call(s32[5]{0:T(128)S(1)} %stack.19.place, bf16[160,1024]{1,0:T(8,128)(2,1)S(1)} %collective-permute-done.near, bf16[160,1024]{1,0:T(8,128)(2,1)S(1)} %collective-permute-done.1.far, f32[265,1024]{1,0:T(8,128)S(1)} %pad_maximum_fusion.both, ...), custom_call_target="tpu_custom_call" | custom-call | flops 1107296256 | bytes 9000000 | tf_op jit(solution)/shard_map/rim_rows/pallas_call | solution.py:290
  19.0 4.6 %attend.1 = (bf16[128,1024]{1,0:T(8,128)(2,1)}, bf16[144,3072]{1,0:T(8,128)(2,1)S(1)}, bf16[4,128,768]{2,1,0:T(8,128)(2,1)S(1)}) custom-call(s32[5]{0:T(128)S(1)} %stack.19.place, bf16[224,3072]{1,0:T(8,128)(2,1)S(1)} %get-tuple-element.20.rim, bf16[112,3072]{1,0:T(8,128)(2,1)S(1)} %get-tuple-element.21.mid, f32[265,1024]{1,0:T(8,128)S(1)} %pad_maximum_fusion.both, ...), custom_call_target="tpu_custom_call" | custom-call | flops 5234491392 | bytes 5000000 | tf_op jit(solution)/shard_map/attend/pallas_call | solution.py:290
  23.7 2.8 %collective-permute-start.8 = (bf16[128,768]{1,0:T(8,128)(2,1)S(1)}, bf16[128,768]{1,0:T(8,128)(2,1)S(1)}, u32[]{:S(2)}, u32[]{:S(2)}) collective-permute-start(bf16[128,768]{1,0:T(8,128)(2,1)S(1)} %get-tuple-element.38), channel_id=1, source_target_pairs={{0,24},{4,28},{8,16},{12,20},{16,8},{20,12},{24,0},{28,4},{1,25},{... | collective-permute-start | bytes 589832 | tf_op jit(solution)/shard_map/ppermute | solution.py:306
  26.7 1.2 %collective-permute-start.6 = (bf16[128,768]{1,0:T(8,128)(2,1)S(1)}, bf16[128,768]{1,0:T(8,128)(2,1)S(1)}, u32[]{:S(2)}, u32[]{:S(2)}) collective-permute-start(bf16[128,768]{1,0:T(8,128)(2,1)S(1)} %get-tuple-element.40), channel_id=1, source_target_pairs={{0,8},{4,12},{8,0},{12,4},{16,24},{20,28},{24,16},{28,20},{1,9},{5... | collective-permute-start | bytes 589832 | tf_op jit(solution)/shard_map/ppermute | solution.py:306
  28.6 1.3 %collective-permute-done.5.tails = bf16[64,1024]{1,0:T(8,128)(2,1)S(1)} collective-permute-done((bf16[64,1024]{1,0:T(8,128)(2,1)S(1)}, bf16[64,1024]{1,0:T(8,128)(2,1)S(1)}, u32[]{:S(2)}, u32[]{:S(2)}) %collective-permute-start.5) | collective-permute-done | bytes 131104 | tf_op jit(solution)/shard_map/ppermute | solution.py:306
  29.9 3.0 %peer_hidden.1.peers = bf16[384,1024]{1,0:T(8,128)(2,1)S(1)} custom-call(s32[5]{0:T(128)S(1)} %stack.19.place, bf16[128,1024]{1,0:T(8,128)(2,1)S(1)} %collective-permute-done.2.f1, bf16[128,1024]{1,0:T(8,128)(2,1)S(1)} %collective-permute-done.3.f2, bf16[128,1024]{1,0:T(8,128)(2,1)S(1)} %collective-permute-done.4.f3, ...), custom_call_target="tpu_custom_call" | custom-call | flops 15728640 | bytes 2000000 | tf_op jit(solution)/shard_map/peer_hidden/pallas_call | solution.py:290
  32.9 2.3 %collective-permute-done.7.b2 = bf16[128,768]{1,0:T(8,128)(2,1)S(1)} collective-permute-done((bf16[128,768]{1,0:T(8,128)(2,1)S(1)}, bf16[128,768]{1,0:T(8,128)(2,1)S(1)}, u32[]{:S(2)}, u32[]{:S(2)}) %collective-permute-start.7) | collective-permute-done | bytes 196640 | tf_op jit(solution)/shard_map/ppermute | solution.py:306
  35.2 0.8 %collective-permute-done.6.b1 = bf16[128,768]{1,0:T(8,128)(2,1)S(1)} collective-permute-done((bf16[128,768]{1,0:T(8,128)(2,1)S(1)}, bf16[128,768]{1,0:T(8,128)(2,1)S(1)}, u32[]{:S(2)}, u32[]{:S(2)}) %collective-permute-start.6) | collective-permute-done | bytes 196640 | tf_op jit(solution)/shard_map/ppermute | solution.py:306
  36.1 1.6 %weight_send.1 = bf16[768,512]{1,0:T(8,128)(2,1)S(1)} custom-call(s32[5]{0:T(128)S(1)} %stack.19.place, bf16[16,1024]{1,0:T(8,128)(2,1)S(1)} %get-tuple-element.26.first, bf16[112,1024]{1,0:T(8,128)(2,1)S(1)} %get-tuple-element.27.mid, bf16[384,1024]{1,0:T(8,128)(2,1)S(1)} %peer_hidden.1.peers, bf16[4,128,768]{2,1,0:T(8,128)(2,1)S(1)} %get-tuple-element.28.b, ...), custom_call_target="tpu_custom_call" | custom-call | flops 402653184 | bytes 6000000 | tf_op jit(solution)/shard_map/weight_send/pallas_call | solution.py:290
  37.7 1.5 %weight_keep.1.keep = f32[768,512]{1,0:T(8,128)S(1)} custom-call(s32[5]{0:T(128)S(1)} %stack.19.place, bf16[16,1024]{1,0:T(8,128)(2,1)S(1)} %get-tuple-element.26.first, bf16[112,1024]{1,0:T(8,128)(2,1)S(1)} %get-tuple-element.27.mid, bf16[384,1024]{1,0:T(8,128)(2,1)S(1)} %peer_hidden.1.peers, bf16[4,128,768]{2,1,0:T(8,128)(2,1)S(1)} %get-tuple-element.28.b, ...), custom_call_target="tpu_custom_call" | custom-call | flops 402653184 | bytes 6000000 | tf_op jit(solution)/shard_map/weight_keep/pallas_call | solution.py:290
  39.3 0.7 %collective-permute-done.9.got = bf16[768,512]{1,0:T(8,128)(2,1)S(1)} collective-permute-done((bf16[768,512]{1,0:T(8,128)(2,1)S(1)}, bf16[768,512]{1,0:T(8,128)(2,1)S(1)}, u32[]{:S(2)}, u32[]{:S(2)}) %collective-permute-start.9) | collective-permute-done | bytes 786464 | tf_op jit(solution)/shard_map/ppermute | solution.py:306
  40.0 0.7 core_sum.1
  40.7 1.6 %collective-permute-start.10 = (bf16[192,512]{1,0:T(8,128)(2,1)S(1)}, bf16[192,512]{1,0:T(8,128)(2,1)S(1)}, u32[]{:S(2)}, u32[]{:S(2)}) collective-permute-start(bf16[192,512]{1,0:T(8,128)(2,1)S(1)} %get-tuple-element.29.refs_0_), channel_id=1, source_target_pairs={{0,1},{1,0},{2,3},{3,2},{4,5},{5,4},{6,7},{7,6},{8,9},{9,8},{10,11... | collective-permute-start | bytes 589832 | tf_op jit(solution)/shard_map/ppermute | solution.py:306
  42.8 5.7 %collective-permute-done.10.got = bf16[192,512]{1,0:T(8,128)(2,1)S(1)} collective-permute-done((bf16[192,512]{1,0:T(8,128)(2,1)S(1)}, bf16[192,512]{1,0:T(8,128)(2,1)S(1)}, u32[]{:S(2)}, u32[]{:S(2)}) %collective-permute-start.10) | collective-permute-done | bytes 196640 | tf_op jit(solution)/shard_map/ppermute | solution.py:306
  48.5 0.6 forward.1
  49.1 3.7 %collective-permute-start.11 = (bf16[192,512]{1,0:T(8,128)(2,1)S(1)}, bf16[192,512]{1,0:T(8,128)(2,1)S(1)}, u32[]{:S(2)}, u32[]{:S(2)}) collective-permute-start(bf16[192,512]{1,0:T(8,128)(2,1)S(1)} %forward.1), channel_id=1, source_target_pairs={{0,3},{1,2},{2,1},{3,0},{4,7},{5,6},{6,5},{7,4},{8,11},{9,10},{10,... | collective-permute-start | bytes 589832 | tf_op jit(solution)/shard_map/ppermute | solution.py:306
  52.7 4.4 %input_grad.1 = (bf16[128,1024]{1,0:T(8,128)(2,1)}, f32[8,128]{1,0:T(8,128)S(1)}) custom-call(s32[5]{0:T(128)S(1)} %stack.19.place, bf16[144,3072]{1,0:T(8,128)(2,1)S(1)} %get-tuple-element.23._.grads, bf16[1024,3072]{1,0:T(8,128)(2,1)S(1)} %get-tuple-element.19.w, f32[112,1024]{1,0:T(8,128)S(1)} %get-tuple-element.24.conv_mid, ...), custom_call_target="tpu_custom_call" | custom-call | flops 905969664 | bytes 9000000 | tf_op jit(solution)/shard_map/input_grad/pallas_call | solution.py:290
  57.2 1.1 %collective-permute-done.11.g1 = bf16[192,512]{1,0:T(8,128)(2,1)S(1)} collective-permute-done((bf16[192,512]{1,0:T(8,128)(2,1)S(1)}, bf16[192,512]{1,0:T(8,128)(2,1)S(1)}, u32[]{:S(2)}, u32[]{:S(2)}) %collective-permute-start.11) | collective-permute-done | bytes 196640 | tf_op jit(solution)/shard_map/ppermute | solution.py:306
  58.2 0.6 part_sum.1.own
  58.9 2.4 %collective-permute-start.15 = (bf16[192,128]{1,0:T(8,128)(2,1)S(1)}, bf16[192,128]{1,0:T(8,128)(2,1)S(1)}, u32[]{:S(2)}, u32[]{:S(2)}) collective-permute-start(bf16[192,128]{1,0:T(8,128)(2,1)S(1)} %get-tuple-element.43), channel_id=1, source_target_pairs={{0,24},{4,28},{8,16},{12,20},{16,8},{20,12},{24,0},{28,4},{1,25},{... | collective-permute-start | bytes 147464 | tf_op jit(solution)/shard_map/ppermute | solution.py:306
  61.3 1.5 %collective-permute-start.14 = (bf16[192,128]{1,0:T(8,128)(2,1)S(1)}, bf16[192,128]{1,0:T(8,128)(2,1)S(1)}, u32[]{:S(2)}, u32[]{:S(2)}) collective-permute-start(bf16[192,128]{1,0:T(8,128)(2,1)S(1)} %get-tuple-element.44), channel_id=1, source_target_pairs={{0,16},{4,20},{8,24},{12,28},{16,0},{20,4},{24,8},{28,12},{1,17},{... | collective-permute-start | bytes 147464 | tf_op jit(solution)/shard_map/ppermute | solution.py:306
  62.7 1.2 %collective-permute-done.15.g3 = bf16[192,128]{1,0:T(8,128)(2,1)S(1)} collective-permute-done((bf16[192,128]{1,0:T(8,128)(2,1)S(1)}, bf16[192,128]{1,0:T(8,128)(2,1)S(1)}, u32[]{:S(2)}, u32[]{:S(2)}) %collective-permute-start.15) | collective-permute-done | bytes 49184 | tf_op jit(solution)/shard_map/ppermute | solution.py:306
  63.9 1.5 %collective-permute-done.14.g2 = bf16[192,128]{1,0:T(8,128)(2,1)S(1)} collective-permute-done((bf16[192,128]{1,0:T(8,128)(2,1)S(1)}, bf16[192,128]{1,0:T(8,128)(2,1)S(1)}, u32[]{:S(2)}, u32[]{:S(2)}) %collective-permute-start.14) | collective-permute-done | bytes 49184 | tf_op jit(solution)/shard_map/ppermute | solution.py:306
  65.4 1.5 %collective-permute-done.13.g1 = bf16[192,128]{1,0:T(8,128)(2,1)S(1)} collective-permute-done((bf16[192,128]{1,0:T(8,128)(2,1)S(1)}, bf16[192,128]{1,0:T(8,128)(2,1)S(1)}, u32[]{:S(2)}, u32[]{:S(2)}) %collective-permute-start.13) | collective-permute-done | bytes 49184 | tf_op jit(solution)/shard_map/ppermute | solution.py:306
  66.8 1.4 %place.1 = f32[6,128,128]{2,1,0:T(8,128)} custom-call(s32[5]{0:T(128)S(1)} %stack.19.place, bf16[4,192,128]{2,1,0:T(8,128)(2,1)S(1)} %part_sum.1.own, bf16[192,128]{1,0:T(8,128)(2,1)S(1)} %collective-permute-done.13.g1, bf16[192,128]{1,0:T(8,128)(2,1)S(1)} %collective-permute-done.14.g2, bf16[192,128]{1,0:T(8,128)(2,1)S(1)} %collective-permute-done.15.g3), custom_call_target="tpu_custom_call" | custom-call | flops 1000000 | bytes 1000000 | tf_op jit(solution)/shard_map/place/pallas_call | solution.py:290
  (24 shorter events, 1.8 us)
Async XLA Ops:
  0.6 2.1 %copy-start.1 = (f32[9,1024]{1,0:T(8,128)S(1)}, f32[9,1024]{1,0:T(8,128)}, u32[]{:S(2)}) copy-start(f32[9,1024]{1,0:T(8,128)} %param.7) | copy-start | bytes 110596
  2.8 5.3 %copy-start = (bf16[1,128,1024]{2,1,0:T(8,128)(2,1)S(1)}, bf16[1,128,1024]{2,1,0:T(8,128)(2,1)}, u32[]{:S(2)}) copy-start(bf16[1,128,1024]{2,1,0:T(8,128)(2,1)} %param.5) | copy-start | bytes 786436
  3.0 13.0 %collective-permute-start.1 = (bf16[160,1024]{1,0:T(8,128)(2,1)S(1)}, bf16[160,1024]{1,0:T(8,128)(2,1)S(1)}, u32[]{:S(2)}, u32[]{:S(2)}) collective-permute-start(bf16[160,1024]{1,0:T(8,128)(2,1)S(1)} %get-tuple-element.41), channel_id=1, source_target_pairs={{4,8},{8,4},{12,16},{16,12},{20,24},{24,20},{5,9},{9,5},{13,17},{1... | collective-permute-start | bytes 983048 | tf_op jit(solution)/shard_map/ppermute | solution.py:326
  3.7 12.3 %collective-permute-start = (bf16[160,1024]{1,0:T(8,128)(2,1)S(1)}, bf16[160,1024]{1,0:T(8,128)(2,1)S(1)}, u32[]{:S(2)}, u32[]{:S(2)}) collective-permute-start(bf16[160,1024]{1,0:T(8,128)(2,1)S(1)} %get-tuple-element.42), channel_id=1, source_target_pairs={{0,4},{4,0},{8,12},{12,8},{16,20},{20,16},{24,28},{28,24},{1,5},{5... | collective-permute-start | bytes 983048 | tf_op jit(solution)/shard_map/ppermute | solution.py:306
  8.0 18.6 %collective-permute-start.3 = (bf16[128,1024]{1,0:T(8,128)(2,1)S(1)}, bf16[128,1024]{1,0:T(8,128)(2,1)S(1)}, u32[]{:S(2)}, u32[]{:S(2)}) collective-permute-start(bf16[128,1024]{1,0:T(8,128)(2,1)S(1)} %bitcast.23), channel_id=1, source_target_pairs={{0,16},{4,20},{8,24},{12,28},{16,0},{20,4},{24,8},{28,12},{1,17},{... | collective-permute-start | bytes 786440 | tf_op jit(solution)/shard_map/ppermute | solution.py:306
  9.6 18.4 %collective-permute-start.2 = (bf16[128,1024]{1,0:T(8,128)(2,1)S(1)}, bf16[128,1024]{1,0:T(8,128)(2,1)S(1)}, u32[]{:S(2)}, u32[]{:S(2)}) collective-permute-start(bf16[128,1024]{1,0:T(8,128)(2,1)S(1)} %bitcast.24), channel_id=1, source_target_pairs={{0,8},{4,12},{8,0},{12,4},{16,24},{20,28},{24,16},{28,20},{1,9},{5... | collective-permute-start | bytes 786440 | tf_op jit(solution)/shard_map/ppermute | solution.py:306
  9.6 18.4 %collective-permute-start.4 = (bf16[128,1024]{1,0:T(8,128)(2,1)S(1)}, bf16[128,1024]{1,0:T(8,128)(2,1)S(1)}, u32[]{:S(2)}, u32[]{:S(2)}) collective-permute-start(bf16[128,1024]{1,0:T(8,128)(2,1)S(1)} %bitcast.25), channel_id=1, source_target_pairs={{0,24},{4,28},{8,16},{12,20},{16,8},{20,12},{24,0},{28,4},{1,25},{... | collective-permute-start | bytes 786440 | tf_op jit(solution)/shard_map/ppermute | solution.py:306
  23.7 9.3 %collective-permute-start.8 = (bf16[128,768]{1,0:T(8,128)(2,1)S(1)}, bf16[128,768]{1,0:T(8,128)(2,1)S(1)}, u32[]{:S(2)}, u32[]{:S(2)}) collective-permute-start(bf16[128,768]{1,0:T(8,128)(2,1)S(1)} %get-tuple-element.38), channel_id=1, source_target_pairs={{0,24},{4,28},{8,16},{12,20},{16,8},{20,12},{24,0},{28,4},{1,25},{... | collective-permute-start | bytes 589832 | tf_op jit(solution)/shard_map/ppermute | solution.py:306
  26.5 8.8 %collective-permute-start.7 = (bf16[128,768]{1,0:T(8,128)(2,1)S(1)}, bf16[128,768]{1,0:T(8,128)(2,1)S(1)}, u32[]{:S(2)}, u32[]{:S(2)}) collective-permute-start(bf16[128,768]{1,0:T(8,128)(2,1)S(1)} %get-tuple-element.39), channel_id=1, source_target_pairs={{0,16},{4,20},{8,24},{12,28},{16,0},{20,4},{24,8},{28,12},{1,17},{... | collective-permute-start | bytes 589832 | tf_op jit(solution)/shard_map/ppermute | solution.py:306
  26.7 9.4 %collective-permute-start.6 = (bf16[128,768]{1,0:T(8,128)(2,1)S(1)}, bf16[128,768]{1,0:T(8,128)(2,1)S(1)}, u32[]{:S(2)}, u32[]{:S(2)}) collective-permute-start(bf16[128,768]{1,0:T(8,128)(2,1)S(1)} %get-tuple-element.40), channel_id=1, source_target_pairs={{0,8},{4,12},{8,0},{12,4},{16,24},{20,28},{24,16},{28,20},{1,9},{5... | collective-permute-start | bytes 589832 | tf_op jit(solution)/shard_map/ppermute | solution.py:306
  28.5 1.4 %collective-permute-start.5 = (bf16[64,1024]{1,0:T(8,128)(2,1)S(1)}, bf16[64,1024]{1,0:T(8,128)(2,1)S(1)}, u32[]{:S(2)}, u32[]{:S(2)}) collective-permute-start(bf16[64,1024]{1,0:T(8,128)(2,1)S(1)} %ends.1), channel_id=1, source_target_pairs={{0,4},{4,0},{8,12},{12,8},{16,20},{20,16},{24,28},{28,24},{1,5},{5... | collective-permute-start | bytes 393224 | tf_op jit(solution)/shard_map/ppermute | solution.py:306
  37.6 2.4 %collective-permute-start.9 = (bf16[768,512]{1,0:T(8,128)(2,1)S(1)}, bf16[768,512]{1,0:T(8,128)(2,1)S(1)}, u32[]{:S(2)}, u32[]{:S(2)}) collective-permute-start(bf16[768,512]{1,0:T(8,128)(2,1)S(1)} %weight_send.1), channel_id=1, source_target_pairs={{0,4},{4,0},{8,12},{12,8},{16,20},{20,16},{24,28},{28,24},{1,5},{5... | collective-permute-start | bytes 2359304 | tf_op jit(solution)/shard_map/ppermute | solution.py:306
  40.7 7.8 %collective-permute-start.10 = (bf16[192,512]{1,0:T(8,128)(2,1)S(1)}, bf16[192,512]{1,0:T(8,128)(2,1)S(1)}, u32[]{:S(2)}, u32[]{:S(2)}) collective-permute-start(bf16[192,512]{1,0:T(8,128)(2,1)S(1)} %get-tuple-element.29.refs_0_), channel_id=1, source_target_pairs={{0,1},{1,0},{2,3},{3,2},{4,5},{5,4},{6,7},{7,6},{8,9},{9,8},{10,11... | collective-permute-start | bytes 589832 | tf_op jit(solution)/shard_map/ppermute | solution.py:306
  42.3 14.9 %collective-permute-start.12 = (bf16[192,512]{1,0:T(8,128)(2,1)S(1)}, bf16[192,512]{1,0:T(8,128)(2,1)S(1)}, u32[]{:S(2)}, u32[]{:S(2)}) collective-permute-start(bf16[192,512]{1,0:T(8,128)(2,1)S(1)} %get-tuple-element.33), channel_id=1, source_target_pairs={{0,1},{1,0},{2,3},{3,2},{4,5},{5,4},{6,7},{7,6},{8,9},{9,8},{10,11... | collective-permute-start | bytes 589832 | tf_op jit(solution)/shard_map/ppermute | solution.py:306
  49.1 9.2 %collective-permute-start.11 = (bf16[192,512]{1,0:T(8,128)(2,1)S(1)}, bf16[192,512]{1,0:T(8,128)(2,1)S(1)}, u32[]{:S(2)}, u32[]{:S(2)}) collective-permute-start(bf16[192,512]{1,0:T(8,128)(2,1)S(1)} %forward.1), channel_id=1, source_target_pairs={{0,3},{1,2},{2,1},{3,0},{4,7},{5,6},{6,5},{7,4},{8,11},{9,10},{10,... | collective-permute-start | bytes 589832 | tf_op jit(solution)/shard_map/ppermute | solution.py:306
  58.9 5.1 %collective-permute-start.15 = (bf16[192,128]{1,0:T(8,128)(2,1)S(1)}, bf16[192,128]{1,0:T(8,128)(2,1)S(1)}, u32[]{:S(2)}, u32[]{:S(2)}) collective-permute-start(bf16[192,128]{1,0:T(8,128)(2,1)S(1)} %get-tuple-element.43), channel_id=1, source_target_pairs={{0,24},{4,28},{8,16},{12,20},{16,8},{20,12},{24,0},{28,4},{1,25},{... | collective-permute-start | bytes 147464 | tf_op jit(solution)/shard_map/ppermute | solution.py:306
  61.3 4.1 %collective-permute-start.14 = (bf16[192,128]{1,0:T(8,128)(2,1)S(1)}, bf16[192,128]{1,0:T(8,128)(2,1)S(1)}, u32[]{:S(2)}, u32[]{:S(2)}) collective-permute-start(bf16[192,128]{1,0:T(8,128)(2,1)S(1)} %get-tuple-element.44), channel_id=1, source_target_pairs={{0,16},{4,20},{8,24},{12,28},{16,0},{20,4},{24,8},{28,12},{1,17},{... | collective-permute-start | bytes 147464 | tf_op jit(solution)/shard_map/ppermute | solution.py:306
  62.7 4.1 %collective-permute-start.13 = (bf16[192,128]{1,0:T(8,128)(2,1)S(1)}, bf16[192,128]{1,0:T(8,128)(2,1)S(1)}, u32[]{:S(2)}, u32[]{:S(2)}) collective-permute-start(bf16[192,128]{1,0:T(8,128)(2,1)S(1)} %get-tuple-element.45), channel_id=1, source_target_pairs={{0,8},{4,12},{8,0},{12,4},{16,24},{20,28},{24,16},{28,20},{1,9},{5... | collective-permute-start | bytes 147464 | tf_op jit(solution)/shard_map/ppermute | solution.py:306

commit v4 on v3

--- a/solution.py
+++ b/solution.py
@@ -251,33 +251,55 @@
         out[:, k * HEAD : (k + 1) * HEAD] = dot(left, right, 0, 0).astype(out.dtype)
 
 
-def core_sum_kernel(place, keep, got, own, near, cross, ahead):
-    for mask, out in ((2, near), (3, ahead), (1, cross), (0, own)):
-        i = place[4] ^ mask
-        at = 0
-        for size, base in ((HEAD, 0), (HEAD // 2, 4 * HEAD)):
-            rows = pl.ds(pl.multiple_of(base + i * size, size), size)
+def block(index):
+    return pl.ds(pl.multiple_of(index * HEAD, HEAD), HEAD)
+
+
+def halves(place, value, same, other):
+    bit = place[2] % 2
+    for out, x in ((other, 1 - bit), (same, bit)):
+        for y in range(2):
+            out[:, y * HEAD : (y + 1) * HEAD] = value(block(2 * y + x)).astype(out.dtype)
+
+
+def core_sum_kernel(place, keep, got, near, ahead, *outs):
+    parts = ((0, HEAD, 0), (HEAD, HEAD // 2, 4 * HEAD))
+
+    def rows_of(mask, size, base):
+        return pl.ds(pl.multiple_of(base + (place[4] ^ mask) * size, size), size)
+
+    for mask, out in ((2, near), (3, ahead)):
+        for at, size, base in parts:
+            rows = rows_of(mask, size, base)
             out[at : at + size] = (keep[rows] + got[rows].astype(F32)).astype(out.dtype)
-            at += size
-
-
-def forward_kernel(place, ahead, got, out):
-    out[...] = (ahead[...] + got[...].astype(F32)).astype(BF16)
-
-
-def part_sum_kernel(place, own, g1, g2, _, sends):
-    chip = place[2]
-    for k in range(4):
-        cols = pl.ds(k * HEAD, HEAD)
-        total = own[:, cols] + g1[:, cols].astype(F32) + g2[:, cols].astype(F32)
-        sends[k ^ chip] = total.astype(BF16)
-
-
-def place_kernel(scale, place, own, g1, g2, g3, out):
-    chip = place[2]
-    for slot, ref in enumerate((own.at[0], g1, g2, g3)):
-        k = chip ^ slot
-        value = ref[...].astype(F32) * scale
+    for mask, same, other in ((1, *outs[:2]), (0, *outs[2:])):
+        for at, size, base in parts:
+            rows = rows_of(mask, size, base)
+            halves(
+                place,
+                lambda cols, rows=rows: keep[rows, cols] + got[rows, cols].astype(F32),
+                same.at[at : at + size],
+                other.at[at : at + size],
+            )
+
+
+def forward_kernel(place, ahead, got, same, other):
+    halves(place, lambda cols: ahead[:, cols] + got[:, cols].astype(F32), same, other)
+
+
+def mid_sum_kernel(place, s0, s1, s2, o0, o1, o2, _, keep, send):
+    bit = place[2] // 2
+    for out, y in ((send, 1 - bit), (keep, bit)):
+        cols = block(y)
+        for i, refs in enumerate(((s0, s1, s2), (o0, o1, o2))):
+            a, b, c = (ref[:, cols].astype(F32) for ref in refs)
+            out[i] = (a + b + c).astype(out.dtype)
+
+
+def place_kernel(scale, place, keep, got, out):
+    for slot, ref in enumerate((keep, keep, got, got)):
+        value = ref[slot % 2].astype(F32) * scale
+        k = place[2] ^ slot
         out[k + (k + 1) // 2] = value[:HEAD]
         start = pl.multiple_of((k % 2) * (HEAD // 2), HEAD // 2)
         out[1 + 3 * (k // 2), pl.ds(start, HEAD // 2)] = value[HEAD:]
@@ -304,6 +326,13 @@
 
 def swap(value, axis, mask):
     return lax.ppermute(value, axis, [(i, i ^ mask) for i in range(lax.axis_size(axis))])
+
+
+def swap_both(value, dp_mask, tm_mask):
+    recs = lax.axis_size("dp")
+    count = lax.axis_size("tm") * recs
+    pairs = [(i, (i // recs ^ tm_mask) * recs + (i % recs ^ dp_mask)) for i in range(count)]
+    return lax.ppermute(value, ("tm", "dp"), pairs)
 
 
 def on_device(frames_in, valid_frames, kernel, w_qkv, cotangent):
@@ -409,10 +438,18 @@
             for mine in (False, True)
         )
         sibling = swap(send, "tm", 1)
-        own, near, cross, ahead = call(
+        half = (shard, 2 * HEAD)
+        near, ahead, cross_same, cross_other, own_same, own_other = call(
             core_sum_kernel,
             "core_sum",
-            [((shard, width // 2), dtype) for dtype in (F32, BF16, BF16, F32)],
+            [
+                ((shard, width // 2), BF16),
+                ((shard, width // 2), F32),
+                (half, BF16),
+                (half, BF16),
+                (half, F32),
+                (half, BF16),
+            ],
             place,
             [keep, sibling],
         )
@@ -429,26 +466,27 @@
             moved=9000000,
             after=late,
         )
-        got_near, got_cross = swap(near, "dp", 1), swap(cross, "dp", 1)
-        (ahead,) = call(
-            forward_kernel, "forward", [((shard, width // 2), BF16)], place, [ahead, got_near]
-        )
-        summed = [swap(ahead, "dp", 3), got_cross]
-        (blocks,) = call(
-            part_sum_kernel,
-            "part_sum",
-            [((4, shard, HEAD), BF16)],
+        got_near = swap(near, "dp", 1)
+        got_cross = swap(cross_same, "dp", 1), swap_both(cross_other, 1, 2)
+        got_own = swap(own_other, "tm", 2)
+        same, other = call(
+            forward_kernel, "forward", [(half, BF16)] * 2, place, [ahead, got_near]
+        )
+        got_sums = swap(same, "dp", 3), swap_both(other, 3, 2)
+        keep, send = call(
+            mid_sum_kernel,
+            "mid_sum",
+            [((2, shard, HEAD), F32), ((2, shard, HEAD), BF16)],
             place,
-            [own, *summed],
+            [own_same, got_cross[0], got_sums[0], got_own, got_cross[1], got_sums[1]],
             after=[done],
         )
-        last = [swap(blocks[slot], "tm", 2 * slot) for slot in (1, 2, 3)]
         (qkv_grad,) = call(
             functools.partial(place_kernel, scale),
             "place",
             [((3 * HEADS // 4, HEAD, HEAD), F32)],
             place,
-            [blocks, *last],
+            [keep, swap(send, "tm", 4)],
         )
     else:
         late = []

time: 68.4 us -> 67.1 us (0.981)
  waiting for transfers between devices: 16.1 us -> 11.7 us
  starting transfers between devices: 22.5 us -> 25.6 us
    ppermute x15 -> x14, waiting for transfers between devices: 16.1 us -> 10.7 us  [swap(): lax.ppermute(value, axis, [(i, i ^ mask) for i in range(lax.axis_size(axi...]
    ppermute x0 -> x2, starting transfers between devices: none -> 3.03 us  [swap_both(): return lax.ppermute(value, ('tm', 'dp'), pairs)]
    ppermute x0 -> x2, waiting for transfers between devices: none -> 1.05 us  [swap_both(): return lax.ppermute(value, ('tm', 'dp'), pairs)]
    ppermute x15 -> x14, starting transfers between devices: 21.9 us -> 21.9 us  [swap(): lax.ppermute(value, axis, [(i, i ^ mask) for i in range(lax.axis_size(axi...]
  transfers between devices with their start and end apart: 16 -> 17, of which waited for: 9 -> 7; matrix products, arithmetic and copies ran while one was open for 0% -> 0% of each run, Pallas kernels for 31% -> 32%
where the time goes in v4:
time: 67.1 us; the launch traced here: 66.9 us
  starting transfers between devices  25.6 us (38%)
  Pallas kernels  25.6 us (38%)
  waiting for transfers between devices  11.7 us (17%)
  other arithmetic  2.23 us (3%)
  between operations  1.51 us (2%)
    pallas_call x12, Pallas kernels, call(): pl.pallas_call(kernel, name=name, out_shape=[jax.ShapeDtypeStruct(shape,...  25.6 us
    ppermute x14, starting transfers between devices, swap(): lax.ppermute(value, axis, [(i, i ^ mask) for i in range(lax.axis_size(axi...  21.9 us
    ppermute x14, waiting for transfers between devices, swap(): lax.ppermute(value, axis, [(i, i ^ mask) for i in range(lax.axis_size(axi...  10.7 us
    ppermute x2, starting transfers between devices, swap_both(): return lax.ppermute(value, ('tm', 'dp'), pairs)  3.03 us
  transfers between devices with their start and end apart: 17, of which 7 were waited for; matrix products, arithmetic and copies ran while one was open for 0% of the time, Pallas kernels for 32%

profile of v4, /device:TPU:0, one launch (start us, length us, event | category | flops | bytes accessed | tf_op | source)
XLA Modules:
  0.0 66.9 jit_solution(13007461407405422183)
XLA Ops:
  0.7 1.0 %bitcast_convert_fusion = f32[128,1024]{1,0:T(8,128)S(1)} fusion(bf16[1,128,1024]{2,1,0:T(8,128)(2,1)} %param.9), kind=kLoop, calls=%fused_computation.7 | loop fusion | flops 131072 | bytes 786432 | tf_op jit(solution)/shard_map/convert_element_type | solution.py:349
  1.7 1.0 %bitcast_convert_fusion.1 = f32[128,1024]{1,0:T(8,128)S(1)} fusion(bf16[1,128,1024]{2,1,0:T(8,128)(2,1)} %param.5), kind=kLoop, calls=%fused_computation.11 | loop fusion | flops 131072 | bytes 786432 | tf_op jit(solution)/shard_map/convert_element_type | solution.py:349
  3.0 0.7 %collective-permute-start.1 = (bf16[160,1024]{1,0:T(8,128)(2,1)S(1)}, bf16[160,1024]{1,0:T(8,128)(2,1)S(1)}, u32[]{:S(2)}, u32[]{:S(2)}) collective-permute-start(bf16[160,1024]{1,0:T(8,128)(2,1)S(1)} %get-tuple-element.53), channel_id=1, source_target_pairs={{4,8},{8,4},{12,16},{16,12},{20,24},{24,20},{5,9},{9,5},{13,17},{1... | collective-permute-start | bytes 983048 | tf_op jit(solution)/shard_map/ppermute | solution.py:355
  3.7 4.3 %collective-permute-start = (bf16[160,1024]{1,0:T(8,128)(2,1)S(1)}, bf16[160,1024]{1,0:T(8,128)(2,1)S(1)}, u32[]{:S(2)}, u32[]{:S(2)}) collective-permute-start(bf16[160,1024]{1,0:T(8,128)(2,1)S(1)} %get-tuple-element.54), channel_id=1, source_target_pairs={{0,4},{4,0},{8,12},{12,8},{16,20},{20,16},{24,28},{28,24},{1,5},{5... | collective-permute-start | bytes 983048 | tf_op jit(solution)/shard_map/ppermute | solution.py:328
  8.0 1.5 %collective-permute-start.3 = (bf16[128,1024]{1,0:T(8,128)(2,1)S(1)}, bf16[128,1024]{1,0:T(8,128)(2,1)S(1)}, u32[]{:S(2)}, u32[]{:S(2)}) collective-permute-start(bf16[128,1024]{1,0:T(8,128)(2,1)S(1)} %bitcast.17), channel_id=1, source_target_pairs={{0,16},{4,20},{8,24},{12,28},{16,0},{20,4},{24,8},{28,12},{1,17},{... | collective-permute-start | bytes 786440 | tf_op jit(solution)/shard_map/ppermute | solution.py:328
  9.6 2.0 %collective-permute-start.4 = (bf16[128,1024]{1,0:T(8,128)(2,1)S(1)}, bf16[128,1024]{1,0:T(8,128)(2,1)S(1)}, u32[]{:S(2)}, u32[]{:S(2)}) collective-permute-start(bf16[128,1024]{1,0:T(8,128)(2,1)S(1)} %bitcast.19), channel_id=1, source_target_pairs={{0,24},{4,28},{8,16},{12,20},{16,8},{20,12},{24,0},{28,4},{1,25},{... | collective-permute-start | bytes 786440 | tf_op jit(solution)/shard_map/ppermute | solution.py:328
  12.3 3.7 %own_rows.1 = (bf16[112,1024]{1,0:T(8,128)(2,1)S(1)}, f32[112,1024]{1,0:T(8,128)S(1)}, bf16[112,3072]{1,0:T(8,128)(2,1)S(1)}, bf16[1024,3072]{1,0:T(8,128)(2,1)S(1)}) custom-call(s32[5]{0:T(128)S(1)} %stack.19.place, f32[265,1024]{1,0:T(8,128)S(1)} %pad_maximum_fusion.both, bf16[1024,3072]{1,0:T(8,128)(2,1)} %w.1), custom_call_target="tpu_custom_call" | custom-call | flops 704643072 | bytes 9000000 | tf_op jit(solution)/shard_map/own_rows/pallas_call | solution.py:312
  16.0 3.0 %rim_rows.1 = (bf16[16,1024]{1,0:T(8,128)(2,1)S(1)}, f32[32,1024]{1,0:T(8,128)S(1)}, bf16[224,3072]{1,0:T(8,128)(2,1)S(1)}) custom-call(s32[5]{0:T(128)S(1)} %stack.19.place, bf16[160,1024]{1,0:T(8,128)(2,1)S(1)} %collective-permute-done.near, bf16[160,1024]{1,0:T(8,128)(2,1)S(1)} %collective-permute-done.1.far, f32[265,1024]{1,0:T(8,128)S(1)} %pad_maximum_fusion.both, ...), custom_call_target="tpu_custom_call" | custom-call | flops 1107296256 | bytes 9000000 | tf_op jit(solution)/shard_map/rim_rows/pallas_call | solution.py:312
  19.0 4.6 %attend.1 = (bf16[128,1024]{1,0:T(8,128)(2,1)}, bf16[144,3072]{1,0:T(8,128)(2,1)S(1)}, bf16[4,128,768]{2,1,0:T(8,128)(2,1)S(1)}) custom-call(s32[5]{0:T(128)S(1)} %stack.19.place, bf16[224,3072]{1,0:T(8,128)(2,1)S(1)} %get-tuple-element.26.rim, bf16[112,3072]{1,0:T(8,128)(2,1)S(1)} %get-tuple-element.27.mid, f32[265,1024]{1,0:T(8,128)S(1)} %pad_maximum_fusion.both, ...), custom_call_target="tpu_custom_call" | custom-call | flops 5234491392 | bytes 5000000 | tf_op jit(solution)/shard_map/attend/pallas_call | solution.py:312
  23.7 2.8 %collective-permute-start.8 = (bf16[128,768]{1,0:T(8,128)(2,1)S(1)}, bf16[128,768]{1,0:T(8,128)(2,1)S(1)}, u32[]{:S(2)}, u32[]{:S(2)}) collective-permute-start(bf16[128,768]{1,0:T(8,128)(2,1)S(1)} %get-tuple-element.50), channel_id=1, source_target_pairs={{0,24},{4,28},{8,16},{12,20},{16,8},{20,12},{24,0},{28,4},{1,25},{... | collective-permute-start | bytes 589832 | tf_op jit(solution)/shard_map/ppermute | solution.py:328
  26.7 1.2 %collective-permute-start.6 = (bf16[128,768]{1,0:T(8,128)(2,1)S(1)}, bf16[128,768]{1,0:T(8,128)(2,1)S(1)}, u32[]{:S(2)}, u32[]{:S(2)}) collective-permute-start(bf16[128,768]{1,0:T(8,128)(2,1)S(1)} %get-tuple-element.52), channel_id=1, source_target_pairs={{0,8},{4,12},{8,0},{12,4},{16,24},{20,28},{24,16},{28,20},{1,9},{5... | collective-permute-start | bytes 589832 | tf_op jit(solution)/shard_map/ppermute | solution.py:328
  28.6 1.3 %collective-permute-done.5.tails = bf16[64,1024]{1,0:T(8,128)(2,1)S(1)} collective-permute-done((bf16[64,1024]{1,0:T(8,128)(2,1)S(1)}, bf16[64,1024]{1,0:T(8,128)(2,1)S(1)}, u32[]{:S(2)}, u32[]{:S(2)}) %collective-permute-start.5) | collective-permute-done | bytes 131104 | tf_op jit(solution)/shard_map/ppermute | solution.py:328
  29.9 3.0 %peer_hidden.1.peers = bf16[384,1024]{1,0:T(8,128)(2,1)S(1)} custom-call(s32[5]{0:T(128)S(1)} %stack.19.place, bf16[128,1024]{1,0:T(8,128)(2,1)S(1)} %collective-permute-done.2.f1, bf16[128,1024]{1,0:T(8,128)(2,1)S(1)} %collective-permute-done.3.f2, bf16[128,1024]{1,0:T(8,128)(2,1)S(1)} %collective-permute-done.4.f3, ...), custom_call_target="tpu_custom_call" | custom-call | flops 15728640 | bytes 2000000 | tf_op jit(solution)/shard_map/peer_hidden/pallas_call | solution.py:312
  32.9 2.3 %collective-permute-done.7.b2 = bf16[128,768]{1,0:T(8,128)(2,1)S(1)} collective-permute-done((bf16[128,768]{1,0:T(8,128)(2,1)S(1)}, bf16[128,768]{1,0:T(8,128)(2,1)S(1)}, u32[]{:S(2)}, u32[]{:S(2)}) %collective-permute-start.7) | collective-permute-done | bytes 196640 | tf_op jit(solution)/shard_map/ppermute | solution.py:328
  35.2 0.8 %collective-permute-done.6.b1 = bf16[128,768]{1,0:T(8,128)(2,1)S(1)} collective-permute-done((bf16[128,768]{1,0:T(8,128)(2,1)S(1)}, bf16[128,768]{1,0:T(8,128)(2,1)S(1)}, u32[]{:S(2)}, u32[]{:S(2)}) %collective-permute-start.6) | collective-permute-done | bytes 196640 | tf_op jit(solution)/shard_map/ppermute | solution.py:328
  36.1 1.6 %weight_send.1 = bf16[768,512]{1,0:T(8,128)(2,1)S(1)} custom-call(s32[5]{0:T(128)S(1)} %stack.19.place, bf16[16,1024]{1,0:T(8,128)(2,1)S(1)} %get-tuple-element.32.first, bf16[112,1024]{1,0:T(8,128)(2,1)S(1)} %get-tuple-element.33.mid, bf16[384,1024]{1,0:T(8,128)(2,1)S(1)} %peer_hidden.1.peers, bf16[4,128,768]{2,1,0:T(8,128)(2,1)S(1)} %get-tuple-element.34.b, ...), custom_call_target="tpu_custom_call" | custom-call | flops 402653184 | bytes 6000000 | tf_op jit(solution)/shard_map/weight_send/pallas_call | solution.py:312
  37.7 1.5 %weight_keep.1.keep = f32[768,512]{1,0:T(8,128)S(1)} custom-call(s32[5]{0:T(128)S(1)} %stack.19.place, bf16[16,1024]{1,0:T(8,128)(2,1)S(1)} %get-tuple-element.32.first, bf16[112,1024]{1,0:T(8,128)(2,1)S(1)} %get-tuple-element.33.mid, bf16[384,1024]{1,0:T(8,128)(2,1)S(1)} %peer_hidden.1.peers, bf16[4,128,768]{2,1,0:T(8,128)(2,1)S(1)} %get-tuple-element.34.b, ...), custom_call_target="tpu_custom_call" | custom-call | flops 402653184 | bytes 6000000 | tf_op jit(solution)/shard_map/weight_keep/pallas_call | solution.py:312
  39.3 0.7 %collective-permute-done.9.got = bf16[768,512]{1,0:T(8,128)(2,1)S(1)} collective-permute-done((bf16[768,512]{1,0:T(8,128)(2,1)S(1)}, bf16[768,512]{1,0:T(8,128)(2,1)S(1)}, u32[]{:S(2)}, u32[]{:S(2)}) %collective-permute-start.9) | collective-permute-done | bytes 786464 | tf_op jit(solution)/shard_map/ppermute | solution.py:328
  40.0 0.8 %core_sum.1 = (bf16[192,512]{1,0:T(8,128)(2,1)S(1)}, f32[192,512]{1,0:T(8,128)S(1)}, bf16[192,256]{1,0:T(8,128)(2,1)S(1)}, bf16[192,256]{1,0:T(8,128)(2,1)S(1)},...) custom-call(s32[5]{0:T(128)S(1)} %stack.19.place, f32[768,512]{1,0:T(8,128)S(1)} %weight_keep.1.keep, ...), custom_call_target="tpu_custom_call" | custom-call | flops 1000000 | bytes 1000000 | tf_op jit(solution)/shard_map/core_sum/pallas_call | solution.py:312
  40.7 1.6 %collective-permute-start.11 = (bf16[192,512]{1,0:T(8,128)(2,1)S(1)}, bf16[192,512]{1,0:T(8,128)(2,1)S(1)}, u32[]{:S(2)}, u32[]{:S(2)}) collective-permute-start(bf16[192,512]{1,0:T(8,128)(2,1)S(1)} %get-tuple-element.35.refs_0_), channel_id=1, source_target_pairs={{0,1},{1,0},{2,3},{3,2},{4,5},{5,4},{6,7},{7,6},{8,9},{9,8},{10,11... | collective-permute-start | bytes 589832 | tf_op jit(solution)/shard_map/ppermute | solution.py:328
  42.8 2.4 %collective-permute-start.13 = (bf16[192,256]{1,0:T(8,128)(2,1)S(1)}, bf16[192,256]{1,0:T(8,128)(2,1)S(1)}, u32[]{:S(2)}, u32[]{:S(2)}) collective-permute-start(bf16[192,256]{1,0:T(8,128)(2,1)S(1)} %get-tuple-element.41), channel_id=1, source_target_pairs={{0,8},{4,12},{8,0},{12,4},{16,24},{20,28},{24,16},{28,20},{1,9},{5... | collective-permute-start | bytes 294920 | tf_op jit(solution)/shard_map/ppermute | solution.py:328
  45.2 1.0 %collective-permute-start.14 = (bf16[192,256]{1,0:T(8,128)(2,1)S(1)}, bf16[192,256]{1,0:T(8,128)(2,1)S(1)}, u32[]{:S(2)}, u32[]{:S(2)}) collective-permute-start(bf16[192,256]{1,0:T(8,128)(2,1)S(1)} %get-tuple-element.42), channel_id=1, source_target_pairs={{0,9},{1,8},{2,11},{3,10},{4,13},{5,12},{6,15},{7,14},{8,1},{9,0},... | collective-permute-start | bytes 294920 | tf_op jit(solution)/shard_map/ppermute | solution.py:335
  46.2 2.3 %collective-permute-done.11.got = bf16[192,512]{1,0:T(8,128)(2,1)S(1)} collective-permute-done((bf16[192,512]{1,0:T(8,128)(2,1)S(1)}, bf16[192,512]{1,0:T(8,128)(2,1)S(1)}, u32[]{:S(2)}, u32[]{:S(2)}) %collective-permute-start.11) | collective-permute-done | bytes 196640 | tf_op jit(solution)/shard_map/ppermute | solution.py:328
  48.6 0.6 forward.1
  49.2 3.7 %collective-permute-start.12 = (bf16[192,256]{1,0:T(8,128)(2,1)S(1)}, bf16[192,256]{1,0:T(8,128)(2,1)S(1)}, u32[]{:S(2)}, u32[]{:S(2)}) collective-permute-start(bf16[192,256]{1,0:T(8,128)(2,1)S(1)} %get-tuple-element.40), channel_id=1, source_target_pairs={{0,3},{1,2},{2,1},{3,0},{4,7},{5,6},{6,5},{7,4},{8,11},{9,10},{10,... | collective-permute-start | bytes 294920 | tf_op jit(solution)/shard_map/ppermute | solution.py:328
  52.9 2.0 %collective-permute-start.15 = (bf16[192,256]{1,0:T(8,128)(2,1)S(1)}, bf16[192,256]{1,0:T(8,128)(2,1)S(1)}, u32[]{:S(2)}, u32[]{:S(2)}) collective-permute-start(bf16[192,256]{1,0:T(8,128)(2,1)S(1)} %get-tuple-element.43), channel_id=1, source_target_pairs={{0,11},{1,10},{2,9},{3,8},{4,15},{5,14},{6,13},{7,12},{8,3},{9,2},... | collective-permute-start | bytes 294920 | tf_op jit(solution)/shard_map/ppermute | solution.py:335
  54.9 4.3 %input_grad.1 = (bf16[128,1024]{1,0:T(8,128)(2,1)}, f32[8,128]{1,0:T(8,128)S(1)}) custom-call(s32[5]{0:T(128)S(1)} %stack.19.place, bf16[144,3072]{1,0:T(8,128)(2,1)S(1)} %get-tuple-element.29._.grads, bf16[1024,3072]{1,0:T(8,128)(2,1)S(1)} %get-tuple-element.25.w, f32[112,1024]{1,0:T(8,128)S(1)} %get-tuple-element.30.conv_mid, ...), custom_call_target="tpu_custom_call" | custom-call | flops 905969664 | bytes 9000000 | tf_op jit(solution)/shard_map/input_grad/pallas_call | solution.py:312
  59.2 1.0 %collective-permute-done.15.o2 = bf16[192,256]{1,0:T(8,128)(2,1)S(1)} collective-permute-done((bf16[192,256]{1,0:T(8,128)(2,1)S(1)}, bf16[192,256]{1,0:T(8,128)(2,1)S(1)}, u32[]{:S(2)}, u32[]{:S(2)}) %collective-permute-start.15) | collective-permute-done | bytes 98336 | tf_op jit(solution)/shard_map/ppermute | solution.py:335
  60.2 0.6 mid_sum.1
  60.9 1.6 %collective-permute-start.16 = (bf16[2,192,128]{2,1,0:T(8,128)(2,1)S(1)}, bf16[2,192,128]{2,1,0:T(8,128)(2,1)S(1)}, u32[]{:S(2)}, u32[]{:S(2)}) collective-permute-start(bf16[2,192,128]{2,1,0:T(8,128)(2,1)S(1)} %get-tuple-element.46), channel_id=1, source_target_pairs={{0,16},{4,20},{8,24},{12,28},{16,0},{20,4},{24,8},{28,12},{1,17},{... | collective-permute-start | bytes 294920 | tf_op jit(solution)/shard_map/ppermute | solution.py:328
  62.4 3.1 %collective-permute-done.16.got = bf16[2,192,128]{2,1,0:T(8,128)(2,1)S(1)} collective-permute-done((bf16[2,192,128]{2,1,0:T(8,128)(2,1)S(1)}, bf16[2,192,128]{2,1,0:T(8,128)(2,1)S(1)}, u32[]{:S(2)}, u32[]{:S(2)}) %collective-permute-start.16) | collective-permute-done | bytes 98336 | tf_op jit(solution)/shard_map/ppermute | solution.py:328
  65.5 1.3 %place.1 = f32[6,128,128]{2,1,0:T(8,128)} custom-call(s32[5]{0:T(128)S(1)} %stack.19.place, f32[2,192,128]{2,1,0:T(8,128)S(1)} %get-tuple-element.45.keep, bf16[2,192,128]{2,1,0:T(8,128)(2,1)S(1)} %collective-permute-done.16.got), custom_call_target="tpu_custom_call" | custom-call | flops 1000000 | bytes 1000000 | tf_op jit(solution)/shard_map/place/pallas_call | solution.py:312
  (25 shorter events, 1.8 us)
Async XLA Ops:
  0.6 2.1 %copy-start.1 = (f32[9,1024]{1,0:T(8,128)S(1)}, f32[9,1024]{1,0:T(8,128)}, u32[]{:S(2)}) copy-start(f32[9,1024]{1,0:T(8,128)} %param.7) | copy-start | bytes 110596
  2.8 5.3 %copy-start = (bf16[1,128,1024]{2,1,0:T(8,128)(2,1)S(1)}, bf16[1,128,1024]{2,1,0:T(8,128)(2,1)}, u32[]{:S(2)}) copy-start(bf16[1,128,1024]{2,1,0:T(8,128)(2,1)} %param.5) | copy-start | bytes 786436
  3.0 13.0 %collective-permute-start.1 = (bf16[160,1024]{1,0:T(8,128)(2,1)S(1)}, bf16[160,1024]{1,0:T(8,128)(2,1)S(1)}, u32[]{:S(2)}, u32[]{:S(2)}) collective-permute-start(bf16[160,1024]{1,0:T(8,128)(2,1)S(1)} %get-tuple-element.53), channel_id=1, source_target_pairs={{4,8},{8,4},{12,16},{16,12},{20,24},{24,20},{5,9},{9,5},{13,17},{1... | collective-permute-start | bytes 983048 | tf_op jit(solution)/shard_map/ppermute | solution.py:355
  3.7 12.3 %collective-permute-start = (bf16[160,1024]{1,0:T(8,128)(2,1)S(1)}, bf16[160,1024]{1,0:T(8,128)(2,1)S(1)}, u32[]{:S(2)}, u32[]{:S(2)}) collective-permute-start(bf16[160,1024]{1,0:T(8,128)(2,1)S(1)} %get-tuple-element.54), channel_id=1, source_target_pairs={{0,4},{4,0},{8,12},{12,8},{16,20},{20,16},{24,28},{28,24},{1,5},{5... | collective-permute-start | bytes 983048 | tf_op jit(solution)/shard_map/ppermute | solution.py:328
  8.0 18.6 %collective-permute-start.3 = (bf16[128,1024]{1,0:T(8,128)(2,1)S(1)}, bf16[128,1024]{1,0:T(8,128)(2,1)S(1)}, u32[]{:S(2)}, u32[]{:S(2)}) collective-permute-start(bf16[128,1024]{1,0:T(8,128)(2,1)S(1)} %bitcast.17), channel_id=1, source_target_pairs={{0,16},{4,20},{8,24},{12,28},{16,0},{20,4},{24,8},{28,12},{1,17},{... | collective-permute-start | bytes 786440 | tf_op jit(solution)/shard_map/ppermute | solution.py:328
  9.6 18.4 %collective-permute-start.2 = (bf16[128,1024]{1,0:T(8,128)(2,1)S(1)}, bf16[128,1024]{1,0:T(8,128)(2,1)S(1)}, u32[]{:S(2)}, u32[]{:S(2)}) collective-permute-start(bf16[128,1024]{1,0:T(8,128)(2,1)S(1)} %bitcast.18), channel_id=1, source_target_pairs={{0,8},{4,12},{8,0},{12,4},{16,24},{20,28},{24,16},{28,20},{1,9},{5... | collective-permute-start | bytes 786440 | tf_op jit(solution)/shard_map/ppermute | solution.py:328
  9.6 18.4 %collective-permute-start.4 = (bf16[128,1024]{1,0:T(8,128)(2,1)S(1)}, bf16[128,1024]{1,0:T(8,128)(2,1)S(1)}, u32[]{:S(2)}, u32[]{:S(2)}) collective-permute-start(bf16[128,1024]{1,0:T(8,128)(2,1)S(1)} %bitcast.19), channel_id=1, source_target_pairs={{0,24},{4,28},{8,16},{12,20},{16,8},{20,12},{24,0},{28,4},{1,25},{... | collective-permute-start | bytes 786440 | tf_op jit(solution)/shard_map/ppermute | solution.py:328
  23.7 9.3 %collective-permute-start.8 = (bf16[128,768]{1,0:T(8,128)(2,1)S(1)}, bf16[128,768]{1,0:T(8,128)(2,1)S(1)}, u32[]{:S(2)}, u32[]{:S(2)}) collective-permute-start(bf16[128,768]{1,0:T(8,128)(2,1)S(1)} %get-tuple-element.50), channel_id=1, source_target_pairs={{0,24},{4,28},{8,16},{12,20},{16,8},{20,12},{24,0},{28,4},{1,25},{... | collective-permute-start | bytes 589832 | tf_op jit(solution)/shard_map/ppermute | solution.py:328
  26.5 8.8 %collective-permute-start.7 = (bf16[128,768]{1,0:T(8,128)(2,1)S(1)}, bf16[128,768]{1,0:T(8,128)(2,1)S(1)}, u32[]{:S(2)}, u32[]{:S(2)}) collective-permute-start(bf16[128,768]{1,0:T(8,128)(2,1)S(1)} %get-tuple-element.51), channel_id=1, source_target_pairs={{0,16},{4,20},{8,24},{12,28},{16,0},{20,4},{24,8},{28,12},{1,17},{... | collective-permute-start | bytes 589832 | tf_op jit(solution)/shard_map/ppermute | solution.py:328
  26.7 9.4 %collective-permute-start.6 = (bf16[128,768]{1,0:T(8,128)(2,1)S(1)}, bf16[128,768]{1,0:T(8,128)(2,1)S(1)}, u32[]{:S(2)}, u32[]{:S(2)}) collective-permute-start(bf16[128,768]{1,0:T(8,128)(2,1)S(1)} %get-tuple-element.52), channel_id=1, source_target_pairs={{0,8},{4,12},{8,0},{12,4},{16,24},{20,28},{24,16},{28,20},{1,9},{5... | collective-permute-start | bytes 589832 | tf_op jit(solution)/shard_map/ppermute | solution.py:328
  28.5 1.4 %collective-permute-start.5 = (bf16[64,1024]{1,0:T(8,128)(2,1)S(1)}, bf16[64,1024]{1,0:T(8,128)(2,1)S(1)}, u32[]{:S(2)}, u32[]{:S(2)}) collective-permute-start(bf16[64,1024]{1,0:T(8,128)(2,1)S(1)} %ends.1), channel_id=1, source_target_pairs={{0,4},{4,0},{8,12},{12,8},{16,20},{20,16},{24,28},{28,24},{1,5},{5... | collective-permute-start | bytes 393224 | tf_op jit(solution)/shard_map/ppermute | solution.py:328
  37.6 2.4 %collective-permute-start.9 = (bf16[768,512]{1,0:T(8,128)(2,1)S(1)}, bf16[768,512]{1,0:T(8,128)(2,1)S(1)}, u32[]{:S(2)}, u32[]{:S(2)}) collective-permute-start(bf16[768,512]{1,0:T(8,128)(2,1)S(1)} %weight_send.1), channel_id=1, source_target_pairs={{0,4},{4,0},{8,12},{12,8},{16,20},{20,16},{24,28},{28,24},{1,5},{5... | collective-permute-start | bytes 2359304 | tf_op jit(solution)/shard_map/ppermute | solution.py:328
  40.7 7.8 %collective-permute-start.11 = (bf16[192,512]{1,0:T(8,128)(2,1)S(1)}, bf16[192,512]{1,0:T(8,128)(2,1)S(1)}, u32[]{:S(2)}, u32[]{:S(2)}) collective-permute-start(bf16[192,512]{1,0:T(8,128)(2,1)S(1)} %get-tuple-element.35.refs_0_), channel_id=1, source_target_pairs={{0,1},{1,0},{2,3},{3,2},{4,5},{5,4},{6,7},{7,6},{8,9},{9,8},{10,11... | collective-permute-start | bytes 589832 | tf_op jit(solution)/shard_map/ppermute | solution.py:328
  42.4 16.8 %collective-permute-start.10 = (bf16[192,256]{1,0:T(8,128)(2,1)S(1)}, bf16[192,256]{1,0:T(8,128)(2,1)S(1)}, u32[]{:S(2)}, u32[]{:S(2)}) collective-permute-start(bf16[192,256]{1,0:T(8,128)(2,1)S(1)} %get-tuple-element.38), channel_id=1, source_target_pairs={{0,1},{1,0},{2,3},{3,2},{4,5},{5,4},{6,7},{7,6},{8,9},{9,8},{10,11... | collective-permute-start | bytes 294920 | tf_op jit(solution)/shard_map/ppermute | solution.py:328
  42.8 16.3 %collective-permute-start.13 = (bf16[192,256]{1,0:T(8,128)(2,1)S(1)}, bf16[192,256]{1,0:T(8,128)(2,1)S(1)}, u32[]{:S(2)}, u32[]{:S(2)}) collective-permute-start(bf16[192,256]{1,0:T(8,128)(2,1)S(1)} %get-tuple-element.41), channel_id=1, source_target_pairs={{0,8},{4,12},{8,0},{12,4},{16,24},{20,28},{24,16},{28,20},{1,9},{5... | collective-permute-start | bytes 294920 | tf_op jit(solution)/shard_map/ppermute | solution.py:328
  45.2 14.0 %collective-permute-start.14 = (bf16[192,256]{1,0:T(8,128)(2,1)S(1)}, bf16[192,256]{1,0:T(8,128)(2,1)S(1)}, u32[]{:S(2)}, u32[]{:S(2)}) collective-permute-start(bf16[192,256]{1,0:T(8,128)(2,1)S(1)} %get-tuple-element.42), channel_id=1, source_target_pairs={{0,9},{1,8},{2,11},{3,10},{4,13},{5,12},{6,15},{7,14},{8,1},{9,0},... | collective-permute-start | bytes 294920 | tf_op jit(solution)/shard_map/ppermute | solution.py:335
  49.2 10.0 %collective-permute-start.12 = (bf16[192,256]{1,0:T(8,128)(2,1)S(1)}, bf16[192,256]{1,0:T(8,128)(2,1)S(1)}, u32[]{:S(2)}, u32[]{:S(2)}) collective-permute-start(bf16[192,256]{1,0:T(8,128)(2,1)S(1)} %get-tuple-element.40), channel_id=1, source_target_pairs={{0,3},{1,2},{2,1},{3,0},{4,7},{5,6},{6,5},{7,4},{8,11},{9,10},{10,... | collective-permute-start | bytes 294920 | tf_op jit(solution)/shard_map/ppermute | solution.py:328
  52.9 7.4 %collective-permute-start.15 = (bf16[192,256]{1,0:T(8,128)(2,1)S(1)}, bf16[192,256]{1,0:T(8,128)(2,1)S(1)}, u32[]{:S(2)}, u32[]{:S(2)}) collective-permute-start(bf16[192,256]{1,0:T(8,128)(2,1)S(1)} %get-tuple-element.43), channel_id=1, source_target_pairs={{0,11},{1,10},{2,9},{3,8},{4,15},{5,14},{6,13},{7,12},{8,3},{9,2},... | collective-permute-start | bytes 294920 | tf_op jit(solution)/shard_map/ppermute | solution.py:335
  60.9 4.7 %collective-permute-start.16 = (bf16[2,192,128]{2,1,0:T(8,128)(2,1)S(1)}, bf16[2,192,128]{2,1,0:T(8,128)(2,1)S(1)}, u32[]{:S(2)}, u32[]{:S(2)}) collective-permute-start(bf16[2,192,128]{2,1,0:T(8,128)(2,1)S(1)} %get-tuple-element.46), channel_id=1, source_target_pairs={{0,16},{4,20},{8,24},{12,28},{16,0},{20,4},{24,8},{28,12},{1,17},{... | collective-permute-start | bytes 294920 | tf_op jit(solution)/shard_map/ppermute | solution.py:328

commit v5 on v4

--- a/solution.py
+++ b/solution.py
@@ -50,62 +50,37 @@
     return both.at[:frames], both.at[frames : 2 * frames], both.at[2 * frames :]
 
 
-def own_kernel(place, both, w, hidden, conv_out, qkv, w_out, ext, sems):
-    frames, width = ext.shape
-    own, _, taps = parts_of(both, frames)
-    rows = frames - EDGE
+def project_kernel(place, near, far, both, w, own_hidden, conv_out, qkv, w_out, ext, hidden, sems):
+    frames, width = own_hidden.shape
+    wide = width
     copies = [
-        pltpu.make_async_copy(w.at[:, pl.ds(col, 512)], w_out.at[:, pl.ds(col, 512)], sems.at[i])
-        for i, col in enumerate(range(0, 3 * width, 512))
+        pltpu.make_async_copy(w.at[:, cols], w_out.at[:, cols], sems.at[i])
+        for i, cols in enumerate(pl.ds(i * wide, wide) for i in range(3))
     ]
     for copy in copies:
         copy.start()
-    live = live_rows(place[0], frames, place[1])
+    own, _, taps = parts_of(both, frames)
+    low_core = place[3] == 0
+    rows, back = frames + 2 * HALO, KERNEL - 1
+    live = live_rows(place[0] - HALO, rows, place[1])
     for col in range(0, width, 128):
         cols = pl.ds(col, 128)
-        masked = jnp.where(live, own[:, cols], 0.0)
-        ext[:, cols] = masked
-        conv, low = conv_hidden(ext, taps, cols, EDGE - KERNEL + 1, rows, masked[EDGE:])
-        conv_out[:, cols] = conv
+        mate, other = near[:HALO, cols].astype(F32), far[:, cols].astype(F32)
+        before, after = jnp.where(low_core, other, mate), jnp.where(low_core, mate, other)
+        raw = jnp.concatenate([before, own[:, cols], after], axis=0)
+        masked = jnp.where(live, raw, 0.0)
+        ext[:back, cols] = jnp.zeros((back, 128), F32)
+        ext[back:, cols] = masked
+        conv, low = conv_hidden(ext, taps, cols, 0, rows, masked)
+        conv_out[:, cols] = conv[HALO : HALO + frames + EDGE]
         hidden[:, cols] = low
+    own_hidden[...] = hidden[HALO : HALO + frames]
     for i, copy in enumerate(copies):
         copy.wait()
-        cols = pl.ds(i * 512, 512)
-        qkv[:, cols] = dot(hidden[...], w_out[:, cols], 1, 0).astype(BF16)
-
-
-def rim_kernel(place, near, far, both, w, first, conv_out, qkv, ext, hidden):
-    frames, width = qkv.shape[0] - HALO - EDGE, w.shape[0]
-    own, _, taps = parts_of(both, frames)
-    low_core = place[3] == 0
-    begin, count = place[0], place[1]
-    head, back = HALO + EDGE, KERNEL - 1
-    live_a = live_rows(begin - HALO, head, count)
-    live_b = live_rows(begin + frames - back, HALO + back, count)
-    for col in range(0, width, 128):
-        cols = pl.ds(col, 128)
-        mate, other = near[:HALO, cols].astype(F32), far[:HALO, cols].astype(F32)
-        prev = jnp.where(low_core, other, mate)
-        raw = jnp.concatenate([prev, own[:EDGE, cols]], axis=0)
-        masked = jnp.where(live_a, raw, 0.0)
-        ext[:back, cols] = jnp.zeros((back, 128), F32)
-        ext[back : back + head, cols] = masked
-        conv, low = conv_hidden(ext, taps, cols, 0, head, masked)
-        conv_out[:EDGE, cols] = conv[HALO:]
-        hidden[:head, cols] = low
-        tail = own[frames - back :, cols]
-        raw = jnp.concatenate([tail, jnp.where(low_core, mate, other)], axis=0)
-        masked = jnp.where(live_b, raw, 0.0)
-        ext[back + head :, cols] = masked
-        conv, low = conv_hidden(ext, taps, cols, back + head, HALO, masked[back:])
-        conv_out[EDGE:, cols] = conv[:EDGE]
-        hidden[head:, cols] = low
-    first[...] = hidden[HALO:head]
-    rows = head + HALO
-    for col in range(0, 3 * width, 512):
-        cols = pl.ds(col, 512)
-        low = HALO if col < width else 0
-        qkv[low:rows, cols] = dot(hidden[low:], w[:, cols], 1, 0).astype(BF16)
+        low = HALO if i * wide < width else 0
+        for col in range(i * wide, (i + 1) * wide, 512):
+            cols = pl.ds(col, 512)
+            qkv[low:rows, cols] = dot(hidden[low:], w_out[:, cols], 1, 0).astype(BF16)
     qkv[rows:, :] = jnp.zeros((qkv.shape[0] - rows, 3 * width), BF16)
 
 
@@ -137,11 +112,10 @@
             hidden[(slot - 1) * frames : slot * frames, cols] = low
 
 
-def attend_kernel(place, rim, mid, both, near, far, attended, grads, sends, later):
+def attend_kernel(place, qkv, both, near, far, attended, grads, sends, later):
     frames, width = attended.shape
     cot = parts_of(both, frames)[1]
     span = frames + HALO
-    head_rows = HALO + EDGE
     begin, count, chip = place[0], place[1], place[2]
 
     skip = (frames - LEFT) // EDGE * EDGE
@@ -158,7 +132,7 @@
 
     masks = [mask(HALO, frames), mask(frames - skip, HALO)]
     row = lax.broadcasted_iota(jnp.int32, (frames, width), 0)
-    after = jnp.where(place[3] == 0, near[HALO:].astype(F32), far[HALO:].astype(F32))
+    after = jnp.where(place[3] == 0, near[HALO:].astype(F32), far[...].astype(F32))
     later[:HALO] = jnp.where(begin + frames + row[:HALO] < count, after, 0.0).astype(BF16)
     later[HALO:] = jnp.zeros((frames - HALO, width), BF16)
     factor = HEAD**-0.5
@@ -175,15 +149,10 @@
         q_cols = pl.ds(head * HEAD, HEAD)
         k_cols = pl.ds(width + head * HEAD, HEAD)
         v_cols = pl.ds(2 * width + head * HEAD, HEAD)
-        query = jnp.concatenate([rim[HALO:head_rows, q_cols], mid[:, q_cols]], axis=0)
-        query_b = rim[head_rows:, q_cols]
-        key, value = (
-            jnp.concatenate(
-                [rim[:head_rows, cols], mid[:, cols], rim[head_rows : head_rows + HALO, cols]],
-                axis=0,
-            )
-            for cols in (k_cols, v_cols)
-        )
+        query = qkv[HALO : HALO + frames, q_cols]
+        query_b = qkv[HALO + frames : HALO + 2 * frames, q_cols]
+        key = qkv[: HALO + span, k_cols]
+        value = qkv[: HALO + span, v_cols]
         grad = jnp.where(own_live, cot[:, q_cols], 0.0).astype(BF16)
         grad_b = later[:, q_cols]
         prob, score = band(query, key[:span], value[:span], grad, *masks[0])
@@ -217,11 +186,11 @@
             sends[slot, :, at : at + HEAD] = jnp.concatenate(halves, axis=1)
 
 
-def attend_alone(place, rim, mid, both, near, far, attended, grads, later):
-    attend_kernel(place, rim, mid, both, near, far, attended, grads, None, later)
-
-
-def input_grad_kernel(place, grads, w, conv_mid, conv_rim, both, *refs):
+def attend_alone(place, qkv, both, near, far, attended, grads, later):
+    attend_kernel(place, qkv, both, near, far, attended, grads, None, later)
+
+
+def input_grad_kernel(place, grads, w, conv, both, *refs):
     grad_in, done, slopes = refs[-3:]
     frames, width = grad_in.shape
     taps = parts_of(both, frames)[2]
@@ -231,8 +200,7 @@
     for col in range(0, width, 256):
         cols = pl.ds(col, 256)
         grad_hidden = dot(grads[...], w[cols, :], 1, 1)
-        rim = conv_rim[:, cols]
-        value = jnp.concatenate([rim[:EDGE], conv_mid[:, cols], rim[EDGE:]], axis=0)
+        value = conv[:, cols]
         logistic = 1.0 / (1.0 + jnp.exp(-value))
         slopes[:, cols] = grad_hidden * (logistic * (1.0 + value * (1.0 - logistic)))
         total = grad_hidden[:frames]
@@ -242,13 +210,14 @@
         grad_in[:, cols] = jnp.where(live, total, 0.0).astype(BF16)
 
 
-def weight_kernel(keep, place, first, mid, peers, b, b1, b2, b3, out):
-    parity = place[3] if keep else 1 - place[3]
+def weight_kernel(mine, place, own, peers, b, b1, b2, b3, out):
+    parity = place[3] if mine else 1 - place[3]
     left = jnp.concatenate([b[0], b1[...], b2[...], b3[...]], axis=0)
-    for k in range(4):
-        cols = pl.ds(pl.multiple_of((2 * k + parity) * HEAD, HEAD), HEAD)
-        right = jnp.concatenate([a[:, cols] for a in (first, mid, peers)], axis=0)
-        out[:, k * HEAD : (k + 1) * HEAD] = dot(left, right, 0, 0).astype(out.dtype)
+    right = jnp.concatenate(
+        [jnp.concatenate([a[:, block(2 * k + parity)] for k in range(4)], axis=1) for a in (own, peers)],
+        axis=0,
+    )
+    out[...] = dot(left, right, 0, 0).astype(out.dtype)
 
 
 def block(index):
@@ -262,24 +231,24 @@
             out[:, y * HEAD : (y + 1) * HEAD] = value(block(2 * y + x)).astype(out.dtype)
 
 
+def shard_rows(place, mask):
+    i = place[4] ^ mask
+    for at, size, base in ((0, HEAD, 0), (HEAD, HEAD // 2, 4 * HEAD)):
+        rows = pl.ds(pl.multiple_of(base + i * size, size), size)
+        yield rows, slice(at, at + size)
+
+
 def core_sum_kernel(place, keep, got, near, ahead, *outs):
-    parts = ((0, HEAD, 0), (HEAD, HEAD // 2, 4 * HEAD))
-
-    def rows_of(mask, size, base):
-        return pl.ds(pl.multiple_of(base + (place[4] ^ mask) * size, size), size)
-
     for mask, out in ((2, near), (3, ahead)):
-        for at, size, base in parts:
-            rows = rows_of(mask, size, base)
-            out[at : at + size] = (keep[rows] + got[rows].astype(F32)).astype(out.dtype)
+        for rows, at in shard_rows(place, mask):
+            out[at] = (keep[rows] + got[rows].astype(F32)).astype(out.dtype)
     for mask, same, other in ((1, *outs[:2]), (0, *outs[2:])):
-        for at, size, base in parts:
-            rows = rows_of(mask, size, base)
+        for rows, at in shard_rows(place, mask):
             halves(
                 place,
                 lambda cols, rows=rows: keep[rows, cols] + got[rows, cols].astype(F32),
-                same.at[at : at + size],
-                other.at[at : at + size],
+                same.at[at],
+                other.at[at],
             )
 
 
@@ -348,49 +317,40 @@
     both = lax.optimization_barrier(
         jnp.concatenate([record.astype(F32), cot.astype(F32), kernel], axis=0)
     )
-    last = jnp.concatenate([both[frames - HALO : frames]] * 2, axis=0)
-    first = jnp.concatenate([both[:HALO], both[frames : frames + HALO]], axis=0)
+    own = both[:frames].astype(BF16)
+    last, first = own[frames - HALO :], own[:HALO]
+    first_cot = both[frames : frames + HALO].astype(BF16)
     low_core = me % 2 == 0
-    near = swap(jnp.where(low_core, last, first).astype(BF16), "tm", 1)
+    edge = jnp.where(low_core, last, first)
+    near = swap(jnp.concatenate([edge, first_cot], axis=0), "tm", 1)
+    down = [(i, i - 1) for i in range(2, parts, 2)]
     far = lax.ppermute(
-        jnp.where(low_core, first, last).astype(BF16),
-        "tm",
-        [(i, i + 1 if i % 2 else i - 1) for i in range(1, parts - 1)],
-    )
+        jnp.where(low_core, first, last), "tm", down + [(i, j) for j, i in down]
+    )
+    far_cot = lax.ppermute(first_cot, "tm", down)
     if split:
-        peers = [swap(record, "tm", mask) for mask in (2, 4, 6)]
-    rows = frames - EDGE
-    mid, conv_mid, qkv_mid, w_near = call(
-        own_kernel,
-        "own_rows",
+        peers = [swap(own, "tm", mask) for mask in (2, 4, 6)]
+    rows = frames + 2 * HALO
+    hidden, conv, qkv, w_near = call(
+        project_kernel,
+        "project",
         [
-            ((rows, width), BF16),
-            ((rows, width), F32),
-            ((rows, 3 * width), BF16),
+            ((frames, width), BF16),
+            ((frames + EDGE, width), F32),
+            ((HALO + 2 * frames, 3 * width), BF16),
             (w_qkv.shape, BF16),
         ],
         place,
-        [both],
-        [((frames, width), F32), pltpu.SemaphoreType.DMA((3 * width // 512,))],
+        [near, far, both],
+        [
+            ((rows + KERNEL - 1, width), F32),
+            ((rows, width), BF16),
+            pltpu.SemaphoreType.DMA((3,)),
+        ],
         flops=rows * width * 3 * width * 2,
         moved=9000000,
         remote=[w_qkv],
         mib=OWN,
-    )
-    rows = 2 * HALO + EDGE
-    first, conv_rim, qkv_rim = call(
-        rim_kernel,
-        "rim_rows",
-        [
-            ((EDGE, width), BF16),
-            ((2 * EDGE, width), F32),
-            ((HALO + EDGE + frames, 3 * width), BF16),
-        ],
-        place,
-        [near, far, both, w_near],
-        [((rows + 2 * (KERNEL - 1), width), F32), ((rows, width), BF16)],
-        flops=rows * width * 3 * width * 2,
-        moved=9000000,
     )
     outs = [((frames, width), BF16), ((frames + EDGE, 3 * width), BF16)]
     attended, grads, *sends = call(
@@ -398,7 +358,7 @@
         "attend",
         outs + [((4, frames, 3 * width // 4), BF16)] * split,
         place,
-        [qkv_rim, qkv_mid, both, near, far],
+        [qkv, both, near, far_cot],
         [((frames, width), BF16)],
         mib=16,
         flops=8 * 12 * span * 128 * 128 * 2 * 8,
@@ -414,7 +374,7 @@
         (ends,) = call(
             ends_kernel, "ends", [((4 * EDGE, width), BF16)], place, [both, *peers], after=[grads]
         )
-        (hidden,) = call(
+        (peers_hidden,) = call(
             peers_kernel,
             "peer_hidden",
             [((3 * frames, width), BF16)],
@@ -424,34 +384,27 @@
             flops=3 * frames * width * 40,
             moved=2000000,
         )
+        operands = [hidden, peers_hidden, sends, *got]
+        whole, half = (shard, width // 2), (shard, 2 * HEAD)
         send, keep = (
             call(
                 functools.partial(weight_kernel, mine),
                 "weight_" + ("keep" if mine else "send"),
                 [((cols, width // 2), F32 if mine else BF16)],
                 place,
-                [first, mid, hidden, sends, *got],
+                operands,
                 mib=20,
                 flops=cols * width * frames * 4,
                 moved=6000000,
             )[0]
             for mine in (False, True)
         )
-        sibling = swap(send, "tm", 1)
-        half = (shard, 2 * HEAD)
         near, ahead, cross_same, cross_other, own_same, own_other = call(
             core_sum_kernel,
             "core_sum",
-            [
-                ((shard, width // 2), BF16),
-                ((shard, width // 2), F32),
-                (half, BF16),
-                (half, BF16),
-                (half, F32),
-                (half, BF16),
-            ],
-            place,
-            [keep, sibling],
+            [(whole, BF16), (whole, F32), (half, BF16), (half, BF16), (half, F32), (half, BF16)],
+            place,
+            [keep, swap(send, "tm", 1)],
         )
         late = [near]
         grad_in, done = call(
@@ -459,7 +412,7 @@
             "input_grad",
             [((frames, width), BF16), ((8, 128), F32)],
             place,
-            [grads, w_near, conv_mid, conv_rim, both],
+            [grads, w_near, conv, both],
             [((frames + EDGE, width), F32)],
             mib=20,
             flops=(frames + EDGE) * width * 3 * width * 2,
@@ -495,14 +448,13 @@
             "input_grad",
             [((frames, width), BF16), ((8, 128), F32)],
             place,
-            [grads, w_near, conv_mid, conv_rim, both],
+            [grads, w_near, conv, both],
             [((frames + EDGE, width), F32)],
             mib=20,
             flops=(frames + EDGE) * width * 3 * width * 2,
             moved=9000000,
             after=late,
         )
-        hidden = jnp.concatenate([first, mid], axis=0)
         partial = dot(hidden, grads[:frames], 0, 0).astype(BF16)
         by_time = lax.psum_scatter(partial, "tm", scatter_dimension=0, tiled=True)
         summed = lax.psum_scatter(by_time, "dp", scatter_dimension=1, tiled=True).astype(F32)

time: 67.1 us -> 66.4 us (0.990)
  waiting for transfers between devices: 11.7 us -> 13.8 us
  Pallas kernels: 25.6 us -> 23.6 us
  other arithmetic: 2.23 us -> 1.38 us
    pallas_call x12 -> x11, Pallas kernels: 25.6 us -> 23.6 us  [call(): pl.pallas_call(kernel, name=name, out_shape=[jax.ShapeDtypeStruct(shape,...]
    convert_element_type x2 -> x0, other arithmetic: 1.13 us -> none  [the longest x1 0.99 us: on_device(): record.astype(F32)]
    ppermute x2, waiting for transfers between devices: 1.05 us -> 2.17 us  [swap_both(): return lax.ppermute(value, ('tm', 'dp'), pairs)]
    ppermute x14, waiting for transfers between devices: 10.7 us -> 11.6 us  [swap(): lax.ppermute(value, axis, [(i, i ^ mask) for i in range(lax.axis_size(axi...]
  transfers between devices with their start and end apart: 17 -> 18, of which waited for: 7 -> 7; matrix products, arithmetic and copies ran while one was open for 0% -> 0% of each run, Pallas kernels for 32% -> 30%
where the time goes in v5:
time: 66.4 us; the launch traced here: 66.2 us
  starting transfers between devices  25.8 us (39%)
  Pallas kernels  23.6 us (36%)
  waiting for transfers between devices  13.8 us (21%)
  between operations  1.49 us (2%)
  other arithmetic  1.38 us (2%)
    pallas_call x11, Pallas kernels, call(): pl.pallas_call(kernel, name=name, out_shape=[jax.ShapeDtypeStruct(shape,...  23.6 us
    ppermute x14, starting transfers between devices, swap(): lax.ppermute(value, axis, [(i, i ^ mask) for i in range(lax.axis_size(axi...  21.8 us
    ppermute x14, waiting for transfers between devices, swap(): lax.ppermute(value, axis, [(i, i ^ mask) for i in range(lax.axis_size(axi...  11.6 us
    ppermute x2, starting transfers between devices, swap_both(): return lax.ppermute(value, ('tm', 'dp'), pairs)  2.7 us
    ppermute x2, waiting for transfers between devices, swap_both(): return lax.ppermute(value, ('tm', 'dp'), pairs)  2.17 us
  transfers between devices with their start and end apart: 18, of which 7 were waited for; matrix products, arithmetic and copies ran while one was open for 0% of the time, Pallas kernels for 30%

profile of v5, /device:TPU:0, one launch (start us, length us, event | category | flops | bytes accessed | tf_op | source)
XLA Modules:
  0.0 66.2 jit_solution(5301691356893953922)
XLA Ops:
  0.7 1.2 %bitcast_convert_fusion = (f32[128,1024]{1,0:T(8,128)S(1)}, f32[128,1024]{1,0:T(8,128)S(1)}) fusion(bf16[1,128,1024]{2,1,0:T(8,128)(2,1)} %param.9, bf16[1,128,1024]{2,1,0:T(8,128)(2,1)} %param.5), kind=kLoop, calls=%fused_computation.2 | loop fusion | flops 262144 | bytes 1572864 | tf_op jit(solution)/shard_map/convert_element_type | solution.py:318
  2.1 0.5 collective-permute-start
  2.6 0.7 collective-permute-start.1
  3.3 0.7 %collective-permute-start.2 = (bf16[80,1024]{1,0:T(8,128)(2,1)S(1)}, bf16[80,1024]{1,0:T(8,128)(2,1)S(1)}, u32[]{:S(2)}, u32[]{:S(2)}) collective-permute-start(bf16[80,1024]{1,0:T(8,128)(2,1)S(1)} %get-tuple-element.45), channel_id=1, source_target_pairs={{8,4},{16,12},{24,20},{9,5},{17,13},{25,21},{10,6},{18,14},{26,22}... | collective-permute-start | bytes 491528 | tf_op jit(solution)/shard_map/ppermute | solution.py:330
  4.0 7.8 %collective-permute-start.5 = (bf16[128,1024]{1,0:T(8,128)(2,1)S(1)}, bf16[128,1024]{1,0:T(8,128)(2,1)S(1)}, u32[]{:S(2)}, u32[]{:S(2)}) collective-permute-start(bf16[128,1024]{1,0:T(8,128)(2,1)S(1)} %slice.35), channel_id=1, source_target_pairs={{0,24},{4,28},{8,16},{12,20},{16,8},{20,12},{24,0},{28,4},{1,25},{... | collective-permute-start | bytes 786440 | tf_op jit(solution)/shard_map/ppermute | solution.py:297
  13.0 0.9 %collective-permute-start.3 = (bf16[128,1024]{1,0:T(8,128)(2,1)S(1)}, bf16[128,1024]{1,0:T(8,128)(2,1)S(1)}, u32[]{:S(2)}, u32[]{:S(2)}) collective-permute-start(bf16[128,1024]{1,0:T(8,128)(2,1)S(1)} %slice.35), channel_id=1, source_target_pairs={{0,8},{4,12},{8,0},{12,4},{16,24},{20,28},{24,16},{28,20},{1,9},{5... | collective-permute-start | bytes 786440 | tf_op jit(solution)/shard_map/ppermute | solution.py:297
  13.9 5.3 %project.1 = (bf16[128,1024]{1,0:T(8,128)(2,1)S(1)}, f32[144,1024]{1,0:T(8,128)S(1)}, bf16[336,3072]{1,0:T(8,128)(2,1)S(1)}, bf16[1024,3072]{1,0:T(8,128)(2,1)S(1)}) custom-call(s32[5]{0:T(128)S(1)} %stack.19.place, bf16[160,1024]{1,0:T(8,128)(2,1)S(1)} %collective-permute-done.near, bf16[80,1024]{1,0:T(8,128)(2,1)S(1)} %collective-permute-done.1.far, ...), custom_call_target="tpu_custom_call" | custom-call | flops 1811939328 | bytes 9000000 | tf_op jit(solution)/shard_map/project/pallas_call | solution.py:281
  19.2 4.6 %attend.1 = (bf16[128,1024]{1,0:T(8,128)(2,1)}, bf16[144,3072]{1,0:T(8,128)(2,1)S(1)}, bf16[4,128,768]{2,1,0:T(8,128)(2,1)S(1)}) custom-call(s32[5]{0:T(128)S(1)} %stack.19.place, bf16[336,3072]{1,0:T(8,128)(2,1)S(1)} %get-tuple-element.22.qkv, f32[265,1024]{1,0:T(8,128)S(1)} %pad_maximum_fusion.both, bf16[160,1024]{1,0:T(8,128)(2,1)S(1)} %collective-permute-done.near, ...), custom_call_target="tpu_custom_call" | custom-call | flops 5234491392 | bytes 5000000 | tf_op jit(solution)/shard_map/attend/pallas_call | solution.py:281
  23.9 2.1 %collective-permute-start.9 = (bf16[128,768]{1,0:T(8,128)(2,1)S(1)}, bf16[128,768]{1,0:T(8,128)(2,1)S(1)}, u32[]{:S(2)}, u32[]{:S(2)}) collective-permute-start(bf16[128,768]{1,0:T(8,128)(2,1)S(1)} %get-tuple-element.41), channel_id=1, source_target_pairs={{0,24},{4,28},{8,16},{12,20},{16,8},{20,12},{24,0},{28,4},{1,25},{... | collective-permute-start | bytes 589832 | tf_op jit(solution)/shard_map/ppermute | solution.py:297
  26.0 0.5 collective-permute-start.8
  26.5 0.9 %collective-permute-start.7 = (bf16[128,768]{1,0:T(8,128)(2,1)S(1)}, bf16[128,768]{1,0:T(8,128)(2,1)S(1)}, u32[]{:S(2)}, u32[]{:S(2)}) collective-permute-start(bf16[128,768]{1,0:T(8,128)(2,1)S(1)} %get-tuple-element.43), channel_id=1, source_target_pairs={{0,8},{4,12},{8,0},{12,4},{16,24},{20,28},{24,16},{28,20},{1,9},{5... | collective-permute-start | bytes 589832 | tf_op jit(solution)/shard_map/ppermute | solution.py:297
  27.4 0.6 ends.1
  28.1 1.3 %collective-permute-done.6.tails = bf16[64,1024]{1,0:T(8,128)(2,1)S(1)} collective-permute-done((bf16[64,1024]{1,0:T(8,128)(2,1)S(1)}, bf16[64,1024]{1,0:T(8,128)(2,1)S(1)}, u32[]{:S(2)}, u32[]{:S(2)}) %collective-permute-start.6) | collective-permute-done | bytes 131104 | tf_op jit(solution)/shard_map/ppermute | solution.py:297
  29.4 3.0 %peer_hidden.1.peers = bf16[384,1024]{1,0:T(8,128)(2,1)S(1)} custom-call(s32[5]{0:T(128)S(1)} %stack.19.place, bf16[128,1024]{1,0:T(8,128)(2,1)S(1)} %collective-permute-done.3.f1, bf16[128,1024]{1,0:T(8,128)(2,1)S(1)} %collective-permute-done.4.f2, bf16[128,1024]{1,0:T(8,128)(2,1)S(1)} %collective-permute-done.5.f3, ...), custom_call_target="tpu_custom_call" | custom-call | flops 15728640 | bytes 2000000 | tf_op jit(solution)/shard_map/peer_hidden/pallas_call | solution.py:281
  32.7 3.1 %collective-permute-done.8.b2 = bf16[128,768]{1,0:T(8,128)(2,1)S(1)} collective-permute-done((bf16[128,768]{1,0:T(8,128)(2,1)S(1)}, bf16[128,768]{1,0:T(8,128)(2,1)S(1)}, u32[]{:S(2)}, u32[]{:S(2)}) %collective-permute-start.8) | collective-permute-done | bytes 196640 | tf_op jit(solution)/shard_map/ppermute | solution.py:297
  35.8 1.2 %weight_send.1 = bf16[768,512]{1,0:T(8,128)(2,1)S(1)} custom-call(s32[5]{0:T(128)S(1)} %stack.19.place, bf16[128,1024]{1,0:T(8,128)(2,1)S(1)} %get-tuple-element.27.own, bf16[384,1024]{1,0:T(8,128)(2,1)S(1)} %peer_hidden.1.peers, bf16[4,128,768]{2,1,0:T(8,128)(2,1)S(1)} %get-tuple-element.28.b, bf16[128,768]{1,0:T(8,128)(2,1)S(1)} %collective-permute-done.7.b1, ...), custom_call_target="tpu_custom_call" | custom-call | flops 402653184 | bytes 6000000 | tf_op jit(solution)/shard_map/weight_send/pallas_call | solution.py:281
  37.0 1.2 %weight_keep.1.keep = f32[768,512]{1,0:T(8,128)S(1)} custom-call(s32[5]{0:T(128)S(1)} %stack.19.place, bf16[128,1024]{1,0:T(8,128)(2,1)S(1)} %get-tuple-element.27.own, bf16[384,1024]{1,0:T(8,128)(2,1)S(1)} %peer_hidden.1.peers, bf16[4,128,768]{2,1,0:T(8,128)(2,1)S(1)} %get-tuple-element.28.b, bf16[128,768]{1,0:T(8,128)(2,1)S(1)} %collective-permute-done.7.b1, ...), custom_call_target="tpu_custom_call" | custom-call | flops 402653184 | bytes 6000000 | tf_op jit(solution)/shard_map/weight_keep/pallas_call | solution.py:281
  38.2 1.1 %collective-permute-done.10.got = bf16[768,512]{1,0:T(8,128)(2,1)S(1)} collective-permute-done((bf16[768,512]{1,0:T(8,128)(2,1)S(1)}, bf16[768,512]{1,0:T(8,128)(2,1)S(1)}, u32[]{:S(2)}, u32[]{:S(2)}) %collective-permute-start.10) | collective-permute-done | bytes 786464 | tf_op jit(solution)/shard_map/ppermute | solution.py:297
  39.3 0.8 %core_sum.1 = (bf16[192,512]{1,0:T(8,128)(2,1)S(1)}, f32[192,512]{1,0:T(8,128)S(1)}, bf16[192,256]{1,0:T(8,128)(2,1)S(1)}, bf16[192,256]{1,0:T(8,128)(2,1)S(1)},...) custom-call(s32[5]{0:T(128)S(1)} %stack.19.place, f32[768,512]{1,0:T(8,128)S(1)} %weight_keep.1.keep, ...), custom_call_target="tpu_custom_call" | custom-call | flops 1000000 | bytes 1000000 | tf_op jit(solution)/shard_map/core_sum/pallas_call | solution.py:281
  40.1 1.6 %collective-permute-start.12 = (bf16[192,512]{1,0:T(8,128)(2,1)S(1)}, bf16[192,512]{1,0:T(8,128)(2,1)S(1)}, u32[]{:S(2)}, u32[]{:S(2)}) collective-permute-start(bf16[192,512]{1,0:T(8,128)(2,1)S(1)} %get-tuple-element.29.refs_0_), channel_id=1, source_target_pairs={{0,1},{1,0},{2,3},{3,2},{4,5},{5,4},{6,7},{7,6},{8,9},{9,8},{10,11... | collective-permute-start | bytes 589832 | tf_op jit(solution)/shard_map/ppermute | solution.py:297
  42.1 1.1 %collective-permute-start.14 = (bf16[192,256]{1,0:T(8,128)(2,1)S(1)}, bf16[192,256]{1,0:T(8,128)(2,1)S(1)}, u32[]{:S(2)}, u32[]{:S(2)}) collective-permute-start(bf16[192,256]{1,0:T(8,128)(2,1)S(1)} %get-tuple-element.35), channel_id=1, source_target_pairs={{0,8},{4,12},{8,0},{12,4},{16,24},{20,28},{24,16},{28,20},{1,9},{5... | collective-permute-start | bytes 294920 | tf_op jit(solution)/shard_map/ppermute | solution.py:297
  43.2 1.9 %collective-permute-start.15 = (bf16[192,256]{1,0:T(8,128)(2,1)S(1)}, bf16[192,256]{1,0:T(8,128)(2,1)S(1)}, u32[]{:S(2)}, u32[]{:S(2)}) collective-permute-start(bf16[192,256]{1,0:T(8,128)(2,1)S(1)} %get-tuple-element.36), channel_id=1, source_target_pairs={{0,9},{1,8},{2,11},{3,10},{4,13},{5,12},{6,15},{7,14},{8,1},{9,0},... | collective-permute-start | bytes 294920 | tf_op jit(solution)/shard_map/ppermute | solution.py:304
  45.2 2.7 %collective-permute-done.12.got = bf16[192,512]{1,0:T(8,128)(2,1)S(1)} collective-permute-done((bf16[192,512]{1,0:T(8,128)(2,1)S(1)}, bf16[192,512]{1,0:T(8,128)(2,1)S(1)}, u32[]{:S(2)}, u32[]{:S(2)}) %collective-permute-start.12) | collective-permute-done | bytes 196640 | tf_op jit(solution)/shard_map/ppermute | solution.py:297
  47.9 0.6 forward.1
  48.5 3.7 %collective-permute-start.13 = (bf16[192,256]{1,0:T(8,128)(2,1)S(1)}, bf16[192,256]{1,0:T(8,128)(2,1)S(1)}, u32[]{:S(2)}, u32[]{:S(2)}) collective-permute-start(bf16[192,256]{1,0:T(8,128)(2,1)S(1)} %get-tuple-element.34), channel_id=1, source_target_pairs={{0,3},{1,2},{2,1},{3,0},{4,7},{5,6},{6,5},{7,4},{8,11},{9,10},{10,... | collective-permute-start | bytes 294920 | tf_op jit(solution)/shard_map/ppermute | solution.py:297
  52.2 0.8 %collective-permute-start.16 = (bf16[192,256]{1,0:T(8,128)(2,1)S(1)}, bf16[192,256]{1,0:T(8,128)(2,1)S(1)}, u32[]{:S(2)}, u32[]{:S(2)}) collective-permute-start(bf16[192,256]{1,0:T(8,128)(2,1)S(1)} %get-tuple-element.37), channel_id=1, source_target_pairs={{0,11},{1,10},{2,9},{3,8},{4,15},{5,14},{6,13},{7,12},{8,3},{9,2},... | collective-permute-start | bytes 294920 | tf_op jit(solution)/shard_map/ppermute | solution.py:304
  52.9 4.5 %input_grad.1 = (bf16[128,1024]{1,0:T(8,128)(2,1)}, f32[8,128]{1,0:T(8,128)S(1)}) custom-call(s32[5]{0:T(128)S(1)} %stack.19.place, bf16[144,3072]{1,0:T(8,128)(2,1)S(1)} %get-tuple-element.24._.grads, bf16[1024,3072]{1,0:T(8,128)(2,1)S(1)} %get-tuple-element.25.w, f32[144,1024]{1,0:T(8,128)S(1)} %get-tuple-element.26.conv, ...), custom_call_target="tpu_custom_call" | custom-call | flops 905969664 | bytes 9000000 | tf_op jit(solution)/shard_map/input_grad/pallas_call | solution.py:281
  57.4 2.2 %collective-permute-done.16.o2 = bf16[192,256]{1,0:T(8,128)(2,1)S(1)} collective-permute-done((bf16[192,256]{1,0:T(8,128)(2,1)S(1)}, bf16[192,256]{1,0:T(8,128)(2,1)S(1)}, u32[]{:S(2)}, u32[]{:S(2)}) %collective-permute-start.16) | collective-permute-done | bytes 98336 | tf_op jit(solution)/shard_map/ppermute | solution.py:304
  59.6 0.6 mid_sum.1
  60.2 1.5 %collective-permute-start.17 = (bf16[2,192,128]{2,1,0:T(8,128)(2,1)S(1)}, bf16[2,192,128]{2,1,0:T(8,128)(2,1)S(1)}, u32[]{:S(2)}, u32[]{:S(2)}) collective-permute-start(bf16[2,192,128]{2,1,0:T(8,128)(2,1)S(1)} %get-tuple-element.40), channel_id=1, source_target_pairs={{0,16},{4,20},{8,24},{12,28},{16,0},{20,4},{24,8},{28,12},{1,17},{... | collective-permute-start | bytes 294920 | tf_op jit(solution)/shard_map/ppermute | solution.py:297
  61.7 3.2 %collective-permute-done.17.got = bf16[2,192,128]{2,1,0:T(8,128)(2,1)S(1)} collective-permute-done((bf16[2,192,128]{2,1,0:T(8,128)(2,1)S(1)}, bf16[2,192,128]{2,1,0:T(8,128)(2,1)S(1)}, u32[]{:S(2)}, u32[]{:S(2)}) %collective-permute-start.17) | collective-permute-done | bytes 98336 | tf_op jit(solution)/shard_map/ppermute | solution.py:297
  64.9 1.3 %place.1 = f32[6,128,128]{2,1,0:T(8,128)} custom-call(s32[5]{0:T(128)S(1)} %stack.19.place, f32[2,192,128]{2,1,0:T(8,128)S(1)} %get-tuple-element.39.keep, bf16[2,192,128]{2,1,0:T(8,128)(2,1)S(1)} %collective-permute-done.17.got), custom_call_target="tpu_custom_call" | custom-call | flops 1000000 | bytes 1000000 | tf_op jit(solution)/shard_map/place/pallas_call | solution.py:281
  (25 shorter events, 1.7 us)
Async XLA Ops:
  0.6 1.2 %copy-start = (f32[9,1024]{1,0:T(8,128)S(1)}, f32[9,1024]{1,0:T(8,128)}, u32[]{:S(2)}) copy-start(f32[9,1024]{1,0:T(8,128)} %param.7) | copy-start | bytes 110596
  2.1 11.8 %collective-permute-start = (bf16[160,1024]{1,0:T(8,128)(2,1)S(1)}, bf16[160,1024]{1,0:T(8,128)(2,1)S(1)}, u32[]{:S(2)}, u32[]{:S(2)}) collective-permute-start(bf16[160,1024]{1,0:T(8,128)(2,1)S(1)} %pad_maximum_fusion.1), channel_id=1, source_target_pairs={{0,4},{4,0},{8,12},{12,8},{16,20},{20,16},{24,28},{28,24},{1,5},{5... | collective-permute-start | bytes 983048 | tf_op jit(solution)/shard_map/ppermute | solution.py:297
  2.6 10.4 %collective-permute-start.1 = (bf16[80,1024]{1,0:T(8,128)(2,1)S(1)}, bf16[80,1024]{1,0:T(8,128)(2,1)S(1)}, u32[]{:S(2)}, u32[]{:S(2)}) collective-permute-start(bf16[80,1024]{1,0:T(8,128)(2,1)S(1)} %get-tuple-element.44), channel_id=1, source_target_pairs={{8,4},{16,12},{24,20},{4,8},{12,16},{20,24},{9,5},{17,13},{25,21},... | collective-permute-start | bytes 491528 | tf_op jit(solution)/shard_map/ppermute | solution.py:327
  3.3 15.9 %collective-permute-start.2 = (bf16[80,1024]{1,0:T(8,128)(2,1)S(1)}, bf16[80,1024]{1,0:T(8,128)(2,1)S(1)}, u32[]{:S(2)}, u32[]{:S(2)}) collective-permute-start(bf16[80,1024]{1,0:T(8,128)(2,1)S(1)} %get-tuple-element.45), channel_id=1, source_target_pairs={{8,4},{16,12},{24,20},{9,5},{17,13},{25,21},{10,6},{18,14},{26,22}... | collective-permute-start | bytes 491528 | tf_op jit(solution)/shard_map/ppermute | solution.py:330
  4.0 22.5 %collective-permute-start.5 = (bf16[128,1024]{1,0:T(8,128)(2,1)S(1)}, bf16[128,1024]{1,0:T(8,128)(2,1)S(1)}, u32[]{:S(2)}, u32[]{:S(2)}) collective-permute-start(bf16[128,1024]{1,0:T(8,128)(2,1)S(1)} %slice.35), channel_id=1, source_target_pairs={{0,24},{4,28},{8,16},{12,20},{16,8},{20,12},{24,0},{28,4},{1,25},{... | collective-permute-start | bytes 786440 | tf_op jit(solution)/shard_map/ppermute | solution.py:297
  11.7 15.7 %collective-permute-start.4 = (bf16[128,1024]{1,0:T(8,128)(2,1)S(1)}, bf16[128,1024]{1,0:T(8,128)(2,1)S(1)}, u32[]{:S(2)}, u32[]{:S(2)}) collective-permute-start(bf16[128,1024]{1,0:T(8,128)(2,1)S(1)} %slice.35), channel_id=1, source_target_pairs={{0,16},{4,20},{8,24},{12,28},{16,0},{20,4},{24,8},{28,12},{1,17},{... | collective-permute-start | bytes 786440 | tf_op jit(solution)/shard_map/ppermute | solution.py:297
  13.0 14.4 %collective-permute-start.3 = (bf16[128,1024]{1,0:T(8,128)(2,1)S(1)}, bf16[128,1024]{1,0:T(8,128)(2,1)S(1)}, u32[]{:S(2)}, u32[]{:S(2)}) collective-permute-start(bf16[128,1024]{1,0:T(8,128)(2,1)S(1)} %slice.35), channel_id=1, source_target_pairs={{0,8},{4,12},{8,0},{12,4},{16,24},{20,28},{24,16},{28,20},{1,9},{5... | collective-permute-start | bytes 786440 | tf_op jit(solution)/shard_map/ppermute | solution.py:297
  23.9 8.8 %collective-permute-start.9 = (bf16[128,768]{1,0:T(8,128)(2,1)S(1)}, bf16[128,768]{1,0:T(8,128)(2,1)S(1)}, u32[]{:S(2)}, u32[]{:S(2)}) collective-permute-start(bf16[128,768]{1,0:T(8,128)(2,1)S(1)} %get-tuple-element.41), channel_id=1, source_target_pairs={{0,24},{4,28},{8,16},{12,20},{16,8},{20,12},{24,0},{28,4},{1,25},{... | collective-permute-start | bytes 589832 | tf_op jit(solution)/shard_map/ppermute | solution.py:297
  26.0 9.8 %collective-permute-start.8 = (bf16[128,768]{1,0:T(8,128)(2,1)S(1)}, bf16[128,768]{1,0:T(8,128)(2,1)S(1)}, u32[]{:S(2)}, u32[]{:S(2)}) collective-permute-start(bf16[128,768]{1,0:T(8,128)(2,1)S(1)} %get-tuple-element.42), channel_id=1, source_target_pairs={{0,16},{4,20},{8,24},{12,28},{16,0},{20,4},{24,8},{28,12},{1,17},{... | collective-permute-start | bytes 589832 | tf_op jit(solution)/shard_map/ppermute | solution.py:297
  26.5 9.3 %collective-permute-start.7 = (bf16[128,768]{1,0:T(8,128)(2,1)S(1)}, bf16[128,768]{1,0:T(8,128)(2,1)S(1)}, u32[]{:S(2)}, u32[]{:S(2)}) collective-permute-start(bf16[128,768]{1,0:T(8,128)(2,1)S(1)} %get-tuple-element.43), channel_id=1, source_target_pairs={{0,8},{4,12},{8,0},{12,4},{16,24},{20,28},{24,16},{28,20},{1,9},{5... | collective-permute-start | bytes 589832 | tf_op jit(solution)/shard_map/ppermute | solution.py:297
  28.0 1.4 %collective-permute-start.6 = (bf16[64,1024]{1,0:T(8,128)(2,1)S(1)}, bf16[64,1024]{1,0:T(8,128)(2,1)S(1)}, u32[]{:S(2)}, u32[]{:S(2)}) collective-permute-start(bf16[64,1024]{1,0:T(8,128)(2,1)S(1)} %ends.1), channel_id=1, source_target_pairs={{0,4},{4,0},{8,12},{12,8},{16,20},{20,16},{24,28},{28,24},{1,5},{5... | collective-permute-start | bytes 393224 | tf_op jit(solution)/shard_map/ppermute | solution.py:297
  36.9 2.4 %collective-permute-start.10 = (bf16[768,512]{1,0:T(8,128)(2,1)S(1)}, bf16[768,512]{1,0:T(8,128)(2,1)S(1)}, u32[]{:S(2)}, u32[]{:S(2)}) collective-permute-start(bf16[768,512]{1,0:T(8,128)(2,1)S(1)} %weight_send.1), channel_id=1, source_target_pairs={{0,4},{4,0},{8,12},{12,8},{16,20},{20,16},{24,28},{28,24},{1,5},{5... | collective-permute-start | bytes 2359304 | tf_op jit(solution)/shard_map/ppermute | solution.py:297
  40.1 7.8 %collective-permute-start.12 = (bf16[192,512]{1,0:T(8,128)(2,1)S(1)}, bf16[192,512]{1,0:T(8,128)(2,1)S(1)}, u32[]{:S(2)}, u32[]{:S(2)}) collective-permute-start(bf16[192,512]{1,0:T(8,128)(2,1)S(1)} %get-tuple-element.29.refs_0_), channel_id=1, source_target_pairs={{0,1},{1,0},{2,3},{3,2},{4,5},{5,4},{6,7},{7,6},{8,9},{9,8},{10,11... | collective-permute-start | bytes 589832 | tf_op jit(solution)/shard_map/ppermute | solution.py:297
  41.7 15.7 %collective-permute-start.11 = (bf16[192,256]{1,0:T(8,128)(2,1)S(1)}, bf16[192,256]{1,0:T(8,128)(2,1)S(1)}, u32[]{:S(2)}, u32[]{:S(2)}) collective-permute-start(bf16[192,256]{1,0:T(8,128)(2,1)S(1)} %get-tuple-element.32), channel_id=1, source_target_pairs={{0,1},{1,0},{2,3},{3,2},{4,5},{5,4},{6,7},{7,6},{8,9},{9,8},{10,11... | collective-permute-start | bytes 294920 | tf_op jit(solution)/shard_map/ppermute | solution.py:297
  42.1 15.2 %collective-permute-start.14 = (bf16[192,256]{1,0:T(8,128)(2,1)S(1)}, bf16[192,256]{1,0:T(8,128)(2,1)S(1)}, u32[]{:S(2)}, u32[]{:S(2)}) collective-permute-start(bf16[192,256]{1,0:T(8,128)(2,1)S(1)} %get-tuple-element.35), channel_id=1, source_target_pairs={{0,8},{4,12},{8,0},{12,4},{16,24},{20,28},{24,16},{28,20},{1,9},{5... | collective-permute-start | bytes 294920 | tf_op jit(solution)/shard_map/ppermute | solution.py:297
  43.2 14.2 %collective-permute-start.15 = (bf16[192,256]{1,0:T(8,128)(2,1)S(1)}, bf16[192,256]{1,0:T(8,128)(2,1)S(1)}, u32[]{:S(2)}, u32[]{:S(2)}) collective-permute-start(bf16[192,256]{1,0:T(8,128)(2,1)S(1)} %get-tuple-element.36), channel_id=1, source_target_pairs={{0,9},{1,8},{2,11},{3,10},{4,13},{5,12},{6,15},{7,14},{8,1},{9,0},... | collective-permute-start | bytes 294920 | tf_op jit(solution)/shard_map/ppermute | solution.py:304
  48.5 8.9 %collective-permute-start.13 = (bf16[192,256]{1,0:T(8,128)(2,1)S(1)}, bf16[192,256]{1,0:T(8,128)(2,1)S(1)}, u32[]{:S(2)}, u32[]{:S(2)}) collective-permute-start(bf16[192,256]{1,0:T(8,128)(2,1)S(1)} %get-tuple-element.34), channel_id=1, source_target_pairs={{0,3},{1,2},{2,1},{3,0},{4,7},{5,6},{6,5},{7,4},{8,11},{9,10},{10,... | collective-permute-start | bytes 294920 | tf_op jit(solution)/shard_map/ppermute | solution.py:297
  52.2 7.4 %collective-permute-start.16 = (bf16[192,256]{1,0:T(8,128)(2,1)S(1)}, bf16[192,256]{1,0:T(8,128)(2,1)S(1)}, u32[]{:S(2)}, u32[]{:S(2)}) collective-permute-start(bf16[192,256]{1,0:T(8,128)(2,1)S(1)} %get-tuple-element.37), channel_id=1, source_target_pairs={{0,11},{1,10},{2,9},{3,8},{4,15},{5,14},{6,13},{7,12},{8,3},{9,2},... | collective-permute-start | bytes 294920 | tf_op jit(solution)/shard_map/ppermute | solution.py:304
  60.2 4.7 %collective-permute-start.17 = (bf16[2,192,128]{2,1,0:T(8,128)(2,1)S(1)}, bf16[2,192,128]{2,1,0:T(8,128)(2,1)S(1)}, u32[]{:S(2)}, u32[]{:S(2)}) collective-permute-start(bf16[2,192,128]{2,1,0:T(8,128)(2,1)S(1)} %get-tuple-element.40), channel_id=1, source_target_pairs={{0,16},{4,20},{8,24},{12,28},{16,0},{20,4},{24,8},{28,12},{1,17},{... | collective-permute-start | bytes 294920 | tf_op jit(solution)/shard_map/ppermute | solution.py:297

commit v6 on v5

--- a/solution.py
+++ b/solution.py
@@ -15,6 +15,8 @@
 EDGE = 16
 MIB = 1024 * 1024
 OWN = 42
+CHUNK = 48
+GROUP = 4
 F32 = jnp.float32
 BF16 = jnp.bfloat16
 
@@ -35,11 +37,19 @@
     return lax.dot_general(a, b, (((left,), (right,)), ((), ())), preferred_element_type=F32)
 
 
-def conv_hidden(ext, taps, cols, low, rows, masked):
-    conv = taps[0:1, cols] * ext[low : low + rows, cols]
-    for tap in range(1, KERNEL):
-        conv = conv + taps[tap : tap + 1, cols] * ext[low + tap : low + tap + rows, cols]
-    return conv, (masked + conv / (1.0 + jnp.exp(-conv))).astype(BF16)
+def conv_hidden(ext, taps, cols, low, rows, hidden, conv_out=None, keep=(0, 0)):
+    weights = [taps[tap : tap + 1, cols] for tap in range(KERNEL)]
+    for start in range(0, rows, CHUNK):
+        size = min(CHUNK, rows - start)
+        at = low + start
+        conv = weights[0] * ext[at : at + size, cols]
+        for tap in range(1, KERNEL):
+            conv = conv + weights[tap] * ext[at + tap : at + tap + size, cols]
+        masked = ext[at + KERNEL - 1 : at + KERNEL - 1 + size, cols]
+        hidden[start : start + size, cols] = (masked + conv / (1.0 + jnp.exp(-conv))).astype(BF16)
+        first, last = max(start, keep[0]), min(start + size, keep[1])
+        if first < last:
+            conv_out[first - keep[0] : last - keep[0], cols] = conv[first - start : last - start]
 
 
 def live_rows(first, rows, count):
@@ -71,9 +81,7 @@
         masked = jnp.where(live, raw, 0.0)
         ext[:back, cols] = jnp.zeros((back, 128), F32)
         ext[back:, cols] = masked
-        conv, low = conv_hidden(ext, taps, cols, 0, rows, masked)
-        conv_out[:, cols] = conv[HALO : HALO + frames + EDGE]
-        hidden[:, cols] = low
+        conv_hidden(ext, taps, cols, 0, rows, hidden, conv_out, (HALO, HALO + frames + EDGE))
     own_hidden[...] = hidden[HALO : HALO + frames]
     for i, copy in enumerate(copies):
         copy.wait()
@@ -108,8 +116,8 @@
             raw = jnp.concatenate([tails[pl.ds(start, EDGE), cols], ref[:, cols]], axis=0)
             masked = jnp.where(live, raw.astype(F32), 0.0)
             ext[:, cols] = masked
-            _, low = conv_hidden(ext, taps, cols, EDGE - KERNEL + 1, frames, masked[EDGE:])
-            hidden[(slot - 1) * frames : slot * frames, cols] = low
+            out = hidden.at[(slot - 1) * frames : slot * frames]
+            conv_hidden(ext, taps, cols, EDGE - KERNEL + 1, frames, out)
 
 
 def attend_kernel(place, qkv, both, near, far, attended, grads, sends, later):
@@ -128,7 +136,7 @@
         seen = first + query - gap
         alive = (first + query < count) & (query < wanted)
         allowed = (gap >= 0) & (gap <= LEFT) & (seen >= 0) & alive
-        return allowed, jnp.where(alive[:1], 0.0, 1.0)
+        return jnp.where(allowed, 0.0, -jnp.inf), jnp.where(alive[:1], 0.0, 1.0)
 
     masks = [mask(HALO, frames), mask(frames - skip, HALO)]
     row = lax.broadcasted_iota(jnp.int32, (frames, width), 0)
@@ -137,38 +145,50 @@
     later[HALO:] = jnp.zeros((frames - HALO, width), BF16)
     factor = HEAD**-0.5
 
-    def band(query, key, value, grad, allowed, missing):
-        raised = jnp.where(allowed, jnp.exp(dot(key, query, 1, 1) * factor), 0.0)
-        prob = raised * (1.0 / (jnp.sum(raised, axis=0, keepdims=True) + missing))
-        grad_prob = dot(value, grad, 1, 1)
+    def probs(scores, bias, missing):
+        raised = jnp.exp(scores * factor + bias)
+        return raised * (1.0 / (jnp.sum(raised, axis=0, keepdims=True) + missing))
+
+    def slopes(prob, grad_prob):
         mean = jnp.sum(prob * grad_prob, axis=0, keepdims=True)
-        return prob.astype(BF16), (prob * (grad_prob - mean) * factor).astype(BF16)
+        return (prob * (grad_prob - mean) * factor).astype(BF16)
 
     own_live = begin + lax.broadcasted_iota(jnp.int32, (frames, HEAD), 0) < count
-    for head in range(HEADS):
-        q_cols = pl.ds(head * HEAD, HEAD)
-        k_cols = pl.ds(width + head * HEAD, HEAD)
-        v_cols = pl.ds(2 * width + head * HEAD, HEAD)
-        query = qkv[HALO : HALO + frames, q_cols]
-        query_b = qkv[HALO + frames : HALO + 2 * frames, q_cols]
-        key = qkv[: HALO + span, k_cols]
-        value = qkv[: HALO + span, v_cols]
-        grad = jnp.where(own_live, cot[:, q_cols], 0.0).astype(BF16)
-        grad_b = later[:, q_cols]
-        prob, score = band(query, key[:span], value[:span], grad, *masks[0])
-        prob_b, score_b = band(query_b, key[HALO + skip :], value[HALO + skip :], grad_b, *masks[1])
-        attended[:, q_cols] = dot(prob, value[:span], 0, 0).astype(BF16)
-        grads[:frames, q_cols] = dot(score, key[:span], 0, 0).astype(BF16)
-        grads[frames:, q_cols] = dot(score_b[:, :EDGE], key[HALO + skip :], 0, 0).astype(BF16)
-        for cols, mine, here, theirs, there in (
-            (k_cols, score, query, score_b, query_b),
-            (v_cols, prob, grad, prob_b, grad_b),
-        ):
-            late = dot(theirs[: frames - skip + EDGE], there, 1, 0)
-            total = dot(mine[HALO:], here, 1, 0)
-            grads[:skip, cols] = total[:skip].astype(BF16)
-            grads[skip:frames, cols] = (total[skip:] + late[: frames - skip]).astype(BF16)
-            grads[frames:, cols] = late[frames - skip :].astype(BF16)
+    lead, trail = jnp.zeros((skip, frames), BF16), jnp.zeros((EDGE, frames), BF16)
+
+    def gather(own, late, rhs, rhs_late):
+        left = jnp.concatenate([own[HALO:], trail], axis=0)
+        right = jnp.concatenate([lead, late[: frames - skip + EDGE]], axis=0)
+        left = jnp.concatenate([left, right], axis=1)
+        return dot(left, jnp.concatenate([rhs, rhs_late], axis=0), 1, 0).astype(BF16)
+
+    for first in range(0, HEADS, GROUP):
+        heads = []
+        for head in range(first, first + GROUP):
+            q_cols = pl.ds(head * HEAD, HEAD)
+            k_cols = pl.ds(width + head * HEAD, HEAD)
+            v_cols = pl.ds(2 * width + head * HEAD, HEAD)
+            query = qkv[HALO : HALO + frames, q_cols]
+            query_b = qkv[HALO + frames : HALO + 2 * frames, q_cols]
+            key, key_b = qkv[:span, k_cols], qkv[HALO + skip : HALO + span, k_cols]
+            value, value_b = qkv[:span, v_cols], qkv[HALO + skip : HALO + span, v_cols]
+            grad = jnp.where(own_live, cot[:, q_cols], 0.0).astype(BF16)
+            grad_b = later[:, q_cols]
+            heads.append((q_cols, k_cols, v_cols, query, query_b, key, key_b, value, grad, grad_b, value_b))
+        scores = [
+            (dot(h[5], h[3], 1, 1), dot(h[6], h[4], 1, 1), dot(h[7], h[8], 1, 1), dot(h[10], h[9], 1, 1))
+            for h in heads
+        ]
+        prob = [(probs(s[0], *masks[0]), probs(s[1], *masks[1])) for s in scores]
+        low = [(p[0].astype(BF16), p[1].astype(BF16)) for p in prob]
+        slope = [(slopes(p[0], s[2]), slopes(p[1], s[3])) for p, s in zip(prob, scores)]
+        for h, p, d in zip(heads, low, slope):
+            q_cols, k_cols, v_cols, query, query_b, key, key_b, value, grad, grad_b, _ = h
+            attended[:, q_cols] = dot(p[0], value, 0, 0).astype(BF16)
+            grads[:frames, q_cols] = dot(d[0], key, 0, 0).astype(BF16)
+            grads[frames:, q_cols] = dot(d[1][:, :EDGE], key_b, 0, 0).astype(BF16)
+            grads[:, k_cols] = gather(d[0], d[1], query, query_b)
+            grads[:, v_cols] = gather(p[0], p[1], grad, grad_b)
     if sends is None:
         return
     for k in range(4):

time: 66.4 us -> 64.8 us (0.976)
  Pallas kernels: 23.6 us -> 21.3 us
  starting transfers between devices: 25.8 us -> 26.8 us
    pallas_call x11, Pallas kernels: 23.6 us -> 21.3 us  [call(): pl.pallas_call(kernel, name=name, out_shape=[jax.ShapeDtypeStruct(shape,...]
    ppermute x14, starting transfers between devices: 21.8 us -> 22.8 us  [swap(): lax.ppermute(value, axis, [(i, i ^ mask) for i in range(lax.axis_size(axi...]
  transfers between devices with their start and end apart: 18 -> 18, of which waited for: 7 -> 7; matrix products, arithmetic and copies ran while one was open for 0% -> 0% of each run, Pallas kernels for 30% -> 27%
where the time goes in v6:
time: 64.8 us; the launch traced here: 64.7 us
  starting transfers between devices  26.8 us (41%)
  Pallas kernels  21.3 us (33%)
  waiting for transfers between devices  13.5 us (21%)
  between operations  1.5 us (2%)
  other arithmetic  1.38 us (2%)
    ppermute x14, starting transfers between devices, swap(): lax.ppermute(value, axis, [(i, i ^ mask) for i in range(lax.axis_size(axi...  22.8 us
    pallas_call x11, Pallas kernels, call(): pl.pallas_call(kernel, name=name, out_shape=[jax.ShapeDtypeStruct(shape,...  21.3 us
    ppermute x14, waiting for transfers between devices, swap(): lax.ppermute(value, axis, [(i, i ^ mask) for i in range(lax.axis_size(axi...  11.7 us
    ppermute x2, starting transfers between devices, swap_both(): return lax.ppermute(value, ('tm', 'dp'), pairs)  2.69 us
    ppermute x2, waiting for transfers between devices, swap_both(): return lax.ppermute(value, ('tm', 'dp'), pairs)  1.79 us
  transfers between devices with their start and end apart: 18, of which 7 were waited for; matrix products, arithmetic and copies ran while one was open for 0% of the time, Pallas kernels for 27%

profile of v6, /device:TPU:0, one launch (start us, length us, event | category | flops | bytes accessed | tf_op | source)
XLA Modules:
  0.0 64.7 jit_solution(16568494326287394455)
XLA Ops:
  0.7 1.2 %bitcast_convert_fusion = (f32[128,1024]{1,0:T(8,128)S(1)}, f32[128,1024]{1,0:T(8,128)S(1)}) fusion(bf16[1,128,1024]{2,1,0:T(8,128)(2,1)} %param.9, bf16[1,128,1024]{2,1,0:T(8,128)(2,1)} %param.5), kind=kLoop, calls=%fused_computation.2 | loop fusion | flops 262144 | bytes 1572864 | tf_op jit(solution)/shard_map/convert_element_type | solution.py:338
  2.1 0.5 collective-permute-start
  2.6 0.7 %collective-permute-start.1 = (bf16[80,1024]{1,0:T(8,128)(2,1)S(1)}, bf16[80,1024]{1,0:T(8,128)(2,1)S(1)}, u32[]{:S(2)}, u32[]{:S(2)}) collective-permute-start(bf16[80,1024]{1,0:T(8,128)(2,1)S(1)} %get-tuple-element.44), channel_id=1, source_target_pairs={{8,4},{16,12},{24,20},{4,8},{12,16},{20,24},{9,5},{17,13},{25,21},... | collective-permute-start | bytes 491528 | tf_op jit(solution)/shard_map/ppermute | solution.py:347
  3.3 0.7 %collective-permute-start.2 = (bf16[80,1024]{1,0:T(8,128)(2,1)S(1)}, bf16[80,1024]{1,0:T(8,128)(2,1)S(1)}, u32[]{:S(2)}, u32[]{:S(2)}) collective-permute-start(bf16[80,1024]{1,0:T(8,128)(2,1)S(1)} %get-tuple-element.45), channel_id=1, source_target_pairs={{8,4},{16,12},{24,20},{9,5},{17,13},{25,21},{10,6},{18,14},{26,22}... | collective-permute-start | bytes 491528 | tf_op jit(solution)/shard_map/ppermute | solution.py:350
  4.0 7.8 %collective-permute-start.5 = (bf16[128,1024]{1,0:T(8,128)(2,1)S(1)}, bf16[128,1024]{1,0:T(8,128)(2,1)S(1)}, u32[]{:S(2)}, u32[]{:S(2)}) collective-permute-start(bf16[128,1024]{1,0:T(8,128)(2,1)S(1)} %slice.35), channel_id=1, source_target_pairs={{0,24},{4,28},{8,16},{12,20},{16,8},{20,12},{24,0},{28,4},{1,25},{... | collective-permute-start | bytes 786440 | tf_op jit(solution)/shard_map/ppermute | solution.py:317
  13.0 0.9 %collective-permute-start.3 = (bf16[128,1024]{1,0:T(8,128)(2,1)S(1)}, bf16[128,1024]{1,0:T(8,128)(2,1)S(1)}, u32[]{:S(2)}, u32[]{:S(2)}) collective-permute-start(bf16[128,1024]{1,0:T(8,128)(2,1)S(1)} %slice.35), channel_id=1, source_target_pairs={{0,8},{4,12},{8,0},{12,4},{16,24},{20,28},{24,16},{28,20},{1,9},{5... | collective-permute-start | bytes 786440 | tf_op jit(solution)/shard_map/ppermute | solution.py:317
  13.9 4.6 %project.1 = (bf16[128,1024]{1,0:T(8,128)(2,1)S(1)}, f32[144,1024]{1,0:T(8,128)S(1)}, bf16[336,3072]{1,0:T(8,128)(2,1)S(1)}, bf16[1024,3072]{1,0:T(8,128)(2,1)S(1)}) custom-call(s32[5]{0:T(128)S(1)} %stack.19.place, bf16[160,1024]{1,0:T(8,128)(2,1)S(1)} %collective-permute-done.near, bf16[80,1024]{1,0:T(8,128)(2,1)S(1)} %collective-permute-done.1.far, ...), custom_call_target="tpu_custom_call" | custom-call | flops 1811939328 | bytes 9000000 | tf_op jit(solution)/shard_map/project/pallas_call | solution.py:301
  18.6 3.1 %attend.1 = (bf16[128,1024]{1,0:T(8,128)(2,1)}, bf16[144,3072]{1,0:T(8,128)(2,1)S(1)}, bf16[4,128,768]{2,1,0:T(8,128)(2,1)S(1)}) custom-call(s32[5]{0:T(128)S(1)} %stack.19.place, bf16[336,3072]{1,0:T(8,128)(2,1)S(1)} %get-tuple-element.22.qkv, f32[265,1024]{1,0:T(8,128)S(1)} %pad_maximum_fusion.both, bf16[160,1024]{1,0:T(8,128)(2,1)S(1)} %collective-permute-done.near, ...), custom_call_target="tpu_custom_call" | custom-call | flops 5234491392 | bytes 5000000 | tf_op jit(solution)/shard_map/attend/pallas_call | solution.py:301
  21.7 2.1 %collective-permute-start.9 = (bf16[128,768]{1,0:T(8,128)(2,1)S(1)}, bf16[128,768]{1,0:T(8,128)(2,1)S(1)}, u32[]{:S(2)}, u32[]{:S(2)}) collective-permute-start(bf16[128,768]{1,0:T(8,128)(2,1)S(1)} %get-tuple-element.41), channel_id=1, source_target_pairs={{0,24},{4,28},{8,16},{12,20},{16,8},{20,12},{24,0},{28,4},{1,25},{... | collective-permute-start | bytes 589832 | tf_op jit(solution)/shard_map/ppermute | solution.py:317
  24.4 0.9 %collective-permute-start.7 = (bf16[128,768]{1,0:T(8,128)(2,1)S(1)}, bf16[128,768]{1,0:T(8,128)(2,1)S(1)}, u32[]{:S(2)}, u32[]{:S(2)}) collective-permute-start(bf16[128,768]{1,0:T(8,128)(2,1)S(1)} %get-tuple-element.43), channel_id=1, source_target_pairs={{0,8},{4,12},{8,0},{12,4},{16,24},{20,28},{24,16},{28,20},{1,9},{5... | collective-permute-start | bytes 589832 | tf_op jit(solution)/shard_map/ppermute | solution.py:317
  25.3 1.2 %collective-permute-done.3.f1 = bf16[128,1024]{1,0:T(8,128)(2,1)S(1)} collective-permute-done((bf16[128,1024]{1,0:T(8,128)(2,1)S(1)}, bf16[128,1024]{1,0:T(8,128)(2,1)S(1)}, u32[]{:S(2)}, u32[]{:S(2)}) %collective-permute-start.3) | collective-permute-done | bytes 262176 | tf_op jit(solution)/shard_map/ppermute | solution.py:317
  26.5 0.6 ends.1
  27.1 1.3 %collective-permute-done.6.tails = bf16[64,1024]{1,0:T(8,128)(2,1)S(1)} collective-permute-done((bf16[64,1024]{1,0:T(8,128)(2,1)S(1)}, bf16[64,1024]{1,0:T(8,128)(2,1)S(1)}, u32[]{:S(2)}, u32[]{:S(2)}) %collective-permute-start.6) | collective-permute-done | bytes 131104 | tf_op jit(solution)/shard_map/ppermute | solution.py:317
  28.5 3.0 %peer_hidden.1.peers = bf16[384,1024]{1,0:T(8,128)(2,1)S(1)} custom-call(s32[5]{0:T(128)S(1)} %stack.19.place, bf16[128,1024]{1,0:T(8,128)(2,1)S(1)} %collective-permute-done.3.f1, bf16[128,1024]{1,0:T(8,128)(2,1)S(1)} %collective-permute-done.4.f2, bf16[128,1024]{1,0:T(8,128)(2,1)S(1)} %collective-permute-done.5.f3, ...), custom_call_target="tpu_custom_call" | custom-call | flops 15728640 | bytes 2000000 | tf_op jit(solution)/shard_map/peer_hidden/pallas_call | solution.py:301
  31.5 2.2 %collective-permute-done.8.b2 = bf16[128,768]{1,0:T(8,128)(2,1)S(1)} collective-permute-done((bf16[128,768]{1,0:T(8,128)(2,1)S(1)}, bf16[128,768]{1,0:T(8,128)(2,1)S(1)}, u32[]{:S(2)}, u32[]{:S(2)}) %collective-permute-start.8) | collective-permute-done | bytes 196640 | tf_op jit(solution)/shard_map/ppermute | solution.py:317
  33.6 1.2 %weight_send.1 = bf16[768,512]{1,0:T(8,128)(2,1)S(1)} custom-call(s32[5]{0:T(128)S(1)} %stack.19.place, bf16[128,1024]{1,0:T(8,128)(2,1)S(1)} %get-tuple-element.27.own, bf16[384,1024]{1,0:T(8,128)(2,1)S(1)} %peer_hidden.1.peers, bf16[4,128,768]{2,1,0:T(8,128)(2,1)S(1)} %get-tuple-element.28.b, bf16[128,768]{1,0:T(8,128)(2,1)S(1)} %collective-permute-done.7.b1, ...), custom_call_target="tpu_custom_call" | custom-call | flops 402653184 | bytes 6000000 | tf_op jit(solution)/shard_map/weight_send/pallas_call | solution.py:301
  34.9 1.2 %weight_keep.1.keep = f32[768,512]{1,0:T(8,128)S(1)} custom-call(s32[5]{0:T(128)S(1)} %stack.19.place, bf16[128,1024]{1,0:T(8,128)(2,1)S(1)} %get-tuple-element.27.own, bf16[384,1024]{1,0:T(8,128)(2,1)S(1)} %peer_hidden.1.peers, bf16[4,128,768]{2,1,0:T(8,128)(2,1)S(1)} %get-tuple-element.28.b, bf16[128,768]{1,0:T(8,128)(2,1)S(1)} %collective-permute-done.7.b1, ...), custom_call_target="tpu_custom_call" | custom-call | flops 402653184 | bytes 6000000 | tf_op jit(solution)/shard_map/weight_keep/pallas_call | solution.py:301
  36.1 1.1 %collective-permute-done.10.got = bf16[768,512]{1,0:T(8,128)(2,1)S(1)} collective-permute-done((bf16[768,512]{1,0:T(8,128)(2,1)S(1)}, bf16[768,512]{1,0:T(8,128)(2,1)S(1)}, u32[]{:S(2)}, u32[]{:S(2)}) %collective-permute-start.10) | collective-permute-done | bytes 786464 | tf_op jit(solution)/shard_map/ppermute | solution.py:317
  37.2 0.8 %core_sum.1 = (bf16[192,512]{1,0:T(8,128)(2,1)S(1)}, f32[192,512]{1,0:T(8,128)S(1)}, bf16[192,256]{1,0:T(8,128)(2,1)S(1)}, bf16[192,256]{1,0:T(8,128)(2,1)S(1)},...) custom-call(s32[5]{0:T(128)S(1)} %stack.19.place, f32[768,512]{1,0:T(8,128)S(1)} %weight_keep.1.keep, ...), custom_call_target="tpu_custom_call" | custom-call | flops 1000000 | bytes 1000000 | tf_op jit(solution)/shard_map/core_sum/pallas_call | solution.py:301
  37.9 2.2 %collective-permute-start.12 = (bf16[192,512]{1,0:T(8,128)(2,1)S(1)}, bf16[192,512]{1,0:T(8,128)(2,1)S(1)}, u32[]{:S(2)}, u32[]{:S(2)}) collective-permute-start(bf16[192,512]{1,0:T(8,128)(2,1)S(1)} %get-tuple-element.29.refs_0_), channel_id=1, source_target_pairs={{0,1},{1,0},{2,3},{3,2},{4,5},{5,4},{6,7},{7,6},{8,9},{9,8},{10,11... | collective-permute-start | bytes 589832 | tf_op jit(solution)/shard_map/ppermute | solution.py:317
  40.2 2.0 %collective-permute-start.14 = (bf16[192,256]{1,0:T(8,128)(2,1)S(1)}, bf16[192,256]{1,0:T(8,128)(2,1)S(1)}, u32[]{:S(2)}, u32[]{:S(2)}) collective-permute-start(bf16[192,256]{1,0:T(8,128)(2,1)S(1)} %get-tuple-element.35), channel_id=1, source_target_pairs={{0,8},{4,12},{8,0},{12,4},{16,24},{20,28},{24,16},{28,20},{1,9},{5... | collective-permute-start | bytes 294920 | tf_op jit(solution)/shard_map/ppermute | solution.py:317
  42.2 1.4 %collective-permute-start.15 = (bf16[192,256]{1,0:T(8,128)(2,1)S(1)}, bf16[192,256]{1,0:T(8,128)(2,1)S(1)}, u32[]{:S(2)}, u32[]{:S(2)}) collective-permute-start(bf16[192,256]{1,0:T(8,128)(2,1)S(1)} %get-tuple-element.36), channel_id=1, source_target_pairs={{0,9},{1,8},{2,11},{3,10},{4,13},{5,12},{6,15},{7,14},{8,1},{9,0},... | collective-permute-start | bytes 294920 | tf_op jit(solution)/shard_map/ppermute | solution.py:324
  43.6 2.2 %collective-permute-done.12.got = bf16[192,512]{1,0:T(8,128)(2,1)S(1)} collective-permute-done((bf16[192,512]{1,0:T(8,128)(2,1)S(1)}, bf16[192,512]{1,0:T(8,128)(2,1)S(1)}, u32[]{:S(2)}, u32[]{:S(2)}) %collective-permute-start.12) | collective-permute-done | bytes 196640 | tf_op jit(solution)/shard_map/ppermute | solution.py:317
  45.8 0.6 forward.1
  46.4 4.2 %collective-permute-start.13 = (bf16[192,256]{1,0:T(8,128)(2,1)S(1)}, bf16[192,256]{1,0:T(8,128)(2,1)S(1)}, u32[]{:S(2)}, u32[]{:S(2)}) collective-permute-start(bf16[192,256]{1,0:T(8,128)(2,1)S(1)} %get-tuple-element.34), channel_id=1, source_target_pairs={{0,3},{1,2},{2,1},{3,0},{4,7},{5,6},{6,5},{7,4},{8,11},{9,10},{10,... | collective-permute-start | bytes 294920 | tf_op jit(solution)/shard_map/ppermute | solution.py:317
  50.6 1.3 %collective-permute-start.16 = (bf16[192,256]{1,0:T(8,128)(2,1)S(1)}, bf16[192,256]{1,0:T(8,128)(2,1)S(1)}, u32[]{:S(2)}, u32[]{:S(2)}) collective-permute-start(bf16[192,256]{1,0:T(8,128)(2,1)S(1)} %get-tuple-element.37), channel_id=1, source_target_pairs={{0,11},{1,10},{2,9},{3,8},{4,15},{5,14},{6,13},{7,12},{8,3},{9,2},... | collective-permute-start | bytes 294920 | tf_op jit(solution)/shard_map/ppermute | solution.py:324
  51.9 4.3 %input_grad.1 = (bf16[128,1024]{1,0:T(8,128)(2,1)}, f32[8,128]{1,0:T(8,128)S(1)}) custom-call(s32[5]{0:T(128)S(1)} %stack.19.place, bf16[144,3072]{1,0:T(8,128)(2,1)S(1)} %get-tuple-element.24._.grads, bf16[1024,3072]{1,0:T(8,128)(2,1)S(1)} %get-tuple-element.25.w, f32[144,1024]{1,0:T(8,128)S(1)} %get-tuple-element.26.conv, ...), custom_call_target="tpu_custom_call" | custom-call | flops 905969664 | bytes 9000000 | tf_op jit(solution)/shard_map/input_grad/pallas_call | solution.py:301
  56.2 1.8 %collective-permute-done.16.o2 = bf16[192,256]{1,0:T(8,128)(2,1)S(1)} collective-permute-done((bf16[192,256]{1,0:T(8,128)(2,1)S(1)}, bf16[192,256]{1,0:T(8,128)(2,1)S(1)}, u32[]{:S(2)}, u32[]{:S(2)}) %collective-permute-start.16) | collective-permute-done | bytes 98336 | tf_op jit(solution)/shard_map/ppermute | solution.py:324
  58.0 0.6 mid_sum.1
  58.6 1.0 %collective-permute-start.17 = (bf16[2,192,128]{2,1,0:T(8,128)(2,1)S(1)}, bf16[2,192,128]{2,1,0:T(8,128)(2,1)S(1)}, u32[]{:S(2)}, u32[]{:S(2)}) collective-permute-start(bf16[2,192,128]{2,1,0:T(8,128)(2,1)S(1)} %get-tuple-element.40), channel_id=1, source_target_pairs={{0,16},{4,20},{8,24},{12,28},{16,0},{20,4},{24,8},{28,12},{1,17},{... | collective-permute-start | bytes 294920 | tf_op jit(solution)/shard_map/ppermute | solution.py:317
  59.6 3.7 %collective-permute-done.17.got = bf16[2,192,128]{2,1,0:T(8,128)(2,1)S(1)} collective-permute-done((bf16[2,192,128]{2,1,0:T(8,128)(2,1)S(1)}, bf16[2,192,128]{2,1,0:T(8,128)(2,1)S(1)}, u32[]{:S(2)}, u32[]{:S(2)}) %collective-permute-start.17) | collective-permute-done | bytes 98336 | tf_op jit(solution)/shard_map/ppermute | solution.py:317
  63.3 1.3 %place.1 = f32[6,128,128]{2,1,0:T(8,128)} custom-call(s32[5]{0:T(128)S(1)} %stack.19.place, f32[2,192,128]{2,1,0:T(8,128)S(1)} %get-tuple-element.39.keep, bf16[2,192,128]{2,1,0:T(8,128)(2,1)S(1)} %collective-permute-done.17.got), custom_call_target="tpu_custom_call" | custom-call | flops 1000000 | bytes 1000000 | tf_op jit(solution)/shard_map/place/pallas_call | solution.py:301
  (25 shorter events, 1.6 us)
Async XLA Ops:
  0.6 1.2 %copy-start = (f32[9,1024]{1,0:T(8,128)S(1)}, f32[9,1024]{1,0:T(8,128)}, u32[]{:S(2)}) copy-start(f32[9,1024]{1,0:T(8,128)} %param.7) | copy-start | bytes 110596
  2.1 11.8 %collective-permute-start = (bf16[160,1024]{1,0:T(8,128)(2,1)S(1)}, bf16[160,1024]{1,0:T(8,128)(2,1)S(1)}, u32[]{:S(2)}, u32[]{:S(2)}) collective-permute-start(bf16[160,1024]{1,0:T(8,128)(2,1)S(1)} %pad_maximum_fusion.1), channel_id=1, source_target_pairs={{0,4},{4,0},{8,12},{12,8},{16,20},{20,16},{24,28},{28,24},{1,5},{5... | collective-permute-start | bytes 983048 | tf_op jit(solution)/shard_map/ppermute | solution.py:317
  2.6 10.4 %collective-permute-start.1 = (bf16[80,1024]{1,0:T(8,128)(2,1)S(1)}, bf16[80,1024]{1,0:T(8,128)(2,1)S(1)}, u32[]{:S(2)}, u32[]{:S(2)}) collective-permute-start(bf16[80,1024]{1,0:T(8,128)(2,1)S(1)} %get-tuple-element.44), channel_id=1, source_target_pairs={{8,4},{16,12},{24,20},{4,8},{12,16},{20,24},{9,5},{17,13},{25,21},... | collective-permute-start | bytes 491528 | tf_op jit(solution)/shard_map/ppermute | solution.py:347
  3.3 15.3 %collective-permute-start.2 = (bf16[80,1024]{1,0:T(8,128)(2,1)S(1)}, bf16[80,1024]{1,0:T(8,128)(2,1)S(1)}, u32[]{:S(2)}, u32[]{:S(2)}) collective-permute-start(bf16[80,1024]{1,0:T(8,128)(2,1)S(1)} %get-tuple-element.45), channel_id=1, source_target_pairs={{8,4},{16,12},{24,20},{9,5},{17,13},{25,21},{10,6},{18,14},{26,22}... | collective-permute-start | bytes 491528 | tf_op jit(solution)/shard_map/ppermute | solution.py:350
  4.0 20.4 %collective-permute-start.5 = (bf16[128,1024]{1,0:T(8,128)(2,1)S(1)}, bf16[128,1024]{1,0:T(8,128)(2,1)S(1)}, u32[]{:S(2)}, u32[]{:S(2)}) collective-permute-start(bf16[128,1024]{1,0:T(8,128)(2,1)S(1)} %slice.35), channel_id=1, source_target_pairs={{0,24},{4,28},{8,16},{12,20},{16,8},{20,12},{24,0},{28,4},{1,25},{... | collective-permute-start | bytes 786440 | tf_op jit(solution)/shard_map/ppermute | solution.py:317
  11.7 13.6 %collective-permute-start.4 = (bf16[128,1024]{1,0:T(8,128)(2,1)S(1)}, bf16[128,1024]{1,0:T(8,128)(2,1)S(1)}, u32[]{:S(2)}, u32[]{:S(2)}) collective-permute-start(bf16[128,1024]{1,0:T(8,128)(2,1)S(1)} %slice.35), channel_id=1, source_target_pairs={{0,16},{4,20},{8,24},{12,28},{16,0},{20,4},{24,8},{28,12},{1,17},{... | collective-permute-start | bytes 786440 | tf_op jit(solution)/shard_map/ppermute | solution.py:317
  13.0 13.5 %collective-permute-start.3 = (bf16[128,1024]{1,0:T(8,128)(2,1)S(1)}, bf16[128,1024]{1,0:T(8,128)(2,1)S(1)}, u32[]{:S(2)}, u32[]{:S(2)}) collective-permute-start(bf16[128,1024]{1,0:T(8,128)(2,1)S(1)} %slice.35), channel_id=1, source_target_pairs={{0,8},{4,12},{8,0},{12,4},{16,24},{20,28},{24,16},{28,20},{1,9},{5... | collective-permute-start | bytes 786440 | tf_op jit(solution)/shard_map/ppermute | solution.py:317
  21.7 9.7 %collective-permute-start.9 = (bf16[128,768]{1,0:T(8,128)(2,1)S(1)}, bf16[128,768]{1,0:T(8,128)(2,1)S(1)}, u32[]{:S(2)}, u32[]{:S(2)}) collective-permute-start(bf16[128,768]{1,0:T(8,128)(2,1)S(1)} %get-tuple-element.41), channel_id=1, source_target_pairs={{0,24},{4,28},{8,16},{12,20},{16,8},{20,12},{24,0},{28,4},{1,25},{... | collective-permute-start | bytes 589832 | tf_op jit(solution)/shard_map/ppermute | solution.py:317
  23.9 9.8 %collective-permute-start.8 = (bf16[128,768]{1,0:T(8,128)(2,1)S(1)}, bf16[128,768]{1,0:T(8,128)(2,1)S(1)}, u32[]{:S(2)}, u32[]{:S(2)}) collective-permute-start(bf16[128,768]{1,0:T(8,128)(2,1)S(1)} %get-tuple-element.42), channel_id=1, source_target_pairs={{0,16},{4,20},{8,24},{12,28},{16,0},{20,4},{24,8},{28,12},{1,17},{... | collective-permute-start | bytes 589832 | tf_op jit(solution)/shard_map/ppermute | solution.py:317
  24.4 9.3 %collective-permute-start.7 = (bf16[128,768]{1,0:T(8,128)(2,1)S(1)}, bf16[128,768]{1,0:T(8,128)(2,1)S(1)}, u32[]{:S(2)}, u32[]{:S(2)}) collective-permute-start(bf16[128,768]{1,0:T(8,128)(2,1)S(1)} %get-tuple-element.43), channel_id=1, source_target_pairs={{0,8},{4,12},{8,0},{12,4},{16,24},{20,28},{24,16},{28,20},{1,9},{5... | collective-permute-start | bytes 589832 | tf_op jit(solution)/shard_map/ppermute | solution.py:317
  27.0 1.4 %collective-permute-start.6 = (bf16[64,1024]{1,0:T(8,128)(2,1)S(1)}, bf16[64,1024]{1,0:T(8,128)(2,1)S(1)}, u32[]{:S(2)}, u32[]{:S(2)}) collective-permute-start(bf16[64,1024]{1,0:T(8,128)(2,1)S(1)} %ends.1), channel_id=1, source_target_pairs={{0,4},{4,0},{8,12},{12,8},{16,20},{20,16},{24,28},{28,24},{1,5},{5... | collective-permute-start | bytes 393224 | tf_op jit(solution)/shard_map/ppermute | solution.py:317
  34.8 2.4 %collective-permute-start.10 = (bf16[768,512]{1,0:T(8,128)(2,1)S(1)}, bf16[768,512]{1,0:T(8,128)(2,1)S(1)}, u32[]{:S(2)}, u32[]{:S(2)}) collective-permute-start(bf16[768,512]{1,0:T(8,128)(2,1)S(1)} %weight_send.1), channel_id=1, source_target_pairs={{0,4},{4,0},{8,12},{12,8},{16,20},{20,16},{24,28},{28,24},{1,5},{5... | collective-permute-start | bytes 2359304 | tf_op jit(solution)/shard_map/ppermute | solution.py:317
  37.9 7.9 %collective-permute-start.12 = (bf16[192,512]{1,0:T(8,128)(2,1)S(1)}, bf16[192,512]{1,0:T(8,128)(2,1)S(1)}, u32[]{:S(2)}, u32[]{:S(2)}) collective-permute-start(bf16[192,512]{1,0:T(8,128)(2,1)S(1)} %get-tuple-element.29.refs_0_), channel_id=1, source_target_pairs={{0,1},{1,0},{2,3},{3,2},{4,5},{5,4},{6,7},{7,6},{8,9},{9,8},{10,11... | collective-permute-start | bytes 589832 | tf_op jit(solution)/shard_map/ppermute | solution.py:317
  40.1 16.1 %collective-permute-start.11 = (bf16[192,256]{1,0:T(8,128)(2,1)S(1)}, bf16[192,256]{1,0:T(8,128)(2,1)S(1)}, u32[]{:S(2)}, u32[]{:S(2)}) collective-permute-start(bf16[192,256]{1,0:T(8,128)(2,1)S(1)} %get-tuple-element.32), channel_id=1, source_target_pairs={{0,1},{1,0},{2,3},{3,2},{4,5},{5,4},{6,7},{7,6},{8,9},{9,8},{10,11... | collective-permute-start | bytes 294920 | tf_op jit(solution)/shard_map/ppermute | solution.py:317
  40.2 16.0 %collective-permute-start.14 = (bf16[192,256]{1,0:T(8,128)(2,1)S(1)}, bf16[192,256]{1,0:T(8,128)(2,1)S(1)}, u32[]{:S(2)}, u32[]{:S(2)}) collective-permute-start(bf16[192,256]{1,0:T(8,128)(2,1)S(1)} %get-tuple-element.35), channel_id=1, source_target_pairs={{0,8},{4,12},{8,0},{12,4},{16,24},{20,28},{24,16},{28,20},{1,9},{5... | collective-permute-start | bytes 294920 | tf_op jit(solution)/shard_map/ppermute | solution.py:317
  42.2 14.0 %collective-permute-start.15 = (bf16[192,256]{1,0:T(8,128)(2,1)S(1)}, bf16[192,256]{1,0:T(8,128)(2,1)S(1)}, u32[]{:S(2)}, u32[]{:S(2)}) collective-permute-start(bf16[192,256]{1,0:T(8,128)(2,1)S(1)} %get-tuple-element.36), channel_id=1, source_target_pairs={{0,9},{1,8},{2,11},{3,10},{4,13},{5,12},{6,15},{7,14},{8,1},{9,0},... | collective-permute-start | bytes 294920 | tf_op jit(solution)/shard_map/ppermute | solution.py:324
  46.4 9.8 %collective-permute-start.13 = (bf16[192,256]{1,0:T(8,128)(2,1)S(1)}, bf16[192,256]{1,0:T(8,128)(2,1)S(1)}, u32[]{:S(2)}, u32[]{:S(2)}) collective-permute-start(bf16[192,256]{1,0:T(8,128)(2,1)S(1)} %get-tuple-element.34), channel_id=1, source_target_pairs={{0,3},{1,2},{2,1},{3,0},{4,7},{5,6},{6,5},{7,4},{8,11},{9,10},{10,... | collective-permute-start | bytes 294920 | tf_op jit(solution)/shard_map/ppermute | solution.py:317
  50.6 7.4 %collective-permute-start.16 = (bf16[192,256]{1,0:T(8,128)(2,1)S(1)}, bf16[192,256]{1,0:T(8,128)(2,1)S(1)}, u32[]{:S(2)}, u32[]{:S(2)}) collective-permute-start(bf16[192,256]{1,0:T(8,128)(2,1)S(1)} %get-tuple-element.37), channel_id=1, source_target_pairs={{0,11},{1,10},{2,9},{3,8},{4,15},{5,14},{6,13},{7,12},{8,3},{9,2},... | collective-permute-start | bytes 294920 | tf_op jit(solution)/shard_map/ppermute | solution.py:324
  58.6 4.7 %collective-permute-start.17 = (bf16[2,192,128]{2,1,0:T(8,128)(2,1)S(1)}, bf16[2,192,128]{2,1,0:T(8,128)(2,1)S(1)}, u32[]{:S(2)}, u32[]{:S(2)}) collective-permute-start(bf16[2,192,128]{2,1,0:T(8,128)(2,1)S(1)} %get-tuple-element.40), channel_id=1, source_target_pairs={{0,16},{4,20},{8,24},{12,28},{16,0},{20,4},{24,8},{28,12},{1,17},{... | collective-permute-start | bytes 294920 | tf_op jit(solution)/shard_map/ppermute | solution.py:317

commit v7 on v6

--- a/solution.py
+++ b/solution.py
@@ -276,18 +276,19 @@
     halves(place, lambda cols: ahead[:, cols] + got[:, cols].astype(F32), same, other)
 
 
-def mid_sum_kernel(place, s0, s1, s2, o0, o1, o2, _, keep, send):
+def mid_sum_kernel(same, place, moved, kept, cross, sums, *refs):
+    keep, send = refs[-2:]
+    own = kept if same else moved
     bit = place[2] // 2
     for out, y in ((send, 1 - bit), (keep, bit)):
         cols = block(y)
-        for i, refs in enumerate(((s0, s1, s2), (o0, o1, o2))):
-            a, b, c = (ref[:, cols].astype(F32) for ref in refs)
-            out[i] = (a + b + c).astype(out.dtype)
-
-
-def place_kernel(scale, place, keep, got, out):
-    for slot, ref in enumerate((keep, keep, got, got)):
-        value = ref[slot % 2].astype(F32) * scale
+        a, b, c = (ref[:, cols].astype(F32) for ref in (own, cross, sums))
+        out[...] = (a + b + c).astype(out.dtype)
+
+
+def place_kernel(scale, place, k0, k1, g0, g1, out):
+    for slot, ref in enumerate((k0, k1, g0, g1)):
+        value = ref[...].astype(F32) * scale
         k = place[2] ^ slot
         out[k + (k + 1) // 2] = value[:HEAD]
         start = pl.multiple_of((k % 2) * (HEAD // 2), HEAD // 2)
@@ -298,11 +299,15 @@
     kernel, name, outs, place, operands, scratch=(), mib=16, flops=1000000, moved=1000000,
     remote=(), after=()
 ):
+    def placed(*refs):
+        begin, left, *rest = (ref[0] for ref in refs[: len(place)])
+        kernel((begin, begin + left, *rest), *refs[len(place) :])
+
     return pl.pallas_call(
-        kernel,
+        placed,
         name=name,
         out_shape=[jax.ShapeDtypeStruct(shape, dtype) for shape, dtype in outs],
-        in_specs=[pl.BlockSpec(memory_space=pltpu.SMEM)]
+        in_specs=[pl.BlockSpec(memory_space=pltpu.SMEM)] * len(place)
         + vmem(len(operands))
         + [pl.BlockSpec(memory_space=pltpu.HBM)] * len(remote)
         + [pl.BlockSpec(memory_space=pl.ANY)] * len(after),
@@ -310,7 +315,7 @@
         scratch_shapes=[pltpu.VMEM(*x) if isinstance(x, tuple) else x for x in scratch],
         compiler_params=params(mib),
         cost_estimate=cost(flops, moved),
-    )(place, *operands, *remote, *after)
+    )(*place, *operands, *remote, *after)
 
 
 def swap(value, axis, mask):
@@ -330,9 +335,11 @@
     span = frames + HALO
     parts, recs = lax.axis_size("tm"), lax.axis_size("dp")
     me = lax.axis_index("tm")
-    place = jnp.stack(
-        [me * frames, valid_frames[0], me // 2, me % 2, lax.axis_index("dp")]
-    ).astype(jnp.int32)
+    begin = me * frames
+    place = [
+        jnp.reshape(x, (1,)).astype(jnp.int32)
+        for x in (begin, valid_frames[0] - begin, me // 2, me % 2, lax.axis_index("dp"))
+    ]
     split = parts == 8 and recs == 4
     both = lax.optimization_barrier(
         jnp.concatenate([record.astype(F32), cot.astype(F32), kernel], axis=0)
@@ -446,20 +453,25 @@
             forward_kernel, "forward", [(half, BF16)] * 2, place, [ahead, got_near]
         )
         got_sums = swap(same, "dp", 3), swap_both(other, 3, 2)
-        keep, send = call(
-            mid_sum_kernel,
-            "mid_sum",
-            [((2, shard, HEAD), F32), ((2, shard, HEAD), BF16)],
-            place,
-            [own_same, got_cross[0], got_sums[0], got_own, got_cross[1], got_sums[1]],
-            after=[done],
-        )
+        kept, moved = [], []
+        early = [got_cross[1], done]
+        for i, name in enumerate(("same", "other")):
+            keep, send = call(
+                functools.partial(mid_sum_kernel, i == 0),
+                "mid_" + name,
+                [((shard, HEAD), F32), ((shard, HEAD), BF16)],
+                place,
+                [got_own, own_same, got_cross[i], got_sums[i]],
+                after=early,
+            )
+            kept.append(keep)
+            moved.append(swap(send, "tm", 4))
         (qkv_grad,) = call(
             functools.partial(place_kernel, scale),
             "place",
             [((3 * HEADS // 4, HEAD, HEAD), F32)],
             place,
-            [keep, swap(send, "tm", 4)],
+            [*kept, *moved],
         )
     else:
         late = []

time: 64.8 us -> 61.4 us (0.948)
  Pallas kernels: 21.3 us -> 15.3 us
  waiting for transfers between devices: 13.5 us -> 15.8 us
    pallas_call x11 -> x12, Pallas kernels: 21.3 us -> 15.3 us  [call(): pl.pallas_call(placed, name=name, out_shape=[jax.ShapeDtypeStruct(shape,...]
    ppermute x14 -> x15, waiting for transfers between devices: 11.7 us -> 14.3 us  [swap(): lax.ppermute(value, axis, [(i, i ^ mask) for i in range(lax.axis_size(axi...]
    ppermute x14 -> x15, starting transfers between devices: 22.8 us -> 23.2 us  [swap(): lax.ppermute(value, axis, [(i, i ^ mask) for i in range(lax.axis_size(axi...]
  transfers between devices with their start and end apart: 18 -> 19, of which waited for: 7 -> 9; matrix products, arithmetic and copies ran while one was open for 0% -> 0% of each run, Pallas kernels for 27% -> 22%
where the time goes in v7:
time: 61.4 us; the launch traced here: 61.3 us
  starting transfers between devices  27.2 us (44%)
  waiting for transfers between devices  15.8 us (26%)
  Pallas kernels  15.3 us (25%)
  between operations  1.5 us (2%)
  other arithmetic  1.38 us (2%)
    ppermute x15, starting transfers between devices, swap(): lax.ppermute(value, axis, [(i, i ^ mask) for i in range(lax.axis_size(axi...  23.2 us
    pallas_call x12, Pallas kernels, call(): pl.pallas_call(placed, name=name, out_shape=[jax.ShapeDtypeStruct(shape,...  15.3 us
    ppermute x15, waiting for transfers between devices, swap(): lax.ppermute(value, axis, [(i, i ^ mask) for i in range(lax.axis_size(axi...  14.3 us
    ppermute x2, starting transfers between devices, swap_both(): return lax.ppermute(value, ('tm', 'dp'), pairs)  2.7 us
    ppermute x2, waiting for transfers between devices, swap_both(): return lax.ppermute(value, ('tm', 'dp'), pairs)  1.48 us
  transfers between devices with their start and end apart: 19, of which 9 were waited for; matrix products, arithmetic and copies ran while one was open for 0% of the time, Pallas kernels for 22%

profile of v7, /device:TPU:0, one launch (start us, length us, event | category | flops | bytes accessed | tf_op | source)
XLA Modules:
  0.0 61.3 jit_solution(13958816589877192182)
XLA Ops:
  0.7 1.2 %bitcast_convert_fusion = (f32[128,1024]{1,0:T(8,128)S(1)}, f32[128,1024]{1,0:T(8,128)S(1)}) fusion(bf16[1,128,1024]{2,1,0:T(8,128)(2,1)} %param.9, bf16[1,128,1024]{2,1,0:T(8,128)(2,1)} %param.5), kind=kLoop, calls=%fused_computation.2 | loop fusion | flops 262144 | bytes 1572864 | tf_op jit(solution)/shard_map/convert_element_type | solution.py:345
  2.1 0.5 collective-permute-start
  2.6 0.7 %collective-permute-start.1 = (bf16[80,1024]{1,0:T(8,128)(2,1)S(1)}, bf16[80,1024]{1,0:T(8,128)(2,1)S(1)}, u32[]{:S(2)}, u32[]{:S(2)}) collective-permute-start(bf16[80,1024]{1,0:T(8,128)(2,1)S(1)} %get-tuple-element.48), channel_id=1, source_target_pairs={{8,4},{16,12},{24,20},{4,8},{12,16},{20,24},{9,5},{17,13},{25,21},... | collective-permute-start | bytes 491528 | tf_op jit(solution)/shard_map/ppermute | solution.py:354
  3.3 0.7 %collective-permute-start.2 = (bf16[80,1024]{1,0:T(8,128)(2,1)S(1)}, bf16[80,1024]{1,0:T(8,128)(2,1)S(1)}, u32[]{:S(2)}, u32[]{:S(2)}) collective-permute-start(bf16[80,1024]{1,0:T(8,128)(2,1)S(1)} %get-tuple-element.49), channel_id=1, source_target_pairs={{8,4},{16,12},{24,20},{9,5},{17,13},{25,21},{10,6},{18,14},{26,22}... | collective-permute-start | bytes 491528 | tf_op jit(solution)/shard_map/ppermute | solution.py:357
  4.0 7.8 %collective-permute-start.5 = (bf16[128,1024]{1,0:T(8,128)(2,1)S(1)}, bf16[128,1024]{1,0:T(8,128)(2,1)S(1)}, u32[]{:S(2)}, u32[]{:S(2)}) collective-permute-start(bf16[128,1024]{1,0:T(8,128)(2,1)S(1)} %slice.35), channel_id=1, source_target_pairs={{0,24},{4,28},{8,16},{12,20},{16,8},{20,12},{24,0},{28,4},{1,25},{... | collective-permute-start | bytes 786440 | tf_op jit(solution)/shard_map/ppermute | solution.py:322
  11.7 0.5 collective-permute-start.4
  12.9 1.0 %collective-permute-start.3 = (bf16[128,1024]{1,0:T(8,128)(2,1)S(1)}, bf16[128,1024]{1,0:T(8,128)(2,1)S(1)}, u32[]{:S(2)}, u32[]{:S(2)}) collective-permute-start(bf16[128,1024]{1,0:T(8,128)(2,1)S(1)} %slice.35), channel_id=1, source_target_pairs={{0,8},{4,12},{8,0},{12,4},{16,24},{20,28},{24,16},{28,20},{1,9},{5... | collective-permute-start | bytes 786440 | tf_op jit(solution)/shard_map/ppermute | solution.py:322
  13.9 4.1 %project.1 = (bf16[128,1024]{1,0:T(8,128)(2,1)S(1)}, f32[144,1024]{1,0:T(8,128)S(1)}, bf16[336,3072]{1,0:T(8,128)(2,1)S(1)}, bf16[1024,3072]{1,0:T(8,128)(2,1)S(1)}) custom-call(s32[1]{0:T(128)} %bitcast.refs_0_, s32[1]{0:T(128)} %bitcast.2.refs_1_, s32[1]{0:T(128)} %bitcast.3.refs_2_, s32[1]{0:T(128)} %bitcast.4.refs_3_, s32[1]{0:T(128)} %bitcast.5.refs_4_, ...), custom_call_target="tpu_custom_call" | custom-call | flops 1811939328 | bytes 9000000 | tf_op jit(solution)/shard_map/project/pallas_call | solution.py:306
  18.0 2.6 %attend.1 = (bf16[128,1024]{1,0:T(8,128)(2,1)}, bf16[144,3072]{1,0:T(8,128)(2,1)S(1)}, bf16[4,128,768]{2,1,0:T(8,128)(2,1)S(1)}) custom-call(s32[1]{0:T(128)} %bitcast.refs_0_, s32[1]{0:T(128)} %bitcast.2.refs_1_, s32[1]{0:T(128)} %bitcast.3.refs_2_, s32[1]{0:T(128)} %bitcast.4.refs_3_, s32[1]{0:T(128)} %bitcast.5.refs_4_, ...), custom_call_target="tpu_custom_call" | custom-call | flops 5234491392 | bytes 5000000 | tf_op jit(solution)/shard_map/attend/pallas_call | solution.py:306
  20.6 2.1 %collective-permute-start.9 = (bf16[128,768]{1,0:T(8,128)(2,1)S(1)}, bf16[128,768]{1,0:T(8,128)(2,1)S(1)}, u32[]{:S(2)}, u32[]{:S(2)}) collective-permute-start(bf16[128,768]{1,0:T(8,128)(2,1)S(1)} %get-tuple-element.45), channel_id=1, source_target_pairs={{0,24},{4,28},{8,16},{12,20},{16,8},{20,12},{24,0},{28,4},{1,25},{... | collective-permute-start | bytes 589832 | tf_op jit(solution)/shard_map/ppermute | solution.py:322
  22.7 0.5 collective-permute-start.8
  23.3 0.9 %collective-permute-start.7 = (bf16[128,768]{1,0:T(8,128)(2,1)S(1)}, bf16[128,768]{1,0:T(8,128)(2,1)S(1)}, u32[]{:S(2)}, u32[]{:S(2)}) collective-permute-start(bf16[128,768]{1,0:T(8,128)(2,1)S(1)} %get-tuple-element.47), channel_id=1, source_target_pairs={{0,8},{4,12},{8,0},{12,4},{16,24},{20,28},{24,16},{28,20},{1,9},{5... | collective-permute-start | bytes 589832 | tf_op jit(solution)/shard_map/ppermute | solution.py:322
  24.2 2.8 %collective-permute-done.3.refs_6_.refs_5_ = bf16[128,1024]{1,0:T(8,128)(2,1)S(1)} collective-permute-done((bf16[128,1024]{1,0:T(8,128)(2,1)S(1)}, bf16[128,1024]{1,0:T(8,128)(2,1)S(1)}, u32[]{:S(2)}, u32[]{:S(2)}) %collective-permute-start.3) | collective-permute-done | bytes 262176 | tf_op jit(solution)/shard_map/ppermute | solution.py:322
  27.1 1.3 %collective-permute-done.6.refs_8_ = bf16[64,1024]{1,0:T(8,128)(2,1)S(1)} collective-permute-done((bf16[64,1024]{1,0:T(8,128)(2,1)S(1)}, bf16[64,1024]{1,0:T(8,128)(2,1)S(1)}, u32[]{:S(2)}, u32[]{:S(2)}) %collective-permute-start.6) | collective-permute-done | bytes 131104 | tf_op jit(solution)/shard_map/ppermute | solution.py:322
  28.4 2.4 %peer_hidden.1.refs_6_ = bf16[384,1024]{1,0:T(8,128)(2,1)S(1)} custom-call(s32[1]{0:T(128)} %bitcast.refs_0_, s32[1]{0:T(128)} %bitcast.2.refs_1_, s32[1]{0:T(128)} %bitcast.3.refs_2_, s32[1]{0:T(128)} %bitcast.4.refs_3_, s32[1]{0:T(128)} %bitcast.5.refs_4_, bf16[128,1024]{1,0:T(8,128)(2,1)S(1)} %collective-permute-done.3.refs_6_.refs_5_, ...), custom_call_target="tpu_custom_call" | custom-call | flops 15728640 | bytes 2000000 | tf_op jit(solution)/shard_map/peer_hidden/pallas_call | solution.py:306
  30.9 1.7 %collective-permute-done.8.refs_9_ = bf16[128,768]{1,0:T(8,128)(2,1)S(1)} collective-permute-done((bf16[128,768]{1,0:T(8,128)(2,1)S(1)}, bf16[128,768]{1,0:T(8,128)(2,1)S(1)}, u32[]{:S(2)}, u32[]{:S(2)}) %collective-permute-start.8) | collective-permute-done | bytes 196640 | tf_op jit(solution)/shard_map/ppermute | solution.py:322
  32.5 1.0 %collective-permute-done.7.refs_8_ = bf16[128,768]{1,0:T(8,128)(2,1)S(1)} collective-permute-done((bf16[128,768]{1,0:T(8,128)(2,1)S(1)}, bf16[128,768]{1,0:T(8,128)(2,1)S(1)}, u32[]{:S(2)}, u32[]{:S(2)}) %collective-permute-start.7) | collective-permute-done | bytes 196640 | tf_op jit(solution)/shard_map/ppermute | solution.py:322
  33.5 0.6 %weight_send.1 = bf16[768,512]{1,0:T(8,128)(2,1)S(1)} custom-call(s32[1]{0:T(128)} %bitcast.refs_0_, s32[1]{0:T(128)} %bitcast.2.refs_1_, s32[1]{0:T(128)} %bitcast.3.refs_2_, s32[1]{0:T(128)} %bitcast.4.refs_3_, s32[1]{0:T(128)} %bitcast.5.refs_4_, bf16[128,1024]{1,0:T(8,128)(2,1)S(1)} %get-tuple-element.29.refs_5_, ...), custom_call_target="tpu_custom_call" | custom-call | flops 402653184 | bytes 6000000 | tf_op jit(solution)/shard_map/weight_send/pallas_call | solution.py:306
  34.3 0.6 %weight_keep.1.refs_5_ = f32[768,512]{1,0:T(8,128)S(1)} custom-call(s32[1]{0:T(128)} %bitcast.refs_0_, s32[1]{0:T(128)} %bitcast.2.refs_1_, s32[1]{0:T(128)} %bitcast.3.refs_2_, s32[1]{0:T(128)} %bitcast.4.refs_3_, s32[1]{0:T(128)} %bitcast.5.refs_4_, bf16[128,1024]{1,0:T(8,128)(2,1)S(1)} %get-tuple-element.29.refs_5_, ...), custom_call_target="tpu_custom_call" | custom-call | flops 402653184 | bytes 6000000 | tf_op jit(solution)/shard_map/weight_keep/pallas_call | solution.py:306
  34.9 1.6 %collective-permute-done.10.refs_6_ = bf16[768,512]{1,0:T(8,128)(2,1)S(1)} collective-permute-done((bf16[768,512]{1,0:T(8,128)(2,1)S(1)}, bf16[768,512]{1,0:T(8,128)(2,1)S(1)}, u32[]{:S(2)}, u32[]{:S(2)}) %collective-permute-start.10) | collective-permute-done | bytes 786464 | tf_op jit(solution)/shard_map/ppermute | solution.py:322
  36.8 2.3 %collective-permute-start.13 = (bf16[192,512]{1,0:T(8,128)(2,1)S(1)}, bf16[192,512]{1,0:T(8,128)(2,1)S(1)}, u32[]{:S(2)}, u32[]{:S(2)}) collective-permute-start(bf16[192,512]{1,0:T(8,128)(2,1)S(1)} %get-tuple-element.31.refs_9_), channel_id=1, source_target_pairs={{0,1},{1,0},{2,3},{3,2},{4,5},{5,4},{6,7},{7,6},{8,9},{9,8},{10,11... | collective-permute-start | bytes 589832 | tf_op jit(solution)/shard_map/ppermute | solution.py:322
  39.0 1.7 %collective-permute-start.11 = (bf16[192,256]{1,0:T(8,128)(2,1)S(1)}, bf16[192,256]{1,0:T(8,128)(2,1)S(1)}, u32[]{:S(2)}, u32[]{:S(2)}) collective-permute-start(bf16[192,256]{1,0:T(8,128)(2,1)S(1)} %get-tuple-element.33), channel_id=1, source_target_pairs={{0,8},{4,12},{8,0},{12,4},{16,24},{20,28},{24,16},{28,20},{1,9},{5... | collective-permute-start | bytes 294920 | tf_op jit(solution)/shard_map/ppermute | solution.py:322
  41.1 1.4 %collective-permute-start.15 = (bf16[192,256]{1,0:T(8,128)(2,1)S(1)}, bf16[192,256]{1,0:T(8,128)(2,1)S(1)}, u32[]{:S(2)}, u32[]{:S(2)}) collective-permute-start(bf16[192,256]{1,0:T(8,128)(2,1)S(1)} %get-tuple-element.38), channel_id=1, source_target_pairs={{0,9},{1,8},{2,11},{3,10},{4,13},{5,12},{6,15},{7,14},{8,1},{9,0},... | collective-permute-start | bytes 294920 | tf_op jit(solution)/shard_map/ppermute | solution.py:329
  42.5 2.2 %collective-permute-done.13.refs_6_ = bf16[192,512]{1,0:T(8,128)(2,1)S(1)} collective-permute-done((bf16[192,512]{1,0:T(8,128)(2,1)S(1)}, bf16[192,512]{1,0:T(8,128)(2,1)S(1)}, u32[]{:S(2)}, u32[]{:S(2)}) %collective-permute-start.13) | collective-permute-done | bytes 196640 | tf_op jit(solution)/shard_map/ppermute | solution.py:322
  44.8 4.1 %collective-permute-start.14 = (bf16[192,256]{1,0:T(8,128)(2,1)S(1)}, bf16[192,256]{1,0:T(8,128)(2,1)S(1)}, u32[]{:S(2)}, u32[]{:S(2)}) collective-permute-start(bf16[192,256]{1,0:T(8,128)(2,1)S(1)} %get-tuple-element.37), channel_id=1, source_target_pairs={{0,3},{1,2},{2,1},{3,0},{4,7},{5,6},{6,5},{7,4},{8,11},{9,10},{10,... | collective-permute-start | bytes 294920 | tf_op jit(solution)/shard_map/ppermute | solution.py:322
  48.9 1.3 %collective-permute-start.16 = (bf16[192,256]{1,0:T(8,128)(2,1)S(1)}, bf16[192,256]{1,0:T(8,128)(2,1)S(1)}, u32[]{:S(2)}, u32[]{:S(2)}) collective-permute-start(bf16[192,256]{1,0:T(8,128)(2,1)S(1)} %get-tuple-element.41), channel_id=1, source_target_pairs={{0,11},{1,10},{2,9},{3,8},{4,15},{5,14},{6,13},{7,12},{8,3},{9,2},... | collective-permute-start | bytes 294920 | tf_op jit(solution)/shard_map/ppermute | solution.py:329
  50.3 3.7 %input_grad.1 = (bf16[128,1024]{1,0:T(8,128)(2,1)}, f32[8,128]{1,0:T(8,128)S(1)}) custom-call(s32[1]{0:T(128)} %bitcast.refs_0_, s32[1]{0:T(128)} %bitcast.2.refs_1_, s32[1]{0:T(128)} %bitcast.3.refs_2_, s32[1]{0:T(128)} %bitcast.4.refs_3_, s32[1]{0:T(128)} %bitcast.5.refs_4_, bf16[144,3072]{1,0:T(8,128)(2,1)S(1)} %get-tuple-element.26.refs_9_.refs_5_, ...), custom_call_target="tpu_custom_call" | custom-call | flops 905969664 | bytes 9000000 | tf_op jit(solution)/shard_map/input_grad/pallas_call | solution.py:306
  54.1 0.7 %collective-permute-start.17 = (bf16[192,128]{1,0:T(8,128)(2,1)S(1)}, bf16[192,128]{1,0:T(8,128)(2,1)S(1)}, u32[]{:S(2)}, u32[]{:S(2)}) collective-permute-start(bf16[192,128]{1,0:T(8,128)(2,1)S(1)} %get-tuple-element.43), channel_id=1, source_target_pairs={{0,16},{4,20},{8,24},{12,28},{16,0},{20,4},{24,8},{28,12},{1,17},{... | collective-permute-start | bytes 147464 | tf_op jit(solution)/shard_map/ppermute | solution.py:322
  54.8 1.5 %collective-permute-done.16.refs_8_ = bf16[192,256]{1,0:T(8,128)(2,1)S(1)} collective-permute-done((bf16[192,256]{1,0:T(8,128)(2,1)S(1)}, bf16[192,256]{1,0:T(8,128)(2,1)S(1)}, u32[]{:S(2)}, u32[]{:S(2)}) %collective-permute-start.16) | collective-permute-done | bytes 98336 | tf_op jit(solution)/shard_map/ppermute | solution.py:329
  56.8 1.8 %collective-permute-done.17.refs_7_ = bf16[192,128]{1,0:T(8,128)(2,1)S(1)} collective-permute-done((bf16[192,128]{1,0:T(8,128)(2,1)S(1)}, bf16[192,128]{1,0:T(8,128)(2,1)S(1)}, u32[]{:S(2)}, u32[]{:S(2)}) %collective-permute-start.17) | collective-permute-done | bytes 49184 | tf_op jit(solution)/shard_map/ppermute | solution.py:322
  58.6 1.9 %collective-permute-done.18.refs_8_ = bf16[192,128]{1,0:T(8,128)(2,1)S(1)} collective-permute-done((bf16[192,128]{1,0:T(8,128)(2,1)S(1)}, bf16[192,128]{1,0:T(8,128)(2,1)S(1)}, u32[]{:S(2)}, u32[]{:S(2)}) %collective-permute-start.18) | collective-permute-done | bytes 49184 | tf_op jit(solution)/shard_map/ppermute | solution.py:322
  60.5 0.8 %place.1 = f32[6,128,128]{2,1,0:T(8,128)} custom-call(s32[1]{0:T(128)} %bitcast.refs_0_, s32[1]{0:T(128)} %bitcast.2.refs_1_, s32[1]{0:T(128)} %bitcast.3.refs_2_, s32[1]{0:T(128)} %bitcast.4.refs_3_, s32[1]{0:T(128)} %bitcast.5.refs_4_, f32[192,128]{1,0:T(8,128)S(1)} %get-tuple-element.40.refs_5_, f32[192,128]{1,0:T(8,128)S(1)} %get-tuple-element.42.refs_6_, ...), custom_call_target="tpu_custom_call" | custom-call | flops 1000000 | bytes 1000000 | tf_op jit(solution)/shard_map/place/pallas_call | solution.py:306
  (27 shorter events, 1.8 us)
Async XLA Ops:
  0.6 1.2 %copy-start = (f32[9,1024]{1,0:T(8,128)S(1)}, f32[9,1024]{1,0:T(8,128)}, u32[]{:S(2)}) copy-start(f32[9,1024]{1,0:T(8,128)} %param.7) | copy-start | bytes 110596
  2.1 11.8 %collective-permute-start = (bf16[160,1024]{1,0:T(8,128)(2,1)S(1)}, bf16[160,1024]{1,0:T(8,128)(2,1)S(1)}, u32[]{:S(2)}, u32[]{:S(2)}) collective-permute-start(bf16[160,1024]{1,0:T(8,128)(2,1)S(1)} %pad_maximum_fusion.1), channel_id=1, source_target_pairs={{0,4},{4,0},{8,12},{12,8},{16,20},{20,16},{24,28},{28,24},{1,5},{5... | collective-permute-start | bytes 983048 | tf_op jit(solution)/shard_map/ppermute | solution.py:322
  2.6 10.3 %collective-permute-start.1 = (bf16[80,1024]{1,0:T(8,128)(2,1)S(1)}, bf16[80,1024]{1,0:T(8,128)(2,1)S(1)}, u32[]{:S(2)}, u32[]{:S(2)}) collective-permute-start(bf16[80,1024]{1,0:T(8,128)(2,1)S(1)} %get-tuple-element.48), channel_id=1, source_target_pairs={{8,4},{16,12},{24,20},{4,8},{12,16},{20,24},{9,5},{17,13},{25,21},... | collective-permute-start | bytes 491528 | tf_op jit(solution)/shard_map/ppermute | solution.py:354
  3.3 14.7 %collective-permute-start.2 = (bf16[80,1024]{1,0:T(8,128)(2,1)S(1)}, bf16[80,1024]{1,0:T(8,128)(2,1)S(1)}, u32[]{:S(2)}, u32[]{:S(2)}) collective-permute-start(bf16[80,1024]{1,0:T(8,128)(2,1)S(1)} %get-tuple-element.49), channel_id=1, source_target_pairs={{8,4},{16,12},{24,20},{9,5},{17,13},{25,21},{10,6},{18,14},{26,22}... | collective-permute-start | bytes 491528 | tf_op jit(solution)/shard_map/ppermute | solution.py:357
  4.0 19.3 %collective-permute-start.5 = (bf16[128,1024]{1,0:T(8,128)(2,1)S(1)}, bf16[128,1024]{1,0:T(8,128)(2,1)S(1)}, u32[]{:S(2)}, u32[]{:S(2)}) collective-permute-start(bf16[128,1024]{1,0:T(8,128)(2,1)S(1)} %slice.35), channel_id=1, source_target_pairs={{0,24},{4,28},{8,16},{12,20},{16,8},{20,12},{24,0},{28,4},{1,25},{... | collective-permute-start | bytes 786440 | tf_op jit(solution)/shard_map/ppermute | solution.py:322
  11.7 12.4 %collective-permute-start.4 = (bf16[128,1024]{1,0:T(8,128)(2,1)S(1)}, bf16[128,1024]{1,0:T(8,128)(2,1)S(1)}, u32[]{:S(2)}, u32[]{:S(2)}) collective-permute-start(bf16[128,1024]{1,0:T(8,128)(2,1)S(1)} %slice.35), channel_id=1, source_target_pairs={{0,16},{4,20},{8,24},{12,28},{16,0},{20,4},{24,8},{28,12},{1,17},{... | collective-permute-start | bytes 786440 | tf_op jit(solution)/shard_map/ppermute | solution.py:322
  12.9 14.1 %collective-permute-start.3 = (bf16[128,1024]{1,0:T(8,128)(2,1)S(1)}, bf16[128,1024]{1,0:T(8,128)(2,1)S(1)}, u32[]{:S(2)}, u32[]{:S(2)}) collective-permute-start(bf16[128,1024]{1,0:T(8,128)(2,1)S(1)} %slice.35), channel_id=1, source_target_pairs={{0,8},{4,12},{8,0},{12,4},{16,24},{20,28},{24,16},{28,20},{1,9},{5... | collective-permute-start | bytes 786440 | tf_op jit(solution)/shard_map/ppermute | solution.py:322
  20.6 10.2 %collective-permute-start.9 = (bf16[128,768]{1,0:T(8,128)(2,1)S(1)}, bf16[128,768]{1,0:T(8,128)(2,1)S(1)}, u32[]{:S(2)}, u32[]{:S(2)}) collective-permute-start(bf16[128,768]{1,0:T(8,128)(2,1)S(1)} %get-tuple-element.45), channel_id=1, source_target_pairs={{0,24},{4,28},{8,16},{12,20},{16,8},{20,12},{24,0},{28,4},{1,25},{... | collective-permute-start | bytes 589832 | tf_op jit(solution)/shard_map/ppermute | solution.py:322
  22.7 9.8 %collective-permute-start.8 = (bf16[128,768]{1,0:T(8,128)(2,1)S(1)}, bf16[128,768]{1,0:T(8,128)(2,1)S(1)}, u32[]{:S(2)}, u32[]{:S(2)}) collective-permute-start(bf16[128,768]{1,0:T(8,128)(2,1)S(1)} %get-tuple-element.46), channel_id=1, source_target_pairs={{0,16},{4,20},{8,24},{12,28},{16,0},{20,4},{24,8},{28,12},{1,17},{... | collective-permute-start | bytes 589832 | tf_op jit(solution)/shard_map/ppermute | solution.py:322
  23.3 10.3 %collective-permute-start.7 = (bf16[128,768]{1,0:T(8,128)(2,1)S(1)}, bf16[128,768]{1,0:T(8,128)(2,1)S(1)}, u32[]{:S(2)}, u32[]{:S(2)}) collective-permute-start(bf16[128,768]{1,0:T(8,128)(2,1)S(1)} %get-tuple-element.47), channel_id=1, source_target_pairs={{0,8},{4,12},{8,0},{12,4},{16,24},{20,28},{24,16},{28,20},{1,9},{5... | collective-permute-start | bytes 589832 | tf_op jit(solution)/shard_map/ppermute | solution.py:322
  27.0 1.4 %collective-permute-start.6 = (bf16[64,1024]{1,0:T(8,128)(2,1)S(1)}, bf16[64,1024]{1,0:T(8,128)(2,1)S(1)}, u32[]{:S(2)}, u32[]{:S(2)}) collective-permute-start(bf16[64,1024]{1,0:T(8,128)(2,1)S(1)} %ends.1), channel_id=1, source_target_pairs={{0,4},{4,0},{8,12},{12,8},{16,20},{20,16},{24,28},{28,24},{1,5},{5... | collective-permute-start | bytes 393224 | tf_op jit(solution)/shard_map/ppermute | solution.py:322
  34.2 2.4 %collective-permute-start.10 = (bf16[768,512]{1,0:T(8,128)(2,1)S(1)}, bf16[768,512]{1,0:T(8,128)(2,1)S(1)}, u32[]{:S(2)}, u32[]{:S(2)}) collective-permute-start(bf16[768,512]{1,0:T(8,128)(2,1)S(1)} %weight_send.1), channel_id=1, source_target_pairs={{0,4},{4,0},{8,12},{12,8},{16,20},{20,16},{24,28},{28,24},{1,5},{5... | collective-permute-start | bytes 2359304 | tf_op jit(solution)/shard_map/ppermute | solution.py:322
  36.8 8.0 %collective-permute-start.13 = (bf16[192,512]{1,0:T(8,128)(2,1)S(1)}, bf16[192,512]{1,0:T(8,128)(2,1)S(1)}, u32[]{:S(2)}, u32[]{:S(2)}) collective-permute-start(bf16[192,512]{1,0:T(8,128)(2,1)S(1)} %get-tuple-element.31.refs_9_), channel_id=1, source_target_pairs={{0,1},{1,0},{2,3},{3,2},{4,5},{5,4},{6,7},{7,6},{8,9},{9,8},{10,11... | collective-permute-start | bytes 589832 | tf_op jit(solution)/shard_map/ppermute | solution.py:322
  39.0 15.0 %collective-permute-start.11 = (bf16[192,256]{1,0:T(8,128)(2,1)S(1)}, bf16[192,256]{1,0:T(8,128)(2,1)S(1)}, u32[]{:S(2)}, u32[]{:S(2)}) collective-permute-start(bf16[192,256]{1,0:T(8,128)(2,1)S(1)} %get-tuple-element.33), channel_id=1, source_target_pairs={{0,8},{4,12},{8,0},{12,4},{16,24},{20,28},{24,16},{28,20},{1,9},{5... | collective-permute-start | bytes 294920 | tf_op jit(solution)/shard_map/ppermute | solution.py:322
  40.7 13.3 %collective-permute-start.12 = (bf16[192,256]{1,0:T(8,128)(2,1)S(1)}, bf16[192,256]{1,0:T(8,128)(2,1)S(1)}, u32[]{:S(2)}, u32[]{:S(2)}) collective-permute-start(bf16[192,256]{1,0:T(8,128)(2,1)S(1)} %get-tuple-element.35), channel_id=1, source_target_pairs={{0,1},{1,0},{2,3},{3,2},{4,5},{5,4},{6,7},{7,6},{8,9},{9,8},{10,11... | collective-permute-start | bytes 294920 | tf_op jit(solution)/shard_map/ppermute | solution.py:322
  41.1 12.9 %collective-permute-start.15 = (bf16[192,256]{1,0:T(8,128)(2,1)S(1)}, bf16[192,256]{1,0:T(8,128)(2,1)S(1)}, u32[]{:S(2)}, u32[]{:S(2)}) collective-permute-start(bf16[192,256]{1,0:T(8,128)(2,1)S(1)} %get-tuple-element.38), channel_id=1, source_target_pairs={{0,9},{1,8},{2,11},{3,10},{4,13},{5,12},{6,15},{7,14},{8,1},{9,0},... | collective-permute-start | bytes 294920 | tf_op jit(solution)/shard_map/ppermute | solution.py:329
  44.8 9.2 %collective-permute-start.14 = (bf16[192,256]{1,0:T(8,128)(2,1)S(1)}, bf16[192,256]{1,0:T(8,128)(2,1)S(1)}, u32[]{:S(2)}, u32[]{:S(2)}) collective-permute-start(bf16[192,256]{1,0:T(8,128)(2,1)S(1)} %get-tuple-element.37), channel_id=1, source_target_pairs={{0,3},{1,2},{2,1},{3,0},{4,7},{5,6},{6,5},{7,4},{8,11},{9,10},{10,... | collective-permute-start | bytes 294920 | tf_op jit(solution)/shard_map/ppermute | solution.py:322
  48.9 7.3 %collective-permute-start.16 = (bf16[192,256]{1,0:T(8,128)(2,1)S(1)}, bf16[192,256]{1,0:T(8,128)(2,1)S(1)}, u32[]{:S(2)}, u32[]{:S(2)}) collective-permute-start(bf16[192,256]{1,0:T(8,128)(2,1)S(1)} %get-tuple-element.41), channel_id=1, source_target_pairs={{0,11},{1,10},{2,9},{3,8},{4,15},{5,14},{6,13},{7,12},{8,3},{9,2},... | collective-permute-start | bytes 294920 | tf_op jit(solution)/shard_map/ppermute | solution.py:329
  54.1 4.5 %collective-permute-start.17 = (bf16[192,128]{1,0:T(8,128)(2,1)S(1)}, bf16[192,128]{1,0:T(8,128)(2,1)S(1)}, u32[]{:S(2)}, u32[]{:S(2)}) collective-permute-start(bf16[192,128]{1,0:T(8,128)(2,1)S(1)} %get-tuple-element.43), channel_id=1, source_target_pairs={{0,16},{4,20},{8,24},{12,28},{16,0},{20,4},{24,8},{28,12},{1,17},{... | collective-permute-start | bytes 147464 | tf_op jit(solution)/shard_map/ppermute | solution.py:322
  56.3 4.2 %collective-permute-start.18 = (bf16[192,128]{1,0:T(8,128)(2,1)S(1)}, bf16[192,128]{1,0:T(8,128)(2,1)S(1)}, u32[]{:S(2)}, u32[]{:S(2)}) collective-permute-start(bf16[192,128]{1,0:T(8,128)(2,1)S(1)} %get-tuple-element.44), channel_id=1, source_target_pairs={{0,16},{4,20},{8,24},{12,28},{16,0},{20,4},{24,8},{28,12},{1,17},{... | collective-permute-start | bytes 147464 | tf_op jit(solution)/shard_map/ppermute | solution.py:322

commit v8 on v7

--- a/solution.py
+++ b/solution.py
@@ -60,8 +60,9 @@
     return both.at[:frames], both.at[frames : 2 * frames], both.at[2 * frames :]
 
 
-def project_kernel(place, near, far, both, w, own_hidden, conv_out, qkv, w_out, ext, hidden, sems):
+def project_kernel(place, near, far, both, w, _, own_hidden, conv_out, qkv, w_out, *scratch):
     frames, width = own_hidden.shape
+    ext, hidden, sems = scratch
     wide = width
     copies = [
         pltpu.make_async_copy(w.at[:, cols], w_out.at[:, cols], sems.at[i])
@@ -72,10 +73,10 @@
     own, _, taps = parts_of(both, frames)
     low_core = place[3] == 0
     rows, back = frames + 2 * HALO, KERNEL - 1
-    live = live_rows(place[0] - HALO, rows, place[1])
+    live = live_rows(place[0] - HALO, rows, place[1]) & ~live_rows(place[0] - HALO, rows, 0)
     for col in range(0, width, 128):
         cols = pl.ds(col, 128)
-        mate, other = near[:HALO, cols].astype(F32), far[:, cols].astype(F32)
+        mate, other = near[:, cols].astype(F32), far[:, cols].astype(F32)
         before, after = jnp.where(low_core, other, mate), jnp.where(low_core, mate, other)
         raw = jnp.concatenate([before, own[:, cols], after], axis=0)
         masked = jnp.where(live, raw, 0.0)
@@ -120,7 +121,7 @@
             conv_hidden(ext, taps, cols, EDGE - KERNEL + 1, frames, out)
 
 
-def attend_kernel(place, qkv, both, near, far, attended, grads, sends, later):
+def attend_kernel(place, qkv, both, next_cot, attended, grads, sends, later):
     frames, width = attended.shape
     cot = parts_of(both, frames)[1]
     span = frames + HALO
@@ -140,7 +141,7 @@
 
     masks = [mask(HALO, frames), mask(frames - skip, HALO)]
     row = lax.broadcasted_iota(jnp.int32, (frames, width), 0)
-    after = jnp.where(place[3] == 0, near[HALO:].astype(F32), far[...].astype(F32))
+    after = next_cot[...].astype(F32)
     later[:HALO] = jnp.where(begin + frames + row[:HALO] < count, after, 0.0).astype(BF16)
     later[HALO:] = jnp.zeros((frames - HALO, width), BF16)
     factor = HEAD**-0.5
@@ -206,8 +207,8 @@
             sends[slot, :, at : at + HEAD] = jnp.concatenate(halves, axis=1)
 
 
-def attend_alone(place, qkv, both, near, far, attended, grads, later):
-    attend_kernel(place, qkv, both, near, far, attended, grads, None, later)
+def attend_alone(place, qkv, both, next_cot, attended, grads, later):
+    attend_kernel(place, qkv, both, next_cot, attended, grads, None, later)
 
 
 def input_grad_kernel(place, grads, w, conv, both, *refs):
@@ -258,22 +259,19 @@
         yield rows, slice(at, at + size)
 
 
-def core_sum_kernel(place, keep, got, near, ahead, *outs):
-    for mask, out in ((2, near), (3, ahead)):
-        for rows, at in shard_rows(place, mask):
-            out[at] = (keep[rows] + got[rows].astype(F32)).astype(out.dtype)
-    for mask, same, other in ((1, *outs[:2]), (0, *outs[2:])):
+def core_sum_kernel(place, keep, got, *outs):
+    for i, mask in enumerate((2, 3, 1, 0)):
         for rows, at in shard_rows(place, mask):
             halves(
                 place,
                 lambda cols, rows=rows: keep[rows, cols] + got[rows, cols].astype(F32),
-                same.at[at],
-                other.at[at],
+                outs[2 * i].at[at],
+                outs[2 * i + 1].at[at],
             )
 
 
-def forward_kernel(place, ahead, got, same, other):
-    halves(place, lambda cols: ahead[:, cols] + got[:, cols].astype(F32), same, other)
+def forward_kernel(place, ahead, got, out):
+    out[...] = (ahead[...] + got[...].astype(F32)).astype(BF16)
 
 
 def mid_sum_kernel(same, place, moved, kept, cross, sums, *refs):
@@ -349,12 +347,13 @@
     first_cot = both[frames : frames + HALO].astype(BF16)
     low_core = me % 2 == 0
     edge = jnp.where(low_core, last, first)
-    near = swap(jnp.concatenate([edge, first_cot], axis=0), "tm", 1)
-    down = [(i, i - 1) for i in range(2, parts, 2)]
+    near = swap(edge, "tm", 1)
     far = lax.ppermute(
-        jnp.where(low_core, first, last), "tm", down + [(i, j) for j, i in down]
+        jnp.where(low_core, first, last),
+        "tm",
+        [(i, (i + 1 if i % 2 else i - 1) % parts) for i in range(parts)],
     )
-    far_cot = lax.ppermute(first_cot, "tm", down)
+    next_cot = lax.ppermute(first_cot, "tm", [(i, (i - 1) % parts) for i in range(parts)])
     if split:
         peers = [swap(own, "tm", mask) for mask in (2, 4, 6)]
     rows = frames + 2 * HALO
@@ -377,6 +376,7 @@
         flops=rows * width * 3 * width * 2,
         moved=9000000,
         remote=[w_qkv],
+        after=[next_cot],
         mib=OWN,
     )
     outs = [((frames, width), BF16), ((frames + EDGE, 3 * width), BF16)]
@@ -385,7 +385,7 @@
         "attend",
         outs + [((4, frames, 3 * width // 4), BF16)] * split,
         place,
-        [qkv, both, near, far_cot],
+        [qkv, both, next_cot],
         [((frames, width), BF16)],
         mib=16,
         flops=8 * 12 * span * 128 * 128 * 2 * 8,
@@ -426,14 +426,15 @@
             )[0]
             for mine in (False, True)
         )
-        near, ahead, cross_same, cross_other, own_same, own_other = call(
+        low, high = (half, BF16), (half, F32)
+        near_same, near_other, *ahead, cross_same, cross_other, own_same, own_other = call(
             core_sum_kernel,
             "core_sum",
-            [(whole, BF16), (whole, F32), (half, BF16), (half, BF16), (half, F32), (half, BF16)],
+            [low, low, high, high, low, low, high, low],
             place,
             [keep, swap(send, "tm", 1)],
         )
-        late = [near]
+        late = [near_same]
         grad_in, done = call(
             input_grad_kernel,
             "input_grad",
@@ -446,11 +447,12 @@
             moved=9000000,
             after=late,
         )
-        got_near = swap(near, "dp", 1)
+        got_near = swap(near_same, "dp", 1), swap(near_other, "dp", 1)
         got_cross = swap(cross_same, "dp", 1), swap_both(cross_other, 1, 2)
         got_own = swap(own_other, "tm", 2)
-        same, other = call(
-            forward_kernel, "forward", [(half, BF16)] * 2, place, [ahead, got_near]
+        same, other = (
+            call(forward_kernel, "forward_" + name, [low], place, [part, got])[0]
+            for name, part, got in zip(("same", "other"), ahead, got_near)
         )
         got_sums = swap(same, "dp", 3), swap_both(other, 3, 2)
         kept, moved = [], []

time: 61.4 us -> 58.1 us (0.946)
  waiting for transfers between devices: 15.8 us -> 13.9 us
  starting transfers between devices: 27.2 us -> 25.8 us
    ppermute x15 -> x16, starting transfers between devices: 23.2 us -> 15.5 us  [swap(): lax.ppermute(value, axis, [(i, i ^ mask) for i in range(lax.axis_size(axi...]
    ppermute x15 -> x16, waiting for transfers between devices: 14.3 us -> 10.6 us  [swap(): lax.ppermute(value, axis, [(i, i ^ mask) for i in range(lax.axis_size(axi...]
    ppermute x2, starting transfers between devices: 2.7 us -> 6.17 us  [swap_both(): return lax.ppermute(value, ('tm', 'dp'), pairs)]
    ppermute x2, waiting for transfers between devices: 0.01 us -> 3.33 us  [the longest x1 3.08 us: on_device(): lax.ppermute(jnp.where(low_core, first, last), 'tm', [(i, (i + 1 if i % 2...]
    ppermute x2, starting transfers between devices: 1.33 us -> 4.14 us  [the longest x1 3.39 us: on_device(): lax.ppermute(first_cot, 'tm', [(i, (i - 1) % parts) for i in range(parts)])]
    ppermute x2, waiting for transfers between devices: 1.48 us -> 0.01 us  [swap_both(): return lax.ppermute(value, ('tm', 'dp'), pairs)]
    pallas_call x12 -> x13, Pallas kernels: 15.3 us -> 15.4 us  [call(): pl.pallas_call(placed, name=name, out_shape=[jax.ShapeDtypeStruct(shape,...]
  transfers between devices with their start and end apart: 19 -> 20, of which waited for: 9 -> 10; matrix products, arithmetic and copies ran while one was open for 0% -> 0% of each run, Pallas kernels for 22% -> 24%
where the time goes in v8:
time: 58.1 us; the launch traced here: 57.9 us
  starting transfers between devices  25.8 us (44%)
  Pallas kernels  15.4 us (27%)
  waiting for transfers between devices  13.9 us (24%)
  between operations  1.45 us (2%)
  other arithmetic  1.36 us (2%)
    ppermute x16, starting transfers between devices, swap(): lax.ppermute(value, axis, [(i, i ^ mask) for i in range(lax.axis_size(axi...  15.5 us
    pallas_call x13, Pallas kernels, call(): pl.pallas_call(placed, name=name, out_shape=[jax.ShapeDtypeStruct(shape,...  15.4 us
    ppermute x16, waiting for transfers between devices, swap(): lax.ppermute(value, axis, [(i, i ^ mask) for i in range(lax.axis_size(axi...  10.6 us
    ppermute x2, starting transfers between devices, swap_both(): return lax.ppermute(value, ('tm', 'dp'), pairs)  6.17 us
    ppermute x1, starting transfers between devices, on_device(): lax.ppermute(first_cot, 'tm', [(i, (i - 1) % parts) for i in range(parts)])  3.39 us
    ppermute x1, waiting for transfers between devices, on_device(): lax.ppermute(jnp.where(low_core, first, last), 'tm', [(i, (i + 1 if i % 2...  3.08 us
    convert_element_type x1, other arithmetic, on_device(): cot.astype(F32)  1.16 us
  transfers between devices with their start and end apart: 20, of which 10 were waited for; matrix products, arithmetic and copies ran while one was open for 0% of the time, Pallas kernels for 24%

profile of v8, /device:TPU:0, one launch (start us, length us, event | category | flops | bytes accessed | tf_op | source)
XLA Modules:
  0.0 57.9 jit_solution(5716652620353676152)
XLA Ops:
  0.7 1.2 %bitcast_convert_fusion = (f32[128,1024]{1,0:T(8,128)S(1)}, f32[128,1024]{1,0:T(8,128)S(1)}) fusion(bf16[1,128,1024]{2,1,0:T(8,128)(2,1)} %param.9, bf16[1,128,1024]{2,1,0:T(8,128)(2,1)} %param.5), kind=kLoop, calls=%fused_computation.1 | loop fusion | flops 262144 | bytes 1572864 | tf_op jit(solution)/shard_map/convert_element_type | solution.py:343
  2.1 3.4 %collective-permute-start.2 = (bf16[80,1024]{1,0:T(8,128)(2,1)S(1)}, bf16[80,1024]{1,0:T(8,128)(2,1)S(1)}, u32[]{:S(2)}, u32[]{:S(2)}) collective-permute-start(bf16[80,1024]{1,0:T(8,128)(2,1)S(1)} %get-tuple-element.48), channel_id=1, source_target_pairs={{0,28},{4,0},{8,4},{12,8},{16,12},{20,16},{24,20},{28,24},{1,29},{... | collective-permute-start | bytes 491528 | tf_op jit(solution)/shard_map/ppermute | solution.py:356
  5.4 0.8 %collective-permute-start.1 = (bf16[80,1024]{1,0:T(8,128)(2,1)S(1)}, bf16[80,1024]{1,0:T(8,128)(2,1)S(1)}, u32[]{:S(2)}, u32[]{:S(2)}) collective-permute-start(bf16[80,1024]{1,0:T(8,128)(2,1)S(1)} %get-tuple-element.50), channel_id=1, source_target_pairs={{0,28},{4,8},{8,4},{12,16},{16,12},{20,24},{24,20},{28,0},{1,29},{... | collective-permute-start | bytes 491528 | tf_op jit(solution)/shard_map/ppermute | solution.py:351
  6.2 1.4 %collective-permute-start.5 = (bf16[128,1024]{1,0:T(8,128)(2,1)S(1)}, bf16[128,1024]{1,0:T(8,128)(2,1)S(1)}, u32[]{:S(2)}, u32[]{:S(2)}) collective-permute-start(bf16[128,1024]{1,0:T(8,128)(2,1)S(1)} %slice.35), channel_id=1, source_target_pairs={{0,24},{4,28},{8,16},{12,20},{16,8},{20,12},{24,0},{28,4},{1,25},{... | collective-permute-start | bytes 786440 | tf_op jit(solution)/shard_map/ppermute | solution.py:320
  7.6 1.5 %collective-permute-start.4 = (bf16[128,1024]{1,0:T(8,128)(2,1)S(1)}, bf16[128,1024]{1,0:T(8,128)(2,1)S(1)}, u32[]{:S(2)}, u32[]{:S(2)}) collective-permute-start(bf16[128,1024]{1,0:T(8,128)(2,1)S(1)} %slice.35), channel_id=1, source_target_pairs={{0,16},{4,20},{8,24},{12,28},{16,0},{20,4},{24,8},{28,12},{1,17},{... | collective-permute-start | bytes 786440 | tf_op jit(solution)/shard_map/ppermute | solution.py:320
  10.0 0.5 collective-permute-start.3
  10.5 3.1 %collective-permute-done.1.refs_6_ = bf16[80,1024]{1,0:T(8,128)(2,1)S(1)} collective-permute-done((bf16[80,1024]{1,0:T(8,128)(2,1)S(1)}, bf16[80,1024]{1,0:T(8,128)(2,1)S(1)}, u32[]{:S(2)}, u32[]{:S(2)}) %collective-permute-start.1) | collective-permute-done | bytes 163872 | tf_op jit(solution)/shard_map/ppermute | solution.py:351
  13.6 4.1 %project.1 = (bf16[128,1024]{1,0:T(8,128)(2,1)S(1)}, f32[144,1024]{1,0:T(8,128)S(1)}, bf16[336,3072]{1,0:T(8,128)(2,1)S(1)}, bf16[1024,3072]{1,0:T(8,128)(2,1)S(1)}) custom-call(s32[1]{0:T(128)} %bitcast.refs_0_, s32[1]{0:T(128)} %bitcast.2.refs_1_, s32[1]{0:T(128)} %bitcast.3.refs_2_, s32[1]{0:T(128)} %bitcast.4.refs_3_, s32[1]{0:T(128)} %bitcast.5.refs_4_, ...), custom_call_target="tpu_custom_call" | custom-call | flops 1811939328 | bytes 9000000 | tf_op jit(solution)/shard_map/project/pallas_call | solution.py:304
  17.7 2.6 %attend.1 = (bf16[128,1024]{1,0:T(8,128)(2,1)}, bf16[144,3072]{1,0:T(8,128)(2,1)S(1)}, bf16[4,128,768]{2,1,0:T(8,128)(2,1)S(1)}) custom-call(s32[1]{0:T(128)} %bitcast.refs_0_, s32[1]{0:T(128)} %bitcast.2.refs_1_, s32[1]{0:T(128)} %bitcast.3.refs_2_, s32[1]{0:T(128)} %bitcast.4.refs_3_, s32[1]{0:T(128)} %bitcast.5.refs_4_, ...), custom_call_target="tpu_custom_call" | custom-call | flops 5234491392 | bytes 5000000 | tf_op jit(solution)/shard_map/attend/pallas_call | solution.py:304
  20.5 3.4 %collective-permute-start.7 = (bf16[128,768]{1,0:T(8,128)(2,1)S(1)}, bf16[128,768]{1,0:T(8,128)(2,1)S(1)}, u32[]{:S(2)}, u32[]{:S(2)}) collective-permute-start(bf16[128,768]{1,0:T(8,128)(2,1)S(1)} %get-tuple-element.47), channel_id=1, source_target_pairs={{0,8},{4,12},{8,0},{12,4},{16,24},{20,28},{24,16},{28,20},{1,9},{5... | collective-permute-start | bytes 589832 | tf_op jit(solution)/shard_map/ppermute | solution.py:320
  24.0 1.3 %collective-permute-done.6.refs_8_ = bf16[64,1024]{1,0:T(8,128)(2,1)S(1)} collective-permute-done((bf16[64,1024]{1,0:T(8,128)(2,1)S(1)}, bf16[64,1024]{1,0:T(8,128)(2,1)S(1)}, u32[]{:S(2)}, u32[]{:S(2)}) %collective-permute-start.6) | collective-permute-done | bytes 131104 | tf_op jit(solution)/shard_map/ppermute | solution.py:320
  25.3 2.4 %peer_hidden.1.refs_6_ = bf16[384,1024]{1,0:T(8,128)(2,1)S(1)} custom-call(s32[1]{0:T(128)} %bitcast.refs_0_, s32[1]{0:T(128)} %bitcast.2.refs_1_, s32[1]{0:T(128)} %bitcast.3.refs_2_, s32[1]{0:T(128)} %bitcast.4.refs_3_, s32[1]{0:T(128)} %bitcast.5.refs_4_, bf16[128,1024]{1,0:T(8,128)(2,1)S(1)} %collective-permute-done.3.refs_6_.refs_5_, ...), custom_call_target="tpu_custom_call" | custom-call | flops 15728640 | bytes 2000000 | tf_op jit(solution)/shard_map/peer_hidden/pallas_call | solution.py:304
  27.7 1.3 %collective-permute-done.9.refs_10_ = bf16[128,768]{1,0:T(8,128)(2,1)S(1)} collective-permute-done((bf16[128,768]{1,0:T(8,128)(2,1)S(1)}, bf16[128,768]{1,0:T(8,128)(2,1)S(1)}, u32[]{:S(2)}, u32[]{:S(2)}) %collective-permute-start.9) | collective-permute-done | bytes 196640 | tf_op jit(solution)/shard_map/ppermute | solution.py:320
  29.0 2.8 %collective-permute-done.8.refs_9_ = bf16[128,768]{1,0:T(8,128)(2,1)S(1)} collective-permute-done((bf16[128,768]{1,0:T(8,128)(2,1)S(1)}, bf16[128,768]{1,0:T(8,128)(2,1)S(1)}, u32[]{:S(2)}, u32[]{:S(2)}) %collective-permute-start.8) | collective-permute-done | bytes 196640 | tf_op jit(solution)/shard_map/ppermute | solution.py:320
  31.8 0.6 %weight_send.1 = bf16[768,512]{1,0:T(8,128)(2,1)S(1)} custom-call(s32[1]{0:T(128)} %bitcast.refs_0_, s32[1]{0:T(128)} %bitcast.2.refs_1_, s32[1]{0:T(128)} %bitcast.3.refs_2_, s32[1]{0:T(128)} %bitcast.4.refs_3_, s32[1]{0:T(128)} %bitcast.5.refs_4_, bf16[128,1024]{1,0:T(8,128)(2,1)S(1)} %get-tuple-element.29.refs_5_, ...), custom_call_target="tpu_custom_call" | custom-call | flops 402653184 | bytes 6000000 | tf_op jit(solution)/shard_map/weight_send/pallas_call | solution.py:304
  32.5 0.5 collective-permute-start.10
  33.0 0.6 %weight_keep.1.refs_5_ = f32[768,512]{1,0:T(8,128)S(1)} custom-call(s32[1]{0:T(128)} %bitcast.refs_0_, s32[1]{0:T(128)} %bitcast.2.refs_1_, s32[1]{0:T(128)} %bitcast.3.refs_2_, s32[1]{0:T(128)} %bitcast.4.refs_3_, s32[1]{0:T(128)} %bitcast.5.refs_4_, bf16[128,1024]{1,0:T(8,128)(2,1)S(1)} %get-tuple-element.29.refs_5_, ...), custom_call_target="tpu_custom_call" | custom-call | flops 402653184 | bytes 6000000 | tf_op jit(solution)/shard_map/weight_keep/pallas_call | solution.py:304
  33.6 1.3 %collective-permute-done.10.refs_6_ = bf16[768,512]{1,0:T(8,128)(2,1)S(1)} collective-permute-done((bf16[768,512]{1,0:T(8,128)(2,1)S(1)}, bf16[768,512]{1,0:T(8,128)(2,1)S(1)}, u32[]{:S(2)}, u32[]{:S(2)}) %collective-permute-start.10) | collective-permute-done | bytes 786464 | tf_op jit(solution)/shard_map/ppermute | solution.py:320
  34.9 0.3 core_sum.1
  35.2 1.7 %collective-permute-start.16 = (bf16[192,256]{1,0:T(8,128)(2,1)S(1)}, bf16[192,256]{1,0:T(8,128)(2,1)S(1)}, u32[]{:S(2)}, u32[]{:S(2)}) collective-permute-start(bf16[192,256]{1,0:T(8,128)(2,1)S(1)} %get-tuple-element.41), channel_id=1, source_target_pairs={{0,1},{1,0},{2,3},{3,2},{4,5},{5,4},{6,7},{7,6},{8,9},{9,8},{10,11... | collective-permute-start | bytes 294920 | tf_op jit(solution)/shard_map/ppermute | solution.py:320
  36.9 0.4 collective-permute-start.13
  37.3 1.7 %collective-permute-start.11 = (bf16[192,256]{1,0:T(8,128)(2,1)S(1)}, bf16[192,256]{1,0:T(8,128)(2,1)S(1)}, u32[]{:S(2)}, u32[]{:S(2)}) collective-permute-start(bf16[192,256]{1,0:T(8,128)(2,1)S(1)} %get-tuple-element.33), channel_id=1, source_target_pairs={{0,8},{4,12},{8,0},{12,4},{16,24},{20,28},{24,16},{28,20},{1,9},{5... | collective-permute-start | bytes 294920 | tf_op jit(solution)/shard_map/ppermute | solution.py:320
  39.0 1.4 %collective-permute-start.15 = (bf16[192,256]{1,0:T(8,128)(2,1)S(1)}, bf16[192,256]{1,0:T(8,128)(2,1)S(1)}, u32[]{:S(2)}, u32[]{:S(2)}) collective-permute-start(bf16[192,256]{1,0:T(8,128)(2,1)S(1)} %get-tuple-element.37), channel_id=1, source_target_pairs={{0,9},{1,8},{2,11},{3,10},{4,13},{5,12},{6,15},{7,14},{8,1},{9,0},... | collective-permute-start | bytes 294920 | tf_op jit(solution)/shard_map/ppermute | solution.py:327
  40.3 0.5 collective-permute-done.16.refs_6_
  40.9 4.8 %collective-permute-start.17 = (bf16[192,256]{1,0:T(8,128)(2,1)S(1)}, bf16[192,256]{1,0:T(8,128)(2,1)S(1)}, u32[]{:S(2)}, u32[]{:S(2)}) collective-permute-start(bf16[192,256]{1,0:T(8,128)(2,1)S(1)} %forward_other.1), channel_id=1, source_target_pairs={{0,11},{1,10},{2,9},{3,8},{4,15},{5,14},{6,13},{7,12},{8,3},{9,2},... | collective-permute-start | bytes 294920 | tf_op jit(solution)/shard_map/ppermute | solution.py:327
  45.7 1.0 %collective-permute-start.14 = (bf16[192,256]{1,0:T(8,128)(2,1)S(1)}, bf16[192,256]{1,0:T(8,128)(2,1)S(1)}, u32[]{:S(2)}, u32[]{:S(2)}) collective-permute-start(bf16[192,256]{1,0:T(8,128)(2,1)S(1)} %forward_same.1), channel_id=1, source_target_pairs={{0,3},{1,2},{2,1},{3,0},{4,7},{5,6},{6,5},{7,4},{8,11},{9,10},{10,... | collective-permute-start | bytes 294920 | tf_op jit(solution)/shard_map/ppermute | solution.py:320
  46.7 3.7 %input_grad.1 = (bf16[128,1024]{1,0:T(8,128)(2,1)}, f32[8,128]{1,0:T(8,128)S(1)}) custom-call(s32[1]{0:T(128)} %bitcast.refs_0_, s32[1]{0:T(128)} %bitcast.2.refs_1_, s32[1]{0:T(128)} %bitcast.3.refs_2_, s32[1]{0:T(128)} %bitcast.4.refs_3_, s32[1]{0:T(128)} %bitcast.5.refs_4_, bf16[144,3072]{1,0:T(8,128)(2,1)S(1)} %get-tuple-element.26.refs_9_.refs_5_, ...), custom_call_target="tpu_custom_call" | custom-call | flops 905969664 | bytes 9000000 | tf_op jit(solution)/shard_map/input_grad/pallas_call | solution.py:304
  50.5 1.8 %collective-permute-start.19 = (bf16[192,128]{1,0:T(8,128)(2,1)S(1)}, bf16[192,128]{1,0:T(8,128)(2,1)S(1)}, u32[]{:S(2)}, u32[]{:S(2)}) collective-permute-start(bf16[192,128]{1,0:T(8,128)(2,1)S(1)} %get-tuple-element.44), channel_id=1, source_target_pairs={{0,16},{4,20},{8,24},{12,28},{16,0},{20,4},{24,8},{28,12},{1,17},{... | collective-permute-start | bytes 147464 | tf_op jit(solution)/shard_map/ppermute | solution.py:320
  52.3 0.7 %collective-permute-done.14.refs_8_ = bf16[192,256]{1,0:T(8,128)(2,1)S(1)} collective-permute-done((bf16[192,256]{1,0:T(8,128)(2,1)S(1)}, bf16[192,256]{1,0:T(8,128)(2,1)S(1)}, u32[]{:S(2)}, u32[]{:S(2)}) %collective-permute-start.14) | collective-permute-done | bytes 98336 | tf_op jit(solution)/shard_map/ppermute | solution.py:320
  53.0 1.5 %collective-permute-start.18 = (bf16[192,128]{1,0:T(8,128)(2,1)S(1)}, bf16[192,128]{1,0:T(8,128)(2,1)S(1)}, u32[]{:S(2)}, u32[]{:S(2)}) collective-permute-start(bf16[192,128]{1,0:T(8,128)(2,1)S(1)} %get-tuple-element.43), channel_id=1, source_target_pairs={{0,16},{4,20},{8,24},{12,28},{16,0},{20,4},{24,8},{28,12},{1,17},{... | collective-permute-start | bytes 147464 | tf_op jit(solution)/shard_map/ppermute | solution.py:320
  54.7 2.5 %collective-permute-done.18.refs_7_ = bf16[192,128]{1,0:T(8,128)(2,1)S(1)} collective-permute-done((bf16[192,128]{1,0:T(8,128)(2,1)S(1)}, bf16[192,128]{1,0:T(8,128)(2,1)S(1)}, u32[]{:S(2)}, u32[]{:S(2)}) %collective-permute-start.18) | collective-permute-done | bytes 49184 | tf_op jit(solution)/shard_map/ppermute | solution.py:320
  57.1 0.8 %place.1 = f32[6,128,128]{2,1,0:T(8,128)} custom-call(s32[1]{0:T(128)} %bitcast.refs_0_, s32[1]{0:T(128)} %bitcast.2.refs_1_, s32[1]{0:T(128)} %bitcast.3.refs_2_, s32[1]{0:T(128)} %bitcast.4.refs_3_, s32[1]{0:T(128)} %bitcast.5.refs_4_, f32[192,128]{1,0:T(8,128)S(1)} %get-tuple-element.39.refs_5_, f32[192,128]{1,0:T(8,128)S(1)} %get-tuple-element.42.refs_6_, ...), custom_call_target="tpu_custom_call" | custom-call | flops 1000000 | bytes 1000000 | tf_op jit(solution)/shard_map/place/pallas_call | solution.py:304
  (29 shorter events, 1.1 us)
Async XLA Ops:
  0.6 1.2 %copy-start = (f32[9,1024]{1,0:T(8,128)S(1)}, f32[9,1024]{1,0:T(8,128)}, u32[]{:S(2)}) copy-start(f32[9,1024]{1,0:T(8,128)} %param.7) | copy-start | bytes 110596
  2.1 8.0 %collective-permute-start.2 = (bf16[80,1024]{1,0:T(8,128)(2,1)S(1)}, bf16[80,1024]{1,0:T(8,128)(2,1)S(1)}, u32[]{:S(2)}, u32[]{:S(2)}) collective-permute-start(bf16[80,1024]{1,0:T(8,128)(2,1)S(1)} %get-tuple-element.48), channel_id=1, source_target_pairs={{0,28},{4,0},{8,4},{12,8},{16,12},{20,16},{24,20},{28,24},{1,29},{... | collective-permute-start | bytes 491528 | tf_op jit(solution)/shard_map/ppermute | solution.py:356
  5.4 5.1 %collective-permute-start = (bf16[80,1024]{1,0:T(8,128)(2,1)S(1)}, bf16[80,1024]{1,0:T(8,128)(2,1)S(1)}, u32[]{:S(2)}, u32[]{:S(2)}) collective-permute-start(bf16[80,1024]{1,0:T(8,128)(2,1)S(1)} %get-tuple-element.49), channel_id=1, source_target_pairs={{0,4},{4,0},{8,12},{12,8},{16,20},{20,16},{24,28},{28,24},{1,5},{5... | collective-permute-start | bytes 491528 | tf_op jit(solution)/shard_map/ppermute | solution.py:320
  5.4 8.1 %collective-permute-start.1 = (bf16[80,1024]{1,0:T(8,128)(2,1)S(1)}, bf16[80,1024]{1,0:T(8,128)(2,1)S(1)}, u32[]{:S(2)}, u32[]{:S(2)}) collective-permute-start(bf16[80,1024]{1,0:T(8,128)(2,1)S(1)} %get-tuple-element.50), channel_id=1, source_target_pairs={{0,28},{4,8},{8,4},{12,16},{16,12},{20,24},{24,20},{28,0},{1,29},{... | collective-permute-start | bytes 491528 | tf_op jit(solution)/shard_map/ppermute | solution.py:351
  6.2 14.3 %collective-permute-start.5 = (bf16[128,1024]{1,0:T(8,128)(2,1)S(1)}, bf16[128,1024]{1,0:T(8,128)(2,1)S(1)}, u32[]{:S(2)}, u32[]{:S(2)}) collective-permute-start(bf16[128,1024]{1,0:T(8,128)(2,1)S(1)} %slice.35), channel_id=1, source_target_pairs={{0,24},{4,28},{8,16},{12,20},{16,8},{20,12},{24,0},{28,4},{1,25},{... | collective-permute-start | bytes 786440 | tf_op jit(solution)/shard_map/ppermute | solution.py:320
  7.6 16.3 %collective-permute-start.4 = (bf16[128,1024]{1,0:T(8,128)(2,1)S(1)}, bf16[128,1024]{1,0:T(8,128)(2,1)S(1)}, u32[]{:S(2)}, u32[]{:S(2)}) collective-permute-start(bf16[128,1024]{1,0:T(8,128)(2,1)S(1)} %slice.35), channel_id=1, source_target_pairs={{0,16},{4,20},{8,24},{12,28},{16,0},{20,4},{24,8},{28,12},{1,17},{... | collective-permute-start | bytes 786440 | tf_op jit(solution)/shard_map/ppermute | solution.py:320
  10.0 13.8 %collective-permute-start.3 = (bf16[128,1024]{1,0:T(8,128)(2,1)S(1)}, bf16[128,1024]{1,0:T(8,128)(2,1)S(1)}, u32[]{:S(2)}, u32[]{:S(2)}) collective-permute-start(bf16[128,1024]{1,0:T(8,128)(2,1)S(1)} %slice.35), channel_id=1, source_target_pairs={{0,8},{4,12},{8,0},{12,4},{16,24},{20,28},{24,16},{28,20},{1,9},{5... | collective-permute-start | bytes 786440 | tf_op jit(solution)/shard_map/ppermute | solution.py:320
  20.3 8.7 %collective-permute-start.9 = (bf16[128,768]{1,0:T(8,128)(2,1)S(1)}, bf16[128,768]{1,0:T(8,128)(2,1)S(1)}, u32[]{:S(2)}, u32[]{:S(2)}) collective-permute-start(bf16[128,768]{1,0:T(8,128)(2,1)S(1)} %get-tuple-element.45), channel_id=1, source_target_pairs={{0,24},{4,28},{8,16},{12,20},{16,8},{20,12},{24,0},{28,4},{1,25},{... | collective-permute-start | bytes 589832 | tf_op jit(solution)/shard_map/ppermute | solution.py:320
  20.4 11.4 %collective-permute-start.8 = (bf16[128,768]{1,0:T(8,128)(2,1)S(1)}, bf16[128,768]{1,0:T(8,128)(2,1)S(1)}, u32[]{:S(2)}, u32[]{:S(2)}) collective-permute-start(bf16[128,768]{1,0:T(8,128)(2,1)S(1)} %get-tuple-element.46), channel_id=1, source_target_pairs={{0,16},{4,20},{8,24},{12,28},{16,0},{20,4},{24,8},{28,12},{1,17},{... | collective-permute-start | bytes 589832 | tf_op jit(solution)/shard_map/ppermute | solution.py:320
  20.5 11.3 %collective-permute-start.7 = (bf16[128,768]{1,0:T(8,128)(2,1)S(1)}, bf16[128,768]{1,0:T(8,128)(2,1)S(1)}, u32[]{:S(2)}, u32[]{:S(2)}) collective-permute-start(bf16[128,768]{1,0:T(8,128)(2,1)S(1)} %get-tuple-element.47), channel_id=1, source_target_pairs={{0,8},{4,12},{8,0},{12,4},{16,24},{20,28},{24,16},{28,20},{1,9},{5... | collective-permute-start | bytes 589832 | tf_op jit(solution)/shard_map/ppermute | solution.py:320
  23.9 1.4 %collective-permute-start.6 = (bf16[64,1024]{1,0:T(8,128)(2,1)S(1)}, bf16[64,1024]{1,0:T(8,128)(2,1)S(1)}, u32[]{:S(2)}, u32[]{:S(2)}) collective-permute-start(bf16[64,1024]{1,0:T(8,128)(2,1)S(1)} %ends.1), channel_id=1, source_target_pairs={{0,4},{4,0},{8,12},{12,8},{16,20},{20,16},{24,28},{28,24},{1,5},{5... | collective-permute-start | bytes 393224 | tf_op jit(solution)/shard_map/ppermute | solution.py:320
  32.5 2.4 %collective-permute-start.10 = (bf16[768,512]{1,0:T(8,128)(2,1)S(1)}, bf16[768,512]{1,0:T(8,128)(2,1)S(1)}, u32[]{:S(2)}, u32[]{:S(2)}) collective-permute-start(bf16[768,512]{1,0:T(8,128)(2,1)S(1)} %weight_send.1), channel_id=1, source_target_pairs={{0,4},{4,0},{8,12},{12,8},{16,20},{20,16},{24,28},{28,24},{1,5},{5... | collective-permute-start | bytes 2359304 | tf_op jit(solution)/shard_map/ppermute | solution.py:320
  35.2 5.7 %collective-permute-start.16 = (bf16[192,256]{1,0:T(8,128)(2,1)S(1)}, bf16[192,256]{1,0:T(8,128)(2,1)S(1)}, u32[]{:S(2)}, u32[]{:S(2)}) collective-permute-start(bf16[192,256]{1,0:T(8,128)(2,1)S(1)} %get-tuple-element.41), channel_id=1, source_target_pairs={{0,1},{1,0},{2,3},{3,2},{4,5},{5,4},{6,7},{7,6},{8,9},{9,8},{10,11... | collective-permute-start | bytes 294920 | tf_op jit(solution)/shard_map/ppermute | solution.py:320
  36.9 8.8 %collective-permute-start.13 = (bf16[192,256]{1,0:T(8,128)(2,1)S(1)}, bf16[192,256]{1,0:T(8,128)(2,1)S(1)}, u32[]{:S(2)}, u32[]{:S(2)}) collective-permute-start(bf16[192,256]{1,0:T(8,128)(2,1)S(1)} %get-tuple-element.31.refs_9_), channel_id=1, source_target_pairs={{0,1},{1,0},{2,3},{3,2},{4,5},{5,4},{6,7},{7,6},{8,9},{9,8},{10,11... | collective-permute-start | bytes 294920 | tf_op jit(solution)/shard_map/ppermute | solution.py:320
  37.3 13.1 %collective-permute-start.11 = (bf16[192,256]{1,0:T(8,128)(2,1)S(1)}, bf16[192,256]{1,0:T(8,128)(2,1)S(1)}, u32[]{:S(2)}, u32[]{:S(2)}) collective-permute-start(bf16[192,256]{1,0:T(8,128)(2,1)S(1)} %get-tuple-element.33), channel_id=1, source_target_pairs={{0,8},{4,12},{8,0},{12,4},{16,24},{20,28},{24,16},{28,20},{1,9},{5... | collective-permute-start | bytes 294920 | tf_op jit(solution)/shard_map/ppermute | solution.py:320
  39.0 11.5 %collective-permute-start.15 = (bf16[192,256]{1,0:T(8,128)(2,1)S(1)}, bf16[192,256]{1,0:T(8,128)(2,1)S(1)}, u32[]{:S(2)}, u32[]{:S(2)}) collective-permute-start(bf16[192,256]{1,0:T(8,128)(2,1)S(1)} %get-tuple-element.37), channel_id=1, source_target_pairs={{0,9},{1,8},{2,11},{3,10},{4,13},{5,12},{6,15},{7,14},{8,1},{9,0},... | collective-permute-start | bytes 294920 | tf_op jit(solution)/shard_map/ppermute | solution.py:327
  40.9 9.5 %collective-permute-start.17 = (bf16[192,256]{1,0:T(8,128)(2,1)S(1)}, bf16[192,256]{1,0:T(8,128)(2,1)S(1)}, u32[]{:S(2)}, u32[]{:S(2)}) collective-permute-start(bf16[192,256]{1,0:T(8,128)(2,1)S(1)} %forward_other.1), channel_id=1, source_target_pairs={{0,11},{1,10},{2,9},{3,8},{4,15},{5,14},{6,13},{7,12},{8,3},{9,2},... | collective-permute-start | bytes 294920 | tf_op jit(solution)/shard_map/ppermute | solution.py:327
  45.7 6.6 %collective-permute-start.12 = (bf16[192,256]{1,0:T(8,128)(2,1)S(1)}, bf16[192,256]{1,0:T(8,128)(2,1)S(1)}, u32[]{:S(2)}, u32[]{:S(2)}) collective-permute-start(bf16[192,256]{1,0:T(8,128)(2,1)S(1)} %get-tuple-element.35), channel_id=1, source_target_pairs={{0,1},{1,0},{2,3},{3,2},{4,5},{5,4},{6,7},{7,6},{8,9},{9,8},{10,11... | collective-permute-start | bytes 294920 | tf_op jit(solution)/shard_map/ppermute | solution.py:320
  45.7 7.2 %collective-permute-start.14 = (bf16[192,256]{1,0:T(8,128)(2,1)S(1)}, bf16[192,256]{1,0:T(8,128)(2,1)S(1)}, u32[]{:S(2)}, u32[]{:S(2)}) collective-permute-start(bf16[192,256]{1,0:T(8,128)(2,1)S(1)} %forward_same.1), channel_id=1, source_target_pairs={{0,3},{1,2},{2,1},{3,0},{4,7},{5,6},{6,5},{7,4},{8,11},{9,10},{10,... | collective-permute-start | bytes 294920 | tf_op jit(solution)/shard_map/ppermute | solution.py:320
  50.5 4.2 %collective-permute-start.19 = (bf16[192,128]{1,0:T(8,128)(2,1)S(1)}, bf16[192,128]{1,0:T(8,128)(2,1)S(1)}, u32[]{:S(2)}, u32[]{:S(2)}) collective-permute-start(bf16[192,128]{1,0:T(8,128)(2,1)S(1)} %get-tuple-element.44), channel_id=1, source_target_pairs={{0,16},{4,20},{8,24},{12,28},{16,0},{20,4},{24,8},{28,12},{1,17},{... | collective-permute-start | bytes 147464 | tf_op jit(solution)/shard_map/ppermute | solution.py:320
  53.0 4.2 %collective-permute-start.18 = (bf16[192,128]{1,0:T(8,128)(2,1)S(1)}, bf16[192,128]{1,0:T(8,128)(2,1)S(1)}, u32[]{:S(2)}, u32[]{:S(2)}) collective-permute-start(bf16[192,128]{1,0:T(8,128)(2,1)S(1)} %get-tuple-element.43), channel_id=1, source_target_pairs={{0,16},{4,20},{8,24},{12,28},{16,0},{20,4},{24,8},{28,12},{1,17},{... | collective-permute-start | bytes 147464 | tf_op jit(solution)/shard_map/ppermute | solution.py:320

commit v9 on v8

--- a/solution.py
+++ b/solution.py
@@ -60,10 +60,9 @@
     return both.at[:frames], both.at[frames : 2 * frames], both.at[2 * frames :]
 
 
-def project_kernel(place, near, far, both, w, _, own_hidden, conv_out, qkv, w_out, *scratch):
-    frames, width = own_hidden.shape
-    ext, hidden, sems = scratch
-    wide = width
+def own_kernel(place, both, w, _, hidden, conv_out, qkv, w_out, ext, sems):
+    frames, width = ext.shape
+    rows, wide = frames - EDGE, width
     copies = [
         pltpu.make_async_copy(w.at[:, cols], w_out.at[:, cols], sems.at[i])
         for i, cols in enumerate(pl.ds(i * wide, wide) for i in range(3))
@@ -71,25 +70,48 @@
     for copy in copies:
         copy.start()
     own, _, taps = parts_of(both, frames)
+    live = live_rows(place[0], frames, place[1])
+    for col in range(0, width, 128):
+        cols = pl.ds(col, 128)
+        ext[:, cols] = jnp.where(live, own[:, cols], 0.0)
+        conv_hidden(ext, taps, cols, EDGE - KERNEL + 1, rows, hidden, conv_out, (0, rows))
+    for i, copy in enumerate(copies):
+        copy.wait()
+        for col in range(i * wide, (i + 1) * wide, 512):
+            cols = pl.ds(col, 512)
+            qkv[:, cols] = dot(hidden[...], w_out[:, cols], 1, 0).astype(BF16)
+
+
+def rim_kernel(place, near, far, both, w, _, first, conv_out, qkv, ext, hidden):
+    width = w.shape[0]
+    frames = qkv.shape[0] - HALO - EDGE
+    own, _, taps = parts_of(both, frames)
     low_core = place[3] == 0
-    rows, back = frames + 2 * HALO, KERNEL - 1
-    live = live_rows(place[0] - HALO, rows, place[1]) & ~live_rows(place[0] - HALO, rows, 0)
+    head, back = HALO + EDGE, KERNEL - 1
+    rows = head + HALO
+    begin, count = place[0], place[1]
+    live_a = live_rows(begin - HALO, head, count) & ~live_rows(begin - HALO, head, 0)
+    live_b = live_rows(begin + frames - back, HALO + back, count)
     for col in range(0, width, 128):
         cols = pl.ds(col, 128)
         mate, other = near[:, cols].astype(F32), far[:, cols].astype(F32)
-        before, after = jnp.where(low_core, other, mate), jnp.where(low_core, mate, other)
-        raw = jnp.concatenate([before, own[:, cols], after], axis=0)
-        masked = jnp.where(live, raw, 0.0)
+        raw = jnp.concatenate([jnp.where(low_core, other, mate), own[:EDGE, cols]], axis=0)
         ext[:back, cols] = jnp.zeros((back, 128), F32)
-        ext[back:, cols] = masked
-        conv_hidden(ext, taps, cols, 0, rows, hidden, conv_out, (HALO, HALO + frames + EDGE))
-    own_hidden[...] = hidden[HALO : HALO + frames]
-    for i, copy in enumerate(copies):
-        copy.wait()
-        low = HALO if i * wide < width else 0
-        for col in range(i * wide, (i + 1) * wide, 512):
-            cols = pl.ds(col, 512)
-            qkv[low:rows, cols] = dot(hidden[low:], w_out[:, cols], 1, 0).astype(BF16)
+        ext[back : back + head, cols] = jnp.where(live_a, raw, 0.0)
+        conv_hidden(
+            ext, taps, cols, 0, head, hidden.at[:head], conv_out.at[:EDGE], (HALO, head)
+        )
+        after = jnp.where(low_core, mate, other)
+        raw = jnp.concatenate([own[frames - back :, cols], after], axis=0)
+        ext[back + head :, cols] = jnp.where(live_b, raw, 0.0)
+        conv_hidden(
+            ext, taps, cols, back + head, HALO, hidden.at[head:], conv_out.at[EDGE:], (0, EDGE)
+        )
+    first[...] = hidden[HALO:head]
+    for col in range(0, 3 * width, 512):
+        cols = pl.ds(col, 512)
+        low = HALO if col < width else 0
+        qkv[low:rows, cols] = dot(hidden[low:], w[:, cols], 1, 0).astype(BF16)
     qkv[rows:, :] = jnp.zeros((qkv.shape[0] - rows, 3 * width), BF16)
 
 
@@ -121,12 +143,13 @@
             conv_hidden(ext, taps, cols, EDGE - KERNEL + 1, frames, out)
 
 
-def attend_kernel(place, qkv, both, next_cot, attended, grads, sends, later):
+def attend_kernel(place, rim, mid, both, next_cot, attended, grads, sends, later):
     frames, width = attended.shape
     cot = parts_of(both, frames)[1]
     span = frames + HALO
     begin, count, chip = place[0], place[1], place[2]
 
+    head = HALO + EDGE
     skip = (frames - LEFT) // EDGE * EDGE
 
     def mask(start, wanted):
@@ -165,14 +188,19 @@
 
     for first in range(0, HEADS, GROUP):
         heads = []
-        for head in range(first, first + GROUP):
-            q_cols = pl.ds(head * HEAD, HEAD)
-            k_cols = pl.ds(width + head * HEAD, HEAD)
-            v_cols = pl.ds(2 * width + head * HEAD, HEAD)
-            query = qkv[HALO : HALO + frames, q_cols]
-            query_b = qkv[HALO + frames : HALO + 2 * frames, q_cols]
-            key, key_b = qkv[:span, k_cols], qkv[HALO + skip : HALO + span, k_cols]
-            value, value_b = qkv[:span, v_cols], qkv[HALO + skip : HALO + span, v_cols]
+        for index in range(first, first + GROUP):
+            q_cols = pl.ds(index * HEAD, HEAD)
+            k_cols = pl.ds(width + index * HEAD, HEAD)
+            v_cols = pl.ds(2 * width + index * HEAD, HEAD)
+            query = jnp.concatenate([rim[HALO:head, q_cols], mid[:, q_cols]], axis=0)
+            query_b = rim[head:, q_cols]
+            key, value = (
+                jnp.concatenate([rim[:head, cols], mid[:, cols]], axis=0) for cols in (k_cols, v_cols)
+            )
+            key_b, value_b = (
+                jnp.concatenate([mid[skip - EDGE :, cols], rim[head : head + HALO, cols]], axis=0)
+                for cols in (k_cols, v_cols)
+            )
             grad = jnp.where(own_live, cot[:, q_cols], 0.0).astype(BF16)
             grad_b = later[:, q_cols]
             heads.append((q_cols, k_cols, v_cols, query, query_b, key, key_b, value, grad, grad_b, value_b))
@@ -207,11 +235,11 @@
             sends[slot, :, at : at + HEAD] = jnp.concatenate(halves, axis=1)
 
 
-def attend_alone(place, qkv, both, next_cot, attended, grads, later):
-    attend_kernel(place, qkv, both, next_cot, attended, grads, None, later)
-
-
-def input_grad_kernel(place, grads, w, conv, both, *refs):
+def attend_alone(place, rim, mid, both, next_cot, attended, grads, later):
+    attend_kernel(place, rim, mid, both, next_cot, attended, grads, None, later)
+
+
+def input_grad_kernel(place, grads, w, conv_mid, conv_rim, both, *refs):
     grad_in, done, slopes = refs[-3:]
     frames, width = grad_in.shape
     taps = parts_of(both, frames)[2]
@@ -221,7 +249,8 @@
     for col in range(0, width, 256):
         cols = pl.ds(col, 256)
         grad_hidden = dot(grads[...], w[cols, :], 1, 1)
-        value = conv[:, cols]
+        rim = conv_rim[:, cols]
+        value = jnp.concatenate([rim[:EDGE], conv_mid[:, cols], rim[EDGE:]], axis=0)
         logistic = 1.0 / (1.0 + jnp.exp(-value))
         slopes[:, cols] = grad_hidden * (logistic * (1.0 + value * (1.0 - logistic)))
         total = grad_hidden[:frames]
@@ -231,11 +260,12 @@
         grad_in[:, cols] = jnp.where(live, total, 0.0).astype(BF16)
 
 
-def weight_kernel(mine, place, own, peers, b, b1, b2, b3, out):
+def weight_kernel(mine, ys, place, first, mid, peers, b, b1, b2, b3, out):
     parity = place[3] if mine else 1 - place[3]
     left = jnp.concatenate([b[0], b1[...], b2[...], b3[...]], axis=0)
+    chips = [2 * y + x for y in ys for x in range(2)]
     right = jnp.concatenate(
-        [jnp.concatenate([a[:, block(2 * k + parity)] for k in range(4)], axis=1) for a in (own, peers)],
+        [jnp.concatenate([a[:, block(2 * k + parity)] for k in chips], axis=1) for a in (first, mid, peers)],
         axis=0,
     )
     out[...] = dot(left, right, 0, 0).astype(out.dtype)
@@ -249,7 +279,7 @@
     bit = place[2] % 2
     for out, x in ((other, 1 - bit), (same, bit)):
         for y in range(2):
-            out[:, y * HEAD : (y + 1) * HEAD] = value(block(2 * y + x)).astype(out.dtype)
+            out[:, y * HEAD : (y + 1) * HEAD] = value(y, x).astype(out.dtype)
 
 
 def shard_rows(place, mask):
@@ -259,15 +289,14 @@
         yield rows, slice(at, at + size)
 
 
-def core_sum_kernel(place, keep, got, *outs):
+def core_sum_kernel(place, keep, got0, got1, *outs):
     for i, mask in enumerate((2, 3, 1, 0)):
         for rows, at in shard_rows(place, mask):
-            halves(
-                place,
-                lambda cols, rows=rows: keep[rows, cols] + got[rows, cols].astype(F32),
-                outs[2 * i].at[at],
-                outs[2 * i + 1].at[at],
-            )
+
+            def value(y, x, rows=rows):
+                return keep[rows, block(2 * y + x)] + (got0, got1)[y][rows, block(x)].astype(F32)
+
+            halves(place, value, outs[2 * i].at[at], outs[2 * i + 1].at[at])
 
 
 def forward_kernel(place, ahead, got, out):
@@ -343,41 +372,44 @@
         jnp.concatenate([record.astype(F32), cot.astype(F32), kernel], axis=0)
     )
     own = both[:frames].astype(BF16)
-    last, first = own[frames - HALO :], own[:HALO]
+    last, start = own[frames - HALO :], own[:HALO]
     first_cot = both[frames : frames + HALO].astype(BF16)
     low_core = me % 2 == 0
-    edge = jnp.where(low_core, last, first)
+    edge = jnp.where(low_core, last, start)
     near = swap(edge, "tm", 1)
     far = lax.ppermute(
-        jnp.where(low_core, first, last),
+        jnp.where(low_core, start, last),
         "tm",
         [(i, (i + 1 if i % 2 else i - 1) % parts) for i in range(parts)],
     )
     next_cot = lax.ppermute(first_cot, "tm", [(i, (i - 1) % parts) for i in range(parts)])
     if split:
         peers = [swap(own, "tm", mask) for mask in (2, 4, 6)]
-    rows = frames + 2 * HALO
-    hidden, conv, qkv, w_near = call(
-        project_kernel,
-        "project",
-        [
-            ((frames, width), BF16),
-            ((frames + EDGE, width), F32),
-            ((HALO + 2 * frames, 3 * width), BF16),
-            (w_qkv.shape, BF16),
-        ],
+    rows = frames - EDGE
+    mid, conv_mid, qkv_mid, w_near = call(
+        own_kernel,
+        "own_rows",
+        [((rows, width), BF16), ((rows, width), F32), ((rows, 3 * width), BF16), (w_qkv.shape, BF16)],
         place,
-        [near, far, both],
-        [
-            ((rows + KERNEL - 1, width), F32),
-            ((rows, width), BF16),
-            pltpu.SemaphoreType.DMA((3,)),
-        ],
+        [both],
+        [((frames, width), F32), pltpu.SemaphoreType.DMA((3,))],
         flops=rows * width * 3 * width * 2,
         moved=9000000,
         remote=[w_qkv],
+        after=[near],
+        mib=OWN,
+    )
+    rows = 2 * HALO + EDGE
+    first, conv_rim, qkv_rim = call(
+        rim_kernel,
+        "rim_rows",
+        [((EDGE, width), BF16), ((2 * EDGE, width), F32), ((HALO + EDGE + frames, 3 * width), BF16)],
+        place,
+        [near, far, both, w_near],
+        [((rows + 2 * (KERNEL - 1), width), F32), ((rows, width), BF16)],
+        flops=rows * width * 3 * width * 2,
+        moved=9000000,
         after=[next_cot],
-        mib=OWN,
     )
     outs = [((frames, width), BF16), ((frames + EDGE, 3 * width), BF16)]
     attended, grads, *sends = call(
@@ -385,7 +417,7 @@
         "attend",
         outs + [((4, frames, 3 * width // 4), BF16)] * split,
         place,
-        [qkv, both, next_cot],
+        [qkv_rim, qkv_mid, both, next_cot],
         [((frames, width), BF16)],
         mib=16,
         flops=8 * 12 * span * 128 * 128 * 2 * 8,
@@ -411,20 +443,20 @@
             flops=3 * frames * width * 40,
             moved=2000000,
         )
-        operands = [hidden, peers_hidden, sends, *got]
+        operands = [first, mid, peers_hidden, sends, *got]
         whole, half = (shard, width // 2), (shard, 2 * HEAD)
-        send, keep = (
+        send0, send1, keep = (
             call(
-                functools.partial(weight_kernel, mine),
-                "weight_" + ("keep" if mine else "send"),
-                [((cols, width // 2), F32 if mine else BF16)],
+                functools.partial(weight_kernel, mine, ys),
+                "weight_" + name,
+                [((cols, len(ys) * 2 * HEAD), F32 if mine else BF16)],
                 place,
                 operands,
                 mib=20,
                 flops=cols * width * frames * 4,
                 moved=6000000,
             )[0]
-            for mine in (False, True)
+            for name, mine, ys in (("send0", False, (0,)), ("send1", False, (1,)), ("keep", True, (0, 1)))
         )
         low, high = (half, BF16), (half, F32)
         near_same, near_other, *ahead, cross_same, cross_other, own_same, own_other = call(
@@ -432,7 +464,7 @@
             "core_sum",
             [low, low, high, high, low, low, high, low],
             place,
-            [keep, swap(send, "tm", 1)],
+            [keep, swap(send0, "tm", 1), swap(send1, "tm", 1)],
         )
         late = [near_same]
         grad_in, done = call(
@@ -440,7 +472,7 @@
             "input_grad",
             [((frames, width), BF16), ((8, 128), F32)],
             place,
-            [grads, w_near, conv, both],
+            [grads, w_near, conv_mid, conv_rim, both],
             [((frames + EDGE, width), F32)],
             mib=20,
             flops=(frames + EDGE) * width * 3 * width * 2,
@@ -482,13 +514,14 @@
             "input_grad",
             [((frames, width), BF16), ((8, 128), F32)],
             place,
-            [grads, w_near, conv, both],
+            [grads, w_near, conv_mid, conv_rim, both],
             [((frames + EDGE, width), F32)],
             mib=20,
             flops=(frames + EDGE) * width * 3 * width * 2,
             moved=9000000,
             after=late,
         )
+        hidden = jnp.concatenate([first, mid], axis=0)
         partial = dot(hidden, grads[:frames], 0, 0).astype(BF16)
         by_time = lax.psum_scatter(partial, "tm", scatter_dimension=0, tiled=True)
         summed = lax.psum_scatter(by_time, "dp", scatter_dimension=1, tiled=True).astype(F32)

time: 58.1 us -> 58.2 us (level)
  waiting for transfers between devices: 13.9 us -> 10.4 us
  starting transfers between devices: 25.8 us -> 27.6 us
  Pallas kernels: 15.4 us -> 17.2 us
    ppermute x1, waiting for transfers between devices: 3.08 us -> 0.01 us  [on_device(): lax.ppermute(jnp.where(low_core, start, last), 'tm', [(i, (i + 1 if i % 2...]
    pallas_call x13 -> x15, Pallas kernels: 15.4 us -> 17.2 us  [call(): pl.pallas_call(placed, name=name, out_shape=[jax.ShapeDtypeStruct(shape,...]
    ppermute x16 -> x17, starting transfers between devices: 15.5 us -> 17.3 us  [swap(): lax.ppermute(value, axis, [(i, i ^ mask) for i in range(lax.axis_size(axi...]
    ppermute x1, starting transfers between devices: 0.75 us -> 0.07 us  [on_device(): lax.ppermute(jnp.where(low_core, start, last), 'tm', [(i, (i + 1 if i % 2...]
    ppermute x16 -> x17, waiting for transfers between devices: 10.6 us -> 10.3 us  [swap(): lax.ppermute(value, axis, [(i, i ^ mask) for i in range(lax.axis_size(axi...]
  transfers between devices with their start and end apart: 20 -> 21, of which waited for: 10 -> 13; matrix products, arithmetic and copies ran while one was open for 0% -> 0% of each run, Pallas kernels for 24% -> 27%
where the time goes in v9:
time: 58.2 us; the launch traced here: 58 us
  starting transfers between devices  27.6 us (47%)
  Pallas kernels  17.2 us (30%)
  waiting for transfers between devices  10.4 us (18%)
  between operations  1.46 us (3%)
  other arithmetic  1.36 us (2%)
    ppermute x17, starting transfers between devices, swap(): lax.ppermute(value, axis, [(i, i ^ mask) for i in range(lax.axis_size(axi...  17.3 us
    pallas_call x15, Pallas kernels, call(): pl.pallas_call(placed, name=name, out_shape=[jax.ShapeDtypeStruct(shape,...  17.2 us
    ppermute x17, waiting for transfers between devices, swap(): lax.ppermute(value, axis, [(i, i ^ mask) for i in range(lax.axis_size(axi...  10.3 us
    ppermute x2, starting transfers between devices, swap_both(): return lax.ppermute(value, ('tm', 'dp'), pairs)  6.67 us
    ppermute x1, starting transfers between devices, on_device(): lax.ppermute(first_cot, 'tm', [(i, (i - 1) % parts) for i in range(parts)])  3.56 us
    convert_element_type x1, other arithmetic, on_device(): cot.astype(F32)  1.16 us
  transfers between devices with their start and end apart: 21, of which 13 were waited for; matrix products, arithmetic and copies ran while one was open for 0% of the time, Pallas kernels for 27%

profile of v9, /device:TPU:0, one launch (start us, length us, event | category | flops | bytes accessed | tf_op | source)
XLA Modules:
  0.0 58.0 jit_solution(11893479560067339566)
XLA Ops:
  0.7 1.2 %bitcast_convert_fusion = (f32[128,1024]{1,0:T(8,128)S(1)}, f32[128,1024]{1,0:T(8,128)S(1)}) fusion(bf16[1,128,1024]{2,1,0:T(8,128)(2,1)} %param.9, bf16[1,128,1024]{2,1,0:T(8,128)(2,1)} %param.5), kind=kLoop, calls=%fused_computation.1 | loop fusion | flops 262144 | bytes 1572864 | tf_op jit(solution)/shard_map/convert_element_type | solution.py:372
  2.1 0.5 collective-permute-start
  2.6 3.6 %collective-permute-start.2 = (bf16[80,1024]{1,0:T(8,128)(2,1)S(1)}, bf16[80,1024]{1,0:T(8,128)(2,1)S(1)}, u32[]{:S(2)}, u32[]{:S(2)}) collective-permute-start(bf16[80,1024]{1,0:T(8,128)(2,1)S(1)} %get-tuple-element.54), channel_id=1, source_target_pairs={{0,28},{4,0},{8,4},{12,8},{16,12},{20,16},{24,20},{28,24},{1,29},{... | collective-permute-start | bytes 491528 | tf_op jit(solution)/shard_map/ppermute | solution.py:385
  6.2 0.6 %collective-permute-start.5 = (bf16[128,1024]{1,0:T(8,128)(2,1)S(1)}, bf16[128,1024]{1,0:T(8,128)(2,1)S(1)}, u32[]{:S(2)}, u32[]{:S(2)}) collective-permute-start(bf16[128,1024]{1,0:T(8,128)(2,1)S(1)} %slice.35), channel_id=1, source_target_pairs={{0,24},{4,28},{8,16},{12,20},{16,8},{20,12},{24,0},{28,4},{1,25},{... | collective-permute-start | bytes 786440 | tf_op jit(solution)/shard_map/ppermute | solution.py:349
  7.5 3.0 %collective-permute-start.3 = (bf16[128,1024]{1,0:T(8,128)(2,1)S(1)}, bf16[128,1024]{1,0:T(8,128)(2,1)S(1)}, u32[]{:S(2)}, u32[]{:S(2)}) collective-permute-start(bf16[128,1024]{1,0:T(8,128)(2,1)S(1)} %slice.35), channel_id=1, source_target_pairs={{0,8},{4,12},{8,0},{12,4},{16,24},{20,28},{24,16},{28,20},{1,9},{5... | collective-permute-start | bytes 786440 | tf_op jit(solution)/shard_map/ppermute | solution.py:349
  10.5 3.4 %own_rows.1 = (bf16[112,1024]{1,0:T(8,128)(2,1)S(1)}, f32[112,1024]{1,0:T(8,128)S(1)}, bf16[112,3072]{1,0:T(8,128)(2,1)S(1)}, bf16[1024,3072]{1,0:T(8,128)(2,1)S(1)}) custom-call(s32[1]{0:T(128)} %bitcast.refs_0_, s32[1]{0:T(128)} %bitcast.2.refs_1_, s32[1]{0:T(128)} %bitcast.3.refs_2_, s32[1]{0:T(128)} %bitcast.4.refs_3_, s32[1]{0:T(128)} %bitcast.5.refs_4_, ...), custom_call_target="tpu_custom_call" | custom-call | flops 704643072 | bytes 9000000 | tf_op jit(solution)/shard_map/own_rows/pallas_call | solution.py:333
  13.9 2.5 %rim_rows.1 = (bf16[16,1024]{1,0:T(8,128)(2,1)S(1)}, f32[32,1024]{1,0:T(8,128)S(1)}, bf16[224,3072]{1,0:T(8,128)(2,1)S(1)}) custom-call(s32[1]{0:T(128)} %bitcast.refs_0_, s32[1]{0:T(128)} %bitcast.2.refs_1_, s32[1]{0:T(128)} %bitcast.3.refs_2_, s32[1]{0:T(128)} %bitcast.4.refs_3_, s32[1]{0:T(128)} %bitcast.5.refs_4_, ...), custom_call_target="tpu_custom_call" | custom-call | flops 1107296256 | bytes 9000000 | tf_op jit(solution)/shard_map/rim_rows/pallas_call | solution.py:333
  16.4 2.6 %attend.1 = (bf16[128,1024]{1,0:T(8,128)(2,1)}, bf16[144,3072]{1,0:T(8,128)(2,1)S(1)}, bf16[4,128,768]{2,1,0:T(8,128)(2,1)S(1)}) custom-call(s32[1]{0:T(128)} %bitcast.refs_0_, s32[1]{0:T(128)} %bitcast.2.refs_1_, s32[1]{0:T(128)} %bitcast.3.refs_2_, s32[1]{0:T(128)} %bitcast.4.refs_3_, s32[1]{0:T(128)} %bitcast.5.refs_4_, ...), custom_call_target="tpu_custom_call" | custom-call | flops 5234491392 | bytes 5000000 | tf_op jit(solution)/shard_map/attend/pallas_call | solution.py:333
  19.0 0.6 %collective-permute-start.9 = (bf16[128,768]{1,0:T(8,128)(2,1)S(1)}, bf16[128,768]{1,0:T(8,128)(2,1)S(1)}, u32[]{:S(2)}, u32[]{:S(2)}) collective-permute-start(bf16[128,768]{1,0:T(8,128)(2,1)S(1)} %get-tuple-element.51), channel_id=1, source_target_pairs={{0,24},{4,28},{8,16},{12,20},{16,8},{20,12},{24,0},{28,4},{1,25},{... | collective-permute-start | bytes 589832 | tf_op jit(solution)/shard_map/ppermute | solution.py:349
  19.6 0.9 %collective-permute-start.8 = (bf16[128,768]{1,0:T(8,128)(2,1)S(1)}, bf16[128,768]{1,0:T(8,128)(2,1)S(1)}, u32[]{:S(2)}, u32[]{:S(2)}) collective-permute-start(bf16[128,768]{1,0:T(8,128)(2,1)S(1)} %get-tuple-element.52), channel_id=1, source_target_pairs={{0,16},{4,20},{8,24},{12,28},{16,0},{20,4},{24,8},{28,12},{1,17},{... | collective-permute-start | bytes 589832 | tf_op jit(solution)/shard_map/ppermute | solution.py:349
  20.5 2.0 %collective-permute-start.7 = (bf16[128,768]{1,0:T(8,128)(2,1)S(1)}, bf16[128,768]{1,0:T(8,128)(2,1)S(1)}, u32[]{:S(2)}, u32[]{:S(2)}) collective-permute-start(bf16[128,768]{1,0:T(8,128)(2,1)S(1)} %get-tuple-element.53), channel_id=1, source_target_pairs={{0,8},{4,12},{8,0},{12,4},{16,24},{20,28},{24,16},{28,20},{1,9},{5... | collective-permute-start | bytes 589832 | tf_op jit(solution)/shard_map/ppermute | solution.py:349
  22.6 0.6 collective-permute-done.3.refs_6_.refs_5_
  23.2 0.5 collective-permute-start.6
  23.7 1.0 %collective-permute-done.6.refs_8_ = bf16[64,1024]{1,0:T(8,128)(2,1)S(1)} collective-permute-done((bf16[64,1024]{1,0:T(8,128)(2,1)S(1)}, bf16[64,1024]{1,0:T(8,128)(2,1)S(1)}, u32[]{:S(2)}, u32[]{:S(2)}) %collective-permute-start.6) | collective-permute-done | bytes 131104 | tf_op jit(solution)/shard_map/ppermute | solution.py:349
  24.6 2.4 %peer_hidden.1.refs_7_ = bf16[384,1024]{1,0:T(8,128)(2,1)S(1)} custom-call(s32[1]{0:T(128)} %bitcast.refs_0_, s32[1]{0:T(128)} %bitcast.2.refs_1_, s32[1]{0:T(128)} %bitcast.3.refs_2_, s32[1]{0:T(128)} %bitcast.4.refs_3_, s32[1]{0:T(128)} %bitcast.5.refs_4_, bf16[128,1024]{1,0:T(8,128)(2,1)S(1)} %collective-permute-done.3.refs_6_.refs_5_, ...), custom_call_target="tpu_custom_call" | custom-call | flops 15728640 | bytes 2000000 | tf_op jit(solution)/shard_map/peer_hidden/pallas_call | solution.py:333
  27.1 1.8 %collective-permute-done.9.refs_11_ = bf16[128,768]{1,0:T(8,128)(2,1)S(1)} collective-permute-done((bf16[128,768]{1,0:T(8,128)(2,1)S(1)}, bf16[128,768]{1,0:T(8,128)(2,1)S(1)}, u32[]{:S(2)}, u32[]{:S(2)}) %collective-permute-start.9) | collective-permute-done | bytes 196640 | tf_op jit(solution)/shard_map/ppermute | solution.py:349
  28.9 2.3 %collective-permute-done.8.refs_10_ = bf16[128,768]{1,0:T(8,128)(2,1)S(1)} collective-permute-done((bf16[128,768]{1,0:T(8,128)(2,1)S(1)}, bf16[128,768]{1,0:T(8,128)(2,1)S(1)}, u32[]{:S(2)}, u32[]{:S(2)}) %collective-permute-start.8) | collective-permute-done | bytes 196640 | tf_op jit(solution)/shard_map/ppermute | solution.py:349
  31.4 0.4 weight_send0.1
  32.5 0.5 collective-permute-start.11
  32.9 0.6 %weight_keep.1.refs_5_ = f32[768,512]{1,0:T(8,128)S(1)} custom-call(s32[1]{0:T(128)} %bitcast.refs_0_, s32[1]{0:T(128)} %bitcast.2.refs_1_, s32[1]{0:T(128)} %bitcast.3.refs_2_, s32[1]{0:T(128)} %bitcast.4.refs_3_, s32[1]{0:T(128)} %bitcast.5.refs_4_, bf16[16,1024]{1,0:T(8,128)(2,1)S(1)} %get-tuple-element.34.refs_5_, ...), custom_call_target="tpu_custom_call" | custom-call | flops 402653184 | bytes 6000000 | tf_op jit(solution)/shard_map/weight_keep/pallas_call | solution.py:333
  33.7 0.6 %collective-permute-done.11.refs_7_ = bf16[768,256]{1,0:T(8,128)(2,1)S(1)} collective-permute-done((bf16[768,256]{1,0:T(8,128)(2,1)S(1)}, bf16[768,256]{1,0:T(8,128)(2,1)S(1)}, u32[]{:S(2)}, u32[]{:S(2)}) %collective-permute-start.11) | collective-permute-done | bytes 393248 | tf_op jit(solution)/shard_map/ppermute | solution.py:349
  34.6 2.4 %collective-permute-start.17 = (bf16[192,256]{1,0:T(8,128)(2,1)S(1)}, bf16[192,256]{1,0:T(8,128)(2,1)S(1)}, u32[]{:S(2)}, u32[]{:S(2)}) collective-permute-start(bf16[192,256]{1,0:T(8,128)(2,1)S(1)} %get-tuple-element.47), channel_id=1, source_target_pairs={{0,1},{1,0},{2,3},{3,2},{4,5},{5,4},{6,7},{7,6},{8,9},{9,8},{10,11... | collective-permute-start | bytes 294920 | tf_op jit(solution)/shard_map/ppermute | solution.py:349
  37.0 1.8 %collective-permute-start.12 = (bf16[192,256]{1,0:T(8,128)(2,1)S(1)}, bf16[192,256]{1,0:T(8,128)(2,1)S(1)}, u32[]{:S(2)}, u32[]{:S(2)}) collective-permute-start(bf16[192,256]{1,0:T(8,128)(2,1)S(1)} %get-tuple-element.39), channel_id=1, source_target_pairs={{0,8},{4,12},{8,0},{12,4},{16,24},{20,28},{24,16},{28,20},{1,9},{5... | collective-permute-start | bytes 294920 | tf_op jit(solution)/shard_map/ppermute | solution.py:349
  38.8 1.6 %collective-permute-start.16 = (bf16[192,256]{1,0:T(8,128)(2,1)S(1)}, bf16[192,256]{1,0:T(8,128)(2,1)S(1)}, u32[]{:S(2)}, u32[]{:S(2)}) collective-permute-start(bf16[192,256]{1,0:T(8,128)(2,1)S(1)} %get-tuple-element.43), channel_id=1, source_target_pairs={{0,9},{1,8},{2,11},{3,10},{4,13},{5,12},{6,15},{7,14},{8,1},{9,0},... | collective-permute-start | bytes 294920 | tf_op jit(solution)/shard_map/ppermute | solution.py:356
  40.6 5.1 %collective-permute-start.18 = (bf16[192,256]{1,0:T(8,128)(2,1)S(1)}, bf16[192,256]{1,0:T(8,128)(2,1)S(1)}, u32[]{:S(2)}, u32[]{:S(2)}) collective-permute-start(bf16[192,256]{1,0:T(8,128)(2,1)S(1)} %forward_other.1), channel_id=1, source_target_pairs={{0,11},{1,10},{2,9},{3,8},{4,15},{5,14},{6,13},{7,12},{8,3},{9,2},... | collective-permute-start | bytes 294920 | tf_op jit(solution)/shard_map/ppermute | solution.py:356
  45.7 1.1 %collective-permute-start.15 = (bf16[192,256]{1,0:T(8,128)(2,1)S(1)}, bf16[192,256]{1,0:T(8,128)(2,1)S(1)}, u32[]{:S(2)}, u32[]{:S(2)}) collective-permute-start(bf16[192,256]{1,0:T(8,128)(2,1)S(1)} %forward_same.1), channel_id=1, source_target_pairs={{0,3},{1,2},{2,1},{3,0},{4,7},{5,6},{6,5},{7,4},{8,11},{9,10},{10,... | collective-permute-start | bytes 294920 | tf_op jit(solution)/shard_map/ppermute | solution.py:349
  46.8 3.7 %input_grad.1 = (bf16[128,1024]{1,0:T(8,128)(2,1)}, f32[8,128]{1,0:T(8,128)S(1)}) custom-call(s32[1]{0:T(128)} %bitcast.refs_0_, s32[1]{0:T(128)} %bitcast.2.refs_1_, s32[1]{0:T(128)} %bitcast.3.refs_2_, s32[1]{0:T(128)} %bitcast.4.refs_3_, s32[1]{0:T(128)} %bitcast.5.refs_4_, bf16[144,3072]{1,0:T(8,128)(2,1)S(1)} %get-tuple-element.31.refs_9_.refs_5_, ...), custom_call_target="tpu_custom_call" | custom-call | flops 905969664 | bytes 9000000 | tf_op jit(solution)/shard_map/input_grad/pallas_call | solution.py:333
  50.6 1.6 %collective-permute-start.20 = (bf16[192,128]{1,0:T(8,128)(2,1)S(1)}, bf16[192,128]{1,0:T(8,128)(2,1)S(1)}, u32[]{:S(2)}, u32[]{:S(2)}) collective-permute-start(bf16[192,128]{1,0:T(8,128)(2,1)S(1)} %get-tuple-element.50), channel_id=1, source_target_pairs={{0,16},{4,20},{8,24},{12,28},{16,0},{20,4},{24,8},{28,12},{1,17},{... | collective-permute-start | bytes 147464 | tf_op jit(solution)/shard_map/ppermute | solution.py:349
  52.2 0.9 %collective-permute-done.15.refs_8_ = bf16[192,256]{1,0:T(8,128)(2,1)S(1)} collective-permute-done((bf16[192,256]{1,0:T(8,128)(2,1)S(1)}, bf16[192,256]{1,0:T(8,128)(2,1)S(1)}, u32[]{:S(2)}, u32[]{:S(2)}) %collective-permute-start.15) | collective-permute-done | bytes 98336 | tf_op jit(solution)/shard_map/ppermute | solution.py:349
  53.1 1.6 %collective-permute-start.19 = (bf16[192,128]{1,0:T(8,128)(2,1)S(1)}, bf16[192,128]{1,0:T(8,128)(2,1)S(1)}, u32[]{:S(2)}, u32[]{:S(2)}) collective-permute-start(bf16[192,128]{1,0:T(8,128)(2,1)S(1)} %get-tuple-element.49), channel_id=1, source_target_pairs={{0,16},{4,20},{8,24},{12,28},{16,0},{20,4},{24,8},{28,12},{1,17},{... | collective-permute-start | bytes 147464 | tf_op jit(solution)/shard_map/ppermute | solution.py:349
  54.8 2.5 %collective-permute-done.19.refs_7_ = bf16[192,128]{1,0:T(8,128)(2,1)S(1)} collective-permute-done((bf16[192,128]{1,0:T(8,128)(2,1)S(1)}, bf16[192,128]{1,0:T(8,128)(2,1)S(1)}, u32[]{:S(2)}, u32[]{:S(2)}) %collective-permute-start.19) | collective-permute-done | bytes 49184 | tf_op jit(solution)/shard_map/ppermute | solution.py:349
  57.3 0.8 %place.1 = f32[6,128,128]{2,1,0:T(8,128)} custom-call(s32[1]{0:T(128)} %bitcast.refs_0_, s32[1]{0:T(128)} %bitcast.2.refs_1_, s32[1]{0:T(128)} %bitcast.3.refs_2_, s32[1]{0:T(128)} %bitcast.4.refs_3_, s32[1]{0:T(128)} %bitcast.5.refs_4_, f32[192,128]{1,0:T(8,128)S(1)} %get-tuple-element.45.refs_5_, f32[192,128]{1,0:T(8,128)S(1)} %get-tuple-element.48.refs_6_, ...), custom_call_target="tpu_custom_call" | custom-call | flops 1000000 | bytes 1000000 | tf_op jit(solution)/shard_map/place/pallas_call | solution.py:333
  (33 shorter events, 2.2 us)
Async XLA Ops:
  0.6 1.2 %copy-start = (f32[9,1024]{1,0:T(8,128)S(1)}, f32[9,1024]{1,0:T(8,128)}, u32[]{:S(2)}) copy-start(f32[9,1024]{1,0:T(8,128)} %param.7) | copy-start | bytes 110596
  2.1 5.5 %collective-permute-start = (bf16[80,1024]{1,0:T(8,128)(2,1)S(1)}, bf16[80,1024]{1,0:T(8,128)(2,1)S(1)}, u32[]{:S(2)}, u32[]{:S(2)}) collective-permute-start(bf16[80,1024]{1,0:T(8,128)(2,1)S(1)} %get-tuple-element.55), channel_id=1, source_target_pairs={{0,4},{4,0},{8,12},{12,8},{16,20},{20,16},{24,28},{28,24},{1,5},{5... | collective-permute-start | bytes 491528 | tf_op jit(solution)/shard_map/ppermute | solution.py:349
  2.6 11.3 %collective-permute-start.2 = (bf16[80,1024]{1,0:T(8,128)(2,1)S(1)}, bf16[80,1024]{1,0:T(8,128)(2,1)S(1)}, u32[]{:S(2)}, u32[]{:S(2)}) collective-permute-start(bf16[80,1024]{1,0:T(8,128)(2,1)S(1)} %get-tuple-element.54), channel_id=1, source_target_pairs={{0,28},{4,0},{8,4},{12,8},{16,12},{20,16},{24,20},{28,24},{1,29},{... | collective-permute-start | bytes 491528 | tf_op jit(solution)/shard_map/ppermute | solution.py:385
  6.1 7.8 %collective-permute-start.1 = (bf16[80,1024]{1,0:T(8,128)(2,1)S(1)}, bf16[80,1024]{1,0:T(8,128)(2,1)S(1)}, u32[]{:S(2)}, u32[]{:S(2)}) collective-permute-start(bf16[80,1024]{1,0:T(8,128)(2,1)S(1)} %get-tuple-element.56), channel_id=1, source_target_pairs={{0,28},{4,8},{8,4},{12,16},{16,12},{20,24},{24,20},{28,0},{1,29},{... | collective-permute-start | bytes 491528 | tf_op jit(solution)/shard_map/ppermute | solution.py:380
  6.2 14.3 %collective-permute-start.5 = (bf16[128,1024]{1,0:T(8,128)(2,1)S(1)}, bf16[128,1024]{1,0:T(8,128)(2,1)S(1)}, u32[]{:S(2)}, u32[]{:S(2)}) collective-permute-start(bf16[128,1024]{1,0:T(8,128)(2,1)S(1)} %slice.35), channel_id=1, source_target_pairs={{0,24},{4,28},{8,16},{12,20},{16,8},{20,12},{24,0},{28,4},{1,25},{... | collective-permute-start | bytes 786440 | tf_op jit(solution)/shard_map/ppermute | solution.py:349
  6.8 15.8 %collective-permute-start.4 = (bf16[128,1024]{1,0:T(8,128)(2,1)S(1)}, bf16[128,1024]{1,0:T(8,128)(2,1)S(1)}, u32[]{:S(2)}, u32[]{:S(2)}) collective-permute-start(bf16[128,1024]{1,0:T(8,128)(2,1)S(1)} %slice.35), channel_id=1, source_target_pairs={{0,16},{4,20},{8,24},{12,28},{16,0},{20,4},{24,8},{28,12},{1,17},{... | collective-permute-start | bytes 786440 | tf_op jit(solution)/shard_map/ppermute | solution.py:349
  7.5 15.6 %collective-permute-start.3 = (bf16[128,1024]{1,0:T(8,128)(2,1)S(1)}, bf16[128,1024]{1,0:T(8,128)(2,1)S(1)}, u32[]{:S(2)}, u32[]{:S(2)}) collective-permute-start(bf16[128,1024]{1,0:T(8,128)(2,1)S(1)} %slice.35), channel_id=1, source_target_pairs={{0,8},{4,12},{8,0},{12,4},{16,24},{20,28},{24,16},{28,20},{1,9},{5... | collective-permute-start | bytes 786440 | tf_op jit(solution)/shard_map/ppermute | solution.py:349
  19.0 10.0 %collective-permute-start.9 = (bf16[128,768]{1,0:T(8,128)(2,1)S(1)}, bf16[128,768]{1,0:T(8,128)(2,1)S(1)}, u32[]{:S(2)}, u32[]{:S(2)}) collective-permute-start(bf16[128,768]{1,0:T(8,128)(2,1)S(1)} %get-tuple-element.51), channel_id=1, source_target_pairs={{0,24},{4,28},{8,16},{12,20},{16,8},{20,12},{24,0},{28,4},{1,25},{... | collective-permute-start | bytes 589832 | tf_op jit(solution)/shard_map/ppermute | solution.py:349
  19.6 11.6 %collective-permute-start.8 = (bf16[128,768]{1,0:T(8,128)(2,1)S(1)}, bf16[128,768]{1,0:T(8,128)(2,1)S(1)}, u32[]{:S(2)}, u32[]{:S(2)}) collective-permute-start(bf16[128,768]{1,0:T(8,128)(2,1)S(1)} %get-tuple-element.52), channel_id=1, source_target_pairs={{0,16},{4,20},{8,24},{12,28},{16,0},{20,4},{24,8},{28,12},{1,17},{... | collective-permute-start | bytes 589832 | tf_op jit(solution)/shard_map/ppermute | solution.py:349
  20.5 10.9 %collective-permute-start.7 = (bf16[128,768]{1,0:T(8,128)(2,1)S(1)}, bf16[128,768]{1,0:T(8,128)(2,1)S(1)}, u32[]{:S(2)}, u32[]{:S(2)}) collective-permute-start(bf16[128,768]{1,0:T(8,128)(2,1)S(1)} %get-tuple-element.53), channel_id=1, source_target_pairs={{0,8},{4,12},{8,0},{12,4},{16,24},{20,28},{24,16},{28,20},{1,9},{5... | collective-permute-start | bytes 589832 | tf_op jit(solution)/shard_map/ppermute | solution.py:349
  23.2 1.5 %collective-permute-start.6 = (bf16[64,1024]{1,0:T(8,128)(2,1)S(1)}, bf16[64,1024]{1,0:T(8,128)(2,1)S(1)}, u32[]{:S(2)}, u32[]{:S(2)}) collective-permute-start(bf16[64,1024]{1,0:T(8,128)(2,1)S(1)} %ends.1), channel_id=1, source_target_pairs={{0,4},{4,0},{8,12},{12,8},{16,20},{20,16},{24,28},{28,24},{1,5},{5... | collective-permute-start | bytes 393224 | tf_op jit(solution)/shard_map/ppermute | solution.py:349
  31.9 1.8 %collective-permute-start.10 = (bf16[768,256]{1,0:T(8,128)(2,1)S(1)}, bf16[768,256]{1,0:T(8,128)(2,1)S(1)}, u32[]{:S(2)}, u32[]{:S(2)}) collective-permute-start(bf16[768,256]{1,0:T(8,128)(2,1)S(1)} %weight_send0.1), channel_id=1, source_target_pairs={{0,4},{4,0},{8,12},{12,8},{16,20},{20,16},{24,28},{28,24},{1,5},{5... | collective-permute-start | bytes 1179656 | tf_op jit(solution)/shard_map/ppermute | solution.py:349
  32.5 1.8 %collective-permute-start.11 = (bf16[768,256]{1,0:T(8,128)(2,1)S(1)}, bf16[768,256]{1,0:T(8,128)(2,1)S(1)}, u32[]{:S(2)}, u32[]{:S(2)}) collective-permute-start(bf16[768,256]{1,0:T(8,128)(2,1)S(1)} %weight_send1.1), channel_id=1, source_target_pairs={{0,4},{4,0},{8,12},{12,8},{16,20},{20,16},{24,28},{28,24},{1,5},{5... | collective-permute-start | bytes 1179656 | tf_op jit(solution)/shard_map/ppermute | solution.py:349
  34.6 6.0 %collective-permute-start.17 = (bf16[192,256]{1,0:T(8,128)(2,1)S(1)}, bf16[192,256]{1,0:T(8,128)(2,1)S(1)}, u32[]{:S(2)}, u32[]{:S(2)}) collective-permute-start(bf16[192,256]{1,0:T(8,128)(2,1)S(1)} %get-tuple-element.47), channel_id=1, source_target_pairs={{0,1},{1,0},{2,3},{3,2},{4,5},{5,4},{6,7},{7,6},{8,9},{9,8},{10,11... | collective-permute-start | bytes 294920 | tf_op jit(solution)/shard_map/ppermute | solution.py:349
  36.9 8.7 %collective-permute-start.14 = (bf16[192,256]{1,0:T(8,128)(2,1)S(1)}, bf16[192,256]{1,0:T(8,128)(2,1)S(1)}, u32[]{:S(2)}, u32[]{:S(2)}) collective-permute-start(bf16[192,256]{1,0:T(8,128)(2,1)S(1)} %get-tuple-element.37.refs_10_), channel_id=1, source_target_pairs={{0,1},{1,0},{2,3},{3,2},{4,5},{5,4},{6,7},{7,6},{8,9},{9,8},{10,11... | collective-permute-start | bytes 294920 | tf_op jit(solution)/shard_map/ppermute | solution.py:349
  37.0 13.5 %collective-permute-start.12 = (bf16[192,256]{1,0:T(8,128)(2,1)S(1)}, bf16[192,256]{1,0:T(8,128)(2,1)S(1)}, u32[]{:S(2)}, u32[]{:S(2)}) collective-permute-start(bf16[192,256]{1,0:T(8,128)(2,1)S(1)} %get-tuple-element.39), channel_id=1, source_target_pairs={{0,8},{4,12},{8,0},{12,4},{16,24},{20,28},{24,16},{28,20},{1,9},{5... | collective-permute-start | bytes 294920 | tf_op jit(solution)/shard_map/ppermute | solution.py:349
  38.8 11.7 %collective-permute-start.16 = (bf16[192,256]{1,0:T(8,128)(2,1)S(1)}, bf16[192,256]{1,0:T(8,128)(2,1)S(1)}, u32[]{:S(2)}, u32[]{:S(2)}) collective-permute-start(bf16[192,256]{1,0:T(8,128)(2,1)S(1)} %get-tuple-element.43), channel_id=1, source_target_pairs={{0,9},{1,8},{2,11},{3,10},{4,13},{5,12},{6,15},{7,14},{8,1},{9,0},... | collective-permute-start | bytes 294920 | tf_op jit(solution)/shard_map/ppermute | solution.py:356
  40.6 10.0 %collective-permute-start.18 = (bf16[192,256]{1,0:T(8,128)(2,1)S(1)}, bf16[192,256]{1,0:T(8,128)(2,1)S(1)}, u32[]{:S(2)}, u32[]{:S(2)}) collective-permute-start(bf16[192,256]{1,0:T(8,128)(2,1)S(1)} %forward_other.1), channel_id=1, source_target_pairs={{0,11},{1,10},{2,9},{3,8},{4,15},{5,14},{6,13},{7,12},{8,3},{9,2},... | collective-permute-start | bytes 294920 | tf_op jit(solution)/shard_map/ppermute | solution.py:356
  45.7 6.5 %collective-permute-start.13 = (bf16[192,256]{1,0:T(8,128)(2,1)S(1)}, bf16[192,256]{1,0:T(8,128)(2,1)S(1)}, u32[]{:S(2)}, u32[]{:S(2)}) collective-permute-start(bf16[192,256]{1,0:T(8,128)(2,1)S(1)} %get-tuple-element.41), channel_id=1, source_target_pairs={{0,1},{1,0},{2,3},{3,2},{4,5},{5,4},{6,7},{7,6},{8,9},{9,8},{10,11... | collective-permute-start | bytes 294920 | tf_op jit(solution)/shard_map/ppermute | solution.py:349
  45.7 7.4 %collective-permute-start.15 = (bf16[192,256]{1,0:T(8,128)(2,1)S(1)}, bf16[192,256]{1,0:T(8,128)(2,1)S(1)}, u32[]{:S(2)}, u32[]{:S(2)}) collective-permute-start(bf16[192,256]{1,0:T(8,128)(2,1)S(1)} %forward_same.1), channel_id=1, source_target_pairs={{0,3},{1,2},{2,1},{3,0},{4,7},{5,6},{6,5},{7,4},{8,11},{9,10},{10,... | collective-permute-start | bytes 294920 | tf_op jit(solution)/shard_map/ppermute | solution.py:349
  50.6 4.2 %collective-permute-start.20 = (bf16[192,128]{1,0:T(8,128)(2,1)S(1)}, bf16[192,128]{1,0:T(8,128)(2,1)S(1)}, u32[]{:S(2)}, u32[]{:S(2)}) collective-permute-start(bf16[192,128]{1,0:T(8,128)(2,1)S(1)} %get-tuple-element.50), channel_id=1, source_target_pairs={{0,16},{4,20},{8,24},{12,28},{16,0},{20,4},{24,8},{28,12},{1,17},{... | collective-permute-start | bytes 147464 | tf_op jit(solution)/shard_map/ppermute | solution.py:349
  53.1 4.2 %collective-permute-start.19 = (bf16[192,128]{1,0:T(8,128)(2,1)S(1)}, bf16[192,128]{1,0:T(8,128)(2,1)S(1)}, u32[]{:S(2)}, u32[]{:S(2)}) collective-permute-start(bf16[192,128]{1,0:T(8,128)(2,1)S(1)} %get-tuple-element.49), channel_id=1, source_target_pairs={{0,16},{4,20},{8,24},{12,28},{16,0},{20,4},{24,8},{28,12},{1,17},{... | collective-permute-start | bytes 147464 | tf_op jit(solution)/shard_map/ppermute | solution.py:349

commit v10 on v8

--- a/solution.py
+++ b/solution.py
@@ -231,11 +231,12 @@
         grad_in[:, cols] = jnp.where(live, total, 0.0).astype(BF16)
 
 
-def weight_kernel(mine, place, own, peers, b, b1, b2, b3, out):
+def weight_kernel(mine, ys, place, own, peers, b, b1, b2, b3, out):
     parity = place[3] if mine else 1 - place[3]
     left = jnp.concatenate([b[0], b1[...], b2[...], b3[...]], axis=0)
+    chips = [2 * y + x for y in ys for x in range(2)]
     right = jnp.concatenate(
-        [jnp.concatenate([a[:, block(2 * k + parity)] for k in range(4)], axis=1) for a in (own, peers)],
+        [jnp.concatenate([a[:, block(2 * k + parity)] for k in chips], axis=1) for a in (own, peers)],
         axis=0,
     )
     out[...] = dot(left, right, 0, 0).astype(out.dtype)
@@ -249,7 +250,7 @@
     bit = place[2] % 2
     for out, x in ((other, 1 - bit), (same, bit)):
         for y in range(2):
-            out[:, y * HEAD : (y + 1) * HEAD] = value(block(2 * y + x)).astype(out.dtype)
+            out[:, y * HEAD : (y + 1) * HEAD] = value(y, x).astype(out.dtype)
 
 
 def shard_rows(place, mask):
@@ -259,15 +260,14 @@
         yield rows, slice(at, at + size)
 
 
-def core_sum_kernel(place, keep, got, *outs):
+def core_sum_kernel(place, keep, got0, got1, *outs):
     for i, mask in enumerate((2, 3, 1, 0)):
         for rows, at in shard_rows(place, mask):
-            halves(
-                place,
-                lambda cols, rows=rows: keep[rows, cols] + got[rows, cols].astype(F32),
-                outs[2 * i].at[at],
-                outs[2 * i + 1].at[at],
-            )
+
+            def value(y, x, rows=rows):
+                return keep[rows, block(2 * y + x)] + (got0, got1)[y][rows, block(x)].astype(F32)
+
+            halves(place, value, outs[2 * i].at[at], outs[2 * i + 1].at[at])
 
 
 def forward_kernel(place, ahead, got, out):
@@ -413,18 +413,18 @@
         )
         operands = [hidden, peers_hidden, sends, *got]
         whole, half = (shard, width // 2), (shard, 2 * HEAD)
-        send, keep = (
+        send0, send1, keep = (
             call(
-                functools.partial(weight_kernel, mine),
-                "weight_" + ("keep" if mine else "send"),
-                [((cols, width // 2), F32 if mine else BF16)],
+                functools.partial(weight_kernel, mine, ys),
+                "weight_" + name,
+                [((cols, len(ys) * 2 * HEAD), F32 if mine else BF16)],
                 place,
                 operands,
                 mib=20,
                 flops=cols * width * frames * 4,
                 moved=6000000,
             )[0]
-            for mine in (False, True)
+            for name, mine, ys in (("send0", False, (0,)), ("send1", False, (1,)), ("keep", True, (0, 1)))
         )
         low, high = (half, BF16), (half, F32)
         near_same, near_other, *ahead, cross_same, cross_other, own_same, own_other = call(
@@ -432,7 +432,7 @@
             "core_sum",
             [low, low, high, high, low, low, high, low],
             place,
-            [keep, swap(send, "tm", 1)],
+            [keep, swap(send0, "tm", 1), swap(send1, "tm", 1)],
         )
         late = [near_same]
         grad_in, done = call(

time: 58.1 us -> 57.9 us (level)
  waiting for transfers between devices: 13.9 us -> 13.3 us
    ppermute x16 -> x17, waiting for transfers between devices: 10.6 us -> 9.91 us  [swap(): lax.ppermute(value, axis, [(i, i ^ mask) for i in range(lax.axis_size(axi...]
    ppermute x16 -> x17, starting transfers between devices: 15.5 us -> 15.8 us  [swap(): lax.ppermute(value, axis, [(i, i ^ mask) for i in range(lax.axis_size(axi...]
    pallas_call x13 -> x14, Pallas kernels: 15.4 us -> 15.5 us  [call(): pl.pallas_call(placed, name=name, out_shape=[jax.ShapeDtypeStruct(shape,...]
  transfers between devices with their start and end apart: 20 -> 21, of which waited for: 10 -> 12; matrix products, arithmetic and copies ran while one was open for 0% -> 0% of each run, Pallas kernels for 24% -> 24%
where the time goes in v10:
time: 57.9 us; the launch traced here: 57.8 us
  starting transfers between devices  26 us (45%)
  Pallas kernels  15.5 us (27%)
  waiting for transfers between devices  13.3 us (23%)
  between operations  1.45 us (3%)
  other arithmetic  1.36 us (2%)
    ppermute x17, starting transfers between devices, swap(): lax.ppermute(value, axis, [(i, i ^ mask) for i in range(lax.axis_size(axi...  15.8 us
    pallas_call x14, Pallas kernels, call(): pl.pallas_call(placed, name=name, out_shape=[jax.ShapeDtypeStruct(shape,...  15.5 us
    ppermute x17, waiting for transfers between devices, swap(): lax.ppermute(value, axis, [(i, i ^ mask) for i in range(lax.axis_size(axi...  9.91 us
    ppermute x2, starting transfers between devices, swap_both(): return lax.ppermute(value, ('tm', 'dp'), pairs)  6.13 us
    ppermute x1, starting transfers between devices, on_device(): lax.ppermute(first_cot, 'tm', [(i, (i - 1) % parts) for i in range(parts)])  3.39 us
    ppermute x1, waiting for transfers between devices, on_device(): lax.ppermute(jnp.where(low_core, first, last), 'tm', [(i, (i + 1 if i % 2...  3.08 us
    convert_element_type x1, other arithmetic, on_device(): cot.astype(F32)  1.16 us
  transfers between devices with their start and end apart: 21, of which 12 were waited for; matrix products, arithmetic and copies ran while one was open for 0% of the time, Pallas kernels for 24%

profile of v10, /device:TPU:0, one launch (start us, length us, event | category | flops | bytes accessed | tf_op | source)
XLA Modules:
  0.0 57.8 jit_solution(1778194650735869975)
XLA Ops:
  0.7 1.2 %bitcast_convert_fusion = (f32[128,1024]{1,0:T(8,128)S(1)}, f32[128,1024]{1,0:T(8,128)S(1)}) fusion(bf16[1,128,1024]{2,1,0:T(8,128)(2,1)} %param.9, bf16[1,128,1024]{2,1,0:T(8,128)(2,1)} %param.5), kind=kLoop, calls=%fused_computation.1 | loop fusion | flops 262144 | bytes 1572864 | tf_op jit(solution)/shard_map/convert_element_type | solution.py:343
  2.1 3.4 %collective-permute-start.2 = (bf16[80,1024]{1,0:T(8,128)(2,1)S(1)}, bf16[80,1024]{1,0:T(8,128)(2,1)S(1)}, u32[]{:S(2)}, u32[]{:S(2)}) collective-permute-start(bf16[80,1024]{1,0:T(8,128)(2,1)S(1)} %get-tuple-element.48), channel_id=1, source_target_pairs={{0,28},{4,0},{8,4},{12,8},{16,12},{20,16},{24,20},{28,24},{1,29},{... | collective-permute-start | bytes 491528 | tf_op jit(solution)/shard_map/ppermute | solution.py:356
  5.4 0.8 %collective-permute-start.1 = (bf16[80,1024]{1,0:T(8,128)(2,1)S(1)}, bf16[80,1024]{1,0:T(8,128)(2,1)S(1)}, u32[]{:S(2)}, u32[]{:S(2)}) collective-permute-start(bf16[80,1024]{1,0:T(8,128)(2,1)S(1)} %get-tuple-element.50), channel_id=1, source_target_pairs={{0,28},{4,8},{8,4},{12,16},{16,12},{20,24},{24,20},{28,0},{1,29},{... | collective-permute-start | bytes 491528 | tf_op jit(solution)/shard_map/ppermute | solution.py:351
  6.2 1.4 %collective-permute-start.5 = (bf16[128,1024]{1,0:T(8,128)(2,1)S(1)}, bf16[128,1024]{1,0:T(8,128)(2,1)S(1)}, u32[]{:S(2)}, u32[]{:S(2)}) collective-permute-start(bf16[128,1024]{1,0:T(8,128)(2,1)S(1)} %slice.35), channel_id=1, source_target_pairs={{0,24},{4,28},{8,16},{12,20},{16,8},{20,12},{24,0},{28,4},{1,25},{... | collective-permute-start | bytes 786440 | tf_op jit(solution)/shard_map/ppermute | solution.py:320
  7.6 1.5 %collective-permute-start.4 = (bf16[128,1024]{1,0:T(8,128)(2,1)S(1)}, bf16[128,1024]{1,0:T(8,128)(2,1)S(1)}, u32[]{:S(2)}, u32[]{:S(2)}) collective-permute-start(bf16[128,1024]{1,0:T(8,128)(2,1)S(1)} %slice.35), channel_id=1, source_target_pairs={{0,16},{4,20},{8,24},{12,28},{16,0},{20,4},{24,8},{28,12},{1,17},{... | collective-permute-start | bytes 786440 | tf_op jit(solution)/shard_map/ppermute | solution.py:320
  10.0 0.5 collective-permute-start.3
  10.5 3.1 %collective-permute-done.1.refs_6_ = bf16[80,1024]{1,0:T(8,128)(2,1)S(1)} collective-permute-done((bf16[80,1024]{1,0:T(8,128)(2,1)S(1)}, bf16[80,1024]{1,0:T(8,128)(2,1)S(1)}, u32[]{:S(2)}, u32[]{:S(2)}) %collective-permute-start.1) | collective-permute-done | bytes 163872 | tf_op jit(solution)/shard_map/ppermute | solution.py:351
  13.6 4.1 %project.1 = (bf16[128,1024]{1,0:T(8,128)(2,1)S(1)}, f32[144,1024]{1,0:T(8,128)S(1)}, bf16[336,3072]{1,0:T(8,128)(2,1)S(1)}, bf16[1024,3072]{1,0:T(8,128)(2,1)S(1)}) custom-call(s32[1]{0:T(128)} %bitcast.refs_0_, s32[1]{0:T(128)} %bitcast.2.refs_1_, s32[1]{0:T(128)} %bitcast.3.refs_2_, s32[1]{0:T(128)} %bitcast.4.refs_3_, s32[1]{0:T(128)} %bitcast.5.refs_4_, ...), custom_call_target="tpu_custom_call" | custom-call | flops 1811939328 | bytes 9000000 | tf_op jit(solution)/shard_map/project/pallas_call | solution.py:304
  17.7 2.6 %attend.1 = (bf16[128,1024]{1,0:T(8,128)(2,1)}, bf16[144,3072]{1,0:T(8,128)(2,1)S(1)}, bf16[4,128,768]{2,1,0:T(8,128)(2,1)S(1)}) custom-call(s32[1]{0:T(128)} %bitcast.refs_0_, s32[1]{0:T(128)} %bitcast.2.refs_1_, s32[1]{0:T(128)} %bitcast.3.refs_2_, s32[1]{0:T(128)} %bitcast.4.refs_3_, s32[1]{0:T(128)} %bitcast.5.refs_4_, ...), custom_call_target="tpu_custom_call" | custom-call | flops 5234491392 | bytes 5000000 | tf_op jit(solution)/shard_map/attend/pallas_call | solution.py:304
  20.5 3.4 %collective-permute-start.7 = (bf16[128,768]{1,0:T(8,128)(2,1)S(1)}, bf16[128,768]{1,0:T(8,128)(2,1)S(1)}, u32[]{:S(2)}, u32[]{:S(2)}) collective-permute-start(bf16[128,768]{1,0:T(8,128)(2,1)S(1)} %get-tuple-element.47), channel_id=1, source_target_pairs={{0,8},{4,12},{8,0},{12,4},{16,24},{20,28},{24,16},{28,20},{1,9},{5... | collective-permute-start | bytes 589832 | tf_op jit(solution)/shard_map/ppermute | solution.py:320
  24.0 1.3 %collective-permute-done.6.refs_8_ = bf16[64,1024]{1,0:T(8,128)(2,1)S(1)} collective-permute-done((bf16[64,1024]{1,0:T(8,128)(2,1)S(1)}, bf16[64,1024]{1,0:T(8,128)(2,1)S(1)}, u32[]{:S(2)}, u32[]{:S(2)}) %collective-permute-start.6) | collective-permute-done | bytes 131104 | tf_op jit(solution)/shard_map/ppermute | solution.py:320
  25.3 2.4 %peer_hidden.1.refs_6_ = bf16[384,1024]{1,0:T(8,128)(2,1)S(1)} custom-call(s32[1]{0:T(128)} %bitcast.refs_0_, s32[1]{0:T(128)} %bitcast.2.refs_1_, s32[1]{0:T(128)} %bitcast.3.refs_2_, s32[1]{0:T(128)} %bitcast.4.refs_3_, s32[1]{0:T(128)} %bitcast.5.refs_4_, bf16[128,1024]{1,0:T(8,128)(2,1)S(1)} %collective-permute-done.3.refs_6_.refs_5_, ...), custom_call_target="tpu_custom_call" | custom-call | flops 15728640 | bytes 2000000 | tf_op jit(solution)/shard_map/peer_hidden/pallas_call | solution.py:304
  27.7 1.3 %collective-permute-done.9.refs_10_ = bf16[128,768]{1,0:T(8,128)(2,1)S(1)} collective-permute-done((bf16[128,768]{1,0:T(8,128)(2,1)S(1)}, bf16[128,768]{1,0:T(8,128)(2,1)S(1)}, u32[]{:S(2)}, u32[]{:S(2)}) %collective-permute-start.9) | collective-permute-done | bytes 196640 | tf_op jit(solution)/shard_map/ppermute | solution.py:320
  29.0 2.8 %collective-permute-done.8.refs_9_ = bf16[128,768]{1,0:T(8,128)(2,1)S(1)} collective-permute-done((bf16[128,768]{1,0:T(8,128)(2,1)S(1)}, bf16[128,768]{1,0:T(8,128)(2,1)S(1)}, u32[]{:S(2)}, u32[]{:S(2)}) %collective-permute-start.8) | collective-permute-done | bytes 196640 | tf_op jit(solution)/shard_map/ppermute | solution.py:320
  32.2 0.5 collective-permute-start.10
  32.8 0.4 weight_send1.1
  33.3 0.6 %weight_keep.1.refs_5_ = f32[768,512]{1,0:T(8,128)S(1)} custom-call(s32[1]{0:T(128)} %bitcast.refs_0_, s32[1]{0:T(128)} %bitcast.2.refs_1_, s32[1]{0:T(128)} %bitcast.3.refs_2_, s32[1]{0:T(128)} %bitcast.4.refs_3_, s32[1]{0:T(128)} %bitcast.5.refs_4_, bf16[128,1024]{1,0:T(8,128)(2,1)S(1)} %get-tuple-element.29.refs_5_, ...), custom_call_target="tpu_custom_call" | custom-call | flops 402653184 | bytes 6000000 | tf_op jit(solution)/shard_map/weight_keep/pallas_call | solution.py:304
  34.1 0.9 %collective-permute-done.11.refs_7_ = bf16[768,256]{1,0:T(8,128)(2,1)S(1)} collective-permute-done((bf16[768,256]{1,0:T(8,128)(2,1)S(1)}, bf16[768,256]{1,0:T(8,128)(2,1)S(1)}, u32[]{:S(2)}, u32[]{:S(2)}) %collective-permute-start.11) | collective-permute-done | bytes 393248 | tf_op jit(solution)/shard_map/ppermute | solution.py:320
  35.3 1.7 %collective-permute-start.17 = (bf16[192,256]{1,0:T(8,128)(2,1)S(1)}, bf16[192,256]{1,0:T(8,128)(2,1)S(1)}, u32[]{:S(2)}, u32[]{:S(2)}) collective-permute-start(bf16[192,256]{1,0:T(8,128)(2,1)S(1)} %get-tuple-element.41), channel_id=1, source_target_pairs={{0,1},{1,0},{2,3},{3,2},{4,5},{5,4},{6,7},{7,6},{8,9},{9,8},{10,11... | collective-permute-start | bytes 294920 | tf_op jit(solution)/shard_map/ppermute | solution.py:320
  36.9 0.4 collective-permute-start.14
  37.4 1.5 %collective-permute-start.12 = (bf16[192,256]{1,0:T(8,128)(2,1)S(1)}, bf16[192,256]{1,0:T(8,128)(2,1)S(1)}, u32[]{:S(2)}, u32[]{:S(2)}) collective-permute-start(bf16[192,256]{1,0:T(8,128)(2,1)S(1)} %get-tuple-element.33), channel_id=1, source_target_pairs={{0,8},{4,12},{8,0},{12,4},{16,24},{20,28},{24,16},{28,20},{1,9},{5... | collective-permute-start | bytes 294920 | tf_op jit(solution)/shard_map/ppermute | solution.py:320
  38.8 1.6 %collective-permute-start.16 = (bf16[192,256]{1,0:T(8,128)(2,1)S(1)}, bf16[192,256]{1,0:T(8,128)(2,1)S(1)}, u32[]{:S(2)}, u32[]{:S(2)}) collective-permute-start(bf16[192,256]{1,0:T(8,128)(2,1)S(1)} %get-tuple-element.37), channel_id=1, source_target_pairs={{0,9},{1,8},{2,11},{3,10},{4,13},{5,12},{6,15},{7,14},{8,1},{9,0},... | collective-permute-start | bytes 294920 | tf_op jit(solution)/shard_map/ppermute | solution.py:327
  40.4 0.6 collective-permute-done.17.refs_6_
  41.0 4.5 %collective-permute-start.18 = (bf16[192,256]{1,0:T(8,128)(2,1)S(1)}, bf16[192,256]{1,0:T(8,128)(2,1)S(1)}, u32[]{:S(2)}, u32[]{:S(2)}) collective-permute-start(bf16[192,256]{1,0:T(8,128)(2,1)S(1)} %forward_other.1), channel_id=1, source_target_pairs={{0,11},{1,10},{2,9},{3,8},{4,15},{5,14},{6,13},{7,12},{8,3},{9,2},... | collective-permute-start | bytes 294920 | tf_op jit(solution)/shard_map/ppermute | solution.py:327
  45.5 1.2 %collective-permute-start.15 = (bf16[192,256]{1,0:T(8,128)(2,1)S(1)}, bf16[192,256]{1,0:T(8,128)(2,1)S(1)}, u32[]{:S(2)}, u32[]{:S(2)}) collective-permute-start(bf16[192,256]{1,0:T(8,128)(2,1)S(1)} %forward_same.1), channel_id=1, source_target_pairs={{0,3},{1,2},{2,1},{3,0},{4,7},{5,6},{6,5},{7,4},{8,11},{9,10},{10,... | collective-permute-start | bytes 294920 | tf_op jit(solution)/shard_map/ppermute | solution.py:320
  46.8 3.7 %input_grad.1 = (bf16[128,1024]{1,0:T(8,128)(2,1)}, f32[8,128]{1,0:T(8,128)S(1)}) custom-call(s32[1]{0:T(128)} %bitcast.refs_0_, s32[1]{0:T(128)} %bitcast.2.refs_1_, s32[1]{0:T(128)} %bitcast.3.refs_2_, s32[1]{0:T(128)} %bitcast.4.refs_3_, s32[1]{0:T(128)} %bitcast.5.refs_4_, bf16[144,3072]{1,0:T(8,128)(2,1)S(1)} %get-tuple-element.26.refs_9_.refs_5_, ...), custom_call_target="tpu_custom_call" | custom-call | flops 905969664 | bytes 9000000 | tf_op jit(solution)/shard_map/input_grad/pallas_call | solution.py:304
  50.6 1.7 %collective-permute-start.20 = (bf16[192,128]{1,0:T(8,128)(2,1)S(1)}, bf16[192,128]{1,0:T(8,128)(2,1)S(1)}, u32[]{:S(2)}, u32[]{:S(2)}) collective-permute-start(bf16[192,128]{1,0:T(8,128)(2,1)S(1)} %get-tuple-element.44), channel_id=1, source_target_pairs={{0,16},{4,20},{8,24},{12,28},{16,0},{20,4},{24,8},{28,12},{1,17},{... | collective-permute-start | bytes 147464 | tf_op jit(solution)/shard_map/ppermute | solution.py:320
  52.3 0.5 collective-permute-done.15.refs_8_
  52.8 1.7 %collective-permute-start.19 = (bf16[192,128]{1,0:T(8,128)(2,1)S(1)}, bf16[192,128]{1,0:T(8,128)(2,1)S(1)}, u32[]{:S(2)}, u32[]{:S(2)}) collective-permute-start(bf16[192,128]{1,0:T(8,128)(2,1)S(1)} %get-tuple-element.43), channel_id=1, source_target_pairs={{0,16},{4,20},{8,24},{12,28},{16,0},{20,4},{24,8},{28,12},{1,17},{... | collective-permute-start | bytes 147464 | tf_op jit(solution)/shard_map/ppermute | solution.py:320
  54.5 0.5 collective-permute-done.20.refs_8_
  55.0 2.0 %collective-permute-done.19.refs_7_ = bf16[192,128]{1,0:T(8,128)(2,1)S(1)} collective-permute-done((bf16[192,128]{1,0:T(8,128)(2,1)S(1)}, bf16[192,128]{1,0:T(8,128)(2,1)S(1)}, u32[]{:S(2)}, u32[]{:S(2)}) %collective-permute-start.19) | collective-permute-done | bytes 49184 | tf_op jit(solution)/shard_map/ppermute | solution.py:320
  57.0 0.8 %place.1 = f32[6,128,128]{2,1,0:T(8,128)} custom-call(s32[1]{0:T(128)} %bitcast.refs_0_, s32[1]{0:T(128)} %bitcast.2.refs_1_, s32[1]{0:T(128)} %bitcast.3.refs_2_, s32[1]{0:T(128)} %bitcast.4.refs_3_, s32[1]{0:T(128)} %bitcast.5.refs_4_, f32[192,128]{1,0:T(8,128)S(1)} %get-tuple-element.39.refs_5_, f32[192,128]{1,0:T(8,128)S(1)} %get-tuple-element.42.refs_6_, ...), custom_call_target="tpu_custom_call" | custom-call | flops 1000000 | bytes 1000000 | tf_op jit(solution)/shard_map/place/pallas_call | solution.py:304
  (32 shorter events, 1.9 us)
Async XLA Ops:
  0.6 1.2 %copy-start = (f32[9,1024]{1,0:T(8,128)S(1)}, f32[9,1024]{1,0:T(8,128)}, u32[]{:S(2)}) copy-start(f32[9,1024]{1,0:T(8,128)} %param.7) | copy-start | bytes 110596
  2.1 8.0 %collective-permute-start.2 = (bf16[80,1024]{1,0:T(8,128)(2,1)S(1)}, bf16[80,1024]{1,0:T(8,128)(2,1)S(1)}, u32[]{:S(2)}, u32[]{:S(2)}) collective-permute-start(bf16[80,1024]{1,0:T(8,128)(2,1)S(1)} %get-tuple-element.48), channel_id=1, source_target_pairs={{0,28},{4,0},{8,4},{12,8},{16,12},{20,16},{24,20},{28,24},{1,29},{... | collective-permute-start | bytes 491528 | tf_op jit(solution)/shard_map/ppermute | solution.py:356
  5.4 5.1 %collective-permute-start = (bf16[80,1024]{1,0:T(8,128)(2,1)S(1)}, bf16[80,1024]{1,0:T(8,128)(2,1)S(1)}, u32[]{:S(2)}, u32[]{:S(2)}) collective-permute-start(bf16[80,1024]{1,0:T(8,128)(2,1)S(1)} %get-tuple-element.49), channel_id=1, source_target_pairs={{0,4},{4,0},{8,12},{12,8},{16,20},{20,16},{24,28},{28,24},{1,5},{5... | collective-permute-start | bytes 491528 | tf_op jit(solution)/shard_map/ppermute | solution.py:320
  5.4 8.1 %collective-permute-start.1 = (bf16[80,1024]{1,0:T(8,128)(2,1)S(1)}, bf16[80,1024]{1,0:T(8,128)(2,1)S(1)}, u32[]{:S(2)}, u32[]{:S(2)}) collective-permute-start(bf16[80,1024]{1,0:T(8,128)(2,1)S(1)} %get-tuple-element.50), channel_id=1, source_target_pairs={{0,28},{4,8},{8,4},{12,16},{16,12},{20,24},{24,20},{28,0},{1,29},{... | collective-permute-start | bytes 491528 | tf_op jit(solution)/shard_map/ppermute | solution.py:351
  6.2 14.3 %collective-permute-start.5 = (bf16[128,1024]{1,0:T(8,128)(2,1)S(1)}, bf16[128,1024]{1,0:T(8,128)(2,1)S(1)}, u32[]{:S(2)}, u32[]{:S(2)}) collective-permute-start(bf16[128,1024]{1,0:T(8,128)(2,1)S(1)} %slice.35), channel_id=1, source_target_pairs={{0,24},{4,28},{8,16},{12,20},{16,8},{20,12},{24,0},{28,4},{1,25},{... | collective-permute-start | bytes 786440 | tf_op jit(solution)/shard_map/ppermute | solution.py:320
  7.6 16.3 %collective-permute-start.4 = (bf16[128,1024]{1,0:T(8,128)(2,1)S(1)}, bf16[128,1024]{1,0:T(8,128)(2,1)S(1)}, u32[]{:S(2)}, u32[]{:S(2)}) collective-permute-start(bf16[128,1024]{1,0:T(8,128)(2,1)S(1)} %slice.35), channel_id=1, source_target_pairs={{0,16},{4,20},{8,24},{12,28},{16,0},{20,4},{24,8},{28,12},{1,17},{... | collective-permute-start | bytes 786440 | tf_op jit(solution)/shard_map/ppermute | solution.py:320
  10.0 13.8 %collective-permute-start.3 = (bf16[128,1024]{1,0:T(8,128)(2,1)S(1)}, bf16[128,1024]{1,0:T(8,128)(2,1)S(1)}, u32[]{:S(2)}, u32[]{:S(2)}) collective-permute-start(bf16[128,1024]{1,0:T(8,128)(2,1)S(1)} %slice.35), channel_id=1, source_target_pairs={{0,8},{4,12},{8,0},{12,4},{16,24},{20,28},{24,16},{28,20},{1,9},{5... | collective-permute-start | bytes 786440 | tf_op jit(solution)/shard_map/ppermute | solution.py:320
  20.3 8.7 %collective-permute-start.9 = (bf16[128,768]{1,0:T(8,128)(2,1)S(1)}, bf16[128,768]{1,0:T(8,128)(2,1)S(1)}, u32[]{:S(2)}, u32[]{:S(2)}) collective-permute-start(bf16[128,768]{1,0:T(8,128)(2,1)S(1)} %get-tuple-element.45), channel_id=1, source_target_pairs={{0,24},{4,28},{8,16},{12,20},{16,8},{20,12},{24,0},{28,4},{1,25},{... | collective-permute-start | bytes 589832 | tf_op jit(solution)/shard_map/ppermute | solution.py:320
  20.4 11.4 %collective-permute-start.8 = (bf16[128,768]{1,0:T(8,128)(2,1)S(1)}, bf16[128,768]{1,0:T(8,128)(2,1)S(1)}, u32[]{:S(2)}, u32[]{:S(2)}) collective-permute-start(bf16[128,768]{1,0:T(8,128)(2,1)S(1)} %get-tuple-element.46), channel_id=1, source_target_pairs={{0,16},{4,20},{8,24},{12,28},{16,0},{20,4},{24,8},{28,12},{1,17},{... | collective-permute-start | bytes 589832 | tf_op jit(solution)/shard_map/ppermute | solution.py:320
  20.5 11.3 %collective-permute-start.7 = (bf16[128,768]{1,0:T(8,128)(2,1)S(1)}, bf16[128,768]{1,0:T(8,128)(2,1)S(1)}, u32[]{:S(2)}, u32[]{:S(2)}) collective-permute-start(bf16[128,768]{1,0:T(8,128)(2,1)S(1)} %get-tuple-element.47), channel_id=1, source_target_pairs={{0,8},{4,12},{8,0},{12,4},{16,24},{20,28},{24,16},{28,20},{1,9},{5... | collective-permute-start | bytes 589832 | tf_op jit(solution)/shard_map/ppermute | solution.py:320
  23.9 1.4 %collective-permute-start.6 = (bf16[64,1024]{1,0:T(8,128)(2,1)S(1)}, bf16[64,1024]{1,0:T(8,128)(2,1)S(1)}, u32[]{:S(2)}, u32[]{:S(2)}) collective-permute-start(bf16[64,1024]{1,0:T(8,128)(2,1)S(1)} %ends.1), channel_id=1, source_target_pairs={{0,4},{4,0},{8,12},{12,8},{16,20},{20,16},{24,28},{28,24},{1,5},{5... | collective-permute-start | bytes 393224 | tf_op jit(solution)/shard_map/ppermute | solution.py:320
  32.2 1.9 %collective-permute-start.10 = (bf16[768,256]{1,0:T(8,128)(2,1)S(1)}, bf16[768,256]{1,0:T(8,128)(2,1)S(1)}, u32[]{:S(2)}, u32[]{:S(2)}) collective-permute-start(bf16[768,256]{1,0:T(8,128)(2,1)S(1)} %weight_send0.1), channel_id=1, source_target_pairs={{0,4},{4,0},{8,12},{12,8},{16,20},{20,16},{24,28},{28,24},{1,5},{5... | collective-permute-start | bytes 1179656 | tf_op jit(solution)/shard_map/ppermute | solution.py:320
  33.2 1.8 %collective-permute-start.11 = (bf16[768,256]{1,0:T(8,128)(2,1)S(1)}, bf16[768,256]{1,0:T(8,128)(2,1)S(1)}, u32[]{:S(2)}, u32[]{:S(2)}) collective-permute-start(bf16[768,256]{1,0:T(8,128)(2,1)S(1)} %weight_send1.1), channel_id=1, source_target_pairs={{0,4},{4,0},{8,12},{12,8},{16,20},{20,16},{24,28},{28,24},{1,5},{5... | collective-permute-start | bytes 1179656 | tf_op jit(solution)/shard_map/ppermute | solution.py:320
  35.3 5.7 %collective-permute-start.17 = (bf16[192,256]{1,0:T(8,128)(2,1)S(1)}, bf16[192,256]{1,0:T(8,128)(2,1)S(1)}, u32[]{:S(2)}, u32[]{:S(2)}) collective-permute-start(bf16[192,256]{1,0:T(8,128)(2,1)S(1)} %get-tuple-element.41), channel_id=1, source_target_pairs={{0,1},{1,0},{2,3},{3,2},{4,5},{5,4},{6,7},{7,6},{8,9},{9,8},{10,11... | collective-permute-start | bytes 294920 | tf_op jit(solution)/shard_map/ppermute | solution.py:320
  36.9 8.6 %collective-permute-start.14 = (bf16[192,256]{1,0:T(8,128)(2,1)S(1)}, bf16[192,256]{1,0:T(8,128)(2,1)S(1)}, u32[]{:S(2)}, u32[]{:S(2)}) collective-permute-start(bf16[192,256]{1,0:T(8,128)(2,1)S(1)} %get-tuple-element.31.refs_9_), channel_id=1, source_target_pairs={{0,1},{1,0},{2,3},{3,2},{4,5},{5,4},{6,7},{7,6},{8,9},{9,8},{10,11... | collective-permute-start | bytes 294920 | tf_op jit(solution)/shard_map/ppermute | solution.py:320
  37.4 13.2 %collective-permute-start.12 = (bf16[192,256]{1,0:T(8,128)(2,1)S(1)}, bf16[192,256]{1,0:T(8,128)(2,1)S(1)}, u32[]{:S(2)}, u32[]{:S(2)}) collective-permute-start(bf16[192,256]{1,0:T(8,128)(2,1)S(1)} %get-tuple-element.33), channel_id=1, source_target_pairs={{0,8},{4,12},{8,0},{12,4},{16,24},{20,28},{24,16},{28,20},{1,9},{5... | collective-permute-start | bytes 294920 | tf_op jit(solution)/shard_map/ppermute | solution.py:320
  38.8 11.7 %collective-permute-start.16 = (bf16[192,256]{1,0:T(8,128)(2,1)S(1)}, bf16[192,256]{1,0:T(8,128)(2,1)S(1)}, u32[]{:S(2)}, u32[]{:S(2)}) collective-permute-start(bf16[192,256]{1,0:T(8,128)(2,1)S(1)} %get-tuple-element.37), channel_id=1, source_target_pairs={{0,9},{1,8},{2,11},{3,10},{4,13},{5,12},{6,15},{7,14},{8,1},{9,0},... | collective-permute-start | bytes 294920 | tf_op jit(solution)/shard_map/ppermute | solution.py:327
  41.0 9.6 %collective-permute-start.18 = (bf16[192,256]{1,0:T(8,128)(2,1)S(1)}, bf16[192,256]{1,0:T(8,128)(2,1)S(1)}, u32[]{:S(2)}, u32[]{:S(2)}) collective-permute-start(bf16[192,256]{1,0:T(8,128)(2,1)S(1)} %forward_other.1), channel_id=1, source_target_pairs={{0,11},{1,10},{2,9},{3,8},{4,15},{5,14},{6,13},{7,12},{8,3},{9,2},... | collective-permute-start | bytes 294920 | tf_op jit(solution)/shard_map/ppermute | solution.py:327
  45.5 6.8 %collective-permute-start.13 = (bf16[192,256]{1,0:T(8,128)(2,1)S(1)}, bf16[192,256]{1,0:T(8,128)(2,1)S(1)}, u32[]{:S(2)}, u32[]{:S(2)}) collective-permute-start(bf16[192,256]{1,0:T(8,128)(2,1)S(1)} %get-tuple-element.35), channel_id=1, source_target_pairs={{0,1},{1,0},{2,3},{3,2},{4,5},{5,4},{6,7},{7,6},{8,9},{9,8},{10,11... | collective-permute-start | bytes 294920 | tf_op jit(solution)/shard_map/ppermute | solution.py:320
  45.5 7.2 %collective-permute-start.15 = (bf16[192,256]{1,0:T(8,128)(2,1)S(1)}, bf16[192,256]{1,0:T(8,128)(2,1)S(1)}, u32[]{:S(2)}, u32[]{:S(2)}) collective-permute-start(bf16[192,256]{1,0:T(8,128)(2,1)S(1)} %forward_same.1), channel_id=1, source_target_pairs={{0,3},{1,2},{2,1},{3,0},{4,7},{5,6},{6,5},{7,4},{8,11},{9,10},{10,... | collective-permute-start | bytes 294920 | tf_op jit(solution)/shard_map/ppermute | solution.py:320
  50.6 4.4 %collective-permute-start.20 = (bf16[192,128]{1,0:T(8,128)(2,1)S(1)}, bf16[192,128]{1,0:T(8,128)(2,1)S(1)}, u32[]{:S(2)}, u32[]{:S(2)}) collective-permute-start(bf16[192,128]{1,0:T(8,128)(2,1)S(1)} %get-tuple-element.44), channel_id=1, source_target_pairs={{0,16},{4,20},{8,24},{12,28},{16,0},{20,4},{24,8},{28,12},{1,17},{... | collective-permute-start | bytes 147464 | tf_op jit(solution)/shard_map/ppermute | solution.py:320
  52.8 4.2 %collective-permute-start.19 = (bf16[192,128]{1,0:T(8,128)(2,1)S(1)}, bf16[192,128]{1,0:T(8,128)(2,1)S(1)}, u32[]{:S(2)}, u32[]{:S(2)}) collective-permute-start(bf16[192,128]{1,0:T(8,128)(2,1)S(1)} %get-tuple-element.43), channel_id=1, source_target_pairs={{0,16},{4,20},{8,24},{12,28},{16,0},{20,4},{24,8},{28,12},{1,17},{... | collective-permute-start | bytes 147464 | tf_op jit(solution)/shard_map/ppermute | solution.py:320
